TPU v7x, 32 devices: a whole 2x2x4 slice. The times are simulated.
32 devices in a mesh: shard: 8 (over y, x, core), tensor: 4 (over z).
Axes of the slice: x: 2, y: 2, z: 4, core: 2. Of those that a mesh axis runs over, the one named last changes fastest.
Arguments:
- grads: bfloat16 [32, 1024, 1024], P(None, 'shard', 'tensor'), may hold values from -48 to 48
- momentum: float32 [32, 1024, 1024], P(None, 'shard', 'tensor'), may hold values from -6 to 6
Outputs:
- momentum_next: float32 [32, 1024, 1024], P(None, 'shard', 'tensor')
- update: bfloat16 [32, 1024, 1024], P(None, 'shard', 'tensor')
All inputs are finite; a program needn't handle non-finite values.
Results may differ from a plain program's by a relative error of at most 0.012.
Values may be sent and summed in bfloat16 or wider, within the bound.
No kernel may reach another device: no remote copies, remote signals or barrier semaphores. Data moves between devices by JAX's collectives and lax.ppermute only.
A program may use at most 64 MiB of HBM per device.

v0:
```python
import jax
import jax.numpy as jnp
from jax import lax
from jax.sharding import PartitionSpec as P

NS_STEPS = 2


def orthogonalize(whole, norm_value):
    current = (whole.astype(jnp.float32) / (norm_value + 1e-07)).astype(jnp.bfloat16)
    for step in range(NS_STEPS):
        gram = lax.dot_general(
            current, current, (((1,), (1,)), ((), ())), preferred_element_type=jnp.float32
        ).astype(jnp.bfloat16)
        power_f = jnp.dot(gram, current, preferred_element_type=jnp.float32)
        power = power_f.astype(jnp.bfloat16)
        square = jnp.dot(gram, power, preferred_element_type=jnp.float32)
        current = (3.4445 * current.astype(jnp.float32) - 4.775 * power_f + 2.0315 * square).astype(
            jnp.bfloat16
        )
    scale = 0.2 * float(whole.shape[0]) ** 0.5
    return (scale * current.astype(jnp.float32)).astype(jnp.bfloat16)


def shards(grads, momentum):
    grads_f = grads.astype(jnp.float32)
    momentum_next = 0.95 * momentum + grads_f
    nesterov = (grads_f + 0.95 * momentum_next).astype(jnp.bfloat16)
    count = nesterov.shape[0]
    row_part = nesterov.shape[1]
    col_part = nesterov.shape[2]
    shard_count = lax.axis_size("shard")
    tensor_count = lax.axis_size("tensor")
    sending = (
        nesterov.reshape(shard_count, tensor_count, row_part, col_part)
        .transpose(1, 0, 2, 3)
        .reshape(count, row_part, col_part)
    )
    first = lax.all_to_all(sending, "tensor", split_axis=0, concat_axis=2, tiled=True)
    whole = lax.all_to_all(first, "shard", split_axis=0, concat_axis=1, tiled=True)
    block = whole[0]
    block_f = block.astype(jnp.float32)
    norm_value = jnp.sqrt(jnp.sum(block_f * block_f))
    result = orthogonalize(block, norm_value)[None]
    back_rows = lax.all_to_all(result, "shard", split_axis=1, concat_axis=0, tiled=True)
    back = lax.all_to_all(back_rows, "tensor", split_axis=2, concat_axis=0, tiled=True)
    update = (
        back.reshape(tensor_count, shard_count, row_part, col_part)
        .transpose(1, 0, 2, 3)
        .reshape(count, row_part, col_part)
    )
    return (momentum_next, update)


def solution(mesh):
    return jax.shard_map(
        shards,
        mesh=mesh,
        in_specs=(P(None, "shard", "tensor"), P(None, "shard", "tensor")),
        out_specs=(P(None, "shard", "tensor"), P(None, "shard", "tensor")),
        check_vma=False,
    )
```

profile of v0, /device:TPU:0, one launch (start us, length us, event | category | flops | bytes accessed | tf_op | source)
XLA Modules:
  0.0 233.1 jit_solution(9498455637912090614)
XLA Ops:
  0.6 5.9 %fusion = (bf16[32,128,256]{2,1,0:T(8,128)(2,1)S(1)}, f32[32,128,256]{2,1,0:T(8,128)}) fusion(bf16[32,128,256]{2,1,0:T(8,128)(2,1)} %param.2, f32[32,128,256]{2,1,0:T(8,128)} %param.3), kind=kLoop, calls=%fused_computation.4 | loop fusion | flops 6291456 | bytes 12582912 | tf_op jit(solution)/shard_map/convert_element_type | solution.py:28
  6.5 0.1 copy.13
  6.7 54.3 %all_to_all.48 = bf16[32,128,256]{2,1,0:T(8,128)(2,1)S(1)} all-to-all(bf16[32,128,256]{2,1,0:T(8,128)(2,1)S(1)} %bitcast.30), channel_id=1, replica_groups=mesh['shard'=8,'tensor'=4] {'tensor'}, dimensions={0} | all-to-all | bytes 4194304 | tf_op jit(solution)/shard_map/all_to_all | solution.py:39
  61.0 2.4 %copy.14 = bf16[8,128,4,256]{1,3,2,0:T(8,128)(2,1)} copy(bf16[8,128,4,256]{3,1,0,2:T(8,128)(2,1)S(1)} %bitcast.31) | data formatting | bytes 4194304 | tf_op jit(solution)/shard_map/all_to_all | solution.py:39
  63.4 30.3 %all_to_all.49 = bf16[8,128,1024]{1,2,0:T(8,128)(2,1)S(1)} all-to-all(bf16[8,128,1024]{1,2,0:T(8,128)(2,1)} %bitcast.32), channel_id=1, replica_groups=mesh['shard'=8,'tensor'=4] {'shard'}, dimensions={0} | all-to-all | bytes 4194304 | tf_op jit(solution)/shard_map/all_to_all | solution.py:40
  93.7 1.7 fusion.1
  96.0 1.7 fusion.2
  97.8 3.0 %copy.15 = bf16[8,128,1024]{2,1,0:T(8,128)(2,1)S(1)} copy(bf16[8,128,1024]{1,2,0:T(8,128)(2,1)} %fusion.2) | data formatting | bytes 4194304 | tf_op jit(solution)/shard_map/convert_element_type | solution.py:10
  100.8 2.4 %convolution_convert_fusion.1 = bf16[1024,1024]{1,0:T(8,128)(2,1)S(1)} fusion(bf16[1024,1024]{1,0:T(8,128)(2,1)S(1)} %bitcast.35), kind=kOutput, calls=%fused_computation.15 | convolution fusion | flops 2148532224 | bytes 4194304 | tf_op jit(solution)/shard_map/dot_general | solution.py:12
  103.2 2.4 %fusion.9 = f32[1024,1024]{1,0:T(8,128)S(1)} fusion(bf16[1024,1024]{1,0:T(8,128)(2,1)S(1)} %convolution_convert_fusion.1, bf16[1024,1024]{1,0:T(8,128)(2,1)S(1)} %bitcast.36), kind=kOutput, calls=%fused_computation.18 | convolution fusion | flops 2147483648 | bytes 8388608 | tf_op jit(solution)/shard_map/dot_general | solution.py:15
  105.5 2.7 %add_convert_fusion.1 = bf16[1024,1024]{1,0:T(8,128)(2,1)S(1)} fusion(f32[1024,1024]{1,0:T(8,128)S(1)} %fusion.9, bf16[1024,1024]{1,0:T(8,128)(2,1)S(1)} %bitcast.37, bf16[1024,1024]{1,0:T(8,128)(2,1)S(1)} %convolution_convert_fusion.1), kind=kOutput, calls=%fused_computation.9 | convolution fusion | flops 2155872256 | bytes 10485760 | tf_op jit(solution)/shard_map/dot_general | solution.py:17
  108.2 2.4 %convolution_convert_fusion = bf16[1024,1024]{1,0:T(8,128)(2,1)S(1)} fusion(bf16[1024,1024]{1,0:T(8,128)(2,1)S(1)} %add_convert_fusion.1), kind=kOutput, calls=%fused_computation.14 | convolution fusion | flops 2148532224 | bytes 4194304 | tf_op jit(solution)/shard_map/dot_general | solution.py:12
  110.6 2.3 %fusion.10 = f32[1024,1024]{1,0:T(8,128)S(1)} fusion(bf16[1024,1024]{1,0:T(8,128)(2,1)S(1)} %convolution_convert_fusion, bf16[1024,1024]{1,0:T(8,128)(2,1)S(1)} %add_convert_fusion.1), kind=kOutput, calls=%fused_computation.19 | convolution fusion | flops 2147483648 | bytes 8388608 | tf_op jit(solution)/shard_map/dot_general | solution.py:15
  112.9 2.7 %fusion.3 = bf16[1,1024,1024]{2,1,0:T(8,128)(2,1)S(1)} fusion(bf16[1024,1024]{1,0:T(8,128)(2,1)S(1)} %convolution_convert_fusion, f32[1024,1024]{1,0:T(8,128)S(1)} %fusion.10, bf16[1024,1024]{1,0:T(8,128)(2,1)S(1)} %add_convert_fusion.1), kind=kOutput, calls=%fused_computation.10 | convolution fusion | flops 2159017984 | bytes 10485760 | tf_op jit(solution)/shard_map/dot_general | solution.py:17
  115.7 5.4 %copy.22 = bf16[1,1024,1024]{2,0,1:T(2,128)(2,1)} copy(bf16[1,1024,1024]{2,1,0:T(8,128)(2,1)S(1)} %fusion.3) | data formatting | bytes 4194304 | tf_op jit(solution)/shard_map/broadcast_in_dim | solution.py:44
  121.1 0.5 broadcast.36
  121.6 12.8 %reduce.3 = bf16[1024,1024]{1,0:T(8,128)(2,1)S(1)} reduce(bf16[1024,1,1024]{2,1,0:T(2,128)(2,1)} %bitcast.27, bf16[]{:T(256)} %broadcast.36), dimensions={1}, to_apply=%bitcast.26.reduce_sub_computation | reduce | bytes 4194306
  134.4 3.8 %reshape.37 = bf16[8,2,65536]{2,1,0:T(2,128)(2,1)} reshape(bf16[1024,1024]{1,0:T(8,128)(2,1)S(1)} %reduce.3) | data formatting | bytes 4194304
  138.2 30.1 %all_to_all.50 = bf16[8,2,65536]{2,1,0:T(2,128)(2,1)S(1)} all-to-all(bf16[8,2,65536]{2,1,0:T(2,128)(2,1)} %reshape.37), channel_id=1, replica_groups=mesh['shard'=8,'tensor'=4] {'shard'}, dimensions={0} | all-to-all | bytes 4194304 | tf_op jit(solution)/shard_map/all_to_all | solution.py:45
  168.3 4.4 %reshape.38 = bf16[1024,1,1024]{2,1,0:T(2,128)(2,1)} reshape(bf16[8,2,65536]{2,1,0:T(2,128)(2,1)S(1)} %all_to_all.50) | data formatting | bytes 4194304
  172.7 3.0 %copy.20 = bf16[1,1024,1024]{2,1,0:T(8,128)(2,1)S(1)} copy(bf16[1,1024,1024]{2,0,1:T(2,128)(2,1)} %bitcast.28) | data formatting | bytes 4194304
  175.7 2.9 %copy.17 = bf16[8,128,1024]{1,0,2:T(8,128)(2,1)} copy(bf16[8,128,1024]{2,1,0:T(8,128)(2,1)S(1)} %bitcast.29) | data formatting | bytes 4194304 | tf_op jit(solution)/shard_map/all_to_all | solution.py:45
  178.6 51.4 %all_to_all.51 = bf16[8,128,1024]{1,0,2:T(8,128)(2,1)S(1)} all-to-all(bf16[8,128,1024]{1,0,2:T(8,128)(2,1)} %copy.17), channel_id=1, replica_groups=mesh['shard'=8,'tensor'=4] {'tensor'}, dimensions={2} | all-to-all | bytes 4194304 | tf_op jit(solution)/shard_map/all_to_all | solution.py:46
  230.0 0.1 fusion.8
  230.1 0.2 pad_maximum_fusion
  230.3 2.7 %copy.19 = bf16[8,512,256]{2,1,0:T(8,128)(2,1)} copy(bf16[8,512,256]{1,0,2:T(8,128)(2,1)S(1)} %pad_maximum_fusion) | data formatting | bytes 4194304
where the time goes:
time: 234 us; the launch traced here: 233 us
  blocking collectives  166 us (71%)
  local copies, waits for them, and re-layouts  28.4 us (12%)
  other arithmetic  22.3 us (10%)
  matrix products  14.9 us (6%)
    all_to_all x1, blocking collectives, shards(): lax.all_to_all(sending, 'tensor', split_axis=0, concat_axis=2, tiled=True)  54.3 us
    all_to_all x1, blocking collectives, shards(): lax.all_to_all(back_rows, 'tensor', split_axis=2, concat_axis=0, tiled=True)  51.4 us
    all_to_all x1, blocking collectives, shards(): lax.all_to_all(first, 'shard', split_axis=0, concat_axis=1, tiled=True)  30.3 us
    all_to_all x1, blocking collectives, shards(): lax.all_to_all(result, 'shard', split_axis=1, concat_axis=0, tiled=True)  30.1 us
    unnamed x5, local copies, waits for them, and re-layouts  14.4 us
    unnamed x1, other arithmetic  12.8 us
    convert_element_type x1, other arithmetic, shards(): nesterov = (grads_f + 0.95 * momentum_next).astype(jnp.bfloat16)  5.91 us
    dot_general x2, matrix products, orthogonalize(): square = jnp.dot(gram, power, preferred_element_type=jnp.float32)  5.43 us

commit v1 on v0

v1 whole, which is shorter than its diff:
```python
import jax
import jax.numpy as jnp
from jax import lax
from jax.sharding import PartitionSpec as P

NS_STEPS = 2


def dot_rows(left, right):
    return lax.dot_general(left, right, (((1,), (1,)), ((), ())), preferred_element_type=jnp.float32)


def dot(left, right):
    return jnp.dot(left, right, preferred_element_type=jnp.float32)


def chain(first, *rest):
    return lax.optimization_barrier((first,) + rest)


def swap(piece, count, k):
    return lax.ppermute(piece, "tensor", [(t, t ^ k) for t in range(count)])


def spread(piece):
    return lax.all_to_all(piece, "shard", split_axis=0, concat_axis=0, tiled=True)


def exchange(pieces, count):
    half = count // 2
    out = {}
    early = swap(pieces[half], count, half)
    late = [k for k in range(half + 1, count)]
    for k in reversed(late):
        out[k] = swap(spread(pieces[k]), count, k)
    rest = [k for k in range(half)]
    both = jnp.concatenate([pieces[k] for k in rest], axis=1)
    both = spread(both)
    rows = pieces[0].shape[1]
    for i, k in enumerate(rest):
        part = both[:, i * rows : (i + 1) * rows]
        out[k] = part if k == 0 else swap(part, count, k)
    out[half] = spread(early)
    return out


def shards(grads, momentum):
    grads_f = grads.astype(jnp.float32)
    momentum_next = 0.95 * momentum + grads_f
    shard_count = lax.axis_size("shard")
    tensor_count = lax.axis_size("tensor")
    count, row_part, col_part = grads.shape
    me = lax.axis_index("tensor")

    def nesterov(k):
        start = (me ^ k) * shard_count
        g = lax.dynamic_slice_in_dim(grads, start, shard_count, 0).astype(jnp.float32)
        m = lax.dynamic_slice_in_dim(momentum, start, shard_count, 0)
        return (g + 0.95 * (0.95 * m + g)).astype(jnp.bfloat16)

    pieces = {k: nesterov(k) for k in range(tensor_count)}
    got = exchange(pieces, tensor_count)
    order = shard_count * row_part
    xs = {k: got[k].reshape(order, col_part) for k in got}

    total = sum(jnp.sum(jnp.square(x.astype(jnp.float32))) for x in xs.values())
    scale = 1.0 / (jnp.sqrt(total) + 1e-07)
    for step in range(NS_STEPS):
        gram = sum(dot_rows(x, x) for x in xs.values())
        if step == 0:
            gram = gram * (scale * scale)
        gram = gram.astype(jnp.bfloat16)
        new = {}
        for k, x in xs.items():
            power_f = dot(gram, x)
            current = x.astype(jnp.float32)
            if step == 0:
                power_f = power_f * scale
                current = current * scale
            square = dot(gram, power_f.astype(jnp.bfloat16))
            new[k] = (3.4445 * current - 4.775 * power_f + 2.0315 * square).astype(jnp.bfloat16)
        xs = new
    gain = 0.2 * float(order) ** 0.5
    back = {
        k: (gain * x.astype(jnp.float32)).astype(jnp.bfloat16).reshape(shard_count, row_part, col_part)
        for k, x in xs.items()
    }
    done = exchange(back, tensor_count)
    update = jnp.zeros(grads.shape, jnp.bfloat16)
    for k in range(tensor_count):
        update = lax.dynamic_update_slice_in_dim(update, done[k], (me ^ k) * shard_count, 0)
    return (momentum_next, update)


def solution(mesh):
    return jax.shard_map(
        shards,
        mesh=mesh,
        in_specs=(P(None, "shard", "tensor"), P(None, "shard", "tensor")),
        out_specs=(P(None, "shard", "tensor"), P(None, "shard", "tensor")),
        check_vma=False,
    )
```

time: 234 us -> 165 us (0.71)
  blocking collectives: 166 us -> 0 us
  waiting for transfers between devices: 0 us -> 73.9 us
  starting transfers between devices: 0 us -> 34.2 us
  local copies, waits for them, and re-layouts: 28.4 us -> 8.5 us
  matrix products: 14.9 us -> 29.2 us
  other arithmetic: 22.3 us -> 15 us
    all_to_all x4 -> x0, blocking collectives: 166 us -> none  [the longest x1 54.3 us: shards(): lax.all_to_all(sending, 'tensor', split_axis=0, concat_axis=2, tiled=True)]
    ppermute x0 -> x6, waiting for transfers between devices: none -> 47.6 us  [swap(): return lax.ppermute(piece, 'tensor', [(t, t ^ k) for t in range(count)])]
    all_to_all x0 -> x6, waiting for transfers between devices: none -> 26.3 us  [spread(): lax.all_to_all(piece, 'shard', split_axis=0, concat_axis=0, tiled=True)]
    all_to_all x0 -> x6, starting transfers between devices: none -> 24.3 us  [spread(): lax.all_to_all(piece, 'shard', split_axis=0, concat_axis=0, tiled=True)]
    dot_general x6 -> x24, matrix products: 14.9 us -> 29.2 us  [the longest x16 16.7 us: dot(): return jnp.dot(left, right, preferred_element_type=jnp.float32)]
    unnamed x5 -> x10, local copies, waits for them, and re-layouts: 14.4 us -> 1.51 us
    unnamed x1 -> x0, other arithmetic: 12.8 us -> none
    ppermute x0 -> x6, starting transfers between devices: none -> 9.94 us  [swap(): return lax.ppermute(piece, 'tensor', [(t, t ^ k) for t in range(count)])]
  transfers between devices with their start and end apart: 0 -> 12, of which waited for: 0 -> 7; matrix products, arithmetic and copies ran while one was open for 0% -> 16% of each run, Pallas kernels for 0% -> 0%
where the time goes in v1:
time: 165 us; the launch traced here: 164 us
  waiting for transfers between devices  73.9 us (45%)
  starting transfers between devices  34.2 us (21%)
  matrix products  29.2 us (18%)
  other arithmetic  15 us (9%)
  local copies, waits for them, and re-layouts  8.5 us (5%)
  between operations  3.43 us (2%)
    ppermute x6, waiting for transfers between devices, swap(): return lax.ppermute(piece, 'tensor', [(t, t ^ k) for t in range(count)])  47.6 us
    all_to_all x6, waiting for transfers between devices, spread(): lax.all_to_all(piece, 'shard', split_axis=0, concat_axis=0, tiled=True)  26.3 us
    all_to_all x6, starting transfers between devices, spread(): lax.all_to_all(piece, 'shard', split_axis=0, concat_axis=0, tiled=True)  24.3 us
    dot_general x16, matrix products, dot(): return jnp.dot(left, right, preferred_element_type=jnp.float32)  16.7 us
    dot_general x8, matrix products, dot_rows(): lax.dot_general(left, right, (((1,), (1,)), ((), ())), preferred_element_...  12.5 us
    ppermute x6, starting transfers between devices, swap(): return lax.ppermute(piece, 'tensor', [(t, t ^ k) for t in range(count)])  9.94 us
    add x1, other arithmetic, shards(): momentum_next = 0.95 * momentum + grads_f  5.06 us
    convert_element_type x1, other arithmetic, nesterov(): return (g + 0.95 * (0.95 * m + g)).astype(jnp.bfloat16)  4.4 us
  transfers between devices with their start and end apart: 12, of which 7 were waited for; matrix products, arithmetic and copies ran while one was open for 16% of the time, Pallas kernels for 0%

profile of v1, /device:TPU:0, one launch (start us, length us, event | category | flops | bytes accessed | tf_op | source)
XLA Modules:
  0.0 164.3 jit_solution(14984073138762841082)
XLA Ops:
  0.7 4.4 %fusion.29 = (bf16[8,128,256]{2,1,0:T(8,128)(2,1)}, bf16[8,128,256]{2,1,0:T(8,128)(2,1)S(1)}, bf16[8,128,256]{2,1,0:T(8,128)(2,1)S(1)}, bf16[8,128,256]{2,1,0:T(8,128)(2,1)S(1)}) fusion(f32[32,128,256]{2,1,0:T(8,128)} %param.3, s32[]{:T(128)S(6)} %select_n.10, bf16[32,128,256]{2,1,0:T(8,128)(2,1)} %param.2, s32[]{:T(128)S(6)} %select_n.9, s32[]{:T(128)S(6)} %select_n.8, ...), kind=kLoop, calls=%fused_computation.52 | loop fusion | flops 6291456 | bytes 8388624 | tf_op jit(solution)/shard_map/convert_element_type | solution.py:59
  5.1 5.2 %all-to-all-start.1 = ((bf16[8,128,256]{2,1,0:T(8,128)(2,1)}), bf16[8,128,256]{2,1,0:T(8,128)(2,1)}, u32[]{:S(2)}, u32[]{:S(2)}) async-start(bf16[8,128,256]{2,1,0:T(8,128)(2,1)} %get-tuple-element.2), calls=%async_computation.1 | async-start | bytes 1048576 | tf_op jit(solution)/shard_map/all_to_all | solution.py:26
  10.2 1.0 pad_maximum_fusion
  11.3 8.8 %all-to-all-done.1 = bf16[8,128,256]{2,1,0:T(8,128)(2,1)} async-done(((bf16[8,128,256]{2,1,0:T(8,128)(2,1)}), bf16[8,128,256]{2,1,0:T(8,128)(2,1)}, u32[]{:S(2)}, u32[]{:S(2)}) %all-to-all-start.1) | async-done | bytes 524320 | tf_op jit(solution)/shard_map/all_to_all | solution.py:26
  20.1 3.6 %all-to-all-start = ((bf16[8,256,256]{2,1,0:T(8,128)(2,1)}), bf16[8,256,256]{2,1,0:T(8,128)(2,1)S(1)}, u32[]{:S(2)}, u32[]{:S(2)}) async-start(bf16[8,256,256]{2,1,0:T(8,128)(2,1)} %pad_maximum_fusion), calls=%async_computation | async-start | bytes 2097152 | tf_op jit(solution)/shard_map/all_to_all | solution.py:26
  23.6 3.0 %collective-permute-start.2 = (bf16[8,128,256]{2,1,0:T(8,128)(2,1)S(1)}, bf16[8,128,256]{2,1,0:T(8,128)(2,1)}, u32[]{:S(2)}, u32[]{:S(2)}) collective-permute-start(bf16[8,128,256]{2,1,0:T(8,128)(2,1)S(1)} %get-tuple-element.5), channel_id=1, source_target_pairs={{0,2},{1,3},{2,0},{3,1},{4,6},{5,7},{6,4},{7,5},{8,10},{9,11},{10,... | collective-permute-start | bytes 1572872 | tf_op jit(solution)/shard_map/ppermute | solution.py:22
  26.6 1.3 collective-permute-start
  28.0 33.9 %collective-permute-done.2 = bf16[8,128,256]{2,1,0:T(8,128)(2,1)} collective-permute-done((bf16[8,128,256]{2,1,0:T(8,128)(2,1)S(1)}, bf16[8,128,256]{2,1,0:T(8,128)(2,1)}, u32[]{:S(2)}, u32[]{:S(2)}) %collective-permute-start.2) | collective-permute-done | bytes 524320 | tf_op jit(solution)/shard_map/ppermute | solution.py:22
  61.9 4.1 %all-to-all-start.2 = ((bf16[8,128,256]{2,1,0:T(8,128)(2,1)}), bf16[8,128,256]{2,1,0:T(8,128)(2,1)S(1)}, u32[]{:S(2)}, u32[]{:S(2)}) async-start(bf16[8,128,256]{2,1,0:T(8,128)(2,1)} %collective-permute-done.2), calls=%async_computation.2 | async-start | bytes 1048576 | tf_op jit(solution)/shard_map/all_to_all | solution.py:26
  68.0 2.7 %fusion.47 = f32[1024,1024]{1,0:T(8,128)} fusion(bf16[1024,256]{1,0:T(8,128)(2,1)S(1)} %bitcast.57), kind=kOutput, calls=%fused_computation.78 | convolution fusion | flops 536870912 | bytes 4718592 | tf_op jit(solution)/shard_map/dot_general | solution.py:10
  72.8 2.9 %all-to-all-done.2 = bf16[8,128,256]{2,1,0:T(8,128)(2,1)S(1)} async-done(((bf16[8,128,256]{2,1,0:T(8,128)(2,1)}), bf16[8,128,256]{2,1,0:T(8,128)(2,1)S(1)}, u32[]{:S(2)}, u32[]{:S(2)}) %all-to-all-start.2) | async-done | bytes 524320 | tf_op jit(solution)/shard_map/all_to_all | solution.py:26
  76.6 2.7 %fusion.46 = f32[1024,1024]{1,0:T(8,128)} fusion(bf16[1024,256]{1,0:T(8,128)(2,1)S(1)} %bitcast.51), kind=kOutput, calls=%fused_computation.77 | convolution fusion | flops 536870912 | bytes 4718592 | tf_op jit(solution)/shard_map/dot_general | solution.py:10
  79.3 2.1 %collective-permute-done.1 = bf16[8,128,256]{2,1,0:T(8,128)(2,1)S(1)} collective-permute-done((bf16[8,128,256]{2,1,0:T(8,128)(2,1)}, bf16[8,128,256]{2,1,0:T(8,128)(2,1)S(1)}, u32[]{:S(2)}, u32[]{:S(2)}) %collective-permute-start.1) | collective-permute-done | bytes 524320 | tf_op jit(solution)/shard_map/ppermute | solution.py:22
  84.3 1.4 copy-done
  85.7 3.3 %multiply_convert_fusion = bf16[1024,1024]{1,0:T(8,128)(2,1)S(1)} fusion(f32[1024,1024]{1,0:T(8,128)S(1)} %fusion.48, f32[1024,1024]{1,0:T(8,128)} %fusion.46, f32[1024,1024]{1,0:T(8,128)S(1)} %copy-done, f32[]{:T(128)S(6)} %mul.190, bf16[1024,256]{1,0:T(8,128)(2,1)S(1)} %bitcast.48), kind=kOutput, calls=%fused_computation.1 | convolution fusion | flops 542113792 | bytes 15204356 | tf_op jit(solution)/shard_map/dot_general | solution.py:10
  98.3 1.7 %fusion.54 = f32[1024,256]{1,0:T(8,128)} fusion(bf16[1024,1024]{1,0:T(8,128)(2,1)S(1)} %add_convert_fusion, bf16[1024,256]{1,0:T(8,128)(2,1)S(1)} %fusion.7), kind=kOutput, calls=%fused_computation.85 | convolution fusion | flops 536870912 | bytes 3670016 | tf_op jit(solution)/shard_map/dot_general | solution.py:14
  100.7 0.9 fusion.53
  103.2 1.0 pad_maximum_fusion.1
  104.3 3.8 %all-to-all-start.3 = ((bf16[8,256,256]{2,1,0:T(8,128)(2,1)}), bf16[8,256,256]{2,1,0:T(8,128)(2,1)S(1)}, u32[]{:S(2)}, u32[]{:S(2)}) async-start(bf16[8,256,256]{2,1,0:T(8,128)(2,1)} %pad_maximum_fusion.1), calls=%async_computation.3 | async-start | bytes 2097152 | tf_op jit(solution)/shard_map/all_to_all | solution.py:26
  108.1 3.4 %fusion.22 = bf16[1024,256]{1,0:T(8,128)(2,1)} fusion(bf16[1024,1024]{1,0:T(8,128)(2,1)S(1)} %add_convert_fusion, f32[1024,256]{1,0:T(8,128)} %fusion.54, bf16[1024,256]{1,0:T(8,128)(2,1)} %copy-done.4), kind=kOutput, calls=%fused_computation.45 | convolution fusion | flops 539754496 | bytes 4194304 | tf_op jit(solution)/shard_map/dot_general | solution.py:14
  111.5 2.0 %collective-permute-start.4 = (bf16[8,128,256]{2,1,0:T(8,128)(2,1)}, bf16[8,128,256]{2,1,0:T(8,128)(2,1)}, u32[]{:S(2)}, u32[]{:S(2)}) collective-permute-start(bf16[8,128,256]{2,1,0:T(8,128)(2,1)} %bitcast.6), channel_id=1, source_target_pairs={{0,2},{1,3},{2,0},{3,1},{4,6},{5,7},{6,4},{7,5},{8,10},{9,11},{10,... | collective-permute-start | bytes 1572872 | tf_op jit(solution)/shard_map/ppermute | solution.py:22
  114.2 1.6 fusion.23
  115.8 7.7 %all-to-all-done.3 = bf16[8,256,256]{2,1,0:T(8,128)(2,1)S(1)} async-done(((bf16[8,256,256]{2,1,0:T(8,128)(2,1)}), bf16[8,256,256]{2,1,0:T(8,128)(2,1)S(1)}, u32[]{:S(2)}, u32[]{:S(2)}) %all-to-all-start.3) | async-done | bytes 1048608 | tf_op jit(solution)/shard_map/all_to_all | solution.py:26
  123.5 4.1 %all-to-all-start.5 = ((bf16[8,128,256]{2,1,0:T(8,128)(2,1)}), bf16[8,128,256]{2,1,0:T(8,128)(2,1)}, u32[]{:S(2)}, u32[]{:S(2)}) async-start(bf16[8,128,256]{2,1,0:T(8,128)(2,1)} %bitcast.60), calls=%async_computation.5 | async-start | bytes 1048576 | tf_op jit(solution)/shard_map/all_to_all | solution.py:26
  127.7 1.6 broadcast_in_dim.3
  129.3 1.0 fusion.44
  130.6 6.9 %all-to-all-done.5 = bf16[8,128,256]{2,1,0:T(8,128)(2,1)} async-done(((bf16[8,128,256]{2,1,0:T(8,128)(2,1)}), bf16[8,128,256]{2,1,0:T(8,128)(2,1)}, u32[]{:S(2)}, u32[]{:S(2)}) %all-to-all-start.5) | async-done | bytes 524320 | tf_op jit(solution)/shard_map/all_to_all | solution.py:26
  137.4 3.1 %collective-permute-start.5 = (bf16[8,128,256]{2,1,0:T(8,128)(2,1)}, bf16[8,128,256]{2,1,0:T(8,128)(2,1)S(1)}, u32[]{:S(2)}, u32[]{:S(2)}) collective-permute-start(bf16[8,128,256]{2,1,0:T(8,128)(2,1)} %all-to-all-done.5), channel_id=1, source_target_pairs={{0,3},{1,2},{2,1},{3,0},{4,7},{5,6},{6,5},{7,4},{8,11},{9,10},{10,... | collective-permute-start | bytes 1572872 | tf_op jit(solution)/shard_map/ppermute | solution.py:22
  140.6 3.5 %all-to-all-start.4 = ((bf16[8,128,256]{2,1,0:T(8,128)(2,1)}), bf16[8,128,256]{2,1,0:T(8,128)(2,1)S(1)}, u32[]{:S(2)}, u32[]{:S(2)}) async-start(bf16[8,128,256]{2,1,0:T(8,128)(2,1)} %collective-permute-done.4), calls=%async_computation.4 | async-start | bytes 1048576 | tf_op jit(solution)/shard_map/all_to_all | solution.py:26
  144.1 5.1 %convert_add_fusion = f32[32,128,256]{2,1,0:T(8,128)} fusion(bf16[32,128,256]{2,1,0:T(8,128)(2,1)S(1)} %copy-done.1, f32[32,128,256]{2,1,0:T(8,128)} %param.3), kind=kLoop, calls=%fused_computation.2 | loop fusion | flops 3145728 | bytes 10485760 | tf_op jit(solution)/shard_map/add | solution.py:49
  149.2 11.6 %collective-permute-done.3 = bf16[8,128,256]{2,1,0:T(8,128)(2,1)} collective-permute-done((bf16[8,128,256]{2,1,0:T(8,128)(2,1)}, bf16[8,128,256]{2,1,0:T(8,128)(2,1)}, u32[]{:S(2)}, u32[]{:S(2)}) %collective-permute-start.3) | collective-permute-done | bytes 524320 | tf_op jit(solution)/shard_map/ppermute | solution.py:22
  160.7 1.9 %constant_dynamic-update-slice_fusion.2 = bf16[32,128,256]{2,1,0:T(8,128)(2,1)} fusion(bf16[32,128,256]{2,1,0:T(8,128)(2,1)} %get-tuple-element.7, bf16[8,128,256]{2,1,0:T(8,128)(2,1)} %collective-permute-done.3, s32[]{:T(128)S(6)} %select_n.9), kind=kLoop, calls=%fused_computation.74 | loop fusion | bytes 1048580 | tf_op jit(solution)/shard_map/dynamic_update_slice | solution.py:91
  (40 shorter events, 19.5 us)
Async XLA Ops:
  5.1 15.0 %all-to-all-start.1 = ((bf16[8,128,256]{2,1,0:T(8,128)(2,1)}), bf16[8,128,256]{2,1,0:T(8,128)(2,1)}, u32[]{:S(2)}, u32[]{:S(2)}) async-start(bf16[8,128,256]{2,1,0:T(8,128)(2,1)} %get-tuple-element.2), calls=%async_computation.1 | async-start | bytes 1048576 | tf_op jit(solution)/shard_map/all_to_all | solution.py:26
  20.1 41.8 %all-to-all-start = ((bf16[8,256,256]{2,1,0:T(8,128)(2,1)}), bf16[8,256,256]{2,1,0:T(8,128)(2,1)S(1)}, u32[]{:S(2)}, u32[]{:S(2)}) async-start(bf16[8,256,256]{2,1,0:T(8,128)(2,1)} %pad_maximum_fusion), calls=%async_computation | async-start | bytes 2097152 | tf_op jit(solution)/shard_map/all_to_all | solution.py:26
  23.6 38.2 %collective-permute-start.2 = (bf16[8,128,256]{2,1,0:T(8,128)(2,1)S(1)}, bf16[8,128,256]{2,1,0:T(8,128)(2,1)}, u32[]{:S(2)}, u32[]{:S(2)}) collective-permute-start(bf16[8,128,256]{2,1,0:T(8,128)(2,1)S(1)} %get-tuple-element.5), channel_id=1, source_target_pairs={{0,2},{1,3},{2,0},{3,1},{4,6},{5,7},{6,4},{7,5},{8,10},{9,11},{10,... | collective-permute-start | bytes 1572872 | tf_op jit(solution)/shard_map/ppermute | solution.py:22
  26.6 44.0 %collective-permute-start = (bf16[8,128,256]{2,1,0:T(8,128)(2,1)}, bf16[8,128,256]{2,1,0:T(8,128)(2,1)S(1)}, u32[]{:S(2)}, u32[]{:S(2)}) collective-permute-start(bf16[8,128,256]{2,1,0:T(8,128)(2,1)} %all-to-all-done.1), channel_id=1, source_target_pairs={{0,3},{1,2},{2,1},{3,0},{4,7},{5,6},{6,5},{7,4},{8,11},{9,10},{10,... | collective-permute-start | bytes 1572872 | tf_op jit(solution)/shard_map/ppermute | solution.py:22
  61.9 13.8 %all-to-all-start.2 = ((bf16[8,128,256]{2,1,0:T(8,128)(2,1)}), bf16[8,128,256]{2,1,0:T(8,128)(2,1)S(1)}, u32[]{:S(2)}, u32[]{:S(2)}) async-start(bf16[8,128,256]{2,1,0:T(8,128)(2,1)} %collective-permute-done.2), calls=%async_computation.2 | async-start | bytes 1048576 | tf_op jit(solution)/shard_map/all_to_all | solution.py:26
  66.9 14.5 %collective-permute-start.1 = (bf16[8,128,256]{2,1,0:T(8,128)(2,1)}, bf16[8,128,256]{2,1,0:T(8,128)(2,1)S(1)}, u32[]{:S(2)}, u32[]{:S(2)}) collective-permute-start(bf16[8,128,256]{2,1,0:T(8,128)(2,1)} %get-tuple-element.9), channel_id=1, source_target_pairs={{0,1},{1,0},{2,3},{3,2},{4,5},{5,4},{6,7},{7,6},{8,9},{9,8},{10,11... | collective-permute-start | bytes 1572872 | tf_op jit(solution)/shard_map/ppermute | solution.py:22
  83.6 2.2 %copy-start = (f32[1024,1024]{1,0:T(8,128)S(1)}, f32[1024,1024]{1,0:T(8,128)}, u32[]{:S(2)}) copy-start(f32[1024,1024]{1,0:T(8,128)} %fusion.47) | copy-start | bytes 12582916
  92.8 5.5 %copy-start.4 = (bf16[1024,256]{1,0:T(8,128)(2,1)}, bf16[1024,256]{1,0:T(8,128)(2,1)S(1)}, u32[]{:S(2)}) copy-start(bf16[1024,256]{1,0:T(8,128)(2,1)S(1)} %fusion.7) | copy-start | bytes 1572868
  95.1 0.8 copy-start.2
  104.3 19.2 %all-to-all-start.3 = ((bf16[8,256,256]{2,1,0:T(8,128)(2,1)}), bf16[8,256,256]{2,1,0:T(8,128)(2,1)S(1)}, u32[]{:S(2)}, u32[]{:S(2)}) async-start(bf16[8,256,256]{2,1,0:T(8,128)(2,1)} %pad_maximum_fusion.1), calls=%async_computation.3 | async-start | bytes 2097152 | tf_op jit(solution)/shard_map/all_to_all | solution.py:26
  108.1 5.3 %copy-start.3 = (bf16[1024,256]{1,0:T(8,128)(2,1)S(1)}, bf16[1024,256]{1,0:T(8,128)(2,1)}, u32[]{:S(2)}) copy-start(bf16[1024,256]{1,0:T(8,128)(2,1)} %copy-done.2) | copy-start | bytes 1572868
  111.5 29.1 %collective-permute-start.4 = (bf16[8,128,256]{2,1,0:T(8,128)(2,1)}, bf16[8,128,256]{2,1,0:T(8,128)(2,1)}, u32[]{:S(2)}, u32[]{:S(2)}) collective-permute-start(bf16[8,128,256]{2,1,0:T(8,128)(2,1)} %bitcast.6), channel_id=1, source_target_pairs={{0,2},{1,3},{2,0},{3,1},{4,6},{5,7},{6,4},{7,5},{8,10},{9,11},{10,... | collective-permute-start | bytes 1572872 | tf_op jit(solution)/shard_map/ppermute | solution.py:22
  123.5 13.9 %all-to-all-start.5 = ((bf16[8,128,256]{2,1,0:T(8,128)(2,1)}), bf16[8,128,256]{2,1,0:T(8,128)(2,1)}, u32[]{:S(2)}, u32[]{:S(2)}) async-start(bf16[8,128,256]{2,1,0:T(8,128)(2,1)} %bitcast.60), calls=%async_computation.5 | async-start | bytes 1048576 | tf_op jit(solution)/shard_map/all_to_all | solution.py:26
  129.3 14.8 %copy-start.1 = (bf16[32,128,256]{2,1,0:T(8,128)(2,1)S(1)}, bf16[32,128,256]{2,1,0:T(8,128)(2,1)}, u32[]{:S(2)}) copy-start(bf16[32,128,256]{2,1,0:T(8,128)(2,1)} %param.2) | copy-start | bytes 6291460
  130.3 30.5 %collective-permute-start.3 = (bf16[8,128,256]{2,1,0:T(8,128)(2,1)}, bf16[8,128,256]{2,1,0:T(8,128)(2,1)}, u32[]{:S(2)}, u32[]{:S(2)}) collective-permute-start(bf16[8,128,256]{2,1,0:T(8,128)(2,1)} %get-tuple-element.6), channel_id=1, source_target_pairs={{0,1},{1,0},{2,3},{3,2},{4,5},{5,4},{6,7},{7,6},{8,9},{9,8},{10,11... | collective-permute-start | bytes 1572872 | tf_op jit(solution)/shard_map/ppermute | solution.py:22
  137.4 26.0 %collective-permute-start.5 = (bf16[8,128,256]{2,1,0:T(8,128)(2,1)}, bf16[8,128,256]{2,1,0:T(8,128)(2,1)S(1)}, u32[]{:S(2)}, u32[]{:S(2)}) collective-permute-start(bf16[8,128,256]{2,1,0:T(8,128)(2,1)} %all-to-all-done.5), channel_id=1, source_target_pairs={{0,3},{1,2},{2,1},{3,0},{4,7},{5,6},{6,5},{7,4},{8,11},{9,10},{10,... | collective-permute-start | bytes 1572872 | tf_op jit(solution)/shard_map/ppermute | solution.py:22
  140.6 22.0 %all-to-all-start.4 = ((bf16[8,128,256]{2,1,0:T(8,128)(2,1)}), bf16[8,128,256]{2,1,0:T(8,128)(2,1)S(1)}, u32[]{:S(2)}, u32[]{:S(2)}) async-start(bf16[8,128,256]{2,1,0:T(8,128)(2,1)} %collective-permute-done.4), calls=%async_computation.4 | async-start | bytes 1048576 | tf_op jit(solution)/shard_map/all_to_all | solution.py:26

commit v2 on v0

v2 whole, which is shorter than its diff:
```python
import functools

import jax
import jax.numpy as jnp
from jax import lax
from jax.experimental import pallas as pl
from jax.experimental.pallas import tpu as pltpu
from jax.sharding import PartitionSpec as P

MIB = 1024 * 1024


def whole(space=pltpu.VMEM):
    return pl.BlockSpec(memory_space=space)


def cost(flops, moved):
    return pl.CostEstimate(flops=flops, bytes_accessed=moved, transcendentals=0)


def params(mib):
    return pltpu.CompilerParams(vmem_limit_bytes=mib * MIB)


def nesterov_kernel(plan, shards, where_ref, g_ref, m_ref, *outs):
    for out, pieces in zip(outs, plan):
        for i, (k, u) in enumerate(pieces):
            source = (where_ref[0] ^ k) * shards + (where_ref[1] ^ u)
            g = g_ref[source].astype(jnp.float32)
            m = 0.95 * m_ref[source] + g
            out[i] = (g + 0.95 * m).astype(jnp.bfloat16)


def nesterov(grads, momentum, where, plan, shards):
    count, rows, cols = grads.shape
    n = sum(len(pieces) for pieces in plan)
    return pl.pallas_call(
        functools.partial(nesterov_kernel, plan, shards),
        in_specs=[whole(pltpu.SMEM), whole(), whole()],
        out_specs=[whole()] * len(plan),
        out_shape=[jax.ShapeDtypeStruct((len(pieces), rows, cols), jnp.bfloat16) for pieces in plan],
        compiler_params=params(8),
        cost_estimate=cost(6 * n * rows * cols, 8 * n * rows * cols),
    )(where, grads, momentum)


def momentum_kernel(g_ref, m_ref, after_ref, o_ref, token_ref):
    o_ref[...] = 0.95 * m_ref[...] + g_ref[...].astype(jnp.float32)
    token_ref[...] = jnp.zeros_like(token_ref)


def next_momentum(grads, momentum, after):
    count, rows, cols = grads.shape
    steps = 8
    spec = pl.BlockSpec((count // steps, rows, cols), lambda i: (i, 0, 0))
    return pl.pallas_call(
        momentum_kernel,
        grid=(steps,),
        in_specs=[spec, spec, whole(pl.ANY)],
        out_specs=[spec, whole()],
        out_shape=[
            jax.ShapeDtypeStruct(grads.shape, jnp.float32),
            jax.ShapeDtypeStruct((8, 128), jnp.float32),
        ],
        compiler_params=params(8),
        cost_estimate=cost(1000, 1000),
    )(grads, momentum, after)


def nesterov_group(grads, momentum, group, shards):
    g = lax.dynamic_slice_in_dim(grads, group * shards, shards, 0).astype(jnp.float32)
    m = lax.dynamic_slice_in_dim(momentum, group * shards, shards, 0)
    return (g + 0.95 * (0.95 * m + g)).astype(jnp.bfloat16)


def plans(shards):
    z2 = [(2, u) for u in range(shards)]
    p31 = [[(3, u), (1, u)] for u in range(shards)]
    a0 = [(0, u) for u in range(shards)]
    return [z2], p31, [a0]


def swap_tensor(piece, k):
    count = lax.axis_size("tensor")
    return lax.ppermute(piece, "tensor", [(t, t ^ k) for t in range(count)])


def swap_shard(piece, u):
    count = lax.axis_size("shard")
    return lax.ppermute(piece, "shard", [(s, s ^ u) for s in range(count)])


def regroup_kernel(plan, n, where_ref, *refs):
    ins, outs = refs[:n], refs[n:]
    for out, slabs in zip(outs, plan):
        for i, (a, b, moved) in enumerate(slabs):
            out[i] = ins[a][b ^ where_ref[1] if moved else b]


def regroup(where, arrays, plan):
    _, rows, cols = arrays[0].shape
    n = sum(len(slabs) for slabs in plan)
    return pl.pallas_call(
        functools.partial(regroup_kernel, plan, len(arrays)),
        in_specs=[whole(pltpu.SMEM)] + [whole()] * len(arrays),
        out_specs=[whole()] * len(plan),
        out_shape=[jax.ShapeDtypeStruct((len(slabs), rows, cols), jnp.bfloat16) for slabs in plan],
        compiler_params=params(8),
        cost_estimate=cost(0, 4 * n * rows * cols),
    )(where, *arrays)


def exchange(where, z2, p31, a0, moved):
    shards = len(p31)
    z2 = swap_tensor(z2, 2)
    p31 = [p31[0]] + [swap_shard(p31[u], u) for u in range(1, shards)]
    w3, w1 = regroup(where, p31, [[(u, i, False) for u in range(shards)] for i in range(2)])
    z3 = swap_tensor(w3, 3)
    z1 = swap_tensor(w1, 1)
    p20 = regroup(where, (z2, a0), [[(0, u, moved), (1, u, False)] for u in range(shards)])
    p20 = [p20[0]] + [swap_shard(p20[u], u) for u in range(1, shards)]
    outs = {3: [(z3, u) for u in range(shards)], 1: [(z1, u) for u in range(shards)]}
    for i, k in enumerate((2, 0)):
        outs[k] = [(a, i) for a in p20]
    return outs


def arrays_of(chunks):
    arrays, places = [], []
    for k in sorted(chunks):
        for u, (a, b) in enumerate(chunks[k]):
            known = [i for i, other in enumerate(arrays) if other is a]
            if not known:
                known = [len(arrays)]
                arrays.append(a)
            places.append((k, u, known[0], b))
    return arrays, places


def mm(a, b):
    return jnp.dot(a, b, preferred_element_type=jnp.float32)


def mm_rows(a, b):
    return lax.dot_general(a, b, (((1,), (1,)), ((), ())), preferred_element_type=jnp.float32)


def step_columns(gram_ref, x, power_ref, scale):
    power = mm(gram_ref[...], x)
    if scale is not None:
        power = power * (scale * scale * scale)
    power_ref[...] = power
    square = mm(gram_ref[...], power.astype(jnp.bfloat16))
    current = x.astype(jnp.float32)
    if scale is not None:
        square = square * (scale * scale)
        current = current * scale
    return (3.4445 * current - 4.775 * power_ref[...] + 2.0315 * square).astype(jnp.bfloat16)


def gram_rows(x_ref, gram_ref, tile, with_trace):
    order = x_ref.shape[0]
    trace = jnp.zeros((tile, tile), jnp.float32)
    eye = lax.broadcasted_iota(jnp.int32, (tile, tile), 0) == lax.broadcasted_iota(jnp.int32, (tile, tile), 1)
    for i in range(order // tile):
        rows = slice(i * tile, (i + 1) * tile)
        part = mm_rows(x_ref[rows, :], x_ref[...])
        if with_trace:
            trace = trace + jnp.where(eye, part[:, rows], 0.0)
        gram_ref[rows, :] = part.astype(jnp.bfloat16)
    return jnp.sum(trace) if with_trace else None


def finish(new, k, plan, outs):
    rows = outs[0].shape[1]
    gain = 0.2 * float(new.shape[0]) ** 0.5
    done = (gain * new.astype(jnp.float32)).astype(jnp.bfloat16)
    for out, pieces in zip(outs, plan):
        for i, (k_of, u) in enumerate(pieces):
            if k_of == k:
                out[i] = done[u * rows : (u + 1) * rows]


def first_kernel(places, plan, n, *refs):
    ins, refs = refs[:n], refs[n + 1 :]
    y_ref, h_ref, refs = refs[0], refs[1], refs[2:]
    outs, (x_ref, g_ref, power_ref) = refs[: len(plan)], refs[len(plan) :]
    order, cols = power_ref.shape
    rows = ins[0].shape[1]
    for k, u, which, b in places:
        x_ref[u * rows : (u + 1) * rows, k * cols : (k + 1) * cols] = ins[which][b]
    tile = min(256, order)
    total = gram_rows(x_ref, g_ref, tile, True)
    scale = 1.0 / (jnp.sqrt(total) + 1e-07)
    for k in range(order // cols):
        c = slice(k * cols, (k + 1) * cols)
        y_ref[:, c] = step_columns(g_ref, x_ref[:, c], power_ref, scale)
    gram_rows(y_ref, h_ref, tile, False)
    for k in sorted({k for pieces in plan for k, _ in pieces}):
        new = step_columns(h_ref, y_ref[:, k * cols : (k + 1) * cols], power_ref, None)
        finish(new, k, plan, outs)


def first(chunks, plan, after):
    arrays, places = arrays_of(chunks)
    _, rows, cols = arrays[0].shape
    order = cols * len(chunks)
    square = jax.ShapeDtypeStruct((order, order), jnp.bfloat16)
    return pl.pallas_call(
        functools.partial(first_kernel, places, plan, len(arrays)),
        in_specs=[whole()] * len(arrays) + [whole(pl.ANY)],
        out_specs=[whole()] * (2 + len(plan)),
        out_shape=[square, square]
        + [jax.ShapeDtypeStruct((len(pieces), rows, cols), jnp.bfloat16) for pieces in plan],
        scratch_shapes=[pltpu.VMEM((order, order), jnp.bfloat16)] * 2 + [pltpu.VMEM((order, cols), jnp.float32)],
        compiler_params=params(24),
        cost_estimate=cost(9 * order**3, 12 * order**2),
    )(*arrays, after)


def last_kernel(plan, x_ref, g_ref, *refs):
    outs, power_ref = refs[:-1], refs[-1]
    order, cols = power_ref.shape
    for k in sorted({k for pieces in plan for k, _ in pieces}, reverse=True):
        new = step_columns(g_ref, x_ref[:, k * cols : (k + 1) * cols], power_ref, None)
        finish(new, k, plan, outs)


def last(x, g, plan, rows, cols):
    order = x.shape[0]
    return pl.pallas_call(
        functools.partial(last_kernel, plan),
        in_specs=[whole()] * 2,
        out_specs=[whole()] * len(plan),
        out_shape=[jax.ShapeDtypeStruct((len(pieces), rows, cols), jnp.bfloat16) for pieces in plan],
        scratch_shapes=[pltpu.VMEM((order, cols), jnp.float32)],
        compiler_params=params(16),
        cost_estimate=cost(len(plan) // 8 * order**3 + order**3, 8 * order**2),
    )(x, g)


def place_kernel(places, shards, where_ref, *refs):
    o_ref, sems = refs[-2:]
    copies = []
    for n, (k, u, which, b) in enumerate(places):
        target = (where_ref[0] ^ k) * shards + (where_ref[1] ^ u)
        copies.append(pltpu.make_async_copy(refs[which].at[b], o_ref.at[target], sems.at[n]))
    for c in copies:
        c.start()
    for c in copies:
        c.wait()


def place(where, chunks, shards, shape, before):
    arrays, places = arrays_of(chunks)
    more = [] if before is None else [before]
    return pl.pallas_call(
        functools.partial(place_kernel, places, shards),
        in_specs=[whole(pltpu.SMEM)] + [whole()] * len(arrays) + [whole(pltpu.HBM)] * len(more),
        out_specs=whole(pltpu.HBM),
        out_shape=jax.ShapeDtypeStruct(shape, jnp.bfloat16),
        scratch_shapes=[pltpu.SemaphoreType.DMA((len(places),))],
        input_output_aliases={len(arrays) + 1: 0} if more else {},
        compiler_params=params(8),
        cost_estimate=cost(0, 4 * len(places) * shape[1] * shape[2]),
    )(where, *arrays, *more)


def shards(grads, momentum):
    count, rows, cols = grads.shape
    shard_count = lax.axis_size("shard")
    t = lax.axis_index("tensor")
    where = jnp.stack([t, lax.axis_index("shard")]).astype(jnp.int32)
    z2_plan, p31_plan, a0_plan = plans(shard_count)
    z2 = nesterov_group(grads, momentum, t ^ 2, shard_count)
    p31 = nesterov(grads, momentum, where, p31_plan, shard_count)
    (a0,) = nesterov(grads, momentum, where, a0_plan, shard_count)
    chunks = exchange(where, z2, p31, a0, True)
    momentum_next, token = next_momentum(grads, momentum, chunks[0][0][0])
    x, g, z2 = first(chunks, z2_plan, token)
    p31 = list(last(x, g, p31_plan, rows, cols))
    (a0,) = last(x, g, a0_plan, rows, cols)
    back = exchange(where, z2, p31, a0, False)
    update = place(where, back, shard_count, grads.shape, None)
    return (momentum_next, update)


def solution(mesh):
    return jax.shard_map(
        shards,
        mesh=mesh,
        in_specs=(P(None, "shard", "tensor"), P(None, "shard", "tensor")),
        out_specs=(P(None, "shard", "tensor"), P(None, "shard", "tensor")),
        check_vma=False,
    )
```

time: 234 us -> 115 us (0.49)
  blocking collectives: 166 us -> 0 us
  starting transfers between devices: 0 us -> 41.4 us
  waiting for transfers between devices: 0 us -> 41.2 us
  Pallas kernels: 0 us -> 27.2 us
  local copies, waits for them, and re-layouts: 28.4 us -> 2.2 us
  other arithmetic: 22.3 us -> 1.77 us
  matrix products: 14.9 us -> 0 us
    all_to_all x4 -> x0, blocking collectives: 166 us -> none  [the longest x1 54.3 us: shards(): lax.all_to_all(sending, 'tensor', split_axis=0, concat_axis=2, tiled=True)]
    ppermute x0 -> x34, starting transfers between devices: none -> 41.4 us  [the longest x28 30.7 us: swap_shard(): return lax.ppermute(piece, 'shard', [(s, s ^ u) for s in range(count)])]
    ppermute x0 -> x34, waiting for transfers between devices: none -> 41.2 us  [the longest x28 31.9 us: swap_shard(): return lax.ppermute(piece, 'shard', [(s, s ^ u) for s in range(count)])]
    pallas_call x0 -> x11, Pallas kernels: none -> 27.2 us  [the longest x1 11.8 us: first(): pl.pallas_call(functools.partial(first_kernel, places, plan, len(arrays))...]
    dot_general x6 -> x0, matrix products: 14.9 us -> none  [the longest x2 5.43 us: orthogonalize(): square = jnp.dot(gram, power, preferred_element_type=jnp.float32)]
    unnamed x1 -> x0, other arithmetic: 12.8 us -> none
    unnamed x5 -> x6, local copies, waits for them, and re-layouts: 14.4 us -> 2.2 us
    convert_element_type x2 -> x1, other arithmetic: 7.64 us -> 1.7 us  [nesterov_group(): return (g + 0.95 * (0.95 * m + g)).astype(jnp.bfloat16)]
  transfers between devices with their start and end apart: 0 -> 34, of which waited for: 0 -> 18; matrix products, arithmetic and copies ran while one was open for 0% -> 0% of each run, Pallas kernels for 0% -> 12%
where the time goes in v2:
time: 115 us
  starting transfers between devices  41.4 us (36%)
  waiting for transfers between devices  41.2 us (36%)
  Pallas kernels  27.2 us (24%)
  local copies, waits for them, and re-layouts  2.2 us (2%)
  other arithmetic  1.77 us (2%)
    ppermute x28, waiting for transfers between devices, swap_shard(): return lax.ppermute(piece, 'shard', [(s, s ^ u) for s in range(count)])  31.9 us
    ppermute x28, starting transfers between devices, swap_shard(): return lax.ppermute(piece, 'shard', [(s, s ^ u) for s in range(count)])  30.7 us
    pallas_call x1, Pallas kernels, first(): pl.pallas_call(functools.partial(first_kernel, places, plan, len(arrays))...  11.8 us
    ppermute x6, starting transfers between devices, swap_tensor(): return lax.ppermute(piece, 'tensor', [(t, t ^ k) for t in range(count)])  10.7 us
    ppermute x6, waiting for transfers between devices, swap_tensor(): return lax.ppermute(piece, 'tensor', [(t, t ^ k) for t in range(count)])  9.31 us
    pallas_call x2, Pallas kernels, last(): pl.pallas_call(functools.partial(last_kernel, plan), in_specs=[whole()] *...  5.57 us
    pallas_call x1, Pallas kernels, next_momentum(): pl.pallas_call(momentum_kernel, grid=(steps,), in_specs=[spec, spec, whol...  3.59 us
    pallas_call x4, Pallas kernels, regroup(): pl.pallas_call(functools.partial(regroup_kernel, plan, len(arrays)), in_s...  2.44 us
  transfers between devices with their start and end apart: 34, of which 18 were waited for; matrix products, arithmetic and copies ran while one was open for 0% of the time, Pallas kernels for 12%

profile of v2, /device:TPU:0, one launch (start us, length us, event | category | flops | bytes accessed | tf_op | source)
XLA Modules:
  0.0 114.8 jit_solution(286854293583913150)
XLA Ops:
  0.6 1.7 %fusion.1 = bf16[8,128,256]{2,1,0:T(8,128)(2,1)S(1)} fusion(f32[32,128,256]{2,1,0:T(8,128)} %m_ref.5, s32[]{:T(128)S(6)} %select_n.4, bf16[32,128,256]{2,1,0:T(8,128)(2,1)} %g_ref.5), kind=kLoop, calls=%fused_computation.3 | loop fusion | flops 1572864 | bytes 2097156 | tf_op jit(solution)/shard_map/convert_element_type | solution.py:73
  2.3 4.1 %collective-permute-start = (bf16[8,128,256]{2,1,0:T(8,128)(2,1)S(1)}, bf16[8,128,256]{2,1,0:T(8,128)(2,1)S(1)}, u32[]{:S(2)}, u32[]{:S(2)}) collective-permute-start(bf16[8,128,256]{2,1,0:T(8,128)(2,1)S(1)} %fusion.1), channel_id=1, source_target_pairs={{0,2},{1,3},{2,0},{3,1},{4,6},{5,7},{6,4},{7,5},{8,10},{9,11},{10,... | collective-permute-start | bytes 1572872 | tf_op jit(solution)/shard_map/ppermute | solution.py:85
  6.5 2.2 %copy-done = f32[32,128,256]{2,1,0:T(8,128)S(1)} copy-done((f32[32,128,256]{2,1,0:T(8,128)S(1)}, f32[32,128,256]{2,1,0:T(8,128)}, u32[]{:S(2)}) %copy-start) | copy-done | bytes 4194328
  9.7 1.6 %collective-permute-start.9 = (bf16[2,128,256]{2,1,0:T(8,128)(2,1)S(1)}, bf16[2,128,256]{2,1,0:T(8,128)(2,1)S(1)}, u32[]{:S(2)}, u32[]{:S(2)}) collective-permute-start(bf16[2,128,256]{2,1,0:T(8,128)(2,1)S(1)} %get-tuple-element.54), channel_id=1, source_target_pairs={{0,8},{4,12},{8,0},{12,4},{16,24},{20,28},{24,16},{28,20},{1,9},{5... | collective-permute-start | bytes 393224 | tf_op jit(solution)/shard_map/ppermute | solution.py:90
  13.3 2.8 %collective-permute-done.9.refs_2_ = bf16[2,128,256]{2,1,0:T(8,128)(2,1)S(1)} collective-permute-done((bf16[2,128,256]{2,1,0:T(8,128)(2,1)S(1)}, bf16[2,128,256]{2,1,0:T(8,128)(2,1)S(1)}, u32[]{:S(2)}, u32[]{:S(2)}) %collective-permute-start.9) | collective-permute-done | bytes 131104 | tf_op jit(solution)/shard_map/ppermute | solution.py:90
  16.1 2.4 %collective-permute-start.13 = (bf16[2,128,256]{2,1,0:T(8,128)(2,1)S(1)}, bf16[2,128,256]{2,1,0:T(8,128)(2,1)S(1)}, u32[]{:S(2)}, u32[]{:S(2)}) collective-permute-start(bf16[2,128,256]{2,1,0:T(8,128)(2,1)S(1)} %get-tuple-element.58), channel_id=1, source_target_pairs={{0,24},{4,28},{8,16},{12,20},{16,8},{20,12},{24,0},{28,4},{1,25},{... | collective-permute-start | bytes 393224 | tf_op jit(solution)/shard_map/ppermute | solution.py:90
  18.5 2.5 %collective-permute-start.14 = (bf16[2,128,256]{2,1,0:T(8,128)(2,1)S(1)}, bf16[2,128,256]{2,1,0:T(8,128)(2,1)S(1)}, u32[]{:S(2)}, u32[]{:S(2)}) collective-permute-start(bf16[2,128,256]{2,1,0:T(8,128)(2,1)S(1)} %get-tuple-element.59), channel_id=1, source_target_pairs={{0,28},{4,24},{8,20},{12,16},{16,12},{20,8},{24,4},{28,0},{1,29},{... | collective-permute-start | bytes 393224 | tf_op jit(solution)/shard_map/ppermute | solution.py:90
  21.1 3.7 %collective-permute-done.12.refs_5_ = bf16[2,128,256]{2,1,0:T(8,128)(2,1)S(1)} collective-permute-done((bf16[2,128,256]{2,1,0:T(8,128)(2,1)S(1)}, bf16[2,128,256]{2,1,0:T(8,128)(2,1)S(1)}, u32[]{:S(2)}, u32[]{:S(2)}) %collective-permute-start.12) | collective-permute-done | bytes 131104 | tf_op jit(solution)/shard_map/ppermute | solution.py:90
  25.7 1.6 %collective-permute-start.15 = (bf16[8,128,256]{2,1,0:T(8,128)(2,1)S(1)}, bf16[8,128,256]{2,1,0:T(8,128)(2,1)S(1)}, u32[]{:S(2)}, u32[]{:S(2)}) collective-permute-start(bf16[8,128,256]{2,1,0:T(8,128)(2,1)S(1)} %get-tuple-element.60), channel_id=1, source_target_pairs={{0,1},{1,0},{2,3},{3,2},{4,5},{5,4},{6,7},{7,6},{8,9},{9,8},{10,11... | collective-permute-start | bytes 1572872 | tf_op jit(solution)/shard_map/ppermute | solution.py:85
  30.3 1.6 %collective-permute-start.2 = (bf16[2,128,256]{2,1,0:T(8,128)(2,1)S(1)}, bf16[2,128,256]{2,1,0:T(8,128)(2,1)S(1)}, u32[]{:S(2)}, u32[]{:S(2)}) collective-permute-start(bf16[2,128,256]{2,1,0:T(8,128)(2,1)S(1)} %get-tuple-element.46), channel_id=1, source_target_pairs={{0,8},{4,12},{8,0},{12,4},{16,24},{20,28},{24,16},{28,20},{1,9},{5... | collective-permute-start | bytes 393224 | tf_op jit(solution)/shard_map/ppermute | solution.py:90
  32.2 1.6 %collective-permute-start.4 = (bf16[2,128,256]{2,1,0:T(8,128)(2,1)S(1)}, bf16[2,128,256]{2,1,0:T(8,128)(2,1)S(1)}, u32[]{:S(2)}, u32[]{:S(2)}) collective-permute-start(bf16[2,128,256]{2,1,0:T(8,128)(2,1)S(1)} %get-tuple-element.48), channel_id=1, source_target_pairs={{0,16},{4,20},{8,24},{12,28},{16,0},{20,4},{24,8},{28,12},{1,17},{... | collective-permute-start | bytes 393224 | tf_op jit(solution)/shard_map/ppermute | solution.py:90
  33.8 2.9 %collective-permute-done.2.refs_2_ = bf16[2,128,256]{2,1,0:T(8,128)(2,1)S(1)} collective-permute-done((bf16[2,128,256]{2,1,0:T(8,128)(2,1)S(1)}, bf16[2,128,256]{2,1,0:T(8,128)(2,1)S(1)}, u32[]{:S(2)}, u32[]{:S(2)}) %collective-permute-start.2) | collective-permute-done | bytes 131104 | tf_op jit(solution)/shard_map/ppermute | solution.py:90
  38.6 2.5 %collective-permute-start.6 = (bf16[2,128,256]{2,1,0:T(8,128)(2,1)S(1)}, bf16[2,128,256]{2,1,0:T(8,128)(2,1)S(1)}, u32[]{:S(2)}, u32[]{:S(2)}) collective-permute-start(bf16[2,128,256]{2,1,0:T(8,128)(2,1)S(1)} %get-tuple-element.50), channel_id=1, source_target_pairs={{0,24},{4,28},{8,16},{12,20},{16,8},{20,12},{24,0},{28,4},{1,25},{... | collective-permute-start | bytes 393224 | tf_op jit(solution)/shard_map/ppermute | solution.py:90
  41.4 3.6 %shard_map.43 = (f32[32,128,256]{2,1,0:T(8,128)}, f32[8,128]{1,0:T(8,128)S(1)}) custom-call(bf16[32,128,256]{2,1,0:T(8,128)(2,1)S(1)} %copy-done.2, f32[32,128,256]{2,1,0:T(8,128)S(1)} %copy-done.1, bf16[2,128,256]{2,1,0:T(8,128)(2,1)S(1)} %get-tuple-element.43.after_ref.refs_0_), custom_call_target="tpu_custom_call" | custom-call | flops 1000 | bytes 1000 | tf_op jit(solution)/shard_map/pallas_call | solution.py:56
  45.8 2.2 %collective-permute-done.7.refs_7_ = bf16[2,128,256]{2,1,0:T(8,128)(2,1)S(1)} collective-permute-done((bf16[2,128,256]{2,1,0:T(8,128)(2,1)S(1)}, bf16[2,128,256]{2,1,0:T(8,128)(2,1)S(1)}, u32[]{:S(2)}, u32[]{:S(2)}) %collective-permute-start.7) | collective-permute-done | bytes 131104 | tf_op jit(solution)/shard_map/ppermute | solution.py:90
  48.0 4.1 %collective-permute-done.15.refs_8_ = bf16[8,128,256]{2,1,0:T(8,128)(2,1)S(1)} collective-permute-done((bf16[8,128,256]{2,1,0:T(8,128)(2,1)S(1)}, bf16[8,128,256]{2,1,0:T(8,128)(2,1)S(1)}, u32[]{:S(2)}, u32[]{:S(2)}) %collective-permute-start.15) | collective-permute-done | bytes 524320 | tf_op jit(solution)/shard_map/ppermute | solution.py:85
  52.1 11.8 %shard_map.46 = (bf16[1024,1024]{1,0:T(8,128)(2,1)S(1)}, bf16[1024,1024]{1,0:T(8,128)(2,1)S(1)}, bf16[8,128,256]{2,1,0:T(8,128)(2,1)S(1)}) custom-call(bf16[2,128,256]{2,1,0:T(8,128)(2,1)S(1)} %get-tuple-element.43.after_ref.refs_0_, bf16[2,128,256]{2,1,0:T(8,128)(2,1)S(1)} %collective-permute-done.1.refs_1_, ...), custom_call_target="tpu_custom_call" | custom-call | flops 9663676416 | bytes 12582912 | tf_op jit(solution)/shard_map/pallas_call | solution.py:209
  63.9 2.7 %collective-permute-start.17 = (bf16[8,128,256]{2,1,0:T(8,128)(2,1)S(1)}, bf16[8,128,256]{2,1,0:T(8,128)(2,1)S(1)}, u32[]{:S(2)}, u32[]{:S(2)}) collective-permute-start(bf16[8,128,256]{2,1,0:T(8,128)(2,1)S(1)} %get-tuple-element.63), channel_id=1, source_target_pairs={{0,2},{1,3},{2,0},{3,1},{4,6},{5,7},{6,4},{7,5},{8,10},{9,11},{10,... | collective-permute-start | bytes 1572872 | tf_op jit(solution)/shard_map/ppermute | solution.py:85
  66.6 3.3 %shard_map.49 = (bf16[2,128,256]{2,1,0:T(8,128)(2,1)S(1)}, bf16[2,128,256]{2,1,0:T(8,128)(2,1)S(1)}, bf16[2,128,256]{2,1,0:T(8,128)(2,1)S(1)}, bf16[2,128,256]{2...) custom-call(bf16[1024,1024]{1,0:T(8,128)(2,1)S(1)} %get-tuple-elemen, ...), custom_call_target="tpu_custom_call" | custom-call | flops 2147483648 | bytes 8388608 | tf_op jit(solution)/shard_map/pallas_call | solution.py:231
  73.6 2.8 %collective-permute-done.26.refs_2_ = bf16[2,128,256]{2,1,0:T(8,128)(2,1)S(1)} collective-permute-done((bf16[2,128,256]{2,1,0:T(8,128)(2,1)S(1)}, bf16[2,128,256]{2,1,0:T(8,128)(2,1)S(1)}, u32[]{:S(2)}, u32[]{:S(2)}) %collective-permute-start.26) | collective-permute-done | bytes 131104 | tf_op jit(solution)/shard_map/ppermute | solution.py:90
  76.4 2.5 %collective-permute-start.30 = (bf16[2,128,256]{2,1,0:T(8,128)(2,1)S(1)}, bf16[2,128,256]{2,1,0:T(8,128)(2,1)S(1)}, u32[]{:S(2)}, u32[]{:S(2)}) collective-permute-start(bf16[2,128,256]{2,1,0:T(8,128)(2,1)S(1)} %get-tuple-element.80), channel_id=1, source_target_pairs={{0,24},{4,28},{8,16},{12,20},{16,8},{20,12},{24,0},{28,4},{1,25},{... | collective-permute-start | bytes 393224 | tf_op jit(solution)/shard_map/ppermute | solution.py:90
  78.9 2.5 %collective-permute-start.31 = (bf16[2,128,256]{2,1,0:T(8,128)(2,1)S(1)}, bf16[2,128,256]{2,1,0:T(8,128)(2,1)S(1)}, u32[]{:S(2)}, u32[]{:S(2)}) collective-permute-start(bf16[2,128,256]{2,1,0:T(8,128)(2,1)S(1)} %get-tuple-element.81), channel_id=1, source_target_pairs={{0,28},{4,24},{8,20},{12,16},{16,12},{20,8},{24,4},{28,0},{1,29},{... | collective-permute-start | bytes 393224 | tf_op jit(solution)/shard_map/ppermute | solution.py:90
  81.4 3.7 %collective-permute-done.29.refs_5_ = bf16[2,128,256]{2,1,0:T(8,128)(2,1)S(1)} collective-permute-done((bf16[2,128,256]{2,1,0:T(8,128)(2,1)S(1)}, bf16[2,128,256]{2,1,0:T(8,128)(2,1)S(1)}, u32[]{:S(2)}, u32[]{:S(2)}) %collective-permute-start.29) | collective-permute-done | bytes 131104 | tf_op jit(solution)/shard_map/ppermute | solution.py:90
  87.9 2.2 %shard_map.47.refs_1_ = bf16[8,128,256]{2,1,0:T(8,128)(2,1)S(1)} custom-call(bf16[1024,1024]{1,0:T(8,128)(2,1)S(1)} %get-tuple-element.64.x_ref, bf16[1024,1024]{1,0:T(8,128)(2,1)S(1)} %get-tuple-element.65.g_ref), custom_call_target="tpu_custom_call" | custom-call | flops 1073741824 | bytes 8388608 | tf_op jit(solution)/shard_map/pallas_call | solution.py:231
  90.9 1.7 %collective-permute-start.19 = (bf16[2,128,256]{2,1,0:T(8,128)(2,1)S(1)}, bf16[2,128,256]{2,1,0:T(8,128)(2,1)S(1)}, u32[]{:S(2)}, u32[]{:S(2)}) collective-permute-start(bf16[2,128,256]{2,1,0:T(8,128)(2,1)S(1)} %get-tuple-element.68), channel_id=1, source_target_pairs={{0,8},{4,12},{8,0},{12,4},{16,24},{20,28},{24,16},{28,20},{1,9},{5... | collective-permute-start | bytes 393224 | tf_op jit(solution)/shard_map/ppermute | solution.py:90
  92.7 1.6 %collective-permute-start.21 = (bf16[2,128,256]{2,1,0:T(8,128)(2,1)S(1)}, bf16[2,128,256]{2,1,0:T(8,128)(2,1)S(1)}, u32[]{:S(2)}, u32[]{:S(2)}) collective-permute-start(bf16[2,128,256]{2,1,0:T(8,128)(2,1)S(1)} %get-tuple-element.70), channel_id=1, source_target_pairs={{0,16},{4,20},{8,24},{12,28},{16,0},{20,4},{24,8},{28,12},{1,17},{... | collective-permute-start | bytes 393224 | tf_op jit(solution)/shard_map/ppermute | solution.py:90
  94.4 2.9 %collective-permute-done.19.refs_2_ = bf16[2,128,256]{2,1,0:T(8,128)(2,1)S(1)} collective-permute-done((bf16[2,128,256]{2,1,0:T(8,128)(2,1)S(1)}, bf16[2,128,256]{2,1,0:T(8,128)(2,1)S(1)}, u32[]{:S(2)}, u32[]{:S(2)}) %collective-permute-start.19) | collective-permute-done | bytes 131104 | tf_op jit(solution)/shard_map/ppermute | solution.py:90
  99.1 2.5 %collective-permute-start.23 = (bf16[2,128,256]{2,1,0:T(8,128)(2,1)S(1)}, bf16[2,128,256]{2,1,0:T(8,128)(2,1)S(1)}, u32[]{:S(2)}, u32[]{:S(2)}) collective-permute-start(bf16[2,128,256]{2,1,0:T(8,128)(2,1)S(1)} %get-tuple-element.72), channel_id=1, source_target_pairs={{0,24},{4,28},{8,16},{12,20},{16,8},{20,12},{24,0},{28,4},{1,25},{... | collective-permute-start | bytes 393224 | tf_op jit(solution)/shard_map/ppermute | solution.py:90
  102.8 3.5 %collective-permute-done.23.refs_6_ = bf16[2,128,256]{2,1,0:T(8,128)(2,1)S(1)} collective-permute-done((bf16[2,128,256]{2,1,0:T(8,128)(2,1)S(1)}, bf16[2,128,256]{2,1,0:T(8,128)(2,1)S(1)}, u32[]{:S(2)}, u32[]{:S(2)}) %collective-permute-start.23) | collective-permute-done | bytes 131104 | tf_op jit(solution)/shard_map/ppermute | solution.py:90
  106.3 2.2 %collective-permute-done.24.refs_7_ = bf16[2,128,256]{2,1,0:T(8,128)(2,1)S(1)} collective-permute-done((bf16[2,128,256]{2,1,0:T(8,128)(2,1)S(1)}, bf16[2,128,256]{2,1,0:T(8,128)(2,1)S(1)}, u32[]{:S(2)}, u32[]{:S(2)}) %collective-permute-start.24) | collective-permute-done | bytes 131104 | tf_op jit(solution)/shard_map/ppermute | solution.py:90
  108.5 4.0 %collective-permute-done.32.refs_8_ = bf16[8,128,256]{2,1,0:T(8,128)(2,1)S(1)} collective-permute-done((bf16[8,128,256]{2,1,0:T(8,128)(2,1)S(1)}, bf16[8,128,256]{2,1,0:T(8,128)(2,1)S(1)}, u32[]{:S(2)}, u32[]{:S(2)}) %collective-permute-start.32) | collective-permute-done | bytes 524320 | tf_op jit(solution)/shard_map/ppermute | solution.py:85
  112.5 2.1 %shard_map.51 = bf16[32,128,256]{2,1,0:T(8,128)(2,1)} custom-call(s32[2]{0:T(128)S(1)} %pad_add_fusion.where_ref, bf16[2,128,256]{2,1,0:T(8,128)(2,1)S(1)} %get-tuple-element.66.refs_0_, bf16[2,128,256]{2,1,0:T(8,128)(2,1)S(1)} %collective-permute-done.18.refs_1_, bf16[2,128,256]{2,1,0:T(8,128)(2,1)S(1)} %collective-permute-done.19.refs_2_, ...), custom_call_target="tpu_custom_call" | custom-call | bytes 4194304 | tf_op jit(solution)/shard_map/pallas_call | solution.py:257
  (55 shorter events, 20.5 us)
Async XLA Ops:
  2.3 27.3 %collective-permute-start = (bf16[8,128,256]{2,1,0:T(8,128)(2,1)S(1)}, bf16[8,128,256]{2,1,0:T(8,128)(2,1)S(1)}, u32[]{:S(2)}, u32[]{:S(2)}) collective-permute-start(bf16[8,128,256]{2,1,0:T(8,128)(2,1)S(1)} %fusion.1), channel_id=1, source_target_pairs={{0,2},{1,3},{2,0},{3,1},{4,6},{5,7},{6,4},{7,5},{8,10},{9,11},{10,... | collective-permute-start | bytes 1572872 | tf_op jit(solution)/shard_map/ppermute | solution.py:85
  9.6 3.5 %collective-permute-start.8 = (bf16[2,128,256]{2,1,0:T(8,128)(2,1)S(1)}, bf16[2,128,256]{2,1,0:T(8,128)(2,1)S(1)}, u32[]{:S(2)}, u32[]{:S(2)}) collective-permute-start(bf16[2,128,256]{2,1,0:T(8,128)(2,1)S(1)} %get-tuple-element.53), channel_id=1, source_target_pairs={{0,4},{4,0},{8,12},{12,8},{16,20},{20,16},{24,28},{28,24},{1,5},{5... | collective-permute-start | bytes 393224 | tf_op jit(solution)/shard_map/ppermute | solution.py:90
  9.7 6.4 %collective-permute-start.9 = (bf16[2,128,256]{2,1,0:T(8,128)(2,1)S(1)}, bf16[2,128,256]{2,1,0:T(8,128)(2,1)S(1)}, u32[]{:S(2)}, u32[]{:S(2)}) collective-permute-start(bf16[2,128,256]{2,1,0:T(8,128)(2,1)S(1)} %get-tuple-element.54), channel_id=1, source_target_pairs={{0,8},{4,12},{8,0},{12,4},{16,24},{20,28},{24,16},{28,20},{1,9},{5... | collective-permute-start | bytes 393224 | tf_op jit(solution)/shard_map/ppermute | solution.py:90
  11.3 7.3 %collective-permute-start.10 = (bf16[2,128,256]{2,1,0:T(8,128)(2,1)S(1)}, bf16[2,128,256]{2,1,0:T(8,128)(2,1)S(1)}, u32[]{:S(2)}, u32[]{:S(2)}) collective-permute-start(bf16[2,128,256]{2,1,0:T(8,128)(2,1)S(1)} %get-tuple-element.55), channel_id=1, source_target_pairs={{0,12},{4,8},{8,4},{12,0},{16,28},{20,24},{24,20},{28,16},{1,13},{... | collective-permute-start | bytes 393224 | tf_op jit(solution)/shard_map/ppermute | solution.py:90
  11.6 9.5 %collective-permute-start.11 = (bf16[2,128,256]{2,1,0:T(8,128)(2,1)S(1)}, bf16[2,128,256]{2,1,0:T(8,128)(2,1)S(1)}, u32[]{:S(2)}, u32[]{:S(2)}) collective-permute-start(bf16[2,128,256]{2,1,0:T(8,128)(2,1)S(1)} %get-tuple-element.56), channel_id=1, source_target_pairs={{0,16},{4,20},{8,24},{12,28},{16,0},{20,4},{24,8},{28,12},{1,17},{... | collective-permute-start | bytes 393224 | tf_op jit(solution)/shard_map/ppermute | solution.py:90
  13.1 11.7 %collective-permute-start.12 = (bf16[2,128,256]{2,1,0:T(8,128)(2,1)S(1)}, bf16[2,128,256]{2,1,0:T(8,128)(2,1)S(1)}, u32[]{:S(2)}, u32[]{:S(2)}) collective-permute-start(bf16[2,128,256]{2,1,0:T(8,128)(2,1)S(1)} %get-tuple-element.57), channel_id=1, source_target_pairs={{0,20},{4,16},{8,28},{12,24},{16,4},{20,0},{24,12},{28,8},{1,21},{... | collective-permute-start | bytes 393224 | tf_op jit(solution)/shard_map/ppermute | solution.py:90
  16.1 8.7 %collective-permute-start.13 = (bf16[2,128,256]{2,1,0:T(8,128)(2,1)S(1)}, bf16[2,128,256]{2,1,0:T(8,128)(2,1)S(1)}, u32[]{:S(2)}, u32[]{:S(2)}) collective-permute-start(bf16[2,128,256]{2,1,0:T(8,128)(2,1)S(1)} %get-tuple-element.58), channel_id=1, source_target_pairs={{0,24},{4,28},{8,16},{12,20},{16,8},{20,12},{24,0},{28,4},{1,25},{... | collective-permute-start | bytes 393224 | tf_op jit(solution)/shard_map/ppermute | solution.py:90
  18.5 6.5 %collective-permute-start.14 = (bf16[2,128,256]{2,1,0:T(8,128)(2,1)S(1)}, bf16[2,128,256]{2,1,0:T(8,128)(2,1)S(1)}, u32[]{:S(2)}, u32[]{:S(2)}) collective-permute-start(bf16[2,128,256]{2,1,0:T(8,128)(2,1)S(1)} %get-tuple-element.59), channel_id=1, source_target_pairs={{0,28},{4,24},{8,20},{12,16},{16,12},{20,8},{24,4},{28,0},{1,29},{... | collective-permute-start | bytes 393224 | tf_op jit(solution)/shard_map/ppermute | solution.py:90
  25.7 26.4 %collective-permute-start.15 = (bf16[8,128,256]{2,1,0:T(8,128)(2,1)S(1)}, bf16[8,128,256]{2,1,0:T(8,128)(2,1)S(1)}, u32[]{:S(2)}, u32[]{:S(2)}) collective-permute-start(bf16[8,128,256]{2,1,0:T(8,128)(2,1)S(1)} %get-tuple-element.60), channel_id=1, source_target_pairs={{0,1},{1,0},{2,3},{3,2},{4,5},{5,4},{6,7},{7,6},{8,9},{9,8},{10,11... | collective-permute-start | bytes 1572872 | tf_op jit(solution)/shard_map/ppermute | solution.py:85
  27.3 24.7 %collective-permute-start.16 = (bf16[8,128,256]{2,1,0:T(8,128)(2,1)S(1)}, bf16[8,128,256]{2,1,0:T(8,128)(2,1)S(1)}, u32[]{:S(2)}, u32[]{:S(2)}) collective-permute-start(bf16[8,128,256]{2,1,0:T(8,128)(2,1)S(1)} %get-tuple-element.61), channel_id=1, source_target_pairs={{0,3},{1,2},{2,1},{3,0},{4,7},{5,6},{6,5},{7,4},{8,11},{9,10},{10,... | collective-permute-start | bytes 1572872 | tf_op jit(solution)/shard_map/ppermute | solution.py:85
  30.3 6.4 %collective-permute-start.2 = (bf16[2,128,256]{2,1,0:T(8,128)(2,1)S(1)}, bf16[2,128,256]{2,1,0:T(8,128)(2,1)S(1)}, u32[]{:S(2)}, u32[]{:S(2)}) collective-permute-start(bf16[2,128,256]{2,1,0:T(8,128)(2,1)S(1)} %get-tuple-element.46), channel_id=1, source_target_pairs={{0,8},{4,12},{8,0},{12,4},{16,24},{20,28},{24,16},{28,20},{1,9},{5... | collective-permute-start | bytes 393224 | tf_op jit(solution)/shard_map/ppermute | solution.py:90
  32.0 6.7 %collective-permute-start.3 = (bf16[2,128,256]{2,1,0:T(8,128)(2,1)S(1)}, bf16[2,128,256]{2,1,0:T(8,128)(2,1)S(1)}, u32[]{:S(2)}, u32[]{:S(2)}) collective-permute-start(bf16[2,128,256]{2,1,0:T(8,128)(2,1)S(1)} %get-tuple-element.47), channel_id=1, source_target_pairs={{0,12},{4,8},{8,4},{12,0},{16,28},{20,24},{24,20},{28,16},{1,13},{... | collective-permute-start | bytes 393224 | tf_op jit(solution)/shard_map/ppermute | solution.py:90
  32.2 8.9 %collective-permute-start.4 = (bf16[2,128,256]{2,1,0:T(8,128)(2,1)S(1)}, bf16[2,128,256]{2,1,0:T(8,128)(2,1)S(1)}, u32[]{:S(2)}, u32[]{:S(2)}) collective-permute-start(bf16[2,128,256]{2,1,0:T(8,128)(2,1)S(1)} %get-tuple-element.48), channel_id=1, source_target_pairs={{0,16},{4,20},{8,24},{12,28},{16,0},{20,4},{24,8},{28,12},{1,17},{... | collective-permute-start | bytes 393224 | tf_op jit(solution)/shard_map/ppermute | solution.py:90
  36.7 8.3 %collective-permute-start.5 = (bf16[2,128,256]{2,1,0:T(8,128)(2,1)S(1)}, bf16[2,128,256]{2,1,0:T(8,128)(2,1)S(1)}, u32[]{:S(2)}, u32[]{:S(2)}) collective-permute-start(bf16[2,128,256]{2,1,0:T(8,128)(2,1)S(1)} %get-tuple-element.49), channel_id=1, source_target_pairs={{0,20},{4,16},{8,28},{12,24},{16,4},{20,0},{24,12},{28,8},{1,21},{... | collective-permute-start | bytes 393224 | tf_op jit(solution)/shard_map/ppermute | solution.py:90
  38.6 7.2 %collective-permute-start.6 = (bf16[2,128,256]{2,1,0:T(8,128)(2,1)S(1)}, bf16[2,128,256]{2,1,0:T(8,128)(2,1)S(1)}, u32[]{:S(2)}, u32[]{:S(2)}) collective-permute-start(bf16[2,128,256]{2,1,0:T(8,128)(2,1)S(1)} %get-tuple-element.50), channel_id=1, source_target_pairs={{0,24},{4,28},{8,16},{12,20},{16,8},{20,12},{24,0},{28,4},{1,25},{... | collective-permute-start | bytes 393224 | tf_op jit(solution)/shard_map/ppermute | solution.py:90
  41.1 6.9 %collective-permute-start.7 = (bf16[2,128,256]{2,1,0:T(8,128)(2,1)S(1)}, bf16[2,128,256]{2,1,0:T(8,128)(2,1)S(1)}, u32[]{:S(2)}, u32[]{:S(2)}) collective-permute-start(bf16[2,128,256]{2,1,0:T(8,128)(2,1)S(1)} %get-tuple-element.51), channel_id=1, source_target_pairs={{0,28},{4,24},{8,20},{12,16},{16,12},{20,8},{24,4},{28,0},{1,29},{... | collective-permute-start | bytes 393224 | tf_op jit(solution)/shard_map/ppermute | solution.py:90
  63.9 26.2 %collective-permute-start.17 = (bf16[8,128,256]{2,1,0:T(8,128)(2,1)S(1)}, bf16[8,128,256]{2,1,0:T(8,128)(2,1)S(1)}, u32[]{:S(2)}, u32[]{:S(2)}) collective-permute-start(bf16[8,128,256]{2,1,0:T(8,128)(2,1)S(1)} %get-tuple-element.63), channel_id=1, source_target_pairs={{0,2},{1,3},{2,0},{3,1},{4,6},{5,7},{6,4},{7,5},{8,10},{9,11},{10,... | collective-permute-start | bytes 1572872 | tf_op jit(solution)/shard_map/ppermute | solution.py:85
  70.0 3.5 %collective-permute-start.25 = (bf16[2,128,256]{2,1,0:T(8,128)(2,1)S(1)}, bf16[2,128,256]{2,1,0:T(8,128)(2,1)S(1)}, u32[]{:S(2)}, u32[]{:S(2)}) collective-permute-start(bf16[2,128,256]{2,1,0:T(8,128)(2,1)S(1)} %get-tuple-element.75), channel_id=1, source_target_pairs={{0,4},{4,0},{8,12},{12,8},{16,20},{20,16},{24,28},{28,24},{1,5},{5... | collective-permute-start | bytes 393224 | tf_op jit(solution)/shard_map/ppermute | solution.py:90
  70.1 6.4 %collective-permute-start.26 = (bf16[2,128,256]{2,1,0:T(8,128)(2,1)S(1)}, bf16[2,128,256]{2,1,0:T(8,128)(2,1)S(1)}, u32[]{:S(2)}, u32[]{:S(2)}) collective-permute-start(bf16[2,128,256]{2,1,0:T(8,128)(2,1)S(1)} %get-tuple-element.76), channel_id=1, source_target_pairs={{0,8},{4,12},{8,0},{12,4},{16,24},{20,28},{24,16},{28,20},{1,9},{5... | collective-permute-start | bytes 393224 | tf_op jit(solution)/shard_map/ppermute | solution.py:90
  71.6 7.3 %collective-permute-start.27 = (bf16[2,128,256]{2,1,0:T(8,128)(2,1)S(1)}, bf16[2,128,256]{2,1,0:T(8,128)(2,1)S(1)}, u32[]{:S(2)}, u32[]{:S(2)}) collective-permute-start(bf16[2,128,256]{2,1,0:T(8,128)(2,1)S(1)} %get-tuple-element.77), channel_id=1, source_target_pairs={{0,12},{4,8},{8,4},{12,0},{16,28},{20,24},{24,20},{28,16},{1,13},{... | collective-permute-start | bytes 393224 | tf_op jit(solution)/shard_map/ppermute | solution.py:90
  71.9 9.5 %collective-permute-start.28 = (bf16[2,128,256]{2,1,0:T(8,128)(2,1)S(1)}, bf16[2,128,256]{2,1,0:T(8,128)(2,1)S(1)}, u32[]{:S(2)}, u32[]{:S(2)}) collective-permute-start(bf16[2,128,256]{2,1,0:T(8,128)(2,1)S(1)} %get-tuple-element.78), channel_id=1, source_target_pairs={{0,16},{4,20},{8,24},{12,28},{16,0},{20,4},{24,8},{28,12},{1,17},{... | collective-permute-start | bytes 393224 | tf_op jit(solution)/shard_map/ppermute | solution.py:90
  73.5 11.7 %collective-permute-start.29 = (bf16[2,128,256]{2,1,0:T(8,128)(2,1)S(1)}, bf16[2,128,256]{2,1,0:T(8,128)(2,1)S(1)}, u32[]{:S(2)}, u32[]{:S(2)}) collective-permute-start(bf16[2,128,256]{2,1,0:T(8,128)(2,1)S(1)} %get-tuple-element.79), channel_id=1, source_target_pairs={{0,20},{4,16},{8,28},{12,24},{16,4},{20,0},{24,12},{28,8},{1,21},{... | collective-permute-start | bytes 393224 | tf_op jit(solution)/shard_map/ppermute | solution.py:90
  76.4 8.7 %collective-permute-start.30 = (bf16[2,128,256]{2,1,0:T(8,128)(2,1)S(1)}, bf16[2,128,256]{2,1,0:T(8,128)(2,1)S(1)}, u32[]{:S(2)}, u32[]{:S(2)}) collective-permute-start(bf16[2,128,256]{2,1,0:T(8,128)(2,1)S(1)} %get-tuple-element.80), channel_id=1, source_target_pairs={{0,24},{4,28},{8,16},{12,20},{16,8},{20,12},{24,0},{28,4},{1,25},{... | collective-permute-start | bytes 393224 | tf_op jit(solution)/shard_map/ppermute | solution.py:90
  78.9 6.5 %collective-permute-start.31 = (bf16[2,128,256]{2,1,0:T(8,128)(2,1)S(1)}, bf16[2,128,256]{2,1,0:T(8,128)(2,1)S(1)}, u32[]{:S(2)}, u32[]{:S(2)}) collective-permute-start(bf16[2,128,256]{2,1,0:T(8,128)(2,1)S(1)} %get-tuple-element.81), channel_id=1, source_target_pairs={{0,28},{4,24},{8,20},{12,16},{16,12},{20,8},{24,4},{28,0},{1,29},{... | collective-permute-start | bytes 393224 | tf_op jit(solution)/shard_map/ppermute | solution.py:90
  86.1 26.5 %collective-permute-start.32 = (bf16[8,128,256]{2,1,0:T(8,128)(2,1)S(1)}, bf16[8,128,256]{2,1,0:T(8,128)(2,1)S(1)}, u32[]{:S(2)}, u32[]{:S(2)}) collective-permute-start(bf16[8,128,256]{2,1,0:T(8,128)(2,1)S(1)} %get-tuple-element.82), channel_id=1, source_target_pairs={{0,1},{1,0},{2,3},{3,2},{4,5},{5,4},{6,7},{7,6},{8,9},{9,8},{10,11... | collective-permute-start | bytes 1572872 | tf_op jit(solution)/shard_map/ppermute | solution.py:85
  87.6 25.0 %collective-permute-start.33 = (bf16[8,128,256]{2,1,0:T(8,128)(2,1)S(1)}, bf16[8,128,256]{2,1,0:T(8,128)(2,1)S(1)}, u32[]{:S(2)}, u32[]{:S(2)}) collective-permute-start(bf16[8,128,256]{2,1,0:T(8,128)(2,1)S(1)} %get-tuple-element.83), channel_id=1, source_target_pairs={{0,3},{1,2},{2,1},{3,0},{4,7},{5,6},{6,5},{7,4},{8,11},{9,10},{10,... | collective-permute-start | bytes 1572872 | tf_op jit(solution)/shard_map/ppermute | solution.py:85
  90.9 6.4 %collective-permute-start.19 = (bf16[2,128,256]{2,1,0:T(8,128)(2,1)S(1)}, bf16[2,128,256]{2,1,0:T(8,128)(2,1)S(1)}, u32[]{:S(2)}, u32[]{:S(2)}) collective-permute-start(bf16[2,128,256]{2,1,0:T(8,128)(2,1)S(1)} %get-tuple-element.68), channel_id=1, source_target_pairs={{0,8},{4,12},{8,0},{12,4},{16,24},{20,28},{24,16},{28,20},{1,9},{5... | collective-permute-start | bytes 393224 | tf_op jit(solution)/shard_map/ppermute | solution.py:90
  92.5 6.6 %collective-permute-start.20 = (bf16[2,128,256]{2,1,0:T(8,128)(2,1)S(1)}, bf16[2,128,256]{2,1,0:T(8,128)(2,1)S(1)}, u32[]{:S(2)}, u32[]{:S(2)}) collective-permute-start(bf16[2,128,256]{2,1,0:T(8,128)(2,1)S(1)} %get-tuple-element.69), channel_id=1, source_target_pairs={{0,12},{4,8},{8,4},{12,0},{16,28},{20,24},{24,20},{28,16},{1,13},{... | collective-permute-start | bytes 393224 | tf_op jit(solution)/shard_map/ppermute | solution.py:90
  92.7 9.0 %collective-permute-start.21 = (bf16[2,128,256]{2,1,0:T(8,128)(2,1)S(1)}, bf16[2,128,256]{2,1,0:T(8,128)(2,1)S(1)}, u32[]{:S(2)}, u32[]{:S(2)}) collective-permute-start(bf16[2,128,256]{2,1,0:T(8,128)(2,1)S(1)} %get-tuple-element.70), channel_id=1, source_target_pairs={{0,16},{4,20},{8,24},{12,28},{16,0},{20,4},{24,8},{28,12},{1,17},{... | collective-permute-start | bytes 393224 | tf_op jit(solution)/shard_map/ppermute | solution.py:90
  97.2 5.6 %collective-permute-start.22 = (bf16[2,128,256]{2,1,0:T(8,128)(2,1)S(1)}, bf16[2,128,256]{2,1,0:T(8,128)(2,1)S(1)}, u32[]{:S(2)}, u32[]{:S(2)}) collective-permute-start(bf16[2,128,256]{2,1,0:T(8,128)(2,1)S(1)} %get-tuple-element.71), channel_id=1, source_target_pairs={{0,20},{4,16},{8,28},{12,24},{16,4},{20,0},{24,12},{28,8},{1,21},{... | collective-permute-start | bytes 393224 | tf_op jit(solution)/shard_map/ppermute | solution.py:90
  99.1 7.2 %collective-permute-start.23 = (bf16[2,128,256]{2,1,0:T(8,128)(2,1)S(1)}, bf16[2,128,256]{2,1,0:T(8,128)(2,1)S(1)}, u32[]{:S(2)}, u32[]{:S(2)}) collective-permute-start(bf16[2,128,256]{2,1,0:T(8,128)(2,1)S(1)} %get-tuple-element.72), channel_id=1, source_target_pairs={{0,24},{4,28},{8,16},{12,20},{16,8},{20,12},{24,0},{28,4},{1,25},{... | collective-permute-start | bytes 393224 | tf_op jit(solution)/shard_map/ppermute | solution.py:90
  101.7 6.8 %collective-permute-start.24 = (bf16[2,128,256]{2,1,0:T(8,128)(2,1)S(1)}, bf16[2,128,256]{2,1,0:T(8,128)(2,1)S(1)}, u32[]{:S(2)}, u32[]{:S(2)}) collective-permute-start(bf16[2,128,256]{2,1,0:T(8,128)(2,1)S(1)} %get-tuple-element.73), channel_id=1, source_target_pairs={{0,28},{4,24},{8,20},{12,16},{16,12},{20,8},{24,4},{28,0},{1,29},{... | collective-permute-start | bytes 393224 | tf_op jit(solution)/shard_map/ppermute | solution.py:90
  (5 other events, 31.0 us)

commit v3 on v2

--- a/solution.py
+++ b/solution.py
@@ -93,8 +93,8 @@
 def regroup_kernel(plan, n, where_ref, *refs):
     ins, outs = refs[:n], refs[n:]
     for out, slabs in zip(outs, plan):
-        for i, (a, b, moved) in enumerate(slabs):
-            out[i] = ins[a][b ^ where_ref[1] if moved else b]
+        for i, (a, b, moved, moves) in enumerate(slabs):
+            out[i ^ where_ref[1] if moves else i] = ins[a][b ^ where_ref[1] if moved else b]
 
 
 def regroup(where, arrays, plan):
@@ -114,14 +114,14 @@
     shards = len(p31)
     z2 = swap_tensor(z2, 2)
     p31 = [p31[0]] + [swap_shard(p31[u], u) for u in range(1, shards)]
-    w3, w1 = regroup(where, p31, [[(u, i, False) for u in range(shards)] for i in range(2)])
+    w3, w1 = regroup(where, p31, [[(u, i, False, not moved) for u in range(shards)] for i in range(2)])
     z3 = swap_tensor(w3, 3)
     z1 = swap_tensor(w1, 1)
-    p20 = regroup(where, (z2, a0), [[(0, u, moved), (1, u, False)] for u in range(shards)])
+    p20 = regroup(where, (z2, a0), [[(0, u, moved, False), (1, u, False, False)] for u in range(shards)])
     p20 = [p20[0]] + [swap_shard(p20[u], u) for u in range(1, shards)]
-    outs = {3: [(z3, u) for u in range(shards)], 1: [(z1, u) for u in range(shards)]}
-    for i, k in enumerate((2, 0)):
-        outs[k] = [(a, i) for a in p20]
+    outs = {k: [(a, i) for a in p20] for i, k in enumerate((2, 0))}
+    for k, a in ((3, z3), (1, z1)):
+        outs[k] = [(a, u) for u in range(shards)] if moved else [(a, None)]
     return outs
 
 
@@ -145,30 +145,31 @@
     return lax.dot_general(a, b, (((1,), (1,)), ((), ())), preferred_element_type=jnp.float32)
 
 
-def step_columns(gram_ref, x, power_ref, scale):
-    power = mm(gram_ref[...], x)
-    if scale is not None:
-        power = power * (scale * scale * scale)
-    power_ref[...] = power
-    square = mm(gram_ref[...], power.astype(jnp.bfloat16))
-    current = x.astype(jnp.float32)
-    if scale is not None:
-        square = square * (scale * scale)
-        current = current * scale
-    return (3.4445 * current - 4.775 * power_ref[...] + 2.0315 * square).astype(jnp.bfloat16)
-
-
-def gram_rows(x_ref, gram_ref, tile, with_trace):
+def symmetric(x_ref, out_ref, with_trace=False, finish=None):
     order = x_ref.shape[0]
+    tile = min(256, order)
     trace = jnp.zeros((tile, tile), jnp.float32)
     eye = lax.broadcasted_iota(jnp.int32, (tile, tile), 0) == lax.broadcasted_iota(jnp.int32, (tile, tile), 1)
     for i in range(order // tile):
-        rows = slice(i * tile, (i + 1) * tile)
-        part = mm_rows(x_ref[rows, :], x_ref[...])
+        cols = slice(i * tile, (i + 1) * tile)
+        below = slice(i * tile, order)
+        part = mm_rows(x_ref[below, :], x_ref[cols, :])
         if with_trace:
-            trace = trace + jnp.where(eye, part[:, rows], 0.0)
-        gram_ref[rows, :] = part.astype(jnp.bfloat16)
+            trace = trace + jnp.where(eye, part[:tile], 0.0)
+        if finish is not None:
+            part = finish(part, below, cols)
+        part = part.astype(jnp.bfloat16)
+        out_ref[below, cols] = part
+        if i + 1 < order // tile:
+            out_ref[cols, (i + 1) * tile :] = part[tile:].T
     return jnp.sum(trace) if with_trace else None
+
+
+def step_columns(gram_ref, x, power_ref):
+    power = mm(gram_ref[...], x)
+    power_ref[...] = power
+    square = mm(gram_ref[...], power.astype(jnp.bfloat16))
+    return 3.4445 * x.astype(jnp.float32) - 4.775 * power_ref[...] + 2.0315 * square
 
 
 def finish(new, k, plan, outs):
@@ -184,21 +185,26 @@
 def first_kernel(places, plan, n, *refs):
     ins, refs = refs[:n], refs[n + 1 :]
     y_ref, h_ref, refs = refs[0], refs[1], refs[2:]
-    outs, (x_ref, g_ref, power_ref) = refs[: len(plan)], refs[len(plan) :]
+    outs, (x_ref, g_ref, w_ref, power_ref) = refs[: len(plan)], refs[len(plan) :]
     order, cols = power_ref.shape
     rows = ins[0].shape[1]
     for k, u, which, b in places:
         x_ref[u * rows : (u + 1) * rows, k * cols : (k + 1) * cols] = ins[which][b]
-    tile = min(256, order)
-    total = gram_rows(x_ref, g_ref, tile, True)
-    scale = 1.0 / (jnp.sqrt(total) + 1e-07)
+    scale = 1.0 / (jnp.sqrt(symmetric(x_ref, g_ref, with_trace=True)) + 1e-07)
+    by_gram, by_square = -4.775 * (scale * scale), 2.0315 * (scale * scale) * (scale * scale)
+
+    def weights(square, rows, cols):
+        return by_gram * g_ref[rows, cols].astype(jnp.float32) + by_square * square
+
+    symmetric(g_ref, w_ref, finish=weights)
     for k in range(order // cols):
         c = slice(k * cols, (k + 1) * cols)
-        y_ref[:, c] = step_columns(g_ref, x_ref[:, c], power_ref, scale)
-    gram_rows(y_ref, h_ref, tile, False)
+        x = x_ref[:, c]
+        y_ref[:, c] = (scale * (3.4445 * x.astype(jnp.float32) + mm(w_ref[...], x))).astype(jnp.bfloat16)
+    symmetric(y_ref, h_ref)
     for k in sorted({k for pieces in plan for k, _ in pieces}):
-        new = step_columns(h_ref, y_ref[:, k * cols : (k + 1) * cols], power_ref, None)
-        finish(new, k, plan, outs)
+        new = step_columns(h_ref, y_ref[:, k * cols : (k + 1) * cols], power_ref)
+        finish(new.astype(jnp.bfloat16), k, plan, outs)
 
 
 def first(chunks, plan, after):
@@ -212,9 +218,9 @@
         out_specs=[whole()] * (2 + len(plan)),
         out_shape=[square, square]
         + [jax.ShapeDtypeStruct((len(pieces), rows, cols), jnp.bfloat16) for pieces in plan],
-        scratch_shapes=[pltpu.VMEM((order, order), jnp.bfloat16)] * 2 + [pltpu.VMEM((order, cols), jnp.float32)],
+        scratch_shapes=[pltpu.VMEM((order, order), jnp.bfloat16)] * 3 + [pltpu.VMEM((order, cols), jnp.float32)],
         compiler_params=params(24),
-        cost_estimate=cost(9 * order**3, 12 * order**2),
+        cost_estimate=cost(7 * order**3, 12 * order**2),
     )(*arrays, after)
 
 
@@ -222,8 +228,8 @@
     outs, power_ref = refs[:-1], refs[-1]
     order, cols = power_ref.shape
     for k in sorted({k for pieces in plan for k, _ in pieces}, reverse=True):
-        new = step_columns(g_ref, x_ref[:, k * cols : (k + 1) * cols], power_ref, None)
-        finish(new, k, plan, outs)
+        new = step_columns(g_ref, x_ref[:, k * cols : (k + 1) * cols], power_ref)
+        finish(new.astype(jnp.bfloat16), k, plan, outs)
 
 
 def last(x, g, plan, rows, cols):
@@ -243,8 +249,12 @@
     o_ref, sems = refs[-2:]
     copies = []
     for n, (k, u, which, b) in enumerate(places):
-        target = (where_ref[0] ^ k) * shards + (where_ref[1] ^ u)
-        copies.append(pltpu.make_async_copy(refs[which].at[b], o_ref.at[target], sems.at[n]))
+        group = (where_ref[0] ^ k) * shards
+        if b is None:
+            src, dst = refs[which], o_ref.at[pl.ds(group, shards)]
+        else:
+            src, dst = refs[which].at[b], o_ref.at[group + (where_ref[1] ^ u)]
+        copies.append(pltpu.make_async_copy(src, dst, sems.at[n]))
     for c in copies:
         c.start()
     for c in copies:
@@ -262,7 +272,7 @@
         scratch_shapes=[pltpu.SemaphoreType.DMA((len(places),))],
         input_output_aliases={len(arrays) + 1: 0} if more else {},
         compiler_params=params(8),
-        cost_estimate=cost(0, 4 * len(places) * shape[1] * shape[2]),
+        cost_estimate=cost(0, 4 * shape[0] * shape[1] * shape[2]),
     )(where, *arrays, *more)
 
 

time: 115 us -> 112 us (0.974)
  Pallas kernels: 27.2 us -> 23.9 us
    pallas_call x1, Pallas kernels: 11.8 us -> 8.65 us  [first(): pl.pallas_call(functools.partial(first_kernel, places, plan, len(arrays))...]
where the time goes in v3:
time: 112 us
  starting transfers between devices  41.4 us (37%)
  waiting for transfers between devices  41.2 us (37%)
  Pallas kernels  23.9 us (21%)
  local copies, waits for them, and re-layouts  2.2 us (2%)
  other arithmetic  1.77 us (2%)
    ppermute x28, waiting for transfers between devices, swap_shard(): return lax.ppermute(piece, 'shard', [(s, s ^ u) for s in range(count)])  31.9 us
    ppermute x28, starting transfers between devices, swap_shard(): return lax.ppermute(piece, 'shard', [(s, s ^ u) for s in range(count)])  30.7 us
    ppermute x6, starting transfers between devices, swap_tensor(): return lax.ppermute(piece, 'tensor', [(t, t ^ k) for t in range(count)])  10.7 us
    ppermute x6, waiting for transfers between devices, swap_tensor(): return lax.ppermute(piece, 'tensor', [(t, t ^ k) for t in range(count)])  9.3 us
    pallas_call x1, Pallas kernels, first(): pl.pallas_call(functools.partial(first_kernel, places, plan, len(arrays))...  8.65 us
    pallas_call x2, Pallas kernels, last(): pl.pallas_call(functools.partial(last_kernel, plan), in_specs=[whole()] *...  5.57 us
    pallas_call x1, Pallas kernels, next_momentum(): pl.pallas_call(momentum_kernel, grid=(steps,), in_specs=[spec, spec, whol...  3.59 us
    pallas_call x4, Pallas kernels, regroup(): pl.pallas_call(functools.partial(regroup_kernel, plan, len(arrays)), in_s...  2.44 us
  transfers between devices with their start and end apart: 34, of which 18 were waited for; matrix products, arithmetic and copies ran while one was open for 0% of the time, Pallas kernels for 12%

profile of v3, /device:TPU:0, one launch (start us, length us, event | category | flops | bytes accessed | tf_op | source)
XLA Modules:
  0.0 111.5 jit_solution(14254252071889107445)
XLA Ops:
  0.6 1.7 %fusion.1 = bf16[8,128,256]{2,1,0:T(8,128)(2,1)S(1)} fusion(f32[32,128,256]{2,1,0:T(8,128)} %m_ref.5, s32[]{:T(128)S(6)} %select_n.4, bf16[32,128,256]{2,1,0:T(8,128)(2,1)} %g_ref.5), kind=kLoop, calls=%fused_computation.3 | loop fusion | flops 1572864 | bytes 2097156 | tf_op jit(solution)/shard_map/convert_element_type | solution.py:73
  2.3 4.1 %collective-permute-start = (bf16[8,128,256]{2,1,0:T(8,128)(2,1)S(1)}, bf16[8,128,256]{2,1,0:T(8,128)(2,1)S(1)}, u32[]{:S(2)}, u32[]{:S(2)}) collective-permute-start(bf16[8,128,256]{2,1,0:T(8,128)(2,1)S(1)} %fusion.1), channel_id=1, source_target_pairs={{0,2},{1,3},{2,0},{3,1},{4,6},{5,7},{6,4},{7,5},{8,10},{9,11},{10,... | collective-permute-start | bytes 1572872 | tf_op jit(solution)/shard_map/ppermute | solution.py:85
  6.5 2.2 %copy-done = f32[32,128,256]{2,1,0:T(8,128)S(1)} copy-done((f32[32,128,256]{2,1,0:T(8,128)S(1)}, f32[32,128,256]{2,1,0:T(8,128)}, u32[]{:S(2)}) %copy-start) | copy-done | bytes 4194328
  13.3 2.8 %collective-permute-done.9.refs_2_ = bf16[2,128,256]{2,1,0:T(8,128)(2,1)S(1)} collective-permute-done((bf16[2,128,256]{2,1,0:T(8,128)(2,1)S(1)}, bf16[2,128,256]{2,1,0:T(8,128)(2,1)S(1)}, u32[]{:S(2)}, u32[]{:S(2)}) %collective-permute-start.9) | collective-permute-done | bytes 131104 | tf_op jit(solution)/shard_map/ppermute | solution.py:90
  16.1 2.4 %collective-permute-start.13 = (bf16[2,128,256]{2,1,0:T(8,128)(2,1)S(1)}, bf16[2,128,256]{2,1,0:T(8,128)(2,1)S(1)}, u32[]{:S(2)}, u32[]{:S(2)}) collective-permute-start(bf16[2,128,256]{2,1,0:T(8,128)(2,1)S(1)} %get-tuple-element.58), channel_id=1, source_target_pairs={{0,24},{4,28},{8,16},{12,20},{16,8},{20,12},{24,0},{28,4},{1,25},{... | collective-permute-start | bytes 393224 | tf_op jit(solution)/shard_map/ppermute | solution.py:90
  18.5 2.5 %collective-permute-start.14 = (bf16[2,128,256]{2,1,0:T(8,128)(2,1)S(1)}, bf16[2,128,256]{2,1,0:T(8,128)(2,1)S(1)}, u32[]{:S(2)}, u32[]{:S(2)}) collective-permute-start(bf16[2,128,256]{2,1,0:T(8,128)(2,1)S(1)} %get-tuple-element.59), channel_id=1, source_target_pairs={{0,28},{4,24},{8,20},{12,16},{16,12},{20,8},{24,4},{28,0},{1,29},{... | collective-permute-start | bytes 393224 | tf_op jit(solution)/shard_map/ppermute | solution.py:90
  21.1 3.7 %collective-permute-done.12.refs_5_ = bf16[2,128,256]{2,1,0:T(8,128)(2,1)S(1)} collective-permute-done((bf16[2,128,256]{2,1,0:T(8,128)(2,1)S(1)}, bf16[2,128,256]{2,1,0:T(8,128)(2,1)S(1)}, u32[]{:S(2)}, u32[]{:S(2)}) %collective-permute-start.12) | collective-permute-done | bytes 131104 | tf_op jit(solution)/shard_map/ppermute | solution.py:90
  25.7 1.6 %collective-permute-start.15 = (bf16[8,128,256]{2,1,0:T(8,128)(2,1)S(1)}, bf16[8,128,256]{2,1,0:T(8,128)(2,1)S(1)}, u32[]{:S(2)}, u32[]{:S(2)}) collective-permute-start(bf16[8,128,256]{2,1,0:T(8,128)(2,1)S(1)} %get-tuple-element.60), channel_id=1, source_target_pairs={{0,1},{1,0},{2,3},{3,2},{4,5},{5,4},{6,7},{7,6},{8,9},{9,8},{10,11... | collective-permute-start | bytes 1572872 | tf_op jit(solution)/shard_map/ppermute | solution.py:85
  30.3 1.6 %collective-permute-start.2 = (bf16[2,128,256]{2,1,0:T(8,128)(2,1)S(1)}, bf16[2,128,256]{2,1,0:T(8,128)(2,1)S(1)}, u32[]{:S(2)}, u32[]{:S(2)}) collective-permute-start(bf16[2,128,256]{2,1,0:T(8,128)(2,1)S(1)} %get-tuple-element.46), channel_id=1, source_target_pairs={{0,8},{4,12},{8,0},{12,4},{16,24},{20,28},{24,16},{28,20},{1,9},{5... | collective-permute-start | bytes 393224 | tf_op jit(solution)/shard_map/ppermute | solution.py:90
  32.2 1.6 %collective-permute-start.4 = (bf16[2,128,256]{2,1,0:T(8,128)(2,1)S(1)}, bf16[2,128,256]{2,1,0:T(8,128)(2,1)S(1)}, u32[]{:S(2)}, u32[]{:S(2)}) collective-permute-start(bf16[2,128,256]{2,1,0:T(8,128)(2,1)S(1)} %get-tuple-element.48), channel_id=1, source_target_pairs={{0,16},{4,20},{8,24},{12,28},{16,0},{20,4},{24,8},{28,12},{1,17},{... | collective-permute-start | bytes 393224 | tf_op jit(solution)/shard_map/ppermute | solution.py:90
  33.8 2.9 %collective-permute-done.2.refs_2_ = bf16[2,128,256]{2,1,0:T(8,128)(2,1)S(1)} collective-permute-done((bf16[2,128,256]{2,1,0:T(8,128)(2,1)S(1)}, bf16[2,128,256]{2,1,0:T(8,128)(2,1)S(1)}, u32[]{:S(2)}, u32[]{:S(2)}) %collective-permute-start.2) | collective-permute-done | bytes 131104 | tf_op jit(solution)/shard_map/ppermute | solution.py:90
  38.6 2.5 %collective-permute-start.6 = (bf16[2,128,256]{2,1,0:T(8,128)(2,1)S(1)}, bf16[2,128,256]{2,1,0:T(8,128)(2,1)S(1)}, u32[]{:S(2)}, u32[]{:S(2)}) collective-permute-start(bf16[2,128,256]{2,1,0:T(8,128)(2,1)S(1)} %get-tuple-element.50), channel_id=1, source_target_pairs={{0,24},{4,28},{8,16},{12,20},{16,8},{20,12},{24,0},{28,4},{1,25},{... | collective-permute-start | bytes 393224 | tf_op jit(solution)/shard_map/ppermute | solution.py:90
  41.4 3.6 %shard_map.43 = (f32[32,128,256]{2,1,0:T(8,128)}, f32[8,128]{1,0:T(8,128)S(1)}) custom-call(bf16[32,128,256]{2,1,0:T(8,128)(2,1)S(1)} %copy-done.2, f32[32,128,256]{2,1,0:T(8,128)S(1)} %copy-done.1, bf16[2,128,256]{2,1,0:T(8,128)(2,1)S(1)} %get-tuple-element.43.after_ref.refs_0_), custom_call_target="tpu_custom_call" | custom-call | flops 1000 | bytes 1000 | tf_op jit(solution)/shard_map/pallas_call | solution.py:56
  45.8 2.2 %collective-permute-done.7.refs_7_ = bf16[2,128,256]{2,1,0:T(8,128)(2,1)S(1)} collective-permute-done((bf16[2,128,256]{2,1,0:T(8,128)(2,1)S(1)}, bf16[2,128,256]{2,1,0:T(8,128)(2,1)S(1)}, u32[]{:S(2)}, u32[]{:S(2)}) %collective-permute-start.7) | collective-permute-done | bytes 131104 | tf_op jit(solution)/shard_map/ppermute | solution.py:90
  48.0 4.1 %collective-permute-done.15.refs_8_ = bf16[8,128,256]{2,1,0:T(8,128)(2,1)S(1)} collective-permute-done((bf16[8,128,256]{2,1,0:T(8,128)(2,1)S(1)}, bf16[8,128,256]{2,1,0:T(8,128)(2,1)S(1)}, u32[]{:S(2)}, u32[]{:S(2)}) %collective-permute-start.15) | collective-permute-done | bytes 524320 | tf_op jit(solution)/shard_map/ppermute | solution.py:85
  52.1 8.7 %shard_map.46 = (bf16[1024,1024]{1,0:T(8,128)(2,1)S(1)}, bf16[1024,1024]{1,0:T(8,128)(2,1)S(1)}, bf16[8,128,256]{2,1,0:T(8,128)(2,1)S(1)}) custom-call(bf16[2,128,256]{2,1,0:T(8,128)(2,1)S(1)} %get-tuple-element.43.after_ref.refs_0_, bf16[2,128,256]{2,1,0:T(8,128)(2,1)S(1)} %collective-permute-done.1.refs_1_, ...), custom_call_target="tpu_custom_call" | custom-call | flops 7516192768 | bytes 12582912 | tf_op jit(solution)/shard_map/pallas_call | solution.py:215
  60.7 2.7 %collective-permute-start.17 = (bf16[8,128,256]{2,1,0:T(8,128)(2,1)S(1)}, bf16[8,128,256]{2,1,0:T(8,128)(2,1)S(1)}, u32[]{:S(2)}, u32[]{:S(2)}) collective-permute-start(bf16[8,128,256]{2,1,0:T(8,128)(2,1)S(1)} %get-tuple-element.63), channel_id=1, source_target_pairs={{0,2},{1,3},{2,0},{3,1},{4,6},{5,7},{6,4},{7,5},{8,10},{9,11},{10,... | collective-permute-start | bytes 1572872 | tf_op jit(solution)/shard_map/ppermute | solution.py:85
  63.5 3.3 %shard_map.49 = (bf16[2,128,256]{2,1,0:T(8,128)(2,1)S(1)}, bf16[2,128,256]{2,1,0:T(8,128)(2,1)S(1)}, bf16[2,128,256]{2,1,0:T(8,128)(2,1)S(1)}, bf16[2,128,256]{2...) custom-call(bf16[1024,1024]{1,0:T(8,128)(2,1)S(1)} %get-tuple-elemen, ...), custom_call_target="tpu_custom_call" | custom-call | flops 2147483648 | bytes 8388608 | tf_op jit(solution)/shard_map/pallas_call | solution.py:237
  66.9 1.6 %collective-permute-start.26 = (bf16[2,128,256]{2,1,0:T(8,128)(2,1)S(1)}, bf16[2,128,256]{2,1,0:T(8,128)(2,1)S(1)}, u32[]{:S(2)}, u32[]{:S(2)}) collective-permute-start(bf16[2,128,256]{2,1,0:T(8,128)(2,1)S(1)} %get-tuple-element.76), channel_id=1, source_target_pairs={{0,8},{4,12},{8,0},{12,4},{16,24},{20,28},{24,16},{28,20},{1,9},{5... | collective-permute-start | bytes 393224 | tf_op jit(solution)/shard_map/ppermute | solution.py:90
  70.5 2.8 %collective-permute-done.26.refs_2_ = bf16[2,128,256]{2,1,0:T(8,128)(2,1)S(1)} collective-permute-done((bf16[2,128,256]{2,1,0:T(8,128)(2,1)S(1)}, bf16[2,128,256]{2,1,0:T(8,128)(2,1)S(1)}, u32[]{:S(2)}, u32[]{:S(2)}) %collective-permute-start.26) | collective-permute-done | bytes 131104 | tf_op jit(solution)/shard_map/ppermute | solution.py:90
  73.3 2.4 %collective-permute-start.30 = (bf16[2,128,256]{2,1,0:T(8,128)(2,1)S(1)}, bf16[2,128,256]{2,1,0:T(8,128)(2,1)S(1)}, u32[]{:S(2)}, u32[]{:S(2)}) collective-permute-start(bf16[2,128,256]{2,1,0:T(8,128)(2,1)S(1)} %get-tuple-element.80), channel_id=1, source_target_pairs={{0,24},{4,28},{8,16},{12,20},{16,8},{20,12},{24,0},{28,4},{1,25},{... | collective-permute-start | bytes 393224 | tf_op jit(solution)/shard_map/ppermute | solution.py:90
  75.7 2.5 %collective-permute-start.31 = (bf16[2,128,256]{2,1,0:T(8,128)(2,1)S(1)}, bf16[2,128,256]{2,1,0:T(8,128)(2,1)S(1)}, u32[]{:S(2)}, u32[]{:S(2)}) collective-permute-start(bf16[2,128,256]{2,1,0:T(8,128)(2,1)S(1)} %get-tuple-element.81), channel_id=1, source_target_pairs={{0,28},{4,24},{8,20},{12,16},{16,12},{20,8},{24,4},{28,0},{1,29},{... | collective-permute-start | bytes 393224 | tf_op jit(solution)/shard_map/ppermute | solution.py:90
  78.2 3.7 %collective-permute-done.29.refs_5_ = bf16[2,128,256]{2,1,0:T(8,128)(2,1)S(1)} collective-permute-done((bf16[2,128,256]{2,1,0:T(8,128)(2,1)S(1)}, bf16[2,128,256]{2,1,0:T(8,128)(2,1)S(1)}, u32[]{:S(2)}, u32[]{:S(2)}) %collective-permute-start.29) | collective-permute-done | bytes 131104 | tf_op jit(solution)/shard_map/ppermute | solution.py:90
  84.8 2.2 %shard_map.47.refs_1_ = bf16[8,128,256]{2,1,0:T(8,128)(2,1)S(1)} custom-call(bf16[1024,1024]{1,0:T(8,128)(2,1)S(1)} %get-tuple-element.64.x_ref, bf16[1024,1024]{1,0:T(8,128)(2,1)S(1)} %get-tuple-element.65.g_ref), custom_call_target="tpu_custom_call" | custom-call | flops 1073741824 | bytes 8388608 | tf_op jit(solution)/shard_map/pallas_call | solution.py:237
  87.7 1.7 %collective-permute-start.19 = (bf16[2,128,256]{2,1,0:T(8,128)(2,1)S(1)}, bf16[2,128,256]{2,1,0:T(8,128)(2,1)S(1)}, u32[]{:S(2)}, u32[]{:S(2)}) collective-permute-start(bf16[2,128,256]{2,1,0:T(8,128)(2,1)S(1)} %get-tuple-element.68), channel_id=1, source_target_pairs={{0,8},{4,12},{8,0},{12,4},{16,24},{20,28},{24,16},{28,20},{1,9},{5... | collective-permute-start | bytes 393224 | tf_op jit(solution)/shard_map/ppermute | solution.py:90
  89.6 1.6 %collective-permute-start.21 = (bf16[2,128,256]{2,1,0:T(8,128)(2,1)S(1)}, bf16[2,128,256]{2,1,0:T(8,128)(2,1)S(1)}, u32[]{:S(2)}, u32[]{:S(2)}) collective-permute-start(bf16[2,128,256]{2,1,0:T(8,128)(2,1)S(1)} %get-tuple-element.70), channel_id=1, source_target_pairs={{0,16},{4,20},{8,24},{12,28},{16,0},{20,4},{24,8},{28,12},{1,17},{... | collective-permute-start | bytes 393224 | tf_op jit(solution)/shard_map/ppermute | solution.py:90
  91.2 2.9 %collective-permute-done.19.refs_2_ = bf16[2,128,256]{2,1,0:T(8,128)(2,1)S(1)} collective-permute-done((bf16[2,128,256]{2,1,0:T(8,128)(2,1)S(1)}, bf16[2,128,256]{2,1,0:T(8,128)(2,1)S(1)}, u32[]{:S(2)}, u32[]{:S(2)}) %collective-permute-start.19) | collective-permute-done | bytes 131104 | tf_op jit(solution)/shard_map/ppermute | solution.py:90
  96.0 2.5 %collective-permute-start.23 = (bf16[2,128,256]{2,1,0:T(8,128)(2,1)S(1)}, bf16[2,128,256]{2,1,0:T(8,128)(2,1)S(1)}, u32[]{:S(2)}, u32[]{:S(2)}) collective-permute-start(bf16[2,128,256]{2,1,0:T(8,128)(2,1)S(1)} %get-tuple-element.72), channel_id=1, source_target_pairs={{0,24},{4,28},{8,16},{12,20},{16,8},{20,12},{24,0},{28,4},{1,25},{... | collective-permute-start | bytes 393224 | tf_op jit(solution)/shard_map/ppermute | solution.py:90
  99.7 3.5 %collective-permute-done.23.refs_6_ = bf16[2,128,256]{2,1,0:T(8,128)(2,1)S(1)} collective-permute-done((bf16[2,128,256]{2,1,0:T(8,128)(2,1)S(1)}, bf16[2,128,256]{2,1,0:T(8,128)(2,1)S(1)}, u32[]{:S(2)}, u32[]{:S(2)}) %collective-permute-start.23) | collective-permute-done | bytes 131104 | tf_op jit(solution)/shard_map/ppermute | solution.py:90
  103.1 2.2 %collective-permute-done.24.refs_7_ = bf16[2,128,256]{2,1,0:T(8,128)(2,1)S(1)} collective-permute-done((bf16[2,128,256]{2,1,0:T(8,128)(2,1)S(1)}, bf16[2,128,256]{2,1,0:T(8,128)(2,1)S(1)}, u32[]{:S(2)}, u32[]{:S(2)}) %collective-permute-start.24) | collective-permute-done | bytes 131104 | tf_op jit(solution)/shard_map/ppermute | solution.py:90
  105.3 4.0 %collective-permute-done.32.refs_8_ = bf16[8,128,256]{2,1,0:T(8,128)(2,1)S(1)} collective-permute-done((bf16[8,128,256]{2,1,0:T(8,128)(2,1)S(1)}, bf16[8,128,256]{2,1,0:T(8,128)(2,1)S(1)}, u32[]{:S(2)}, u32[]{:S(2)}) %collective-permute-start.32) | collective-permute-done | bytes 524320 | tf_op jit(solution)/shard_map/ppermute | solution.py:85
  109.3 2.0 %shard_map.51 = bf16[32,128,256]{2,1,0:T(8,128)(2,1)} custom-call(s32[2]{0:T(128)S(1)} %pad_add_fusion.where_ref, bf16[2,128,256]{2,1,0:T(8,128)(2,1)S(1)} %get-tuple-element.66.refs_0_, bf16[2,128,256]{2,1,0:T(8,128)(2,1)S(1)} %collective-permute-done.18.refs_1_, bf16[2,128,256]{2,1,0:T(8,128)(2,1)S(1)} %collective-permute-done.19.refs_2_, ...), custom_call_target="tpu_custom_call" | custom-call | bytes 4194304 | tf_op jit(solution)/shard_map/pallas_call | solution.py:267
  (55 shorter events, 20.5 us)
Async XLA Ops:
  2.3 27.3 %collective-permute-start = (bf16[8,128,256]{2,1,0:T(8,128)(2,1)S(1)}, bf16[8,128,256]{2,1,0:T(8,128)(2,1)S(1)}, u32[]{:S(2)}, u32[]{:S(2)}) collective-permute-start(bf16[8,128,256]{2,1,0:T(8,128)(2,1)S(1)} %fusion.1), channel_id=1, source_target_pairs={{0,2},{1,3},{2,0},{3,1},{4,6},{5,7},{6,4},{7,5},{8,10},{9,11},{10,... | collective-permute-start | bytes 1572872 | tf_op jit(solution)/shard_map/ppermute | solution.py:85
  9.6 3.5 %collective-permute-start.8 = (bf16[2,128,256]{2,1,0:T(8,128)(2,1)S(1)}, bf16[2,128,256]{2,1,0:T(8,128)(2,1)S(1)}, u32[]{:S(2)}, u32[]{:S(2)}) collective-permute-start(bf16[2,128,256]{2,1,0:T(8,128)(2,1)S(1)} %get-tuple-element.53), channel_id=1, source_target_pairs={{0,4},{4,0},{8,12},{12,8},{16,20},{20,16},{24,28},{28,24},{1,5},{5... | collective-permute-start | bytes 393224 | tf_op jit(solution)/shard_map/ppermute | solution.py:90
  9.7 6.4 %collective-permute-start.9 = (bf16[2,128,256]{2,1,0:T(8,128)(2,1)S(1)}, bf16[2,128,256]{2,1,0:T(8,128)(2,1)S(1)}, u32[]{:S(2)}, u32[]{:S(2)}) collective-permute-start(bf16[2,128,256]{2,1,0:T(8,128)(2,1)S(1)} %get-tuple-element.54), channel_id=1, source_target_pairs={{0,8},{4,12},{8,0},{12,4},{16,24},{20,28},{24,16},{28,20},{1,9},{5... | collective-permute-start | bytes 393224 | tf_op jit(solution)/shard_map/ppermute | solution.py:90
  11.3 7.3 %collective-permute-start.10 = (bf16[2,128,256]{2,1,0:T(8,128)(2,1)S(1)}, bf16[2,128,256]{2,1,0:T(8,128)(2,1)S(1)}, u32[]{:S(2)}, u32[]{:S(2)}) collective-permute-start(bf16[2,128,256]{2,1,0:T(8,128)(2,1)S(1)} %get-tuple-element.55), channel_id=1, source_target_pairs={{0,12},{4,8},{8,4},{12,0},{16,28},{20,24},{24,20},{28,16},{1,13},{... | collective-permute-start | bytes 393224 | tf_op jit(solution)/shard_map/ppermute | solution.py:90
  11.6 9.5 %collective-permute-start.11 = (bf16[2,128,256]{2,1,0:T(8,128)(2,1)S(1)}, bf16[2,128,256]{2,1,0:T(8,128)(2,1)S(1)}, u32[]{:S(2)}, u32[]{:S(2)}) collective-permute-start(bf16[2,128,256]{2,1,0:T(8,128)(2,1)S(1)} %get-tuple-element.56), channel_id=1, source_target_pairs={{0,16},{4,20},{8,24},{12,28},{16,0},{20,4},{24,8},{28,12},{1,17},{... | collective-permute-start | bytes 393224 | tf_op jit(solution)/shard_map/ppermute | solution.py:90
  13.1 11.7 %collective-permute-start.12 = (bf16[2,128,256]{2,1,0:T(8,128)(2,1)S(1)}, bf16[2,128,256]{2,1,0:T(8,128)(2,1)S(1)}, u32[]{:S(2)}, u32[]{:S(2)}) collective-permute-start(bf16[2,128,256]{2,1,0:T(8,128)(2,1)S(1)} %get-tuple-element.57), channel_id=1, source_target_pairs={{0,20},{4,16},{8,28},{12,24},{16,4},{20,0},{24,12},{28,8},{1,21},{... | collective-permute-start | bytes 393224 | tf_op jit(solution)/shard_map/ppermute | solution.py:90
  16.1 8.7 %collective-permute-start.13 = (bf16[2,128,256]{2,1,0:T(8,128)(2,1)S(1)}, bf16[2,128,256]{2,1,0:T(8,128)(2,1)S(1)}, u32[]{:S(2)}, u32[]{:S(2)}) collective-permute-start(bf16[2,128,256]{2,1,0:T(8,128)(2,1)S(1)} %get-tuple-element.58), channel_id=1, source_target_pairs={{0,24},{4,28},{8,16},{12,20},{16,8},{20,12},{24,0},{28,4},{1,25},{... | collective-permute-start | bytes 393224 | tf_op jit(solution)/shard_map/ppermute | solution.py:90
  18.5 6.5 %collective-permute-start.14 = (bf16[2,128,256]{2,1,0:T(8,128)(2,1)S(1)}, bf16[2,128,256]{2,1,0:T(8,128)(2,1)S(1)}, u32[]{:S(2)}, u32[]{:S(2)}) collective-permute-start(bf16[2,128,256]{2,1,0:T(8,128)(2,1)S(1)} %get-tuple-element.59), channel_id=1, source_target_pairs={{0,28},{4,24},{8,20},{12,16},{16,12},{20,8},{24,4},{28,0},{1,29},{... | collective-permute-start | bytes 393224 | tf_op jit(solution)/shard_map/ppermute | solution.py:90
  25.7 26.4 %collective-permute-start.15 = (bf16[8,128,256]{2,1,0:T(8,128)(2,1)S(1)}, bf16[8,128,256]{2,1,0:T(8,128)(2,1)S(1)}, u32[]{:S(2)}, u32[]{:S(2)}) collective-permute-start(bf16[8,128,256]{2,1,0:T(8,128)(2,1)S(1)} %get-tuple-element.60), channel_id=1, source_target_pairs={{0,1},{1,0},{2,3},{3,2},{4,5},{5,4},{6,7},{7,6},{8,9},{9,8},{10,11... | collective-permute-start | bytes 1572872 | tf_op jit(solution)/shard_map/ppermute | solution.py:85
  27.3 24.7 %collective-permute-start.16 = (bf16[8,128,256]{2,1,0:T(8,128)(2,1)S(1)}, bf16[8,128,256]{2,1,0:T(8,128)(2,1)S(1)}, u32[]{:S(2)}, u32[]{:S(2)}) collective-permute-start(bf16[8,128,256]{2,1,0:T(8,128)(2,1)S(1)} %get-tuple-element.61), channel_id=1, source_target_pairs={{0,3},{1,2},{2,1},{3,0},{4,7},{5,6},{6,5},{7,4},{8,11},{9,10},{10,... | collective-permute-start | bytes 1572872 | tf_op jit(solution)/shard_map/ppermute | solution.py:85
  30.3 6.4 %collective-permute-start.2 = (bf16[2,128,256]{2,1,0:T(8,128)(2,1)S(1)}, bf16[2,128,256]{2,1,0:T(8,128)(2,1)S(1)}, u32[]{:S(2)}, u32[]{:S(2)}) collective-permute-start(bf16[2,128,256]{2,1,0:T(8,128)(2,1)S(1)} %get-tuple-element.46), channel_id=1, source_target_pairs={{0,8},{4,12},{8,0},{12,4},{16,24},{20,28},{24,16},{28,20},{1,9},{5... | collective-permute-start | bytes 393224 | tf_op jit(solution)/shard_map/ppermute | solution.py:90
  32.0 6.7 %collective-permute-start.3 = (bf16[2,128,256]{2,1,0:T(8,128)(2,1)S(1)}, bf16[2,128,256]{2,1,0:T(8,128)(2,1)S(1)}, u32[]{:S(2)}, u32[]{:S(2)}) collective-permute-start(bf16[2,128,256]{2,1,0:T(8,128)(2,1)S(1)} %get-tuple-element.47), channel_id=1, source_target_pairs={{0,12},{4,8},{8,4},{12,0},{16,28},{20,24},{24,20},{28,16},{1,13},{... | collective-permute-start | bytes 393224 | tf_op jit(solution)/shard_map/ppermute | solution.py:90
  32.2 8.9 %collective-permute-start.4 = (bf16[2,128,256]{2,1,0:T(8,128)(2,1)S(1)}, bf16[2,128,256]{2,1,0:T(8,128)(2,1)S(1)}, u32[]{:S(2)}, u32[]{:S(2)}) collective-permute-start(bf16[2,128,256]{2,1,0:T(8,128)(2,1)S(1)} %get-tuple-element.48), channel_id=1, source_target_pairs={{0,16},{4,20},{8,24},{12,28},{16,0},{20,4},{24,8},{28,12},{1,17},{... | collective-permute-start | bytes 393224 | tf_op jit(solution)/shard_map/ppermute | solution.py:90
  36.7 8.3 %collective-permute-start.5 = (bf16[2,128,256]{2,1,0:T(8,128)(2,1)S(1)}, bf16[2,128,256]{2,1,0:T(8,128)(2,1)S(1)}, u32[]{:S(2)}, u32[]{:S(2)}) collective-permute-start(bf16[2,128,256]{2,1,0:T(8,128)(2,1)S(1)} %get-tuple-element.49), channel_id=1, source_target_pairs={{0,20},{4,16},{8,28},{12,24},{16,4},{20,0},{24,12},{28,8},{1,21},{... | collective-permute-start | bytes 393224 | tf_op jit(solution)/shard_map/ppermute | solution.py:90
  38.6 7.2 %collective-permute-start.6 = (bf16[2,128,256]{2,1,0:T(8,128)(2,1)S(1)}, bf16[2,128,256]{2,1,0:T(8,128)(2,1)S(1)}, u32[]{:S(2)}, u32[]{:S(2)}) collective-permute-start(bf16[2,128,256]{2,1,0:T(8,128)(2,1)S(1)} %get-tuple-element.50), channel_id=1, source_target_pairs={{0,24},{4,28},{8,16},{12,20},{16,8},{20,12},{24,0},{28,4},{1,25},{... | collective-permute-start | bytes 393224 | tf_op jit(solution)/shard_map/ppermute | solution.py:90
  41.1 6.9 %collective-permute-start.7 = (bf16[2,128,256]{2,1,0:T(8,128)(2,1)S(1)}, bf16[2,128,256]{2,1,0:T(8,128)(2,1)S(1)}, u32[]{:S(2)}, u32[]{:S(2)}) collective-permute-start(bf16[2,128,256]{2,1,0:T(8,128)(2,1)S(1)} %get-tuple-element.51), channel_id=1, source_target_pairs={{0,28},{4,24},{8,20},{12,16},{16,12},{20,8},{24,4},{28,0},{1,29},{... | collective-permute-start | bytes 393224 | tf_op jit(solution)/shard_map/ppermute | solution.py:90
  60.7 26.3 %collective-permute-start.17 = (bf16[8,128,256]{2,1,0:T(8,128)(2,1)S(1)}, bf16[8,128,256]{2,1,0:T(8,128)(2,1)S(1)}, u32[]{:S(2)}, u32[]{:S(2)}) collective-permute-start(bf16[8,128,256]{2,1,0:T(8,128)(2,1)S(1)} %get-tuple-element.63), channel_id=1, source_target_pairs={{0,2},{1,3},{2,0},{3,1},{4,6},{5,7},{6,4},{7,5},{8,10},{9,11},{10,... | collective-permute-start | bytes 1572872 | tf_op jit(solution)/shard_map/ppermute | solution.py:85
  66.8 3.5 %collective-permute-start.25 = (bf16[2,128,256]{2,1,0:T(8,128)(2,1)S(1)}, bf16[2,128,256]{2,1,0:T(8,128)(2,1)S(1)}, u32[]{:S(2)}, u32[]{:S(2)}) collective-permute-start(bf16[2,128,256]{2,1,0:T(8,128)(2,1)S(1)} %get-tuple-element.75), channel_id=1, source_target_pairs={{0,4},{4,0},{8,12},{12,8},{16,20},{20,16},{24,28},{28,24},{1,5},{5... | collective-permute-start | bytes 393224 | tf_op jit(solution)/shard_map/ppermute | solution.py:90
  66.9 6.4 %collective-permute-start.26 = (bf16[2,128,256]{2,1,0:T(8,128)(2,1)S(1)}, bf16[2,128,256]{2,1,0:T(8,128)(2,1)S(1)}, u32[]{:S(2)}, u32[]{:S(2)}) collective-permute-start(bf16[2,128,256]{2,1,0:T(8,128)(2,1)S(1)} %get-tuple-element.76), channel_id=1, source_target_pairs={{0,8},{4,12},{8,0},{12,4},{16,24},{20,28},{24,16},{28,20},{1,9},{5... | collective-permute-start | bytes 393224 | tf_op jit(solution)/shard_map/ppermute | solution.py:90
  68.5 7.3 %collective-permute-start.27 = (bf16[2,128,256]{2,1,0:T(8,128)(2,1)S(1)}, bf16[2,128,256]{2,1,0:T(8,128)(2,1)S(1)}, u32[]{:S(2)}, u32[]{:S(2)}) collective-permute-start(bf16[2,128,256]{2,1,0:T(8,128)(2,1)S(1)} %get-tuple-element.77), channel_id=1, source_target_pairs={{0,12},{4,8},{8,4},{12,0},{16,28},{20,24},{24,20},{28,16},{1,13},{... | collective-permute-start | bytes 393224 | tf_op jit(solution)/shard_map/ppermute | solution.py:90
  68.8 9.5 %collective-permute-start.28 = (bf16[2,128,256]{2,1,0:T(8,128)(2,1)S(1)}, bf16[2,128,256]{2,1,0:T(8,128)(2,1)S(1)}, u32[]{:S(2)}, u32[]{:S(2)}) collective-permute-start(bf16[2,128,256]{2,1,0:T(8,128)(2,1)S(1)} %get-tuple-element.78), channel_id=1, source_target_pairs={{0,16},{4,20},{8,24},{12,28},{16,0},{20,4},{24,8},{28,12},{1,17},{... | collective-permute-start | bytes 393224 | tf_op jit(solution)/shard_map/ppermute | solution.py:90
  70.3 11.7 %collective-permute-start.29 = (bf16[2,128,256]{2,1,0:T(8,128)(2,1)S(1)}, bf16[2,128,256]{2,1,0:T(8,128)(2,1)S(1)}, u32[]{:S(2)}, u32[]{:S(2)}) collective-permute-start(bf16[2,128,256]{2,1,0:T(8,128)(2,1)S(1)} %get-tuple-element.79), channel_id=1, source_target_pairs={{0,20},{4,16},{8,28},{12,24},{16,4},{20,0},{24,12},{28,8},{1,21},{... | collective-permute-start | bytes 393224 | tf_op jit(solution)/shard_map/ppermute | solution.py:90
  73.3 8.7 %collective-permute-start.30 = (bf16[2,128,256]{2,1,0:T(8,128)(2,1)S(1)}, bf16[2,128,256]{2,1,0:T(8,128)(2,1)S(1)}, u32[]{:S(2)}, u32[]{:S(2)}) collective-permute-start(bf16[2,128,256]{2,1,0:T(8,128)(2,1)S(1)} %get-tuple-element.80), channel_id=1, source_target_pairs={{0,24},{4,28},{8,16},{12,20},{16,8},{20,12},{24,0},{28,4},{1,25},{... | collective-permute-start | bytes 393224 | tf_op jit(solution)/shard_map/ppermute | solution.py:90
  75.7 6.5 %collective-permute-start.31 = (bf16[2,128,256]{2,1,0:T(8,128)(2,1)S(1)}, bf16[2,128,256]{2,1,0:T(8,128)(2,1)S(1)}, u32[]{:S(2)}, u32[]{:S(2)}) collective-permute-start(bf16[2,128,256]{2,1,0:T(8,128)(2,1)S(1)} %get-tuple-element.81), channel_id=1, source_target_pairs={{0,28},{4,24},{8,20},{12,16},{16,12},{20,8},{24,4},{28,0},{1,29},{... | collective-permute-start | bytes 393224 | tf_op jit(solution)/shard_map/ppermute | solution.py:90
  82.9 26.4 %collective-permute-start.32 = (bf16[8,128,256]{2,1,0:T(8,128)(2,1)S(1)}, bf16[8,128,256]{2,1,0:T(8,128)(2,1)S(1)}, u32[]{:S(2)}, u32[]{:S(2)}) collective-permute-start(bf16[8,128,256]{2,1,0:T(8,128)(2,1)S(1)} %get-tuple-element.82), channel_id=1, source_target_pairs={{0,1},{1,0},{2,3},{3,2},{4,5},{5,4},{6,7},{7,6},{8,9},{9,8},{10,11... | collective-permute-start | bytes 1572872 | tf_op jit(solution)/shard_map/ppermute | solution.py:85
  84.4 25.0 %collective-permute-start.33 = (bf16[8,128,256]{2,1,0:T(8,128)(2,1)S(1)}, bf16[8,128,256]{2,1,0:T(8,128)(2,1)S(1)}, u32[]{:S(2)}, u32[]{:S(2)}) collective-permute-start(bf16[8,128,256]{2,1,0:T(8,128)(2,1)S(1)} %get-tuple-element.83), channel_id=1, source_target_pairs={{0,3},{1,2},{2,1},{3,0},{4,7},{5,6},{6,5},{7,4},{8,11},{9,10},{10,... | collective-permute-start | bytes 1572872 | tf_op jit(solution)/shard_map/ppermute | solution.py:85
  87.7 6.4 %collective-permute-start.19 = (bf16[2,128,256]{2,1,0:T(8,128)(2,1)S(1)}, bf16[2,128,256]{2,1,0:T(8,128)(2,1)S(1)}, u32[]{:S(2)}, u32[]{:S(2)}) collective-permute-start(bf16[2,128,256]{2,1,0:T(8,128)(2,1)S(1)} %get-tuple-element.68), channel_id=1, source_target_pairs={{0,8},{4,12},{8,0},{12,4},{16,24},{20,28},{24,16},{28,20},{1,9},{5... | collective-permute-start | bytes 393224 | tf_op jit(solution)/shard_map/ppermute | solution.py:90
  89.4 6.6 %collective-permute-start.20 = (bf16[2,128,256]{2,1,0:T(8,128)(2,1)S(1)}, bf16[2,128,256]{2,1,0:T(8,128)(2,1)S(1)}, u32[]{:S(2)}, u32[]{:S(2)}) collective-permute-start(bf16[2,128,256]{2,1,0:T(8,128)(2,1)S(1)} %get-tuple-element.69), channel_id=1, source_target_pairs={{0,12},{4,8},{8,4},{12,0},{16,28},{20,24},{24,20},{28,16},{1,13},{... | collective-permute-start | bytes 393224 | tf_op jit(solution)/shard_map/ppermute | solution.py:90
  89.6 9.0 %collective-permute-start.21 = (bf16[2,128,256]{2,1,0:T(8,128)(2,1)S(1)}, bf16[2,128,256]{2,1,0:T(8,128)(2,1)S(1)}, u32[]{:S(2)}, u32[]{:S(2)}) collective-permute-start(bf16[2,128,256]{2,1,0:T(8,128)(2,1)S(1)} %get-tuple-element.70), channel_id=1, source_target_pairs={{0,16},{4,20},{8,24},{12,28},{16,0},{20,4},{24,8},{28,12},{1,17},{... | collective-permute-start | bytes 393224 | tf_op jit(solution)/shard_map/ppermute | solution.py:90
  94.1 5.6 %collective-permute-start.22 = (bf16[2,128,256]{2,1,0:T(8,128)(2,1)S(1)}, bf16[2,128,256]{2,1,0:T(8,128)(2,1)S(1)}, u32[]{:S(2)}, u32[]{:S(2)}) collective-permute-start(bf16[2,128,256]{2,1,0:T(8,128)(2,1)S(1)} %get-tuple-element.71), channel_id=1, source_target_pairs={{0,20},{4,16},{8,28},{12,24},{16,4},{20,0},{24,12},{28,8},{1,21},{... | collective-permute-start | bytes 393224 | tf_op jit(solution)/shard_map/ppermute | solution.py:90
  96.0 7.2 %collective-permute-start.23 = (bf16[2,128,256]{2,1,0:T(8,128)(2,1)S(1)}, bf16[2,128,256]{2,1,0:T(8,128)(2,1)S(1)}, u32[]{:S(2)}, u32[]{:S(2)}) collective-permute-start(bf16[2,128,256]{2,1,0:T(8,128)(2,1)S(1)} %get-tuple-element.72), channel_id=1, source_target_pairs={{0,24},{4,28},{8,16},{12,20},{16,8},{20,12},{24,0},{28,4},{1,25},{... | collective-permute-start | bytes 393224 | tf_op jit(solution)/shard_map/ppermute | solution.py:90
  98.5 6.8 %collective-permute-start.24 = (bf16[2,128,256]{2,1,0:T(8,128)(2,1)S(1)}, bf16[2,128,256]{2,1,0:T(8,128)(2,1)S(1)}, u32[]{:S(2)}, u32[]{:S(2)}) collective-permute-start(bf16[2,128,256]{2,1,0:T(8,128)(2,1)S(1)} %get-tuple-element.73), channel_id=1, source_target_pairs={{0,28},{4,24},{8,20},{12,16},{16,12},{20,8},{24,4},{28,0},{1,29},{... | collective-permute-start | bytes 393224 | tf_op jit(solution)/shard_map/ppermute | solution.py:90
  (5 other events, 31.0 us)

commit v4 on v3

--- a/solution.py
+++ b/solution.py
@@ -145,7 +145,7 @@
     return lax.dot_general(a, b, (((1,), (1,)), ((), ())), preferred_element_type=jnp.float32)
 
 
-def symmetric(x_ref, out_ref, with_trace=False, finish=None):
+def symmetric(x_ref, out_ref, with_trace=False, finish=None, mirror=True):
     order = x_ref.shape[0]
     tile = min(256, order)
     trace = jnp.zeros((tile, tile), jnp.float32)
@@ -154,13 +154,13 @@
         cols = slice(i * tile, (i + 1) * tile)
         below = slice(i * tile, order)
         part = mm_rows(x_ref[below, :], x_ref[cols, :])
+        if finish is not None:
+            part = finish(part, below, cols)
         if with_trace:
             trace = trace + jnp.where(eye, part[:tile], 0.0)
-        if finish is not None:
-            part = finish(part, below, cols)
-        part = part.astype(jnp.bfloat16)
+        part = part.astype(out_ref.dtype)
         out_ref[below, cols] = part
-        if i + 1 < order // tile:
+        if mirror and i + 1 < order // tile:
             out_ref[cols, (i + 1) * tile :] = part[tile:].T
     return jnp.sum(trace) if with_trace else None
 
@@ -182,15 +182,52 @@
                 out[i] = done[u * rows : (u + 1) * rows]
 
 
-def first_kernel(places, plan, n, *refs):
-    ins, refs = refs[:n], refs[n + 1 :]
-    y_ref, h_ref, refs = refs[0], refs[1], refs[2:]
+def early_kernel(places, n, *refs):
+    ins, (x_ref, part_ref) = refs[:n], refs[n:]
+    rows, cols = ins[0].shape[1:]
+    at = {k: i * cols for i, k in enumerate(sorted({p[0] for p in places}))}
+    for k, u, which, b in places:
+        x_ref[u * rows : (u + 1) * rows, at[k] : at[k] + cols] = ins[which][b]
+    symmetric(x_ref, part_ref, mirror=False)
+
+
+def early(chunks):
+    arrays, places = arrays_of(chunks)
+    _, rows, cols = arrays[0].shape
+    order = rows * len(chunks[0])
+    return pl.pallas_call(
+        functools.partial(early_kernel, places, len(arrays)),
+        in_specs=[whole()] * len(arrays),
+        out_specs=[whole()] * 2,
+        out_shape=[
+            jax.ShapeDtypeStruct((order, cols * len(chunks)), jnp.bfloat16),
+            jax.ShapeDtypeStruct((order, order), jnp.float32),
+        ],
+        compiler_params=params(16),
+        cost_estimate=cost(1000, 1000),
+    )(*arrays)
+
+
+def first_kernel(early_ks, late_ks, plan, *refs):
+    before_ref, part_ref, refs = refs[0], refs[1], refs[2:]
+    late_refs, (y_ref, h_ref), refs = refs[: len(late_ks)], refs[len(late_ks) + 1 :][:2], refs[len(late_ks) + 3 :]
     outs, (x_ref, g_ref, w_ref, power_ref) = refs[: len(plan)], refs[len(plan) :]
     order, cols = power_ref.shape
-    rows = ins[0].shape[1]
-    for k, u, which, b in places:
-        x_ref[u * rows : (u + 1) * rows, k * cols : (k + 1) * cols] = ins[which][b]
-    scale = 1.0 / (jnp.sqrt(symmetric(x_ref, g_ref, with_trace=True)) + 1e-07)
+    where = {}
+    for i, (k, ref) in enumerate(zip(late_ks, late_refs)):
+        where[k] = (x_ref, slice(i * cols, (i + 1) * cols))
+        x_ref[:, i * cols : (i + 1) * cols] = ref[...].reshape(order, cols)
+    for i, k in enumerate(early_ks):
+        where[k] = (before_ref, slice(i * cols, (i + 1) * cols))
+
+    def chunk(k):
+        ref, c = where[k]
+        return ref[:, c]
+
+    def add(part, rows, cols):
+        return part + part_ref[rows, cols]
+
+    scale = 1.0 / (jnp.sqrt(symmetric(x_ref, g_ref, with_trace=True, finish=add)) + 1e-07)
     by_gram, by_square = -4.775 * (scale * scale), 2.0315 * (scale * scale) * (scale * scale)
 
     def weights(square, rows, cols):
@@ -199,7 +236,7 @@
     symmetric(g_ref, w_ref, finish=weights)
     for k in range(order // cols):
         c = slice(k * cols, (k + 1) * cols)
-        x = x_ref[:, c]
+        x = chunk(k)
         y_ref[:, c] = (scale * (3.4445 * x.astype(jnp.float32) + mm(w_ref[...], x))).astype(jnp.bfloat16)
     symmetric(y_ref, h_ref)
     for k in sorted({k for pieces in plan for k, _ in pieces}):
@@ -207,21 +244,23 @@
         finish(new.astype(jnp.bfloat16), k, plan, outs)
 
 
-def first(chunks, plan, after):
-    arrays, places = arrays_of(chunks)
-    _, rows, cols = arrays[0].shape
-    order = cols * len(chunks)
+def first(early_ks, before, part, late, plan, after):
+    shards, rows, cols = late[max(late)].shape
+    order = shards * rows
+    late_ks = sorted(late)
     square = jax.ShapeDtypeStruct((order, order), jnp.bfloat16)
     return pl.pallas_call(
-        functools.partial(first_kernel, places, plan, len(arrays)),
-        in_specs=[whole()] * len(arrays) + [whole(pl.ANY)],
+        functools.partial(first_kernel, early_ks, late_ks, plan),
+        in_specs=[whole()] * (2 + len(late)) + [whole(pl.ANY)],
         out_specs=[whole()] * (2 + len(plan)),
         out_shape=[square, square]
         + [jax.ShapeDtypeStruct((len(pieces), rows, cols), jnp.bfloat16) for pieces in plan],
-        scratch_shapes=[pltpu.VMEM((order, order), jnp.bfloat16)] * 3 + [pltpu.VMEM((order, cols), jnp.float32)],
-        compiler_params=params(24),
+        scratch_shapes=[pltpu.VMEM((order, len(late) * cols), jnp.bfloat16)]
+        + [pltpu.VMEM((order, order), jnp.bfloat16)] * 2
+        + [pltpu.VMEM((order, cols), jnp.float32)],
+        compiler_params=params(20),
         cost_estimate=cost(7 * order**3, 12 * order**2),
-    )(*arrays, after)
+    )(before, part, *[late[k] for k in late_ks], after)
 
 
 def last_kernel(plan, x_ref, g_ref, *refs):
@@ -272,7 +311,7 @@
         scratch_shapes=[pltpu.SemaphoreType.DMA((len(places),))],
         input_output_aliases={len(arrays) + 1: 0} if more else {},
         compiler_params=params(8),
-        cost_estimate=cost(0, 4 * shape[0] * shape[1] * shape[2]),
+        cost_estimate=cost(1000, 1000),
     )(where, *arrays, *more)
 
 
@@ -283,15 +322,18 @@
     where = jnp.stack([t, lax.axis_index("shard")]).astype(jnp.int32)
     z2_plan, p31_plan, a0_plan = plans(shard_count)
     z2 = nesterov_group(grads, momentum, t ^ 2, shard_count)
+    z2, grads, momentum = lax.optimization_barrier((z2, grads, momentum))
     p31 = nesterov(grads, momentum, where, p31_plan, shard_count)
     (a0,) = nesterov(grads, momentum, where, a0_plan, shard_count)
     chunks = exchange(where, z2, p31, a0, True)
     momentum_next, token = next_momentum(grads, momentum, chunks[0][0][0])
-    x, g, z2 = first(chunks, z2_plan, token)
+    before, part = early({k: chunks[k] for k in (0, 2)})
+    x, g, z2 = first((0, 2), before, part, {k: chunks[k][0][0] for k in (1, 3)}, z2_plan, token)
     p31 = list(last(x, g, p31_plan, rows, cols))
     (a0,) = last(x, g, a0_plan, rows, cols)
     back = exchange(where, z2, p31, a0, False)
-    update = place(where, back, shard_count, grads.shape, None)
+    update = place(where, {k: back[k] for k in (0, 2)}, shard_count, grads.shape, None)
+    update = place(where, {k: back[k] for k in (1, 3)}, shard_count, grads.shape, update)
     return (momentum_next, update)
 
 

time: 112 us -> 111 us (level)
  waiting for transfers between devices: 41.2 us -> 38.7 us
  Pallas kernels: 23.9 us -> 25.3 us
    ppermute x6, waiting for transfers between devices: 9.3 us -> 6.76 us  [swap_tensor(): return lax.ppermute(piece, 'tensor', [(t, t ^ k) for t in range(count)])]
    pallas_call x1 -> x2, Pallas kernels: 2.01 us -> 3.16 us  [place(): pl.pallas_call(functools.partial(place_kernel, places, shards), in_specs=...]
    pallas_call x1 -> x2, Pallas kernels: 8.65 us -> 8.87 us  [the longest x1 7.99 us: first(): pl.pallas_call(functools.partial(first_kernel, early_ks, late_ks, plan),...]
  transfers between devices with their start and end apart: 34 -> 34, of which waited for: 18 -> 18; matrix products, arithmetic and copies ran while one was open for 0% -> 0% of each run, Pallas kernels for 12% -> 14%
where the time goes in v4:
time: 111 us; the launch traced here: 110 us
  starting transfers between devices  41.4 us (37%)
  waiting for transfers between devices  38.7 us (35%)
  Pallas kernels  25.3 us (23%)
  local copies, waits for them, and re-layouts  2.2 us (2%)
  other arithmetic  1.77 us (2%)
    ppermute x28, waiting for transfers between devices, swap_shard(): return lax.ppermute(piece, 'shard', [(s, s ^ u) for s in range(count)])  32 us
    ppermute x28, starting transfers between devices, swap_shard(): return lax.ppermute(piece, 'shard', [(s, s ^ u) for s in range(count)])  30.7 us
    ppermute x6, starting transfers between devices, swap_tensor(): return lax.ppermute(piece, 'tensor', [(t, t ^ k) for t in range(count)])  10.7 us
    pallas_call x1, Pallas kernels, first(): pl.pallas_call(functools.partial(first_kernel, early_ks, late_ks, plan),...  7.99 us
    ppermute x6, waiting for transfers between devices, swap_tensor(): return lax.ppermute(piece, 'tensor', [(t, t ^ k) for t in range(count)])  6.76 us
    pallas_call x2, Pallas kernels, last(): pl.pallas_call(functools.partial(last_kernel, plan), in_specs=[whole()] *...  5.57 us
    pallas_call x1, Pallas kernels, next_momentum(): pl.pallas_call(momentum_kernel, grid=(steps,), in_specs=[spec, spec, whol...  3.59 us
    pallas_call x2, Pallas kernels, place(): pl.pallas_call(functools.partial(place_kernel, places, shards), in_specs=...  3.16 us
  transfers between devices with their start and end apart: 34, of which 18 were waited for; matrix products, arithmetic and copies ran while one was open for 0% of the time, Pallas kernels for 14%

profile of v4, /device:TPU:0, one launch (start us, length us, event | category | flops | bytes accessed | tf_op | source)
XLA Modules:
  0.0 110.4 jit_solution(3527707733836950822)
XLA Ops:
  0.6 1.7 %fusion.1 = bf16[8,128,256]{2,1,0:T(8,128)(2,1)S(1)} fusion(f32[32,128,256]{2,1,0:T(8,128)} %m_ref.2, s32[]{:T(128)S(6)} %select_n.4, bf16[32,128,256]{2,1,0:T(8,128)(2,1)} %g_ref.2), kind=kLoop, calls=%fused_computation.3 | loop fusion | flops 1572864 | bytes 2097156 | tf_op jit(solution)/shard_map/convert_element_type | solution.py:73
  2.3 4.1 %collective-permute-start = (bf16[8,128,256]{2,1,0:T(8,128)(2,1)S(1)}, bf16[8,128,256]{2,1,0:T(8,128)(2,1)S(1)}, u32[]{:S(2)}, u32[]{:S(2)}) collective-permute-start(bf16[8,128,256]{2,1,0:T(8,128)(2,1)S(1)} %fusion.1), channel_id=1, source_target_pairs={{0,2},{1,3},{2,0},{3,1},{4,6},{5,7},{6,4},{7,5},{8,10},{9,11},{10,... | collective-permute-start | bytes 1572872 | tf_op jit(solution)/shard_map/ppermute | solution.py:85
  6.5 2.2 %copy-done = f32[32,128,256]{2,1,0:T(8,128)S(1)} copy-done((f32[32,128,256]{2,1,0:T(8,128)S(1)}, f32[32,128,256]{2,1,0:T(8,128)}, u32[]{:S(2)}) %copy-start) | copy-done | bytes 4194328
  9.7 1.6 %collective-permute-start.9 = (bf16[2,128,256]{2,1,0:T(8,128)(2,1)S(1)}, bf16[2,128,256]{2,1,0:T(8,128)(2,1)S(1)}, u32[]{:S(2)}, u32[]{:S(2)}) collective-permute-start(bf16[2,128,256]{2,1,0:T(8,128)(2,1)S(1)} %get-tuple-element.64), channel_id=1, source_target_pairs={{0,8},{4,12},{8,0},{12,4},{16,24},{20,28},{24,16},{28,20},{1,9},{5... | collective-permute-start | bytes 393224 | tf_op jit(solution)/shard_map/ppermute | solution.py:90
  13.3 2.8 %collective-permute-done.9.refs_2_ = bf16[2,128,256]{2,1,0:T(8,128)(2,1)S(1)} collective-permute-done((bf16[2,128,256]{2,1,0:T(8,128)(2,1)S(1)}, bf16[2,128,256]{2,1,0:T(8,128)(2,1)S(1)}, u32[]{:S(2)}, u32[]{:S(2)}) %collective-permute-start.9) | collective-permute-done | bytes 131104 | tf_op jit(solution)/shard_map/ppermute | solution.py:90
  16.1 2.4 %collective-permute-start.13 = (bf16[2,128,256]{2,1,0:T(8,128)(2,1)S(1)}, bf16[2,128,256]{2,1,0:T(8,128)(2,1)S(1)}, u32[]{:S(2)}, u32[]{:S(2)}) collective-permute-start(bf16[2,128,256]{2,1,0:T(8,128)(2,1)S(1)} %get-tuple-element.68), channel_id=1, source_target_pairs={{0,24},{4,28},{8,16},{12,20},{16,8},{20,12},{24,0},{28,4},{1,25},{... | collective-permute-start | bytes 393224 | tf_op jit(solution)/shard_map/ppermute | solution.py:90
  18.5 2.5 %collective-permute-start.14 = (bf16[2,128,256]{2,1,0:T(8,128)(2,1)S(1)}, bf16[2,128,256]{2,1,0:T(8,128)(2,1)S(1)}, u32[]{:S(2)}, u32[]{:S(2)}) collective-permute-start(bf16[2,128,256]{2,1,0:T(8,128)(2,1)S(1)} %get-tuple-element.69), channel_id=1, source_target_pairs={{0,28},{4,24},{8,20},{12,16},{16,12},{20,8},{24,4},{28,0},{1,29},{... | collective-permute-start | bytes 393224 | tf_op jit(solution)/shard_map/ppermute | solution.py:90
  21.1 3.7 %collective-permute-done.12.refs_5_ = bf16[2,128,256]{2,1,0:T(8,128)(2,1)S(1)} collective-permute-done((bf16[2,128,256]{2,1,0:T(8,128)(2,1)S(1)}, bf16[2,128,256]{2,1,0:T(8,128)(2,1)S(1)}, u32[]{:S(2)}, u32[]{:S(2)}) %collective-permute-start.12) | collective-permute-done | bytes 131104 | tf_op jit(solution)/shard_map/ppermute | solution.py:90
  25.7 1.6 %collective-permute-start.15 = (bf16[8,128,256]{2,1,0:T(8,128)(2,1)S(1)}, bf16[8,128,256]{2,1,0:T(8,128)(2,1)S(1)}, u32[]{:S(2)}, u32[]{:S(2)}) collective-permute-start(bf16[8,128,256]{2,1,0:T(8,128)(2,1)S(1)} %get-tuple-element.70), channel_id=1, source_target_pairs={{0,1},{1,0},{2,3},{3,2},{4,5},{5,4},{6,7},{7,6},{8,9},{9,8},{10,11... | collective-permute-start | bytes 1572872 | tf_op jit(solution)/shard_map/ppermute | solution.py:85
  30.3 1.6 %collective-permute-start.2 = (bf16[2,128,256]{2,1,0:T(8,128)(2,1)S(1)}, bf16[2,128,256]{2,1,0:T(8,128)(2,1)S(1)}, u32[]{:S(2)}, u32[]{:S(2)}) collective-permute-start(bf16[2,128,256]{2,1,0:T(8,128)(2,1)S(1)} %get-tuple-element.54), channel_id=1, source_target_pairs={{0,8},{4,12},{8,0},{12,4},{16,24},{20,28},{24,16},{28,20},{1,9},{5... | collective-permute-start | bytes 393224 | tf_op jit(solution)/shard_map/ppermute | solution.py:90
  32.2 1.6 %collective-permute-start.4 = (bf16[2,128,256]{2,1,0:T(8,128)(2,1)S(1)}, bf16[2,128,256]{2,1,0:T(8,128)(2,1)S(1)}, u32[]{:S(2)}, u32[]{:S(2)}) collective-permute-start(bf16[2,128,256]{2,1,0:T(8,128)(2,1)S(1)} %get-tuple-element.56), channel_id=1, source_target_pairs={{0,16},{4,20},{8,24},{12,28},{16,0},{20,4},{24,8},{28,12},{1,17},{... | collective-permute-start | bytes 393224 | tf_op jit(solution)/shard_map/ppermute | solution.py:90
  33.8 2.9 %collective-permute-done.2.refs_2_ = bf16[2,128,256]{2,1,0:T(8,128)(2,1)S(1)} collective-permute-done((bf16[2,128,256]{2,1,0:T(8,128)(2,1)S(1)}, bf16[2,128,256]{2,1,0:T(8,128)(2,1)S(1)}, u32[]{:S(2)}, u32[]{:S(2)}) %collective-permute-start.2) | collective-permute-done | bytes 131104 | tf_op jit(solution)/shard_map/ppermute | solution.py:90
  38.6 2.5 %collective-permute-start.6 = (bf16[2,128,256]{2,1,0:T(8,128)(2,1)S(1)}, bf16[2,128,256]{2,1,0:T(8,128)(2,1)S(1)}, u32[]{:S(2)}, u32[]{:S(2)}) collective-permute-start(bf16[2,128,256]{2,1,0:T(8,128)(2,1)S(1)} %get-tuple-element.58), channel_id=1, source_target_pairs={{0,24},{4,28},{8,16},{12,20},{16,8},{20,12},{24,0},{28,4},{1,25},{... | collective-permute-start | bytes 393224 | tf_op jit(solution)/shard_map/ppermute | solution.py:90
  41.4 3.6 %shard_map.43 = (f32[32,128,256]{2,1,0:T(8,128)}, f32[8,128]{1,0:T(8,128)S(1)}) custom-call(bf16[32,128,256]{2,1,0:T(8,128)(2,1)S(1)} %copy-done.2, f32[32,128,256]{2,1,0:T(8,128)S(1)} %copy-done.1, bf16[2,128,256]{2,1,0:T(8,128)(2,1)S(1)} %get-tuple-element.51.after_ref.refs_0_), custom_call_target="tpu_custom_call" | custom-call | flops 1000 | bytes 1000 | tf_op jit(solution)/shard_map/pallas_call | solution.py:56
  45.8 2.2 %collective-permute-done.7.refs_7_ = bf16[2,128,256]{2,1,0:T(8,128)(2,1)S(1)} collective-permute-done((bf16[2,128,256]{2,1,0:T(8,128)(2,1)S(1)}, bf16[2,128,256]{2,1,0:T(8,128)(2,1)S(1)}, u32[]{:S(2)}, u32[]{:S(2)}) %collective-permute-start.7) | collective-permute-done | bytes 131104 | tf_op jit(solution)/shard_map/ppermute | solution.py:90
  48.9 3.2 %collective-permute-done.15.refs_2_ = bf16[8,128,256]{2,1,0:T(8,128)(2,1)S(1)} collective-permute-done((bf16[8,128,256]{2,1,0:T(8,128)(2,1)S(1)}, bf16[8,128,256]{2,1,0:T(8,128)(2,1)S(1)}, u32[]{:S(2)}, u32[]{:S(2)}) %collective-permute-start.15) | collective-permute-done | bytes 524320 | tf_op jit(solution)/shard_map/ppermute | solution.py:85
  52.1 8.0 %shard_map.47 = (bf16[1024,1024]{1,0:T(8,128)(2,1)S(1)}, bf16[1024,1024]{1,0:T(8,128)(2,1)S(1)}, bf16[8,128,256]{2,1,0:T(8,128)(2,1)S(1)}) custom-call(bf16[1024,512]{1,0:T(8,128)(2,1)S(1)} %get-tuple-element.60.refs_0_, f32[1024,1024]{1,0:T(8,128)S(1)} %get-tuple-element.61.refs_1_, bf16[8,128,256]{2,1,0:T(8,128)(2,1)S(1)} %collective-permute-done.15.refs_2_, ...), custom_call_target="tpu_custom_call" | custom-call | flops 7516192768 | bytes 12582912 | tf_op jit(solution)/shard_map/pallas_call | solution.py:252
  60.1 2.7 %collective-permute-start.26 = (bf16[8,128,256]{2,1,0:T(8,128)(2,1)S(1)}, bf16[8,128,256]{2,1,0:T(8,128)(2,1)S(1)}, u32[]{:S(2)}, u32[]{:S(2)}) collective-permute-start(bf16[8,128,256]{2,1,0:T(8,128)(2,1)S(1)} %get-tuple-element.85), channel_id=1, source_target_pairs={{0,2},{1,3},{2,0},{3,1},{4,6},{5,7},{6,4},{7,5},{8,10},{9,11},{10,... | collective-permute-start | bytes 1572872 | tf_op jit(solution)/shard_map/ppermute | solution.py:85
  62.8 3.3 %shard_map.48 = (bf16[2,128,256]{2,1,0:T(8,128)(2,1)S(1)}, bf16[2,128,256]{2,1,0:T(8,128)(2,1)S(1)}, bf16[2,128,256]{2,1,0:T(8,128)(2,1)S(1)}, bf16[2,128,256]{2...) custom-call(bf16[1024,1024]{1,0:T(8,128)(2,1)S(1)} %get-tuple-elemen, ...), custom_call_target="tpu_custom_call" | custom-call | flops 2147483648 | bytes 8388608 | tf_op jit(solution)/shard_map/pallas_call | solution.py:276
  69.8 2.8 %collective-permute-done.18.refs_2_ = bf16[2,128,256]{2,1,0:T(8,128)(2,1)S(1)} collective-permute-done((bf16[2,128,256]{2,1,0:T(8,128)(2,1)S(1)}, bf16[2,128,256]{2,1,0:T(8,128)(2,1)S(1)}, u32[]{:S(2)}, u32[]{:S(2)}) %collective-permute-start.18) | collective-permute-done | bytes 131104 | tf_op jit(solution)/shard_map/ppermute | solution.py:90
  72.6 2.4 %collective-permute-start.22 = (bf16[2,128,256]{2,1,0:T(8,128)(2,1)S(1)}, bf16[2,128,256]{2,1,0:T(8,128)(2,1)S(1)}, u32[]{:S(2)}, u32[]{:S(2)}) collective-permute-start(bf16[2,128,256]{2,1,0:T(8,128)(2,1)S(1)} %get-tuple-element.81), channel_id=1, source_target_pairs={{0,24},{4,28},{8,16},{12,20},{16,8},{20,12},{24,0},{28,4},{1,25},{... | collective-permute-start | bytes 393224 | tf_op jit(solution)/shard_map/ppermute | solution.py:90
  75.1 2.5 %collective-permute-start.23 = (bf16[2,128,256]{2,1,0:T(8,128)(2,1)S(1)}, bf16[2,128,256]{2,1,0:T(8,128)(2,1)S(1)}, u32[]{:S(2)}, u32[]{:S(2)}) collective-permute-start(bf16[2,128,256]{2,1,0:T(8,128)(2,1)S(1)} %get-tuple-element.82), channel_id=1, source_target_pairs={{0,28},{4,24},{8,20},{12,16},{16,12},{20,8},{24,4},{28,0},{1,29},{... | collective-permute-start | bytes 393224 | tf_op jit(solution)/shard_map/ppermute | solution.py:90
  77.6 3.7 %collective-permute-done.21.refs_5_ = bf16[2,128,256]{2,1,0:T(8,128)(2,1)S(1)} collective-permute-done((bf16[2,128,256]{2,1,0:T(8,128)(2,1)S(1)}, bf16[2,128,256]{2,1,0:T(8,128)(2,1)S(1)}, u32[]{:S(2)}, u32[]{:S(2)}) %collective-permute-start.21) | collective-permute-done | bytes 131104 | tf_op jit(solution)/shard_map/ppermute | solution.py:90
  84.1 2.2 %shard_map.50.refs_1_ = bf16[8,128,256]{2,1,0:T(8,128)(2,1)S(1)} custom-call(bf16[1024,1024]{1,0:T(8,128)(2,1)S(1)} %get-tuple-element.73.x_ref, bf16[1024,1024]{1,0:T(8,128)(2,1)S(1)} %get-tuple-element.74.g_ref), custom_call_target="tpu_custom_call" | custom-call | flops 1073741824 | bytes 8388608 | tf_op jit(solution)/shard_map/pallas_call | solution.py:276
  87.1 1.6 %collective-permute-start.28 = (bf16[2,128,256]{2,1,0:T(8,128)(2,1)S(1)}, bf16[2,128,256]{2,1,0:T(8,128)(2,1)S(1)}, u32[]{:S(2)}, u32[]{:S(2)}) collective-permute-start(bf16[2,128,256]{2,1,0:T(8,128)(2,1)S(1)} %get-tuple-element.88), channel_id=1, source_target_pairs={{0,8},{4,12},{8,0},{12,4},{16,24},{20,28},{24,16},{28,20},{1,9},{5... | collective-permute-start | bytes 393224 | tf_op jit(solution)/shard_map/ppermute | solution.py:90
  88.9 1.6 %collective-permute-start.30 = (bf16[2,128,256]{2,1,0:T(8,128)(2,1)S(1)}, bf16[2,128,256]{2,1,0:T(8,128)(2,1)S(1)}, u32[]{:S(2)}, u32[]{:S(2)}) collective-permute-start(bf16[2,128,256]{2,1,0:T(8,128)(2,1)S(1)} %get-tuple-element.90), channel_id=1, source_target_pairs={{0,16},{4,20},{8,24},{12,28},{16,0},{20,4},{24,8},{28,12},{1,17},{... | collective-permute-start | bytes 393224 | tf_op jit(solution)/shard_map/ppermute | solution.py:90
  90.5 2.9 %collective-permute-done.28.refs_2_ = bf16[2,128,256]{2,1,0:T(8,128)(2,1)S(1)} collective-permute-done((bf16[2,128,256]{2,1,0:T(8,128)(2,1)S(1)}, bf16[2,128,256]{2,1,0:T(8,128)(2,1)S(1)}, u32[]{:S(2)}, u32[]{:S(2)}) %collective-permute-start.28) | collective-permute-done | bytes 131104 | tf_op jit(solution)/shard_map/ppermute | solution.py:90
  95.3 2.5 %collective-permute-start.32 = (bf16[2,128,256]{2,1,0:T(8,128)(2,1)S(1)}, bf16[2,128,256]{2,1,0:T(8,128)(2,1)S(1)}, u32[]{:S(2)}, u32[]{:S(2)}) collective-permute-start(bf16[2,128,256]{2,1,0:T(8,128)(2,1)S(1)} %get-tuple-element.92), channel_id=1, source_target_pairs={{0,24},{4,28},{8,16},{12,20},{16,8},{20,12},{24,0},{28,4},{1,25},{... | collective-permute-start | bytes 393224 | tf_op jit(solution)/shard_map/ppermute | solution.py:90
  99.1 3.4 %collective-permute-done.32.refs_6_ = bf16[2,128,256]{2,1,0:T(8,128)(2,1)S(1)} collective-permute-done((bf16[2,128,256]{2,1,0:T(8,128)(2,1)S(1)}, bf16[2,128,256]{2,1,0:T(8,128)(2,1)S(1)}, u32[]{:S(2)}, u32[]{:S(2)}) %collective-permute-start.32) | collective-permute-done | bytes 131104 | tf_op jit(solution)/shard_map/ppermute | solution.py:90
  102.5 2.2 %collective-permute-done.33.refs_7_ = bf16[2,128,256]{2,1,0:T(8,128)(2,1)S(1)} collective-permute-done((bf16[2,128,256]{2,1,0:T(8,128)(2,1)S(1)}, bf16[2,128,256]{2,1,0:T(8,128)(2,1)S(1)}, u32[]{:S(2)}, u32[]{:S(2)}) %collective-permute-start.33) | collective-permute-done | bytes 131104 | tf_op jit(solution)/shard_map/ppermute | solution.py:90
  104.7 1.6 %shard_map.52.refs_2_ = bf16[32,128,256]{2,1,0:T(8,128)(2,1)} custom-call(s32[2]{0:T(128)S(1)} %pad_add_fusion.where_ref, bf16[2,128,256]{2,1,0:T(8,128)(2,1)S(1)} %get-tuple-element.86.refs_0_, bf16[2,128,256]{2,1,0:T(8,128)(2,1)S(1)} %collective-permute-done.27.refs_1_, bf16[2,128,256]{2,1,0:T(8,128)(2,1)S(1)} %collective-permute-done.28.refs_2_, ...), custom_call_target="tpu_custom_call" | custom-call | flops 1000 | bytes 1000 | tf_op jit(solution)/shard_map/pallas_call | solution.py:306
  106.3 2.3 %collective-permute-done.24.refs_0_ = bf16[8,128,256]{2,1,0:T(8,128)(2,1)S(1)} collective-permute-done((bf16[8,128,256]{2,1,0:T(8,128)(2,1)S(1)}, bf16[8,128,256]{2,1,0:T(8,128)(2,1)S(1)}, u32[]{:S(2)}, u32[]{:S(2)}) %collective-permute-start.24) | collective-permute-done | bytes 524320 | tf_op jit(solution)/shard_map/ppermute | solution.py:85
  (57 shorter events, 23.0 us)
Async XLA Ops:
  2.3 27.3 %collective-permute-start = (bf16[8,128,256]{2,1,0:T(8,128)(2,1)S(1)}, bf16[8,128,256]{2,1,0:T(8,128)(2,1)S(1)}, u32[]{:S(2)}, u32[]{:S(2)}) collective-permute-start(bf16[8,128,256]{2,1,0:T(8,128)(2,1)S(1)} %fusion.1), channel_id=1, source_target_pairs={{0,2},{1,3},{2,0},{3,1},{4,6},{5,7},{6,4},{7,5},{8,10},{9,11},{10,... | collective-permute-start | bytes 1572872 | tf_op jit(solution)/shard_map/ppermute | solution.py:85
  9.6 3.5 %collective-permute-start.8 = (bf16[2,128,256]{2,1,0:T(8,128)(2,1)S(1)}, bf16[2,128,256]{2,1,0:T(8,128)(2,1)S(1)}, u32[]{:S(2)}, u32[]{:S(2)}) collective-permute-start(bf16[2,128,256]{2,1,0:T(8,128)(2,1)S(1)} %get-tuple-element.63), channel_id=1, source_target_pairs={{0,4},{4,0},{8,12},{12,8},{16,20},{20,16},{24,28},{28,24},{1,5},{5... | collective-permute-start | bytes 393224 | tf_op jit(solution)/shard_map/ppermute | solution.py:90
  9.7 6.4 %collective-permute-start.9 = (bf16[2,128,256]{2,1,0:T(8,128)(2,1)S(1)}, bf16[2,128,256]{2,1,0:T(8,128)(2,1)S(1)}, u32[]{:S(2)}, u32[]{:S(2)}) collective-permute-start(bf16[2,128,256]{2,1,0:T(8,128)(2,1)S(1)} %get-tuple-element.64), channel_id=1, source_target_pairs={{0,8},{4,12},{8,0},{12,4},{16,24},{20,28},{24,16},{28,20},{1,9},{5... | collective-permute-start | bytes 393224 | tf_op jit(solution)/shard_map/ppermute | solution.py:90
  11.3 7.3 %collective-permute-start.10 = (bf16[2,128,256]{2,1,0:T(8,128)(2,1)S(1)}, bf16[2,128,256]{2,1,0:T(8,128)(2,1)S(1)}, u32[]{:S(2)}, u32[]{:S(2)}) collective-permute-start(bf16[2,128,256]{2,1,0:T(8,128)(2,1)S(1)} %get-tuple-element.65), channel_id=1, source_target_pairs={{0,12},{4,8},{8,4},{12,0},{16,28},{20,24},{24,20},{28,16},{1,13},{... | collective-permute-start | bytes 393224 | tf_op jit(solution)/shard_map/ppermute | solution.py:90
  11.6 9.5 %collective-permute-start.11 = (bf16[2,128,256]{2,1,0:T(8,128)(2,1)S(1)}, bf16[2,128,256]{2,1,0:T(8,128)(2,1)S(1)}, u32[]{:S(2)}, u32[]{:S(2)}) collective-permute-start(bf16[2,128,256]{2,1,0:T(8,128)(2,1)S(1)} %get-tuple-element.66), channel_id=1, source_target_pairs={{0,16},{4,20},{8,24},{12,28},{16,0},{20,4},{24,8},{28,12},{1,17},{... | collective-permute-start | bytes 393224 | tf_op jit(solution)/shard_map/ppermute | solution.py:90
  13.1 11.7 %collective-permute-start.12 = (bf16[2,128,256]{2,1,0:T(8,128)(2,1)S(1)}, bf16[2,128,256]{2,1,0:T(8,128)(2,1)S(1)}, u32[]{:S(2)}, u32[]{:S(2)}) collective-permute-start(bf16[2,128,256]{2,1,0:T(8,128)(2,1)S(1)} %get-tuple-element.67), channel_id=1, source_target_pairs={{0,20},{4,16},{8,28},{12,24},{16,4},{20,0},{24,12},{28,8},{1,21},{... | collective-permute-start | bytes 393224 | tf_op jit(solution)/shard_map/ppermute | solution.py:90
  16.1 8.7 %collective-permute-start.13 = (bf16[2,128,256]{2,1,0:T(8,128)(2,1)S(1)}, bf16[2,128,256]{2,1,0:T(8,128)(2,1)S(1)}, u32[]{:S(2)}, u32[]{:S(2)}) collective-permute-start(bf16[2,128,256]{2,1,0:T(8,128)(2,1)S(1)} %get-tuple-element.68), channel_id=1, source_target_pairs={{0,24},{4,28},{8,16},{12,20},{16,8},{20,12},{24,0},{28,4},{1,25},{... | collective-permute-start | bytes 393224 | tf_op jit(solution)/shard_map/ppermute | solution.py:90
  18.5 6.5 %collective-permute-start.14 = (bf16[2,128,256]{2,1,0:T(8,128)(2,1)S(1)}, bf16[2,128,256]{2,1,0:T(8,128)(2,1)S(1)}, u32[]{:S(2)}, u32[]{:S(2)}) collective-permute-start(bf16[2,128,256]{2,1,0:T(8,128)(2,1)S(1)} %get-tuple-element.69), channel_id=1, source_target_pairs={{0,28},{4,24},{8,20},{12,16},{16,12},{20,8},{24,4},{28,0},{1,29},{... | collective-permute-start | bytes 393224 | tf_op jit(solution)/shard_map/ppermute | solution.py:90
  25.7 26.4 %collective-permute-start.15 = (bf16[8,128,256]{2,1,0:T(8,128)(2,1)S(1)}, bf16[8,128,256]{2,1,0:T(8,128)(2,1)S(1)}, u32[]{:S(2)}, u32[]{:S(2)}) collective-permute-start(bf16[8,128,256]{2,1,0:T(8,128)(2,1)S(1)} %get-tuple-element.70), channel_id=1, source_target_pairs={{0,1},{1,0},{2,3},{3,2},{4,5},{5,4},{6,7},{7,6},{8,9},{9,8},{10,11... | collective-permute-start | bytes 1572872 | tf_op jit(solution)/shard_map/ppermute | solution.py:85
  27.3 24.7 %collective-permute-start.16 = (bf16[8,128,256]{2,1,0:T(8,128)(2,1)S(1)}, bf16[8,128,256]{2,1,0:T(8,128)(2,1)S(1)}, u32[]{:S(2)}, u32[]{:S(2)}) collective-permute-start(bf16[8,128,256]{2,1,0:T(8,128)(2,1)S(1)} %get-tuple-element.71), channel_id=1, source_target_pairs={{0,3},{1,2},{2,1},{3,0},{4,7},{5,6},{6,5},{7,4},{8,11},{9,10},{10,... | collective-permute-start | bytes 1572872 | tf_op jit(solution)/shard_map/ppermute | solution.py:85
  30.3 6.4 %collective-permute-start.2 = (bf16[2,128,256]{2,1,0:T(8,128)(2,1)S(1)}, bf16[2,128,256]{2,1,0:T(8,128)(2,1)S(1)}, u32[]{:S(2)}, u32[]{:S(2)}) collective-permute-start(bf16[2,128,256]{2,1,0:T(8,128)(2,1)S(1)} %get-tuple-element.54), channel_id=1, source_target_pairs={{0,8},{4,12},{8,0},{12,4},{16,24},{20,28},{24,16},{28,20},{1,9},{5... | collective-permute-start | bytes 393224 | tf_op jit(solution)/shard_map/ppermute | solution.py:90
  32.0 6.7 %collective-permute-start.3 = (bf16[2,128,256]{2,1,0:T(8,128)(2,1)S(1)}, bf16[2,128,256]{2,1,0:T(8,128)(2,1)S(1)}, u32[]{:S(2)}, u32[]{:S(2)}) collective-permute-start(bf16[2,128,256]{2,1,0:T(8,128)(2,1)S(1)} %get-tuple-element.55), channel_id=1, source_target_pairs={{0,12},{4,8},{8,4},{12,0},{16,28},{20,24},{24,20},{28,16},{1,13},{... | collective-permute-start | bytes 393224 | tf_op jit(solution)/shard_map/ppermute | solution.py:90
  32.2 8.9 %collective-permute-start.4 = (bf16[2,128,256]{2,1,0:T(8,128)(2,1)S(1)}, bf16[2,128,256]{2,1,0:T(8,128)(2,1)S(1)}, u32[]{:S(2)}, u32[]{:S(2)}) collective-permute-start(bf16[2,128,256]{2,1,0:T(8,128)(2,1)S(1)} %get-tuple-element.56), channel_id=1, source_target_pairs={{0,16},{4,20},{8,24},{12,28},{16,0},{20,4},{24,8},{28,12},{1,17},{... | collective-permute-start | bytes 393224 | tf_op jit(solution)/shard_map/ppermute | solution.py:90
  36.7 8.3 %collective-permute-start.5 = (bf16[2,128,256]{2,1,0:T(8,128)(2,1)S(1)}, bf16[2,128,256]{2,1,0:T(8,128)(2,1)S(1)}, u32[]{:S(2)}, u32[]{:S(2)}) collective-permute-start(bf16[2,128,256]{2,1,0:T(8,128)(2,1)S(1)} %get-tuple-element.57), channel_id=1, source_target_pairs={{0,20},{4,16},{8,28},{12,24},{16,4},{20,0},{24,12},{28,8},{1,21},{... | collective-permute-start | bytes 393224 | tf_op jit(solution)/shard_map/ppermute | solution.py:90
  38.6 7.2 %collective-permute-start.6 = (bf16[2,128,256]{2,1,0:T(8,128)(2,1)S(1)}, bf16[2,128,256]{2,1,0:T(8,128)(2,1)S(1)}, u32[]{:S(2)}, u32[]{:S(2)}) collective-permute-start(bf16[2,128,256]{2,1,0:T(8,128)(2,1)S(1)} %get-tuple-element.58), channel_id=1, source_target_pairs={{0,24},{4,28},{8,16},{12,20},{16,8},{20,12},{24,0},{28,4},{1,25},{... | collective-permute-start | bytes 393224 | tf_op jit(solution)/shard_map/ppermute | solution.py:90
  41.1 6.9 %collective-permute-start.7 = (bf16[2,128,256]{2,1,0:T(8,128)(2,1)S(1)}, bf16[2,128,256]{2,1,0:T(8,128)(2,1)S(1)}, u32[]{:S(2)}, u32[]{:S(2)}) collective-permute-start(bf16[2,128,256]{2,1,0:T(8,128)(2,1)S(1)} %get-tuple-element.59), channel_id=1, source_target_pairs={{0,28},{4,24},{8,20},{12,16},{16,12},{20,8},{24,4},{28,0},{1,29},{... | collective-permute-start | bytes 393224 | tf_op jit(solution)/shard_map/ppermute | solution.py:90
  60.1 26.3 %collective-permute-start.26 = (bf16[8,128,256]{2,1,0:T(8,128)(2,1)S(1)}, bf16[8,128,256]{2,1,0:T(8,128)(2,1)S(1)}, u32[]{:S(2)}, u32[]{:S(2)}) collective-permute-start(bf16[8,128,256]{2,1,0:T(8,128)(2,1)S(1)} %get-tuple-element.85), channel_id=1, source_target_pairs={{0,2},{1,3},{2,0},{3,1},{4,6},{5,7},{6,4},{7,5},{8,10},{9,11},{10,... | collective-permute-start | bytes 1572872 | tf_op jit(solution)/shard_map/ppermute | solution.py:85
  66.2 3.5 %collective-permute-start.17 = (bf16[2,128,256]{2,1,0:T(8,128)(2,1)S(1)}, bf16[2,128,256]{2,1,0:T(8,128)(2,1)S(1)}, u32[]{:S(2)}, u32[]{:S(2)}) collective-permute-start(bf16[2,128,256]{2,1,0:T(8,128)(2,1)S(1)} %get-tuple-element.76), channel_id=1, source_target_pairs={{0,4},{4,0},{8,12},{12,8},{16,20},{20,16},{24,28},{28,24},{1,5},{5... | collective-permute-start | bytes 393224 | tf_op jit(solution)/shard_map/ppermute | solution.py:90
  66.2 6.4 %collective-permute-start.18 = (bf16[2,128,256]{2,1,0:T(8,128)(2,1)S(1)}, bf16[2,128,256]{2,1,0:T(8,128)(2,1)S(1)}, u32[]{:S(2)}, u32[]{:S(2)}) collective-permute-start(bf16[2,128,256]{2,1,0:T(8,128)(2,1)S(1)} %get-tuple-element.77), channel_id=1, source_target_pairs={{0,8},{4,12},{8,0},{12,4},{16,24},{20,28},{24,16},{28,20},{1,9},{5... | collective-permute-start | bytes 393224 | tf_op jit(solution)/shard_map/ppermute | solution.py:90
  67.8 7.3 %collective-permute-start.19 = (bf16[2,128,256]{2,1,0:T(8,128)(2,1)S(1)}, bf16[2,128,256]{2,1,0:T(8,128)(2,1)S(1)}, u32[]{:S(2)}, u32[]{:S(2)}) collective-permute-start(bf16[2,128,256]{2,1,0:T(8,128)(2,1)S(1)} %get-tuple-element.78), channel_id=1, source_target_pairs={{0,12},{4,8},{8,4},{12,0},{16,28},{20,24},{24,20},{28,16},{1,13},{... | collective-permute-start | bytes 393224 | tf_op jit(solution)/shard_map/ppermute | solution.py:90
  68.1 9.5 %collective-permute-start.20 = (bf16[2,128,256]{2,1,0:T(8,128)(2,1)S(1)}, bf16[2,128,256]{2,1,0:T(8,128)(2,1)S(1)}, u32[]{:S(2)}, u32[]{:S(2)}) collective-permute-start(bf16[2,128,256]{2,1,0:T(8,128)(2,1)S(1)} %get-tuple-element.79), channel_id=1, source_target_pairs={{0,16},{4,20},{8,24},{12,28},{16,0},{20,4},{24,8},{28,12},{1,17},{... | collective-permute-start | bytes 393224 | tf_op jit(solution)/shard_map/ppermute | solution.py:90
  69.6 11.7 %collective-permute-start.21 = (bf16[2,128,256]{2,1,0:T(8,128)(2,1)S(1)}, bf16[2,128,256]{2,1,0:T(8,128)(2,1)S(1)}, u32[]{:S(2)}, u32[]{:S(2)}) collective-permute-start(bf16[2,128,256]{2,1,0:T(8,128)(2,1)S(1)} %get-tuple-element.80), channel_id=1, source_target_pairs={{0,20},{4,16},{8,28},{12,24},{16,4},{20,0},{24,12},{28,8},{1,21},{... | collective-permute-start | bytes 393224 | tf_op jit(solution)/shard_map/ppermute | solution.py:90
  72.6 8.7 %collective-permute-start.22 = (bf16[2,128,256]{2,1,0:T(8,128)(2,1)S(1)}, bf16[2,128,256]{2,1,0:T(8,128)(2,1)S(1)}, u32[]{:S(2)}, u32[]{:S(2)}) collective-permute-start(bf16[2,128,256]{2,1,0:T(8,128)(2,1)S(1)} %get-tuple-element.81), channel_id=1, source_target_pairs={{0,24},{4,28},{8,16},{12,20},{16,8},{20,12},{24,0},{28,4},{1,25},{... | collective-permute-start | bytes 393224 | tf_op jit(solution)/shard_map/ppermute | solution.py:90
  75.1 6.5 %collective-permute-start.23 = (bf16[2,128,256]{2,1,0:T(8,128)(2,1)S(1)}, bf16[2,128,256]{2,1,0:T(8,128)(2,1)S(1)}, u32[]{:S(2)}, u32[]{:S(2)}) collective-permute-start(bf16[2,128,256]{2,1,0:T(8,128)(2,1)S(1)} %get-tuple-element.82), channel_id=1, source_target_pairs={{0,28},{4,24},{8,20},{12,16},{16,12},{20,8},{24,4},{28,0},{1,29},{... | collective-permute-start | bytes 393224 | tf_op jit(solution)/shard_map/ppermute | solution.py:90
  82.2 26.4 %collective-permute-start.24 = (bf16[8,128,256]{2,1,0:T(8,128)(2,1)S(1)}, bf16[8,128,256]{2,1,0:T(8,128)(2,1)S(1)}, u32[]{:S(2)}, u32[]{:S(2)}) collective-permute-start(bf16[8,128,256]{2,1,0:T(8,128)(2,1)S(1)} %get-tuple-element.83), channel_id=1, source_target_pairs={{0,1},{1,0},{2,3},{3,2},{4,5},{5,4},{6,7},{7,6},{8,9},{9,8},{10,11... | collective-permute-start | bytes 1572872 | tf_op jit(solution)/shard_map/ppermute | solution.py:85
  83.7 25.0 %collective-permute-start.25 = (bf16[8,128,256]{2,1,0:T(8,128)(2,1)S(1)}, bf16[8,128,256]{2,1,0:T(8,128)(2,1)S(1)}, u32[]{:S(2)}, u32[]{:S(2)}) collective-permute-start(bf16[8,128,256]{2,1,0:T(8,128)(2,1)S(1)} %get-tuple-element.84), channel_id=1, source_target_pairs={{0,3},{1,2},{2,1},{3,0},{4,7},{5,6},{6,5},{7,4},{8,11},{9,10},{10,... | collective-permute-start | bytes 1572872 | tf_op jit(solution)/shard_map/ppermute | solution.py:85
  87.1 6.4 %collective-permute-start.28 = (bf16[2,128,256]{2,1,0:T(8,128)(2,1)S(1)}, bf16[2,128,256]{2,1,0:T(8,128)(2,1)S(1)}, u32[]{:S(2)}, u32[]{:S(2)}) collective-permute-start(bf16[2,128,256]{2,1,0:T(8,128)(2,1)S(1)} %get-tuple-element.88), channel_id=1, source_target_pairs={{0,8},{4,12},{8,0},{12,4},{16,24},{20,28},{24,16},{28,20},{1,9},{5... | collective-permute-start | bytes 393224 | tf_op jit(solution)/shard_map/ppermute | solution.py:90
  88.7 6.6 %collective-permute-start.29 = (bf16[2,128,256]{2,1,0:T(8,128)(2,1)S(1)}, bf16[2,128,256]{2,1,0:T(8,128)(2,1)S(1)}, u32[]{:S(2)}, u32[]{:S(2)}) collective-permute-start(bf16[2,128,256]{2,1,0:T(8,128)(2,1)S(1)} %get-tuple-element.89), channel_id=1, source_target_pairs={{0,12},{4,8},{8,4},{12,0},{16,28},{20,24},{24,20},{28,16},{1,13},{... | collective-permute-start | bytes 393224 | tf_op jit(solution)/shard_map/ppermute | solution.py:90
  88.9 8.9 %collective-permute-start.30 = (bf16[2,128,256]{2,1,0:T(8,128)(2,1)S(1)}, bf16[2,128,256]{2,1,0:T(8,128)(2,1)S(1)}, u32[]{:S(2)}, u32[]{:S(2)}) collective-permute-start(bf16[2,128,256]{2,1,0:T(8,128)(2,1)S(1)} %get-tuple-element.90), channel_id=1, source_target_pairs={{0,16},{4,20},{8,24},{12,28},{16,0},{20,4},{24,8},{28,12},{1,17},{... | collective-permute-start | bytes 393224 | tf_op jit(solution)/shard_map/ppermute | solution.py:90
  93.4 5.6 %collective-permute-start.31 = (bf16[2,128,256]{2,1,0:T(8,128)(2,1)S(1)}, bf16[2,128,256]{2,1,0:T(8,128)(2,1)S(1)}, u32[]{:S(2)}, u32[]{:S(2)}) collective-permute-start(bf16[2,128,256]{2,1,0:T(8,128)(2,1)S(1)} %get-tuple-element.91), channel_id=1, source_target_pairs={{0,20},{4,16},{8,28},{12,24},{16,4},{20,0},{24,12},{28,8},{1,21},{... | collective-permute-start | bytes 393224 | tf_op jit(solution)/shard_map/ppermute | solution.py:90
  95.3 7.2 %collective-permute-start.32 = (bf16[2,128,256]{2,1,0:T(8,128)(2,1)S(1)}, bf16[2,128,256]{2,1,0:T(8,128)(2,1)S(1)}, u32[]{:S(2)}, u32[]{:S(2)}) collective-permute-start(bf16[2,128,256]{2,1,0:T(8,128)(2,1)S(1)} %get-tuple-element.92), channel_id=1, source_target_pairs={{0,24},{4,28},{8,16},{12,20},{16,8},{20,12},{24,0},{28,4},{1,25},{... | collective-permute-start | bytes 393224 | tf_op jit(solution)/shard_map/ppermute | solution.py:90
  97.9 6.8 %collective-permute-start.33 = (bf16[2,128,256]{2,1,0:T(8,128)(2,1)S(1)}, bf16[2,128,256]{2,1,0:T(8,128)(2,1)S(1)}, u32[]{:S(2)}, u32[]{:S(2)}) collective-permute-start(bf16[2,128,256]{2,1,0:T(8,128)(2,1)S(1)} %get-tuple-element.93), channel_id=1, source_target_pairs={{0,28},{4,24},{8,20},{12,16},{16,12},{20,8},{24,4},{28,0},{1,29},{... | collective-permute-start | bytes 393224 | tf_op jit(solution)/shard_map/ppermute | solution.py:90
  (5 other events, 31.0 us)

commit v5 on v4

--- a/solution.py
+++ b/solution.py
@@ -22,26 +22,27 @@
     return pltpu.CompilerParams(vmem_limit_bytes=mib * MIB)
 
 
-def nesterov_kernel(plan, shards, where_ref, g_ref, m_ref, *outs):
+def nesterov_kernel(plan, shards, g_ref, m_ref, *outs):
+    t, s = lax.axis_index("tensor"), lax.axis_index("shard")
     for out, pieces in zip(outs, plan):
         for i, (k, u) in enumerate(pieces):
-            source = (where_ref[0] ^ k) * shards + (where_ref[1] ^ u)
+            source = (t ^ k) * shards + (s ^ u)
             g = g_ref[source].astype(jnp.float32)
             m = 0.95 * m_ref[source] + g
             out[i] = (g + 0.95 * m).astype(jnp.bfloat16)
 
 
-def nesterov(grads, momentum, where, plan, shards):
+def nesterov(grads, momentum, plan, shards):
     count, rows, cols = grads.shape
     n = sum(len(pieces) for pieces in plan)
     return pl.pallas_call(
         functools.partial(nesterov_kernel, plan, shards),
-        in_specs=[whole(pltpu.SMEM), whole(), whole()],
+        in_specs=[whole(), whole()],
         out_specs=[whole()] * len(plan),
         out_shape=[jax.ShapeDtypeStruct((len(pieces), rows, cols), jnp.bfloat16) for pieces in plan],
         compiler_params=params(8),
         cost_estimate=cost(6 * n * rows * cols, 8 * n * rows * cols),
-    )(where, grads, momentum)
+    )(grads, momentum)
 
 
 def momentum_kernel(g_ref, m_ref, after_ref, o_ref, token_ref):
@@ -90,34 +91,35 @@
     return lax.ppermute(piece, "shard", [(s, s ^ u) for s in range(count)])
 
 
-def regroup_kernel(plan, n, where_ref, *refs):
+def regroup_kernel(plan, n, *refs):
     ins, outs = refs[:n], refs[n:]
+    s = lax.axis_index("shard")
     for out, slabs in zip(outs, plan):
         for i, (a, b, moved, moves) in enumerate(slabs):
-            out[i ^ where_ref[1] if moves else i] = ins[a][b ^ where_ref[1] if moved else b]
-
-
-def regroup(where, arrays, plan):
+            out[i ^ s if moves else i] = ins[a][b ^ s if moved else b]
+
+
+def regroup(arrays, plan):
     _, rows, cols = arrays[0].shape
     n = sum(len(slabs) for slabs in plan)
     return pl.pallas_call(
         functools.partial(regroup_kernel, plan, len(arrays)),
-        in_specs=[whole(pltpu.SMEM)] + [whole()] * len(arrays),
+        in_specs=[whole()] * len(arrays),
         out_specs=[whole()] * len(plan),
         out_shape=[jax.ShapeDtypeStruct((len(slabs), rows, cols), jnp.bfloat16) for slabs in plan],
         compiler_params=params(8),
         cost_estimate=cost(0, 4 * n * rows * cols),
-    )(where, *arrays)
-
-
-def exchange(where, z2, p31, a0, moved):
+    )(*arrays)
+
+
+def exchange(z2, p31, a0, moved):
     shards = len(p31)
     z2 = swap_tensor(z2, 2)
     p31 = [p31[0]] + [swap_shard(p31[u], u) for u in range(1, shards)]
-    w3, w1 = regroup(where, p31, [[(u, i, False, not moved) for u in range(shards)] for i in range(2)])
+    w3, w1 = regroup(p31, [[(u, i, False, not moved) for u in range(shards)] for i in range(2)])
     z3 = swap_tensor(w3, 3)
     z1 = swap_tensor(w1, 1)
-    p20 = regroup(where, (z2, a0), [[(0, u, moved, False), (1, u, False, False)] for u in range(shards)])
+    p20 = regroup((z2, a0), [[(0, u, moved, False), (1, u, False, False)] for u in range(shards)])
     p20 = [p20[0]] + [swap_shard(p20[u], u) for u in range(1, shards)]
     outs = {k: [(a, i) for a in p20] for i, k in enumerate((2, 0))}
     for k, a in ((3, z3), (1, z1)):
@@ -284,15 +286,16 @@
     )(x, g)
 
 
-def place_kernel(places, shards, where_ref, *refs):
+def place_kernel(places, shards, *refs):
     o_ref, sems = refs[-2:]
+    t, s = lax.axis_index("tensor"), lax.axis_index("shard")
     copies = []
     for n, (k, u, which, b) in enumerate(places):
-        group = (where_ref[0] ^ k) * shards
+        group = (t ^ k) * shards
         if b is None:
             src, dst = refs[which], o_ref.at[pl.ds(group, shards)]
         else:
-            src, dst = refs[which].at[b], o_ref.at[group + (where_ref[1] ^ u)]
+            src, dst = refs[which].at[b], o_ref.at[group + (s ^ u)]
         copies.append(pltpu.make_async_copy(src, dst, sems.at[n]))
     for c in copies:
         c.start()
@@ -300,40 +303,39 @@
         c.wait()
 
 
-def place(where, chunks, shards, shape, before):
+def place(chunks, shards, shape, before):
     arrays, places = arrays_of(chunks)
     more = [] if before is None else [before]
     return pl.pallas_call(
         functools.partial(place_kernel, places, shards),
-        in_specs=[whole(pltpu.SMEM)] + [whole()] * len(arrays) + [whole(pltpu.HBM)] * len(more),
+        in_specs=[whole()] * len(arrays) + [whole(pltpu.HBM)] * len(more),
         out_specs=whole(pltpu.HBM),
         out_shape=jax.ShapeDtypeStruct(shape, jnp.bfloat16),
         scratch_shapes=[pltpu.SemaphoreType.DMA((len(places),))],
-        input_output_aliases={len(arrays) + 1: 0} if more else {},
+        input_output_aliases={len(arrays): 0} if more else {},
         compiler_params=params(8),
         cost_estimate=cost(1000, 1000),
-    )(where, *arrays, *more)
+    )(*arrays, *more)
 
 
 def shards(grads, momentum):
     count, rows, cols = grads.shape
     shard_count = lax.axis_size("shard")
     t = lax.axis_index("tensor")
-    where = jnp.stack([t, lax.axis_index("shard")]).astype(jnp.int32)
     z2_plan, p31_plan, a0_plan = plans(shard_count)
     z2 = nesterov_group(grads, momentum, t ^ 2, shard_count)
     z2, grads, momentum = lax.optimization_barrier((z2, grads, momentum))
-    p31 = nesterov(grads, momentum, where, p31_plan, shard_count)
-    (a0,) = nesterov(grads, momentum, where, a0_plan, shard_count)
-    chunks = exchange(where, z2, p31, a0, True)
+    p31 = nesterov(grads, momentum, p31_plan, shard_count)
+    (a0,) = nesterov(grads, momentum, a0_plan, shard_count)
+    chunks = exchange(z2, p31, a0, True)
     momentum_next, token = next_momentum(grads, momentum, chunks[0][0][0])
     before, part = early({k: chunks[k] for k in (0, 2)})
     x, g, z2 = first((0, 2), before, part, {k: chunks[k][0][0] for k in (1, 3)}, z2_plan, token)
     p31 = list(last(x, g, p31_plan, rows, cols))
     (a0,) = last(x, g, a0_plan, rows, cols)
-    back = exchange(where, z2, p31, a0, False)
-    update = place(where, {k: back[k] for k in (0, 2)}, shard_count, grads.shape, None)
-    update = place(where, {k: back[k] for k in (1, 3)}, shard_count, grads.shape, update)
+    back = exchange(z2, p31, a0, False)
+    update = place({k: back[k] for k in (0, 2)}, shard_count, grads.shape, None)
+    update = place({k: back[k] for k in (1, 3)}, shard_count, grads.shape, update)
     return (momentum_next, update)
 
 

time: 111 us -> 110 us (level)
  Pallas kernels: 25.3 us -> 20.9 us
  waiting for transfers between devices: 38.7 us -> 42.8 us
    ppermute x6, waiting for transfers between devices: 6.76 us -> 10.7 us  [swap_tensor(): return lax.ppermute(piece, 'tensor', [(t, t ^ k) for t in range(count)])]
    pallas_call x4, Pallas kernels: 2.44 us -> 0.29 us  [regroup(): pl.pallas_call(functools.partial(regroup_kernel, plan, len(arrays)), in_s...]
  transfers between devices with their start and end apart: 34 -> 34, of which waited for: 18 -> 19; matrix products, arithmetic and copies ran while one was open for 0% -> 0% of each run, Pallas kernels for 14% -> 11%
where the time goes in v5:
time: 110 us
  waiting for transfers between devices  42.8 us (39%)
  starting transfers between devices  41.3 us (38%)
  Pallas kernels  20.9 us (19%)
  local copies, waits for them, and re-layouts  2.2 us (2%)
  other arithmetic  1.7 us (2%)
    ppermute x28, waiting for transfers between devices, swap_shard(): return lax.ppermute(piece, 'shard', [(s, s ^ u) for s in range(count)])  32 us
    ppermute x28, starting transfers between devices, swap_shard(): return lax.ppermute(piece, 'shard', [(s, s ^ u) for s in range(count)])  30.6 us
    ppermute x6, waiting for transfers between devices, swap_tensor(): return lax.ppermute(piece, 'tensor', [(t, t ^ k) for t in range(count)])  10.7 us
    ppermute x6, starting transfers between devices, swap_tensor(): return lax.ppermute(piece, 'tensor', [(t, t ^ k) for t in range(count)])  10.7 us
    pallas_call x1, Pallas kernels, first(): pl.pallas_call(functools.partial(first_kernel, early_ks, late_ks, plan),...  7.98 us
    pallas_call x2, Pallas kernels, last(): pl.pallas_call(functools.partial(last_kernel, plan), in_specs=[whole()] *...  5.57 us
    pallas_call x1, Pallas kernels, next_momentum(): pl.pallas_call(momentum_kernel, grid=(steps,), in_specs=[spec, spec, whol...  3.56 us
  transfers between devices with their start and end apart: 34, of which 19 were waited for; matrix products, arithmetic and copies ran while one was open for 0% of the time, Pallas kernels for 11%

profile of v5, /device:TPU:0, one launch (start us, length us, event | category | flops | bytes accessed | tf_op | source)
XLA Modules:
  0.0 109.8 jit_solution(16688653152502942070)
XLA Ops:
  0.6 1.7 %fusion.1 = bf16[8,128,256]{2,1,0:T(8,128)(2,1)S(1)} fusion(f32[32,128,256]{2,1,0:T(8,128)} %m_ref.2, s32[]{:T(128)S(6)} %select_n.4, bf16[32,128,256]{2,1,0:T(8,128)(2,1)} %g_ref.2), kind=kLoop, calls=%fused_computation.3 | loop fusion | flops 1572864 | bytes 2097156 | tf_op jit(solution)/shard_map/convert_element_type | solution.py:74
  2.3 4.1 %collective-permute-start = (bf16[8,128,256]{2,1,0:T(8,128)(2,1)S(1)}, bf16[8,128,256]{2,1,0:T(8,128)(2,1)S(1)}, u32[]{:S(2)}, u32[]{:S(2)}) collective-permute-start(bf16[8,128,256]{2,1,0:T(8,128)(2,1)S(1)} %fusion.1), channel_id=1, source_target_pairs={{0,2},{1,3},{2,0},{3,1},{4,6},{5,7},{6,4},{7,5},{8,10},{9,11},{10,... | collective-permute-start | bytes 1572872 | tf_op jit(solution)/shard_map/ppermute | solution.py:86
  6.5 2.2 %copy-done = f32[32,128,256]{2,1,0:T(8,128)S(1)} copy-done((f32[32,128,256]{2,1,0:T(8,128)S(1)}, f32[32,128,256]{2,1,0:T(8,128)}, u32[]{:S(2)}) %copy-start) | copy-done | bytes 4194328
  9.1 1.6 %collective-permute-start.9 = (bf16[2,128,256]{2,1,0:T(8,128)(2,1)S(1)}, bf16[2,128,256]{2,1,0:T(8,128)(2,1)S(1)}, u32[]{:S(2)}, u32[]{:S(2)}) collective-permute-start(bf16[2,128,256]{2,1,0:T(8,128)(2,1)S(1)} %get-tuple-element.64), channel_id=1, source_target_pairs={{0,8},{4,12},{8,0},{12,4},{16,24},{20,28},{24,16},{28,20},{1,9},{5... | collective-permute-start | bytes 393224 | tf_op jit(solution)/shard_map/ppermute | solution.py:91
  12.7 2.8 %collective-permute-done.9.refs_2_ = bf16[2,128,256]{2,1,0:T(8,128)(2,1)S(1)} collective-permute-done((bf16[2,128,256]{2,1,0:T(8,128)(2,1)S(1)}, bf16[2,128,256]{2,1,0:T(8,128)(2,1)S(1)}, u32[]{:S(2)}, u32[]{:S(2)}) %collective-permute-start.9) | collective-permute-done | bytes 131104 | tf_op jit(solution)/shard_map/ppermute | solution.py:91
  15.5 2.4 %collective-permute-start.13 = (bf16[2,128,256]{2,1,0:T(8,128)(2,1)S(1)}, bf16[2,128,256]{2,1,0:T(8,128)(2,1)S(1)}, u32[]{:S(2)}, u32[]{:S(2)}) collective-permute-start(bf16[2,128,256]{2,1,0:T(8,128)(2,1)S(1)} %get-tuple-element.68), channel_id=1, source_target_pairs={{0,24},{4,28},{8,16},{12,20},{16,8},{20,12},{24,0},{28,4},{1,25},{... | collective-permute-start | bytes 393224 | tf_op jit(solution)/shard_map/ppermute | solution.py:91
  17.9 2.5 %collective-permute-start.14 = (bf16[2,128,256]{2,1,0:T(8,128)(2,1)S(1)}, bf16[2,128,256]{2,1,0:T(8,128)(2,1)S(1)}, u32[]{:S(2)}, u32[]{:S(2)}) collective-permute-start(bf16[2,128,256]{2,1,0:T(8,128)(2,1)S(1)} %get-tuple-element.69), channel_id=1, source_target_pairs={{0,28},{4,24},{8,20},{12,16},{16,12},{20,8},{24,4},{28,0},{1,29},{... | collective-permute-start | bytes 393224 | tf_op jit(solution)/shard_map/ppermute | solution.py:91
  20.4 3.7 %collective-permute-done.12.refs_5_ = bf16[2,128,256]{2,1,0:T(8,128)(2,1)S(1)} collective-permute-done((bf16[2,128,256]{2,1,0:T(8,128)(2,1)S(1)}, bf16[2,128,256]{2,1,0:T(8,128)(2,1)S(1)}, u32[]{:S(2)}, u32[]{:S(2)}) %collective-permute-start.12) | collective-permute-done | bytes 131104 | tf_op jit(solution)/shard_map/ppermute | solution.py:91
  24.5 1.6 %collective-permute-start.15 = (bf16[8,128,256]{2,1,0:T(8,128)(2,1)S(1)}, bf16[8,128,256]{2,1,0:T(8,128)(2,1)S(1)}, u32[]{:S(2)}, u32[]{:S(2)}) collective-permute-start(bf16[8,128,256]{2,1,0:T(8,128)(2,1)S(1)} %get-tuple-element.70), channel_id=1, source_target_pairs={{0,1},{1,0},{2,3},{3,2},{4,5},{5,4},{6,7},{7,6},{8,9},{9,8},{10,11... | collective-permute-start | bytes 1572872 | tf_op jit(solution)/shard_map/ppermute | solution.py:86
  26.7 3.3 %collective-permute-done.refs_0_ = bf16[8,128,256]{2,1,0:T(8,128)(2,1)S(1)} collective-permute-done((bf16[8,128,256]{2,1,0:T(8,128)(2,1)S(1)}, bf16[8,128,256]{2,1,0:T(8,128)(2,1)S(1)}, u32[]{:S(2)}, u32[]{:S(2)}) %collective-permute-start) | collective-permute-done | bytes 524320 | tf_op jit(solution)/shard_map/ppermute | solution.py:86
  30.1 1.6 %collective-permute-start.2 = (bf16[2,128,256]{2,1,0:T(8,128)(2,1)S(1)}, bf16[2,128,256]{2,1,0:T(8,128)(2,1)S(1)}, u32[]{:S(2)}, u32[]{:S(2)}) collective-permute-start(bf16[2,128,256]{2,1,0:T(8,128)(2,1)S(1)} %get-tuple-element.54), channel_id=1, source_target_pairs={{0,8},{4,12},{8,0},{12,4},{16,24},{20,28},{24,16},{28,20},{1,9},{5... | collective-permute-start | bytes 393224 | tf_op jit(solution)/shard_map/ppermute | solution.py:91
  32.0 1.6 %collective-permute-start.4 = (bf16[2,128,256]{2,1,0:T(8,128)(2,1)S(1)}, bf16[2,128,256]{2,1,0:T(8,128)(2,1)S(1)}, u32[]{:S(2)}, u32[]{:S(2)}) collective-permute-start(bf16[2,128,256]{2,1,0:T(8,128)(2,1)S(1)} %get-tuple-element.56), channel_id=1, source_target_pairs={{0,16},{4,20},{8,24},{12,28},{16,0},{20,4},{24,8},{28,12},{1,17},{... | collective-permute-start | bytes 393224 | tf_op jit(solution)/shard_map/ppermute | solution.py:91
  33.6 2.9 %collective-permute-done.2.refs_2_ = bf16[2,128,256]{2,1,0:T(8,128)(2,1)S(1)} collective-permute-done((bf16[2,128,256]{2,1,0:T(8,128)(2,1)S(1)}, bf16[2,128,256]{2,1,0:T(8,128)(2,1)S(1)}, u32[]{:S(2)}, u32[]{:S(2)}) %collective-permute-start.2) | collective-permute-done | bytes 131104 | tf_op jit(solution)/shard_map/ppermute | solution.py:91
  38.4 2.5 %collective-permute-start.6 = (bf16[2,128,256]{2,1,0:T(8,128)(2,1)S(1)}, bf16[2,128,256]{2,1,0:T(8,128)(2,1)S(1)}, u32[]{:S(2)}, u32[]{:S(2)}) collective-permute-start(bf16[2,128,256]{2,1,0:T(8,128)(2,1)S(1)} %get-tuple-element.58), channel_id=1, source_target_pairs={{0,24},{4,28},{8,16},{12,20},{16,8},{20,12},{24,0},{28,4},{1,25},{... | collective-permute-start | bytes 393224 | tf_op jit(solution)/shard_map/ppermute | solution.py:91
  41.2 3.6 %shard_map.43 = (f32[32,128,256]{2,1,0:T(8,128)}, f32[8,128]{1,0:T(8,128)S(1)}) custom-call(bf16[32,128,256]{2,1,0:T(8,128)(2,1)S(1)} %copy-done.2, f32[32,128,256]{2,1,0:T(8,128)S(1)} %copy-done.1, bf16[2,128,256]{2,1,0:T(8,128)(2,1)S(1)} %get-tuple-element.51.after_ref.refs_0_), custom_call_target="tpu_custom_call" | custom-call | flops 1000 | bytes 1000 | tf_op jit(solution)/shard_map/pallas_call | solution.py:57
  45.6 2.2 %collective-permute-done.7.refs_7_ = bf16[2,128,256]{2,1,0:T(8,128)(2,1)S(1)} collective-permute-done((bf16[2,128,256]{2,1,0:T(8,128)(2,1)S(1)}, bf16[2,128,256]{2,1,0:T(8,128)(2,1)S(1)}, u32[]{:S(2)}, u32[]{:S(2)}) %collective-permute-start.7) | collective-permute-done | bytes 131104 | tf_op jit(solution)/shard_map/ppermute | solution.py:91
  48.6 3.4 %collective-permute-done.15.refs_2_ = bf16[8,128,256]{2,1,0:T(8,128)(2,1)S(1)} collective-permute-done((bf16[8,128,256]{2,1,0:T(8,128)(2,1)S(1)}, bf16[8,128,256]{2,1,0:T(8,128)(2,1)S(1)}, u32[]{:S(2)}, u32[]{:S(2)}) %collective-permute-start.15) | collective-permute-done | bytes 524320 | tf_op jit(solution)/shard_map/ppermute | solution.py:86
  52.1 8.0 %shard_map.47 = (bf16[1024,1024]{1,0:T(8,128)(2,1)S(1)}, bf16[1024,1024]{1,0:T(8,128)(2,1)S(1)}, bf16[8,128,256]{2,1,0:T(8,128)(2,1)S(1)}) custom-call(bf16[1024,512]{1,0:T(8,128)(2,1)S(1)} %get-tuple-element.60.refs_0_, f32[1024,1024]{1,0:T(8,128)S(1)} %get-tuple-element.61.refs_1_, bf16[8,128,256]{2,1,0:T(8,128)(2,1)S(1)} %collective-permute-done.15.refs_2_, ...), custom_call_target="tpu_custom_call" | custom-call | flops 7516192768 | bytes 12582912 | tf_op jit(solution)/shard_map/pallas_call | solution.py:254
  60.1 2.7 %collective-permute-start.26 = (bf16[8,128,256]{2,1,0:T(8,128)(2,1)S(1)}, bf16[8,128,256]{2,1,0:T(8,128)(2,1)S(1)}, u32[]{:S(2)}, u32[]{:S(2)}) collective-permute-start(bf16[8,128,256]{2,1,0:T(8,128)(2,1)S(1)} %get-tuple-element.85), channel_id=1, source_target_pairs={{0,2},{1,3},{2,0},{3,1},{4,6},{5,7},{6,4},{7,5},{8,10},{9,11},{10,... | collective-permute-start | bytes 1572872 | tf_op jit(solution)/shard_map/ppermute | solution.py:86
  62.8 3.3 %shard_map.48 = (bf16[2,128,256]{2,1,0:T(8,128)(2,1)S(1)}, bf16[2,128,256]{2,1,0:T(8,128)(2,1)S(1)}, bf16[2,128,256]{2,1,0:T(8,128)(2,1)S(1)}, bf16[2,128,256]{2...) custom-call(bf16[1024,1024]{1,0:T(8,128)(2,1)S(1)} %get-tuple-elemen, ...), custom_call_target="tpu_custom_call" | custom-call | flops 2147483648 | bytes 8388608 | tf_op jit(solution)/shard_map/pallas_call | solution.py:278
  69.8 2.8 %collective-permute-done.18.refs_2_ = bf16[2,128,256]{2,1,0:T(8,128)(2,1)S(1)} collective-permute-done((bf16[2,128,256]{2,1,0:T(8,128)(2,1)S(1)}, bf16[2,128,256]{2,1,0:T(8,128)(2,1)S(1)}, u32[]{:S(2)}, u32[]{:S(2)}) %collective-permute-start.18) | collective-permute-done | bytes 131104 | tf_op jit(solution)/shard_map/ppermute | solution.py:91
  72.6 2.4 %collective-permute-start.22 = (bf16[2,128,256]{2,1,0:T(8,128)(2,1)S(1)}, bf16[2,128,256]{2,1,0:T(8,128)(2,1)S(1)}, u32[]{:S(2)}, u32[]{:S(2)}) collective-permute-start(bf16[2,128,256]{2,1,0:T(8,128)(2,1)S(1)} %get-tuple-element.81), channel_id=1, source_target_pairs={{0,24},{4,28},{8,16},{12,20},{16,8},{20,12},{24,0},{28,4},{1,25},{... | collective-permute-start | bytes 393224 | tf_op jit(solution)/shard_map/ppermute | solution.py:91
  75.0 2.5 %collective-permute-start.23 = (bf16[2,128,256]{2,1,0:T(8,128)(2,1)S(1)}, bf16[2,128,256]{2,1,0:T(8,128)(2,1)S(1)}, u32[]{:S(2)}, u32[]{:S(2)}) collective-permute-start(bf16[2,128,256]{2,1,0:T(8,128)(2,1)S(1)} %get-tuple-element.82), channel_id=1, source_target_pairs={{0,28},{4,24},{8,20},{12,16},{16,12},{20,8},{24,4},{28,0},{1,29},{... | collective-permute-start | bytes 393224 | tf_op jit(solution)/shard_map/ppermute | solution.py:91
  77.6 3.7 %collective-permute-done.21.refs_5_ = bf16[2,128,256]{2,1,0:T(8,128)(2,1)S(1)} collective-permute-done((bf16[2,128,256]{2,1,0:T(8,128)(2,1)S(1)}, bf16[2,128,256]{2,1,0:T(8,128)(2,1)S(1)}, u32[]{:S(2)}, u32[]{:S(2)}) %collective-permute-start.21) | collective-permute-done | bytes 131104 | tf_op jit(solution)/shard_map/ppermute | solution.py:91
  83.6 2.2 %shard_map.50.refs_1_ = bf16[8,128,256]{2,1,0:T(8,128)(2,1)S(1)} custom-call(bf16[1024,1024]{1,0:T(8,128)(2,1)S(1)} %get-tuple-element.73.x_ref, bf16[1024,1024]{1,0:T(8,128)(2,1)S(1)} %get-tuple-element.74.g_ref), custom_call_target="tpu_custom_call" | custom-call | flops 1073741824 | bytes 8388608 | tf_op jit(solution)/shard_map/pallas_call | solution.py:278
  86.4 1.6 %collective-permute-start.28 = (bf16[2,128,256]{2,1,0:T(8,128)(2,1)S(1)}, bf16[2,128,256]{2,1,0:T(8,128)(2,1)S(1)}, u32[]{:S(2)}, u32[]{:S(2)}) collective-permute-start(bf16[2,128,256]{2,1,0:T(8,128)(2,1)S(1)} %get-tuple-element.88), channel_id=1, source_target_pairs={{0,8},{4,12},{8,0},{12,4},{16,24},{20,28},{24,16},{28,20},{1,9},{5... | collective-permute-start | bytes 393224 | tf_op jit(solution)/shard_map/ppermute | solution.py:91
  88.3 1.6 %collective-permute-start.30 = (bf16[2,128,256]{2,1,0:T(8,128)(2,1)S(1)}, bf16[2,128,256]{2,1,0:T(8,128)(2,1)S(1)}, u32[]{:S(2)}, u32[]{:S(2)}) collective-permute-start(bf16[2,128,256]{2,1,0:T(8,128)(2,1)S(1)} %get-tuple-element.90), channel_id=1, source_target_pairs={{0,16},{4,20},{8,24},{12,28},{16,0},{20,4},{24,8},{28,12},{1,17},{... | collective-permute-start | bytes 393224 | tf_op jit(solution)/shard_map/ppermute | solution.py:91
  89.9 2.9 %collective-permute-done.28.refs_2_ = bf16[2,128,256]{2,1,0:T(8,128)(2,1)S(1)} collective-permute-done((bf16[2,128,256]{2,1,0:T(8,128)(2,1)S(1)}, bf16[2,128,256]{2,1,0:T(8,128)(2,1)S(1)}, u32[]{:S(2)}, u32[]{:S(2)}) %collective-permute-start.28) | collective-permute-done | bytes 131104 | tf_op jit(solution)/shard_map/ppermute | solution.py:91
  94.7 2.5 %collective-permute-start.32 = (bf16[2,128,256]{2,1,0:T(8,128)(2,1)S(1)}, bf16[2,128,256]{2,1,0:T(8,128)(2,1)S(1)}, u32[]{:S(2)}, u32[]{:S(2)}) collective-permute-start(bf16[2,128,256]{2,1,0:T(8,128)(2,1)S(1)} %get-tuple-element.92), channel_id=1, source_target_pairs={{0,24},{4,28},{8,16},{12,20},{16,8},{20,12},{24,0},{28,4},{1,25},{... | collective-permute-start | bytes 393224 | tf_op jit(solution)/shard_map/ppermute | solution.py:91
  98.5 3.4 %collective-permute-done.32.refs_6_ = bf16[2,128,256]{2,1,0:T(8,128)(2,1)S(1)} collective-permute-done((bf16[2,128,256]{2,1,0:T(8,128)(2,1)S(1)}, bf16[2,128,256]{2,1,0:T(8,128)(2,1)S(1)}, u32[]{:S(2)}, u32[]{:S(2)}) %collective-permute-start.32) | collective-permute-done | bytes 131104 | tf_op jit(solution)/shard_map/ppermute | solution.py:91
  101.9 2.2 %collective-permute-done.33.refs_7_ = bf16[2,128,256]{2,1,0:T(8,128)(2,1)S(1)} collective-permute-done((bf16[2,128,256]{2,1,0:T(8,128)(2,1)S(1)}, bf16[2,128,256]{2,1,0:T(8,128)(2,1)S(1)}, u32[]{:S(2)}, u32[]{:S(2)}) %collective-permute-start.33) | collective-permute-done | bytes 131104 | tf_op jit(solution)/shard_map/ppermute | solution.py:91
  105.2 3.5 %collective-permute-done.24.refs_0_ = bf16[8,128,256]{2,1,0:T(8,128)(2,1)S(1)} collective-permute-done((bf16[8,128,256]{2,1,0:T(8,128)(2,1)S(1)}, bf16[8,128,256]{2,1,0:T(8,128)(2,1)S(1)}, u32[]{:S(2)}, u32[]{:S(2)}) %collective-permute-start.24) | collective-permute-done | bytes 524320 | tf_op jit(solution)/shard_map/ppermute | solution.py:86
  (56 shorter events, 19.6 us)
Async XLA Ops:
  2.3 27.6 %collective-permute-start = (bf16[8,128,256]{2,1,0:T(8,128)(2,1)S(1)}, bf16[8,128,256]{2,1,0:T(8,128)(2,1)S(1)}, u32[]{:S(2)}, u32[]{:S(2)}) collective-permute-start(bf16[8,128,256]{2,1,0:T(8,128)(2,1)S(1)} %fusion.1), channel_id=1, source_target_pairs={{0,2},{1,3},{2,0},{3,1},{4,6},{5,7},{6,4},{7,5},{8,10},{9,11},{10,... | collective-permute-start | bytes 1572872 | tf_op jit(solution)/shard_map/ppermute | solution.py:86
  9.0 3.5 %collective-permute-start.8 = (bf16[2,128,256]{2,1,0:T(8,128)(2,1)S(1)}, bf16[2,128,256]{2,1,0:T(8,128)(2,1)S(1)}, u32[]{:S(2)}, u32[]{:S(2)}) collective-permute-start(bf16[2,128,256]{2,1,0:T(8,128)(2,1)S(1)} %get-tuple-element.63), channel_id=1, source_target_pairs={{0,4},{4,0},{8,12},{12,8},{16,20},{20,16},{24,28},{28,24},{1,5},{5... | collective-permute-start | bytes 393224 | tf_op jit(solution)/shard_map/ppermute | solution.py:91
  9.1 6.4 %collective-permute-start.9 = (bf16[2,128,256]{2,1,0:T(8,128)(2,1)S(1)}, bf16[2,128,256]{2,1,0:T(8,128)(2,1)S(1)}, u32[]{:S(2)}, u32[]{:S(2)}) collective-permute-start(bf16[2,128,256]{2,1,0:T(8,128)(2,1)S(1)} %get-tuple-element.64), channel_id=1, source_target_pairs={{0,8},{4,12},{8,0},{12,4},{16,24},{20,28},{24,16},{28,20},{1,9},{5... | collective-permute-start | bytes 393224 | tf_op jit(solution)/shard_map/ppermute | solution.py:91
  10.7 7.3 %collective-permute-start.10 = (bf16[2,128,256]{2,1,0:T(8,128)(2,1)S(1)}, bf16[2,128,256]{2,1,0:T(8,128)(2,1)S(1)}, u32[]{:S(2)}, u32[]{:S(2)}) collective-permute-start(bf16[2,128,256]{2,1,0:T(8,128)(2,1)S(1)} %get-tuple-element.65), channel_id=1, source_target_pairs={{0,12},{4,8},{8,4},{12,0},{16,28},{20,24},{24,20},{28,16},{1,13},{... | collective-permute-start | bytes 393224 | tf_op jit(solution)/shard_map/ppermute | solution.py:91
  11.0 9.5 %collective-permute-start.11 = (bf16[2,128,256]{2,1,0:T(8,128)(2,1)S(1)}, bf16[2,128,256]{2,1,0:T(8,128)(2,1)S(1)}, u32[]{:S(2)}, u32[]{:S(2)}) collective-permute-start(bf16[2,128,256]{2,1,0:T(8,128)(2,1)S(1)} %get-tuple-element.66), channel_id=1, source_target_pairs={{0,16},{4,20},{8,24},{12,28},{16,0},{20,4},{24,8},{28,12},{1,17},{... | collective-permute-start | bytes 393224 | tf_op jit(solution)/shard_map/ppermute | solution.py:91
  12.5 11.7 %collective-permute-start.12 = (bf16[2,128,256]{2,1,0:T(8,128)(2,1)S(1)}, bf16[2,128,256]{2,1,0:T(8,128)(2,1)S(1)}, u32[]{:S(2)}, u32[]{:S(2)}) collective-permute-start(bf16[2,128,256]{2,1,0:T(8,128)(2,1)S(1)} %get-tuple-element.67), channel_id=1, source_target_pairs={{0,20},{4,16},{8,28},{12,24},{16,4},{20,0},{24,12},{28,8},{1,21},{... | collective-permute-start | bytes 393224 | tf_op jit(solution)/shard_map/ppermute | solution.py:91
  15.5 8.7 %collective-permute-start.13 = (bf16[2,128,256]{2,1,0:T(8,128)(2,1)S(1)}, bf16[2,128,256]{2,1,0:T(8,128)(2,1)S(1)}, u32[]{:S(2)}, u32[]{:S(2)}) collective-permute-start(bf16[2,128,256]{2,1,0:T(8,128)(2,1)S(1)} %get-tuple-element.68), channel_id=1, source_target_pairs={{0,24},{4,28},{8,16},{12,20},{16,8},{20,12},{24,0},{28,4},{1,25},{... | collective-permute-start | bytes 393224 | tf_op jit(solution)/shard_map/ppermute | solution.py:91
  17.9 6.5 %collective-permute-start.14 = (bf16[2,128,256]{2,1,0:T(8,128)(2,1)S(1)}, bf16[2,128,256]{2,1,0:T(8,128)(2,1)S(1)}, u32[]{:S(2)}, u32[]{:S(2)}) collective-permute-start(bf16[2,128,256]{2,1,0:T(8,128)(2,1)S(1)} %get-tuple-element.69), channel_id=1, source_target_pairs={{0,28},{4,24},{8,20},{12,16},{16,12},{20,8},{24,4},{28,0},{1,29},{... | collective-permute-start | bytes 393224 | tf_op jit(solution)/shard_map/ppermute | solution.py:91
  24.5 27.5 %collective-permute-start.15 = (bf16[8,128,256]{2,1,0:T(8,128)(2,1)S(1)}, bf16[8,128,256]{2,1,0:T(8,128)(2,1)S(1)}, u32[]{:S(2)}, u32[]{:S(2)}) collective-permute-start(bf16[8,128,256]{2,1,0:T(8,128)(2,1)S(1)} %get-tuple-element.70), channel_id=1, source_target_pairs={{0,1},{1,0},{2,3},{3,2},{4,5},{5,4},{6,7},{7,6},{8,9},{9,8},{10,11... | collective-permute-start | bytes 1572872 | tf_op jit(solution)/shard_map/ppermute | solution.py:86
  26.2 25.9 %collective-permute-start.16 = (bf16[8,128,256]{2,1,0:T(8,128)(2,1)S(1)}, bf16[8,128,256]{2,1,0:T(8,128)(2,1)S(1)}, u32[]{:S(2)}, u32[]{:S(2)}) collective-permute-start(bf16[8,128,256]{2,1,0:T(8,128)(2,1)S(1)} %get-tuple-element.71), channel_id=1, source_target_pairs={{0,3},{1,2},{2,1},{3,0},{4,7},{5,6},{6,5},{7,4},{8,11},{9,10},{10,... | collective-permute-start | bytes 1572872 | tf_op jit(solution)/shard_map/ppermute | solution.py:86
  30.1 6.4 %collective-permute-start.2 = (bf16[2,128,256]{2,1,0:T(8,128)(2,1)S(1)}, bf16[2,128,256]{2,1,0:T(8,128)(2,1)S(1)}, u32[]{:S(2)}, u32[]{:S(2)}) collective-permute-start(bf16[2,128,256]{2,1,0:T(8,128)(2,1)S(1)} %get-tuple-element.54), channel_id=1, source_target_pairs={{0,8},{4,12},{8,0},{12,4},{16,24},{20,28},{24,16},{28,20},{1,9},{5... | collective-permute-start | bytes 393224 | tf_op jit(solution)/shard_map/ppermute | solution.py:91
  31.8 6.6 %collective-permute-start.3 = (bf16[2,128,256]{2,1,0:T(8,128)(2,1)S(1)}, bf16[2,128,256]{2,1,0:T(8,128)(2,1)S(1)}, u32[]{:S(2)}, u32[]{:S(2)}) collective-permute-start(bf16[2,128,256]{2,1,0:T(8,128)(2,1)S(1)} %get-tuple-element.55), channel_id=1, source_target_pairs={{0,12},{4,8},{8,4},{12,0},{16,28},{20,24},{24,20},{28,16},{1,13},{... | collective-permute-start | bytes 393224 | tf_op jit(solution)/shard_map/ppermute | solution.py:91
  32.0 8.9 %collective-permute-start.4 = (bf16[2,128,256]{2,1,0:T(8,128)(2,1)S(1)}, bf16[2,128,256]{2,1,0:T(8,128)(2,1)S(1)}, u32[]{:S(2)}, u32[]{:S(2)}) collective-permute-start(bf16[2,128,256]{2,1,0:T(8,128)(2,1)S(1)} %get-tuple-element.56), channel_id=1, source_target_pairs={{0,16},{4,20},{8,24},{12,28},{16,0},{20,4},{24,8},{28,12},{1,17},{... | collective-permute-start | bytes 393224 | tf_op jit(solution)/shard_map/ppermute | solution.py:91
  36.5 8.3 %collective-permute-start.5 = (bf16[2,128,256]{2,1,0:T(8,128)(2,1)S(1)}, bf16[2,128,256]{2,1,0:T(8,128)(2,1)S(1)}, u32[]{:S(2)}, u32[]{:S(2)}) collective-permute-start(bf16[2,128,256]{2,1,0:T(8,128)(2,1)S(1)} %get-tuple-element.57), channel_id=1, source_target_pairs={{0,20},{4,16},{8,28},{12,24},{16,4},{20,0},{24,12},{28,8},{1,21},{... | collective-permute-start | bytes 393224 | tf_op jit(solution)/shard_map/ppermute | solution.py:91
  38.4 7.2 %collective-permute-start.6 = (bf16[2,128,256]{2,1,0:T(8,128)(2,1)S(1)}, bf16[2,128,256]{2,1,0:T(8,128)(2,1)S(1)}, u32[]{:S(2)}, u32[]{:S(2)}) collective-permute-start(bf16[2,128,256]{2,1,0:T(8,128)(2,1)S(1)} %get-tuple-element.58), channel_id=1, source_target_pairs={{0,24},{4,28},{8,16},{12,20},{16,8},{20,12},{24,0},{28,4},{1,25},{... | collective-permute-start | bytes 393224 | tf_op jit(solution)/shard_map/ppermute | solution.py:91
  40.9 6.8 %collective-permute-start.7 = (bf16[2,128,256]{2,1,0:T(8,128)(2,1)S(1)}, bf16[2,128,256]{2,1,0:T(8,128)(2,1)S(1)}, u32[]{:S(2)}, u32[]{:S(2)}) collective-permute-start(bf16[2,128,256]{2,1,0:T(8,128)(2,1)S(1)} %get-tuple-element.59), channel_id=1, source_target_pairs={{0,28},{4,24},{8,20},{12,16},{16,12},{20,8},{24,4},{28,0},{1,29},{... | collective-permute-start | bytes 393224 | tf_op jit(solution)/shard_map/ppermute | solution.py:91
  60.1 26.2 %collective-permute-start.26 = (bf16[8,128,256]{2,1,0:T(8,128)(2,1)S(1)}, bf16[8,128,256]{2,1,0:T(8,128)(2,1)S(1)}, u32[]{:S(2)}, u32[]{:S(2)}) collective-permute-start(bf16[8,128,256]{2,1,0:T(8,128)(2,1)S(1)} %get-tuple-element.85), channel_id=1, source_target_pairs={{0,2},{1,3},{2,0},{3,1},{4,6},{5,7},{6,4},{7,5},{8,10},{9,11},{10,... | collective-permute-start | bytes 1572872 | tf_op jit(solution)/shard_map/ppermute | solution.py:86
  66.2 3.5 %collective-permute-start.17 = (bf16[2,128,256]{2,1,0:T(8,128)(2,1)S(1)}, bf16[2,128,256]{2,1,0:T(8,128)(2,1)S(1)}, u32[]{:S(2)}, u32[]{:S(2)}) collective-permute-start(bf16[2,128,256]{2,1,0:T(8,128)(2,1)S(1)} %get-tuple-element.76), channel_id=1, source_target_pairs={{0,4},{4,0},{8,12},{12,8},{16,20},{20,16},{24,28},{28,24},{1,5},{5... | collective-permute-start | bytes 393224 | tf_op jit(solution)/shard_map/ppermute | solution.py:91
  66.2 6.4 %collective-permute-start.18 = (bf16[2,128,256]{2,1,0:T(8,128)(2,1)S(1)}, bf16[2,128,256]{2,1,0:T(8,128)(2,1)S(1)}, u32[]{:S(2)}, u32[]{:S(2)}) collective-permute-start(bf16[2,128,256]{2,1,0:T(8,128)(2,1)S(1)} %get-tuple-element.77), channel_id=1, source_target_pairs={{0,8},{4,12},{8,0},{12,4},{16,24},{20,28},{24,16},{28,20},{1,9},{5... | collective-permute-start | bytes 393224 | tf_op jit(solution)/shard_map/ppermute | solution.py:91
  67.8 7.3 %collective-permute-start.19 = (bf16[2,128,256]{2,1,0:T(8,128)(2,1)S(1)}, bf16[2,128,256]{2,1,0:T(8,128)(2,1)S(1)}, u32[]{:S(2)}, u32[]{:S(2)}) collective-permute-start(bf16[2,128,256]{2,1,0:T(8,128)(2,1)S(1)} %get-tuple-element.78), channel_id=1, source_target_pairs={{0,12},{4,8},{8,4},{12,0},{16,28},{20,24},{24,20},{28,16},{1,13},{... | collective-permute-start | bytes 393224 | tf_op jit(solution)/shard_map/ppermute | solution.py:91
  68.1 9.5 %collective-permute-start.20 = (bf16[2,128,256]{2,1,0:T(8,128)(2,1)S(1)}, bf16[2,128,256]{2,1,0:T(8,128)(2,1)S(1)}, u32[]{:S(2)}, u32[]{:S(2)}) collective-permute-start(bf16[2,128,256]{2,1,0:T(8,128)(2,1)S(1)} %get-tuple-element.79), channel_id=1, source_target_pairs={{0,16},{4,20},{8,24},{12,28},{16,0},{20,4},{24,8},{28,12},{1,17},{... | collective-permute-start | bytes 393224 | tf_op jit(solution)/shard_map/ppermute | solution.py:91
  69.6 11.7 %collective-permute-start.21 = (bf16[2,128,256]{2,1,0:T(8,128)(2,1)S(1)}, bf16[2,128,256]{2,1,0:T(8,128)(2,1)S(1)}, u32[]{:S(2)}, u32[]{:S(2)}) collective-permute-start(bf16[2,128,256]{2,1,0:T(8,128)(2,1)S(1)} %get-tuple-element.80), channel_id=1, source_target_pairs={{0,20},{4,16},{8,28},{12,24},{16,4},{20,0},{24,12},{28,8},{1,21},{... | collective-permute-start | bytes 393224 | tf_op jit(solution)/shard_map/ppermute | solution.py:91
  72.6 8.7 %collective-permute-start.22 = (bf16[2,128,256]{2,1,0:T(8,128)(2,1)S(1)}, bf16[2,128,256]{2,1,0:T(8,128)(2,1)S(1)}, u32[]{:S(2)}, u32[]{:S(2)}) collective-permute-start(bf16[2,128,256]{2,1,0:T(8,128)(2,1)S(1)} %get-tuple-element.81), channel_id=1, source_target_pairs={{0,24},{4,28},{8,16},{12,20},{16,8},{20,12},{24,0},{28,4},{1,25},{... | collective-permute-start | bytes 393224 | tf_op jit(solution)/shard_map/ppermute | solution.py:91
  75.0 6.5 %collective-permute-start.23 = (bf16[2,128,256]{2,1,0:T(8,128)(2,1)S(1)}, bf16[2,128,256]{2,1,0:T(8,128)(2,1)S(1)}, u32[]{:S(2)}, u32[]{:S(2)}) collective-permute-start(bf16[2,128,256]{2,1,0:T(8,128)(2,1)S(1)} %get-tuple-element.82), channel_id=1, source_target_pairs={{0,28},{4,24},{8,20},{12,16},{16,12},{20,8},{24,4},{28,0},{1,29},{... | collective-permute-start | bytes 393224 | tf_op jit(solution)/shard_map/ppermute | solution.py:91
  81.7 27.0 %collective-permute-start.24 = (bf16[8,128,256]{2,1,0:T(8,128)(2,1)S(1)}, bf16[8,128,256]{2,1,0:T(8,128)(2,1)S(1)}, u32[]{:S(2)}, u32[]{:S(2)}) collective-permute-start(bf16[8,128,256]{2,1,0:T(8,128)(2,1)S(1)} %get-tuple-element.83), channel_id=1, source_target_pairs={{0,1},{1,0},{2,3},{3,2},{4,5},{5,4},{6,7},{7,6},{8,9},{9,8},{10,11... | collective-permute-start | bytes 1572872 | tf_op jit(solution)/shard_map/ppermute | solution.py:86
  83.2 25.5 %collective-permute-start.25 = (bf16[8,128,256]{2,1,0:T(8,128)(2,1)S(1)}, bf16[8,128,256]{2,1,0:T(8,128)(2,1)S(1)}, u32[]{:S(2)}, u32[]{:S(2)}) collective-permute-start(bf16[8,128,256]{2,1,0:T(8,128)(2,1)S(1)} %get-tuple-element.84), channel_id=1, source_target_pairs={{0,3},{1,2},{2,1},{3,0},{4,7},{5,6},{6,5},{7,4},{8,11},{9,10},{10,... | collective-permute-start | bytes 1572872 | tf_op jit(solution)/shard_map/ppermute | solution.py:86
  86.4 6.4 %collective-permute-start.28 = (bf16[2,128,256]{2,1,0:T(8,128)(2,1)S(1)}, bf16[2,128,256]{2,1,0:T(8,128)(2,1)S(1)}, u32[]{:S(2)}, u32[]{:S(2)}) collective-permute-start(bf16[2,128,256]{2,1,0:T(8,128)(2,1)S(1)} %get-tuple-element.88), channel_id=1, source_target_pairs={{0,8},{4,12},{8,0},{12,4},{16,24},{20,28},{24,16},{28,20},{1,9},{5... | collective-permute-start | bytes 393224 | tf_op jit(solution)/shard_map/ppermute | solution.py:91
  88.0 6.7 %collective-permute-start.29 = (bf16[2,128,256]{2,1,0:T(8,128)(2,1)S(1)}, bf16[2,128,256]{2,1,0:T(8,128)(2,1)S(1)}, u32[]{:S(2)}, u32[]{:S(2)}) collective-permute-start(bf16[2,128,256]{2,1,0:T(8,128)(2,1)S(1)} %get-tuple-element.89), channel_id=1, source_target_pairs={{0,12},{4,8},{8,4},{12,0},{16,28},{20,24},{24,20},{28,16},{1,13},{... | collective-permute-start | bytes 393224 | tf_op jit(solution)/shard_map/ppermute | solution.py:91
  88.3 8.9 %collective-permute-start.30 = (bf16[2,128,256]{2,1,0:T(8,128)(2,1)S(1)}, bf16[2,128,256]{2,1,0:T(8,128)(2,1)S(1)}, u32[]{:S(2)}, u32[]{:S(2)}) collective-permute-start(bf16[2,128,256]{2,1,0:T(8,128)(2,1)S(1)} %get-tuple-element.90), channel_id=1, source_target_pairs={{0,16},{4,20},{8,24},{12,28},{16,0},{20,4},{24,8},{28,12},{1,17},{... | collective-permute-start | bytes 393224 | tf_op jit(solution)/shard_map/ppermute | solution.py:91
  92.8 5.7 %collective-permute-start.31 = (bf16[2,128,256]{2,1,0:T(8,128)(2,1)S(1)}, bf16[2,128,256]{2,1,0:T(8,128)(2,1)S(1)}, u32[]{:S(2)}, u32[]{:S(2)}) collective-permute-start(bf16[2,128,256]{2,1,0:T(8,128)(2,1)S(1)} %get-tuple-element.91), channel_id=1, source_target_pairs={{0,20},{4,16},{8,28},{12,24},{16,4},{20,0},{24,12},{28,8},{1,21},{... | collective-permute-start | bytes 393224 | tf_op jit(solution)/shard_map/ppermute | solution.py:91
  94.7 7.2 %collective-permute-start.32 = (bf16[2,128,256]{2,1,0:T(8,128)(2,1)S(1)}, bf16[2,128,256]{2,1,0:T(8,128)(2,1)S(1)}, u32[]{:S(2)}, u32[]{:S(2)}) collective-permute-start(bf16[2,128,256]{2,1,0:T(8,128)(2,1)S(1)} %get-tuple-element.92), channel_id=1, source_target_pairs={{0,24},{4,28},{8,16},{12,20},{16,8},{20,12},{24,0},{28,4},{1,25},{... | collective-permute-start | bytes 393224 | tf_op jit(solution)/shard_map/ppermute | solution.py:91
  97.2 6.9 %collective-permute-start.33 = (bf16[2,128,256]{2,1,0:T(8,128)(2,1)S(1)}, bf16[2,128,256]{2,1,0:T(8,128)(2,1)S(1)}, u32[]{:S(2)}, u32[]{:S(2)}) collective-permute-start(bf16[2,128,256]{2,1,0:T(8,128)(2,1)S(1)} %get-tuple-element.93), channel_id=1, source_target_pairs={{0,28},{4,24},{8,20},{12,16},{16,12},{20,8},{24,4},{28,0},{1,29},{... | collective-permute-start | bytes 393224 | tf_op jit(solution)/shard_map/ppermute | solution.py:91
  (5 other events, 29.7 us)

commit v6 on v5

--- a/solution.py
+++ b/solution.py
@@ -147,10 +147,9 @@
     return lax.dot_general(a, b, (((1,), (1,)), ((), ())), preferred_element_type=jnp.float32)
 
 
-def symmetric(x_ref, out_ref, with_trace=False, finish=None, mirror=True):
+def symmetric(x_ref, out_ref, finish=None, diagonal=0.0, mirror=True):
     order = x_ref.shape[0]
     tile = min(256, order)
-    trace = jnp.zeros((tile, tile), jnp.float32)
     eye = lax.broadcasted_iota(jnp.int32, (tile, tile), 0) == lax.broadcasted_iota(jnp.int32, (tile, tile), 1)
     for i in range(order // tile):
         cols = slice(i * tile, (i + 1) * tile)
@@ -158,13 +157,24 @@
         part = mm_rows(x_ref[below, :], x_ref[cols, :])
         if finish is not None:
             part = finish(part, below, cols)
-        if with_trace:
-            trace = trace + jnp.where(eye, part[:tile], 0.0)
-        part = part.astype(out_ref.dtype)
-        out_ref[below, cols] = part
+        if diagonal:
+            top = part[:tile] + jnp.where(eye, diagonal, 0.0)
+            out_ref[cols, cols] = top.astype(out_ref.dtype)
+            if i + 1 == order // tile:
+                break
+            part = part[tile:].astype(out_ref.dtype)
+            out_ref[(i + 1) * tile :, cols] = part
+        else:
+            part = part.astype(out_ref.dtype)
+            out_ref[below, cols] = part
+            part = part[tile:]
         if mirror and i + 1 < order // tile:
-            out_ref[cols, (i + 1) * tile :] = part[tile:].T
-    return jnp.sum(trace) if with_trace else None
+            out_ref[cols, (i + 1) * tile :] = part.T
+
+
+def squares(x):
+    x = x.astype(jnp.float32)
+    return jnp.sum((x * x).reshape(x.shape[0] // 8, 8, x.shape[1]), axis=0)
 
 
 def step_columns(gram_ref, x, power_ref):
@@ -185,11 +195,12 @@
 
 
 def early_kernel(places, n, *refs):
-    ins, (x_ref, part_ref) = refs[:n], refs[n:]
+    ins, (x_ref, part_ref, sum_ref) = refs[:n], refs[n:]
     rows, cols = ins[0].shape[1:]
     at = {k: i * cols for i, k in enumerate(sorted({p[0] for p in places}))}
     for k, u, which, b in places:
         x_ref[u * rows : (u + 1) * rows, at[k] : at[k] + cols] = ins[which][b]
+    sum_ref[...] = squares(x_ref[...])
     symmetric(x_ref, part_ref, mirror=False)
 
 
@@ -200,10 +211,11 @@
     return pl.pallas_call(
         functools.partial(early_kernel, places, len(arrays)),
         in_specs=[whole()] * len(arrays),
-        out_specs=[whole()] * 2,
+        out_specs=[whole()] * 3,
         out_shape=[
             jax.ShapeDtypeStruct((order, cols * len(chunks)), jnp.bfloat16),
             jax.ShapeDtypeStruct((order, order), jnp.float32),
+            jax.ShapeDtypeStruct((8, cols * len(chunks)), jnp.float32),
         ],
         compiler_params=params(16),
         cost_estimate=cost(1000, 1000),
@@ -211,7 +223,7 @@
 
 
 def first_kernel(early_ks, late_ks, plan, *refs):
-    before_ref, part_ref, refs = refs[0], refs[1], refs[2:]
+    before_ref, part_ref, sum_ref, refs = refs[0], refs[1], refs[2], refs[3:]
     late_refs, (y_ref, h_ref), refs = refs[: len(late_ks)], refs[len(late_ks) + 1 :][:2], refs[len(late_ks) + 3 :]
     outs, (x_ref, g_ref, w_ref, power_ref) = refs[: len(plan)], refs[len(plan) :]
     order, cols = power_ref.shape
@@ -226,34 +238,37 @@
         ref, c = where[k]
         return ref[:, c]
 
-    def add(part, rows, cols):
-        return part + part_ref[rows, cols]
-
-    scale = 1.0 / (jnp.sqrt(symmetric(x_ref, g_ref, with_trace=True, finish=add)) + 1e-07)
-    by_gram, by_square = -4.775 * (scale * scale), 2.0315 * (scale * scale) * (scale * scale)
+    total = jnp.sum(sum_ref[...]) + jnp.sum(squares(x_ref[...]))
+    scale = 1.0 / (jnp.sqrt(total) + 1e-07)
+
+    def normalised(part, rows, cols):
+        return (part + part_ref[rows, cols]) * (scale * scale)
+
+    shift = 2.0
 
     def weights(square, rows, cols):
-        return by_gram * g_ref[rows, cols].astype(jnp.float32) + by_square * square
-
-    symmetric(g_ref, w_ref, finish=weights)
+        return -4.775 * g_ref[rows, cols].astype(jnp.float32) + 2.0315 * square
+
+    symmetric(x_ref, g_ref, finish=normalised)
+    symmetric(g_ref, w_ref, finish=weights, diagonal=shift)
     for k in range(order // cols):
         c = slice(k * cols, (k + 1) * cols)
-        x = chunk(k)
-        y_ref[:, c] = (scale * (3.4445 * x.astype(jnp.float32) + mm(w_ref[...], x))).astype(jnp.bfloat16)
+        x = (scale * chunk(k).astype(jnp.float32)).astype(jnp.bfloat16)
+        y_ref[:, c] = ((3.4445 - shift) * x.astype(jnp.float32) + mm(w_ref[...], x)).astype(jnp.bfloat16)
     symmetric(y_ref, h_ref)
     for k in sorted({k for pieces in plan for k, _ in pieces}):
         new = step_columns(h_ref, y_ref[:, k * cols : (k + 1) * cols], power_ref)
         finish(new.astype(jnp.bfloat16), k, plan, outs)
 
 
-def first(early_ks, before, part, late, plan, after):
+def first(early_ks, before, part, sums, late, plan, after):
     shards, rows, cols = late[max(late)].shape
     order = shards * rows
     late_ks = sorted(late)
     square = jax.ShapeDtypeStruct((order, order), jnp.bfloat16)
     return pl.pallas_call(
         functools.partial(first_kernel, early_ks, late_ks, plan),
-        in_specs=[whole()] * (2 + len(late)) + [whole(pl.ANY)],
+        in_specs=[whole()] * (3 + len(late)) + [whole(pl.ANY)],
         out_specs=[whole()] * (2 + len(plan)),
         out_shape=[square, square]
         + [jax.ShapeDtypeStruct((len(pieces), rows, cols), jnp.bfloat16) for pieces in plan],
@@ -262,7 +277,7 @@
         + [pltpu.VMEM((order, cols), jnp.float32)],
         compiler_params=params(20),
         cost_estimate=cost(7 * order**3, 12 * order**2),
-    )(before, part, *[late[k] for k in late_ks], after)
+    )(before, part, sums, *[late[k] for k in late_ks], after)
 
 
 def last_kernel(plan, x_ref, g_ref, *refs):
@@ -329,8 +344,8 @@
     (a0,) = nesterov(grads, momentum, a0_plan, shard_count)
     chunks = exchange(z2, p31, a0, True)
     momentum_next, token = next_momentum(grads, momentum, chunks[0][0][0])
-    before, part = early({k: chunks[k] for k in (0, 2)})
-    x, g, z2 = first((0, 2), before, part, {k: chunks[k][0][0] for k in (1, 3)}, z2_plan, token)
+    before, part, sums = early({k: chunks[k] for k in (0, 2)})
+    x, g, z2 = first((0, 2), before, part, sums, {k: chunks[k][0][0] for k in (1, 3)}, z2_plan, token)
     p31 = list(last(x, g, p31_plan, rows, cols))
     (a0,) = last(x, g, a0_plan, rows, cols)
     back = exchange(z2, p31, a0, False)

time: 110 us -> 110 us (level)
  no operation moved by 1% of the time
where the time goes in v6:
time: 110 us
  waiting for transfers between devices  42.8 us (39%)
  starting transfers between devices  41.3 us (38%)
  Pallas kernels  20.9 us (19%)
  local copies, waits for them, and re-layouts  2.2 us (2%)
  other arithmetic  1.7 us (2%)
    ppermute x28, waiting for transfers between devices, swap_shard(): return lax.ppermute(piece, 'shard', [(s, s ^ u) for s in range(count)])  32 us
    ppermute x28, starting transfers between devices, swap_shard(): return lax.ppermute(piece, 'shard', [(s, s ^ u) for s in range(count)])  30.6 us
    ppermute x6, waiting for transfers between devices, swap_tensor(): return lax.ppermute(piece, 'tensor', [(t, t ^ k) for t in range(count)])  10.7 us
    ppermute x6, starting transfers between devices, swap_tensor(): return lax.ppermute(piece, 'tensor', [(t, t ^ k) for t in range(count)])  10.7 us
    pallas_call x1, Pallas kernels, first(): pl.pallas_call(functools.partial(first_kernel, early_ks, late_ks, plan),...  7.98 us
    pallas_call x2, Pallas kernels, last(): pl.pallas_call(functools.partial(last_kernel, plan), in_specs=[whole()] *...  5.57 us
    pallas_call x1, Pallas kernels, next_momentum(): pl.pallas_call(momentum_kernel, grid=(steps,), in_specs=[spec, spec, whol...  3.56 us
  transfers between devices with their start and end apart: 34, of which 19 were waited for; matrix products, arithmetic and copies ran while one was open for 0% of the time, Pallas kernels for 11%

profile of v6, /device:TPU:0, one launch (start us, length us, event | category | flops | bytes accessed | tf_op | source)
XLA Modules:
  0.0 109.8 jit_solution(1619128879298429297)
XLA Ops:
  0.6 1.7 %fusion.1 = bf16[8,128,256]{2,1,0:T(8,128)(2,1)S(1)} fusion(f32[32,128,256]{2,1,0:T(8,128)} %m_ref.2, s32[]{:T(128)S(6)} %select_n.4, bf16[32,128,256]{2,1,0:T(8,128)(2,1)} %g_ref.2), kind=kLoop, calls=%fused_computation.3 | loop fusion | flops 1572864 | bytes 2097156 | tf_op jit(solution)/shard_map/convert_element_type | solution.py:74
  2.3 4.1 %collective-permute-start = (bf16[8,128,256]{2,1,0:T(8,128)(2,1)S(1)}, bf16[8,128,256]{2,1,0:T(8,128)(2,1)S(1)}, u32[]{:S(2)}, u32[]{:S(2)}) collective-permute-start(bf16[8,128,256]{2,1,0:T(8,128)(2,1)S(1)} %fusion.1), channel_id=1, source_target_pairs={{0,2},{1,3},{2,0},{3,1},{4,6},{5,7},{6,4},{7,5},{8,10},{9,11},{10,... | collective-permute-start | bytes 1572872 | tf_op jit(solution)/shard_map/ppermute | solution.py:86
  6.5 2.2 %copy-done = f32[32,128,256]{2,1,0:T(8,128)S(1)} copy-done((f32[32,128,256]{2,1,0:T(8,128)S(1)}, f32[32,128,256]{2,1,0:T(8,128)}, u32[]{:S(2)}) %copy-start) | copy-done | bytes 4194328
  9.1 1.6 %collective-permute-start.9 = (bf16[2,128,256]{2,1,0:T(8,128)(2,1)S(1)}, bf16[2,128,256]{2,1,0:T(8,128)(2,1)S(1)}, u32[]{:S(2)}, u32[]{:S(2)}) collective-permute-start(bf16[2,128,256]{2,1,0:T(8,128)(2,1)S(1)} %get-tuple-element.66), channel_id=1, source_target_pairs={{0,8},{4,12},{8,0},{12,4},{16,24},{20,28},{24,16},{28,20},{1,9},{5... | collective-permute-start | bytes 393224 | tf_op jit(solution)/shard_map/ppermute | solution.py:91
  12.7 2.8 %collective-permute-done.9.refs_2_ = bf16[2,128,256]{2,1,0:T(8,128)(2,1)S(1)} collective-permute-done((bf16[2,128,256]{2,1,0:T(8,128)(2,1)S(1)}, bf16[2,128,256]{2,1,0:T(8,128)(2,1)S(1)}, u32[]{:S(2)}, u32[]{:S(2)}) %collective-permute-start.9) | collective-permute-done | bytes 131104 | tf_op jit(solution)/shard_map/ppermute | solution.py:91
  15.5 2.4 %collective-permute-start.13 = (bf16[2,128,256]{2,1,0:T(8,128)(2,1)S(1)}, bf16[2,128,256]{2,1,0:T(8,128)(2,1)S(1)}, u32[]{:S(2)}, u32[]{:S(2)}) collective-permute-start(bf16[2,128,256]{2,1,0:T(8,128)(2,1)S(1)} %get-tuple-element.70), channel_id=1, source_target_pairs={{0,24},{4,28},{8,16},{12,20},{16,8},{20,12},{24,0},{28,4},{1,25},{... | collective-permute-start | bytes 393224 | tf_op jit(solution)/shard_map/ppermute | solution.py:91
  17.9 2.5 %collective-permute-start.14 = (bf16[2,128,256]{2,1,0:T(8,128)(2,1)S(1)}, bf16[2,128,256]{2,1,0:T(8,128)(2,1)S(1)}, u32[]{:S(2)}, u32[]{:S(2)}) collective-permute-start(bf16[2,128,256]{2,1,0:T(8,128)(2,1)S(1)} %get-tuple-element.71), channel_id=1, source_target_pairs={{0,28},{4,24},{8,20},{12,16},{16,12},{20,8},{24,4},{28,0},{1,29},{... | collective-permute-start | bytes 393224 | tf_op jit(solution)/shard_map/ppermute | solution.py:91
  20.4 3.7 %collective-permute-done.12.refs_5_ = bf16[2,128,256]{2,1,0:T(8,128)(2,1)S(1)} collective-permute-done((bf16[2,128,256]{2,1,0:T(8,128)(2,1)S(1)}, bf16[2,128,256]{2,1,0:T(8,128)(2,1)S(1)}, u32[]{:S(2)}, u32[]{:S(2)}) %collective-permute-start.12) | collective-permute-done | bytes 131104 | tf_op jit(solution)/shard_map/ppermute | solution.py:91
  24.5 1.6 %collective-permute-start.15 = (bf16[8,128,256]{2,1,0:T(8,128)(2,1)S(1)}, bf16[8,128,256]{2,1,0:T(8,128)(2,1)S(1)}, u32[]{:S(2)}, u32[]{:S(2)}) collective-permute-start(bf16[8,128,256]{2,1,0:T(8,128)(2,1)S(1)} %get-tuple-element.72), channel_id=1, source_target_pairs={{0,1},{1,0},{2,3},{3,2},{4,5},{5,4},{6,7},{7,6},{8,9},{9,8},{10,11... | collective-permute-start | bytes 1572872 | tf_op jit(solution)/shard_map/ppermute | solution.py:86
  26.7 3.3 %collective-permute-done.refs_0_ = bf16[8,128,256]{2,1,0:T(8,128)(2,1)S(1)} collective-permute-done((bf16[8,128,256]{2,1,0:T(8,128)(2,1)S(1)}, bf16[8,128,256]{2,1,0:T(8,128)(2,1)S(1)}, u32[]{:S(2)}, u32[]{:S(2)}) %collective-permute-start) | collective-permute-done | bytes 524320 | tf_op jit(solution)/shard_map/ppermute | solution.py:86
  30.1 1.6 %collective-permute-start.2 = (bf16[2,128,256]{2,1,0:T(8,128)(2,1)S(1)}, bf16[2,128,256]{2,1,0:T(8,128)(2,1)S(1)}, u32[]{:S(2)}, u32[]{:S(2)}) collective-permute-start(bf16[2,128,256]{2,1,0:T(8,128)(2,1)S(1)} %get-tuple-element.55), channel_id=1, source_target_pairs={{0,8},{4,12},{8,0},{12,4},{16,24},{20,28},{24,16},{28,20},{1,9},{5... | collective-permute-start | bytes 393224 | tf_op jit(solution)/shard_map/ppermute | solution.py:91
  32.0 1.6 %collective-permute-start.4 = (bf16[2,128,256]{2,1,0:T(8,128)(2,1)S(1)}, bf16[2,128,256]{2,1,0:T(8,128)(2,1)S(1)}, u32[]{:S(2)}, u32[]{:S(2)}) collective-permute-start(bf16[2,128,256]{2,1,0:T(8,128)(2,1)S(1)} %get-tuple-element.57), channel_id=1, source_target_pairs={{0,16},{4,20},{8,24},{12,28},{16,0},{20,4},{24,8},{28,12},{1,17},{... | collective-permute-start | bytes 393224 | tf_op jit(solution)/shard_map/ppermute | solution.py:91
  33.6 2.9 %collective-permute-done.2.refs_2_ = bf16[2,128,256]{2,1,0:T(8,128)(2,1)S(1)} collective-permute-done((bf16[2,128,256]{2,1,0:T(8,128)(2,1)S(1)}, bf16[2,128,256]{2,1,0:T(8,128)(2,1)S(1)}, u32[]{:S(2)}, u32[]{:S(2)}) %collective-permute-start.2) | collective-permute-done | bytes 131104 | tf_op jit(solution)/shard_map/ppermute | solution.py:91
  38.4 2.5 %collective-permute-start.6 = (bf16[2,128,256]{2,1,0:T(8,128)(2,1)S(1)}, bf16[2,128,256]{2,1,0:T(8,128)(2,1)S(1)}, u32[]{:S(2)}, u32[]{:S(2)}) collective-permute-start(bf16[2,128,256]{2,1,0:T(8,128)(2,1)S(1)} %get-tuple-element.59), channel_id=1, source_target_pairs={{0,24},{4,28},{8,16},{12,20},{16,8},{20,12},{24,0},{28,4},{1,25},{... | collective-permute-start | bytes 393224 | tf_op jit(solution)/shard_map/ppermute | solution.py:91
  41.2 3.6 %shard_map.43 = (f32[32,128,256]{2,1,0:T(8,128)}, f32[8,128]{1,0:T(8,128)S(1)}) custom-call(bf16[32,128,256]{2,1,0:T(8,128)(2,1)S(1)} %copy-done.2, f32[32,128,256]{2,1,0:T(8,128)S(1)} %copy-done.1, bf16[2,128,256]{2,1,0:T(8,128)(2,1)S(1)} %get-tuple-element.52.after_ref.refs_0_), custom_call_target="tpu_custom_call" | custom-call | flops 1000 | bytes 1000 | tf_op jit(solution)/shard_map/pallas_call | solution.py:57
  45.6 2.2 %collective-permute-done.7.refs_7_ = bf16[2,128,256]{2,1,0:T(8,128)(2,1)S(1)} collective-permute-done((bf16[2,128,256]{2,1,0:T(8,128)(2,1)S(1)}, bf16[2,128,256]{2,1,0:T(8,128)(2,1)S(1)}, u32[]{:S(2)}, u32[]{:S(2)}) %collective-permute-start.7) | collective-permute-done | bytes 131104 | tf_op jit(solution)/shard_map/ppermute | solution.py:91
  48.6 3.4 %collective-permute-done.15.refs_3_ = bf16[8,128,256]{2,1,0:T(8,128)(2,1)S(1)} collective-permute-done((bf16[8,128,256]{2,1,0:T(8,128)(2,1)S(1)}, bf16[8,128,256]{2,1,0:T(8,128)(2,1)S(1)}, u32[]{:S(2)}, u32[]{:S(2)}) %collective-permute-start.15) | collective-permute-done | bytes 524320 | tf_op jit(solution)/shard_map/ppermute | solution.py:86
  52.1 8.0 %shard_map.47 = (bf16[1024,1024]{1,0:T(8,128)(2,1)S(1)}, bf16[1024,1024]{1,0:T(8,128)(2,1)S(1)}, bf16[8,128,256]{2,1,0:T(8,128)(2,1)S(1)}) custom-call(bf16[1024,512]{1,0:T(8,128)(2,1)S(1)} %get-tuple-element.61.refs_0_, f32[1024,1024]{1,0:T(8,128)S(1)} %get-tuple-element.62.refs_1_, f32[8,512]{1,0:T(8,128)S(1)} %get-tuple-element.63.refs_2_, ...), custom_call_target="tpu_custom_call" | custom-call | flops 7516192768 | bytes 12582912 | tf_op jit(solution)/shard_map/pallas_call | solution.py:269
  60.1 2.7 %collective-permute-start.26 = (bf16[8,128,256]{2,1,0:T(8,128)(2,1)S(1)}, bf16[8,128,256]{2,1,0:T(8,128)(2,1)S(1)}, u32[]{:S(2)}, u32[]{:S(2)}) collective-permute-start(bf16[8,128,256]{2,1,0:T(8,128)(2,1)S(1)} %get-tuple-element.87), channel_id=1, source_target_pairs={{0,2},{1,3},{2,0},{3,1},{4,6},{5,7},{6,4},{7,5},{8,10},{9,11},{10,... | collective-permute-start | bytes 1572872 | tf_op jit(solution)/shard_map/ppermute | solution.py:86
  62.8 3.3 %shard_map.48 = (bf16[2,128,256]{2,1,0:T(8,128)(2,1)S(1)}, bf16[2,128,256]{2,1,0:T(8,128)(2,1)S(1)}, bf16[2,128,256]{2,1,0:T(8,128)(2,1)S(1)}, bf16[2,128,256]{2...) custom-call(bf16[1024,1024]{1,0:T(8,128)(2,1)S(1)} %get-tuple-elemen, ...), custom_call_target="tpu_custom_call" | custom-call | flops 2147483648 | bytes 8388608 | tf_op jit(solution)/shard_map/pallas_call | solution.py:293
  69.8 2.8 %collective-permute-done.18.refs_2_ = bf16[2,128,256]{2,1,0:T(8,128)(2,1)S(1)} collective-permute-done((bf16[2,128,256]{2,1,0:T(8,128)(2,1)S(1)}, bf16[2,128,256]{2,1,0:T(8,128)(2,1)S(1)}, u32[]{:S(2)}, u32[]{:S(2)}) %collective-permute-start.18) | collective-permute-done | bytes 131104 | tf_op jit(solution)/shard_map/ppermute | solution.py:91
  72.6 2.4 %collective-permute-start.22 = (bf16[2,128,256]{2,1,0:T(8,128)(2,1)S(1)}, bf16[2,128,256]{2,1,0:T(8,128)(2,1)S(1)}, u32[]{:S(2)}, u32[]{:S(2)}) collective-permute-start(bf16[2,128,256]{2,1,0:T(8,128)(2,1)S(1)} %get-tuple-element.83), channel_id=1, source_target_pairs={{0,24},{4,28},{8,16},{12,20},{16,8},{20,12},{24,0},{28,4},{1,25},{... | collective-permute-start | bytes 393224 | tf_op jit(solution)/shard_map/ppermute | solution.py:91
  75.0 2.5 %collective-permute-start.23 = (bf16[2,128,256]{2,1,0:T(8,128)(2,1)S(1)}, bf16[2,128,256]{2,1,0:T(8,128)(2,1)S(1)}, u32[]{:S(2)}, u32[]{:S(2)}) collective-permute-start(bf16[2,128,256]{2,1,0:T(8,128)(2,1)S(1)} %get-tuple-element.84), channel_id=1, source_target_pairs={{0,28},{4,24},{8,20},{12,16},{16,12},{20,8},{24,4},{28,0},{1,29},{... | collective-permute-start | bytes 393224 | tf_op jit(solution)/shard_map/ppermute | solution.py:91
  77.6 3.7 %collective-permute-done.21.refs_5_ = bf16[2,128,256]{2,1,0:T(8,128)(2,1)S(1)} collective-permute-done((bf16[2,128,256]{2,1,0:T(8,128)(2,1)S(1)}, bf16[2,128,256]{2,1,0:T(8,128)(2,1)S(1)}, u32[]{:S(2)}, u32[]{:S(2)}) %collective-permute-start.21) | collective-permute-done | bytes 131104 | tf_op jit(solution)/shard_map/ppermute | solution.py:91
  83.6 2.2 %shard_map.50.refs_1_ = bf16[8,128,256]{2,1,0:T(8,128)(2,1)S(1)} custom-call(bf16[1024,1024]{1,0:T(8,128)(2,1)S(1)} %get-tuple-element.75.x_ref, bf16[1024,1024]{1,0:T(8,128)(2,1)S(1)} %get-tuple-element.76.g_ref), custom_call_target="tpu_custom_call" | custom-call | flops 1073741824 | bytes 8388608 | tf_op jit(solution)/shard_map/pallas_call | solution.py:293
  86.4 1.6 %collective-permute-start.28 = (bf16[2,128,256]{2,1,0:T(8,128)(2,1)S(1)}, bf16[2,128,256]{2,1,0:T(8,128)(2,1)S(1)}, u32[]{:S(2)}, u32[]{:S(2)}) collective-permute-start(bf16[2,128,256]{2,1,0:T(8,128)(2,1)S(1)} %get-tuple-element.90), channel_id=1, source_target_pairs={{0,8},{4,12},{8,0},{12,4},{16,24},{20,28},{24,16},{28,20},{1,9},{5... | collective-permute-start | bytes 393224 | tf_op jit(solution)/shard_map/ppermute | solution.py:91
  88.3 1.6 %collective-permute-start.30 = (bf16[2,128,256]{2,1,0:T(8,128)(2,1)S(1)}, bf16[2,128,256]{2,1,0:T(8,128)(2,1)S(1)}, u32[]{:S(2)}, u32[]{:S(2)}) collective-permute-start(bf16[2,128,256]{2,1,0:T(8,128)(2,1)S(1)} %get-tuple-element.92), channel_id=1, source_target_pairs={{0,16},{4,20},{8,24},{12,28},{16,0},{20,4},{24,8},{28,12},{1,17},{... | collective-permute-start | bytes 393224 | tf_op jit(solution)/shard_map/ppermute | solution.py:91
  89.9 2.9 %collective-permute-done.28.refs_2_ = bf16[2,128,256]{2,1,0:T(8,128)(2,1)S(1)} collective-permute-done((bf16[2,128,256]{2,1,0:T(8,128)(2,1)S(1)}, bf16[2,128,256]{2,1,0:T(8,128)(2,1)S(1)}, u32[]{:S(2)}, u32[]{:S(2)}) %collective-permute-start.28) | collective-permute-done | bytes 131104 | tf_op jit(solution)/shard_map/ppermute | solution.py:91
  94.7 2.5 %collective-permute-start.32 = (bf16[2,128,256]{2,1,0:T(8,128)(2,1)S(1)}, bf16[2,128,256]{2,1,0:T(8,128)(2,1)S(1)}, u32[]{:S(2)}, u32[]{:S(2)}) collective-permute-start(bf16[2,128,256]{2,1,0:T(8,128)(2,1)S(1)} %get-tuple-element.94), channel_id=1, source_target_pairs={{0,24},{4,28},{8,16},{12,20},{16,8},{20,12},{24,0},{28,4},{1,25},{... | collective-permute-start | bytes 393224 | tf_op jit(solution)/shard_map/ppermute | solution.py:91
  98.5 3.4 %collective-permute-done.32.refs_6_ = bf16[2,128,256]{2,1,0:T(8,128)(2,1)S(1)} collective-permute-done((bf16[2,128,256]{2,1,0:T(8,128)(2,1)S(1)}, bf16[2,128,256]{2,1,0:T(8,128)(2,1)S(1)}, u32[]{:S(2)}, u32[]{:S(2)}) %collective-permute-start.32) | collective-permute-done | bytes 131104 | tf_op jit(solution)/shard_map/ppermute | solution.py:91
  101.9 2.2 %collective-permute-done.33.refs_7_ = bf16[2,128,256]{2,1,0:T(8,128)(2,1)S(1)} collective-permute-done((bf16[2,128,256]{2,1,0:T(8,128)(2,1)S(1)}, bf16[2,128,256]{2,1,0:T(8,128)(2,1)S(1)}, u32[]{:S(2)}, u32[]{:S(2)}) %collective-permute-start.33) | collective-permute-done | bytes 131104 | tf_op jit(solution)/shard_map/ppermute | solution.py:91
  105.2 3.5 %collective-permute-done.24.refs_0_ = bf16[8,128,256]{2,1,0:T(8,128)(2,1)S(1)} collective-permute-done((bf16[8,128,256]{2,1,0:T(8,128)(2,1)S(1)}, bf16[8,128,256]{2,1,0:T(8,128)(2,1)S(1)}, u32[]{:S(2)}, u32[]{:S(2)}) %collective-permute-start.24) | collective-permute-done | bytes 524320 | tf_op jit(solution)/shard_map/ppermute | solution.py:86
  (56 shorter events, 19.6 us)
Async XLA Ops:
  2.3 27.6 %collective-permute-start = (bf16[8,128,256]{2,1,0:T(8,128)(2,1)S(1)}, bf16[8,128,256]{2,1,0:T(8,128)(2,1)S(1)}, u32[]{:S(2)}, u32[]{:S(2)}) collective-permute-start(bf16[8,128,256]{2,1,0:T(8,128)(2,1)S(1)} %fusion.1), channel_id=1, source_target_pairs={{0,2},{1,3},{2,0},{3,1},{4,6},{5,7},{6,4},{7,5},{8,10},{9,11},{10,... | collective-permute-start | bytes 1572872 | tf_op jit(solution)/shard_map/ppermute | solution.py:86
  9.0 3.5 %collective-permute-start.8 = (bf16[2,128,256]{2,1,0:T(8,128)(2,1)S(1)}, bf16[2,128,256]{2,1,0:T(8,128)(2,1)S(1)}, u32[]{:S(2)}, u32[]{:S(2)}) collective-permute-start(bf16[2,128,256]{2,1,0:T(8,128)(2,1)S(1)} %get-tuple-element.65), channel_id=1, source_target_pairs={{0,4},{4,0},{8,12},{12,8},{16,20},{20,16},{24,28},{28,24},{1,5},{5... | collective-permute-start | bytes 393224 | tf_op jit(solution)/shard_map/ppermute | solution.py:91
  9.1 6.4 %collective-permute-start.9 = (bf16[2,128,256]{2,1,0:T(8,128)(2,1)S(1)}, bf16[2,128,256]{2,1,0:T(8,128)(2,1)S(1)}, u32[]{:S(2)}, u32[]{:S(2)}) collective-permute-start(bf16[2,128,256]{2,1,0:T(8,128)(2,1)S(1)} %get-tuple-element.66), channel_id=1, source_target_pairs={{0,8},{4,12},{8,0},{12,4},{16,24},{20,28},{24,16},{28,20},{1,9},{5... | collective-permute-start | bytes 393224 | tf_op jit(solution)/shard_map/ppermute | solution.py:91
  10.7 7.3 %collective-permute-start.10 = (bf16[2,128,256]{2,1,0:T(8,128)(2,1)S(1)}, bf16[2,128,256]{2,1,0:T(8,128)(2,1)S(1)}, u32[]{:S(2)}, u32[]{:S(2)}) collective-permute-start(bf16[2,128,256]{2,1,0:T(8,128)(2,1)S(1)} %get-tuple-element.67), channel_id=1, source_target_pairs={{0,12},{4,8},{8,4},{12,0},{16,28},{20,24},{24,20},{28,16},{1,13},{... | collective-permute-start | bytes 393224 | tf_op jit(solution)/shard_map/ppermute | solution.py:91
  11.0 9.5 %collective-permute-start.11 = (bf16[2,128,256]{2,1,0:T(8,128)(2,1)S(1)}, bf16[2,128,256]{2,1,0:T(8,128)(2,1)S(1)}, u32[]{:S(2)}, u32[]{:S(2)}) collective-permute-start(bf16[2,128,256]{2,1,0:T(8,128)(2,1)S(1)} %get-tuple-element.68), channel_id=1, source_target_pairs={{0,16},{4,20},{8,24},{12,28},{16,0},{20,4},{24,8},{28,12},{1,17},{... | collective-permute-start | bytes 393224 | tf_op jit(solution)/shard_map/ppermute | solution.py:91
  12.5 11.7 %collective-permute-start.12 = (bf16[2,128,256]{2,1,0:T(8,128)(2,1)S(1)}, bf16[2,128,256]{2,1,0:T(8,128)(2,1)S(1)}, u32[]{:S(2)}, u32[]{:S(2)}) collective-permute-start(bf16[2,128,256]{2,1,0:T(8,128)(2,1)S(1)} %get-tuple-element.69), channel_id=1, source_target_pairs={{0,20},{4,16},{8,28},{12,24},{16,4},{20,0},{24,12},{28,8},{1,21},{... | collective-permute-start | bytes 393224 | tf_op jit(solution)/shard_map/ppermute | solution.py:91
  15.5 8.7 %collective-permute-start.13 = (bf16[2,128,256]{2,1,0:T(8,128)(2,1)S(1)}, bf16[2,128,256]{2,1,0:T(8,128)(2,1)S(1)}, u32[]{:S(2)}, u32[]{:S(2)}) collective-permute-start(bf16[2,128,256]{2,1,0:T(8,128)(2,1)S(1)} %get-tuple-element.70), channel_id=1, source_target_pairs={{0,24},{4,28},{8,16},{12,20},{16,8},{20,12},{24,0},{28,4},{1,25},{... | collective-permute-start | bytes 393224 | tf_op jit(solution)/shard_map/ppermute | solution.py:91
  17.9 6.5 %collective-permute-start.14 = (bf16[2,128,256]{2,1,0:T(8,128)(2,1)S(1)}, bf16[2,128,256]{2,1,0:T(8,128)(2,1)S(1)}, u32[]{:S(2)}, u32[]{:S(2)}) collective-permute-start(bf16[2,128,256]{2,1,0:T(8,128)(2,1)S(1)} %get-tuple-element.71), channel_id=1, source_target_pairs={{0,28},{4,24},{8,20},{12,16},{16,12},{20,8},{24,4},{28,0},{1,29},{... | collective-permute-start | bytes 393224 | tf_op jit(solution)/shard_map/ppermute | solution.py:91
  24.5 27.5 %collective-permute-start.15 = (bf16[8,128,256]{2,1,0:T(8,128)(2,1)S(1)}, bf16[8,128,256]{2,1,0:T(8,128)(2,1)S(1)}, u32[]{:S(2)}, u32[]{:S(2)}) collective-permute-start(bf16[8,128,256]{2,1,0:T(8,128)(2,1)S(1)} %get-tuple-element.72), channel_id=1, source_target_pairs={{0,1},{1,0},{2,3},{3,2},{4,5},{5,4},{6,7},{7,6},{8,9},{9,8},{10,11... | collective-permute-start | bytes 1572872 | tf_op jit(solution)/shard_map/ppermute | solution.py:86
  26.2 25.9 %collective-permute-start.16 = (bf16[8,128,256]{2,1,0:T(8,128)(2,1)S(1)}, bf16[8,128,256]{2,1,0:T(8,128)(2,1)S(1)}, u32[]{:S(2)}, u32[]{:S(2)}) collective-permute-start(bf16[8,128,256]{2,1,0:T(8,128)(2,1)S(1)} %get-tuple-element.73), channel_id=1, source_target_pairs={{0,3},{1,2},{2,1},{3,0},{4,7},{5,6},{6,5},{7,4},{8,11},{9,10},{10,... | collective-permute-start | bytes 1572872 | tf_op jit(solution)/shard_map/ppermute | solution.py:86
  30.1 6.4 %collective-permute-start.2 = (bf16[2,128,256]{2,1,0:T(8,128)(2,1)S(1)}, bf16[2,128,256]{2,1,0:T(8,128)(2,1)S(1)}, u32[]{:S(2)}, u32[]{:S(2)}) collective-permute-start(bf16[2,128,256]{2,1,0:T(8,128)(2,1)S(1)} %get-tuple-element.55), channel_id=1, source_target_pairs={{0,8},{4,12},{8,0},{12,4},{16,24},{20,28},{24,16},{28,20},{1,9},{5... | collective-permute-start | bytes 393224 | tf_op jit(solution)/shard_map/ppermute | solution.py:91
  31.8 6.6 %collective-permute-start.3 = (bf16[2,128,256]{2,1,0:T(8,128)(2,1)S(1)}, bf16[2,128,256]{2,1,0:T(8,128)(2,1)S(1)}, u32[]{:S(2)}, u32[]{:S(2)}) collective-permute-start(bf16[2,128,256]{2,1,0:T(8,128)(2,1)S(1)} %get-tuple-element.56), channel_id=1, source_target_pairs={{0,12},{4,8},{8,4},{12,0},{16,28},{20,24},{24,20},{28,16},{1,13},{... | collective-permute-start | bytes 393224 | tf_op jit(solution)/shard_map/ppermute | solution.py:91
  32.0 8.9 %collective-permute-start.4 = (bf16[2,128,256]{2,1,0:T(8,128)(2,1)S(1)}, bf16[2,128,256]{2,1,0:T(8,128)(2,1)S(1)}, u32[]{:S(2)}, u32[]{:S(2)}) collective-permute-start(bf16[2,128,256]{2,1,0:T(8,128)(2,1)S(1)} %get-tuple-element.57), channel_id=1, source_target_pairs={{0,16},{4,20},{8,24},{12,28},{16,0},{20,4},{24,8},{28,12},{1,17},{... | collective-permute-start | bytes 393224 | tf_op jit(solution)/shard_map/ppermute | solution.py:91
  36.5 8.3 %collective-permute-start.5 = (bf16[2,128,256]{2,1,0:T(8,128)(2,1)S(1)}, bf16[2,128,256]{2,1,0:T(8,128)(2,1)S(1)}, u32[]{:S(2)}, u32[]{:S(2)}) collective-permute-start(bf16[2,128,256]{2,1,0:T(8,128)(2,1)S(1)} %get-tuple-element.58), channel_id=1, source_target_pairs={{0,20},{4,16},{8,28},{12,24},{16,4},{20,0},{24,12},{28,8},{1,21},{... | collective-permute-start | bytes 393224 | tf_op jit(solution)/shard_map/ppermute | solution.py:91
  38.4 7.2 %collective-permute-start.6 = (bf16[2,128,256]{2,1,0:T(8,128)(2,1)S(1)}, bf16[2,128,256]{2,1,0:T(8,128)(2,1)S(1)}, u32[]{:S(2)}, u32[]{:S(2)}) collective-permute-start(bf16[2,128,256]{2,1,0:T(8,128)(2,1)S(1)} %get-tuple-element.59), channel_id=1, source_target_pairs={{0,24},{4,28},{8,16},{12,20},{16,8},{20,12},{24,0},{28,4},{1,25},{... | collective-permute-start | bytes 393224 | tf_op jit(solution)/shard_map/ppermute | solution.py:91
  40.9 6.8 %collective-permute-start.7 = (bf16[2,128,256]{2,1,0:T(8,128)(2,1)S(1)}, bf16[2,128,256]{2,1,0:T(8,128)(2,1)S(1)}, u32[]{:S(2)}, u32[]{:S(2)}) collective-permute-start(bf16[2,128,256]{2,1,0:T(8,128)(2,1)S(1)} %get-tuple-element.60), channel_id=1, source_target_pairs={{0,28},{4,24},{8,20},{12,16},{16,12},{20,8},{24,4},{28,0},{1,29},{... | collective-permute-start | bytes 393224 | tf_op jit(solution)/shard_map/ppermute | solution.py:91
  60.1 26.2 %collective-permute-start.26 = (bf16[8,128,256]{2,1,0:T(8,128)(2,1)S(1)}, bf16[8,128,256]{2,1,0:T(8,128)(2,1)S(1)}, u32[]{:S(2)}, u32[]{:S(2)}) collective-permute-start(bf16[8,128,256]{2,1,0:T(8,128)(2,1)S(1)} %get-tuple-element.87), channel_id=1, source_target_pairs={{0,2},{1,3},{2,0},{3,1},{4,6},{5,7},{6,4},{7,5},{8,10},{9,11},{10,... | collective-permute-start | bytes 1572872 | tf_op jit(solution)/shard_map/ppermute | solution.py:86
  66.2 3.5 %collective-permute-start.17 = (bf16[2,128,256]{2,1,0:T(8,128)(2,1)S(1)}, bf16[2,128,256]{2,1,0:T(8,128)(2,1)S(1)}, u32[]{:S(2)}, u32[]{:S(2)}) collective-permute-start(bf16[2,128,256]{2,1,0:T(8,128)(2,1)S(1)} %get-tuple-element.78), channel_id=1, source_target_pairs={{0,4},{4,0},{8,12},{12,8},{16,20},{20,16},{24,28},{28,24},{1,5},{5... | collective-permute-start | bytes 393224 | tf_op jit(solution)/shard_map/ppermute | solution.py:91
  66.2 6.4 %collective-permute-start.18 = (bf16[2,128,256]{2,1,0:T(8,128)(2,1)S(1)}, bf16[2,128,256]{2,1,0:T(8,128)(2,1)S(1)}, u32[]{:S(2)}, u32[]{:S(2)}) collective-permute-start(bf16[2,128,256]{2,1,0:T(8,128)(2,1)S(1)} %get-tuple-element.79), channel_id=1, source_target_pairs={{0,8},{4,12},{8,0},{12,4},{16,24},{20,28},{24,16},{28,20},{1,9},{5... | collective-permute-start | bytes 393224 | tf_op jit(solution)/shard_map/ppermute | solution.py:91
  67.8 7.3 %collective-permute-start.19 = (bf16[2,128,256]{2,1,0:T(8,128)(2,1)S(1)}, bf16[2,128,256]{2,1,0:T(8,128)(2,1)S(1)}, u32[]{:S(2)}, u32[]{:S(2)}) collective-permute-start(bf16[2,128,256]{2,1,0:T(8,128)(2,1)S(1)} %get-tuple-element.80), channel_id=1, source_target_pairs={{0,12},{4,8},{8,4},{12,0},{16,28},{20,24},{24,20},{28,16},{1,13},{... | collective-permute-start | bytes 393224 | tf_op jit(solution)/shard_map/ppermute | solution.py:91
  68.1 9.5 %collective-permute-start.20 = (bf16[2,128,256]{2,1,0:T(8,128)(2,1)S(1)}, bf16[2,128,256]{2,1,0:T(8,128)(2,1)S(1)}, u32[]{:S(2)}, u32[]{:S(2)}) collective-permute-start(bf16[2,128,256]{2,1,0:T(8,128)(2,1)S(1)} %get-tuple-element.81), channel_id=1, source_target_pairs={{0,16},{4,20},{8,24},{12,28},{16,0},{20,4},{24,8},{28,12},{1,17},{... | collective-permute-start | bytes 393224 | tf_op jit(solution)/shard_map/ppermute | solution.py:91
  69.6 11.7 %collective-permute-start.21 = (bf16[2,128,256]{2,1,0:T(8,128)(2,1)S(1)}, bf16[2,128,256]{2,1,0:T(8,128)(2,1)S(1)}, u32[]{:S(2)}, u32[]{:S(2)}) collective-permute-start(bf16[2,128,256]{2,1,0:T(8,128)(2,1)S(1)} %get-tuple-element.82), channel_id=1, source_target_pairs={{0,20},{4,16},{8,28},{12,24},{16,4},{20,0},{24,12},{28,8},{1,21},{... | collective-permute-start | bytes 393224 | tf_op jit(solution)/shard_map/ppermute | solution.py:91
  72.6 8.7 %collective-permute-start.22 = (bf16[2,128,256]{2,1,0:T(8,128)(2,1)S(1)}, bf16[2,128,256]{2,1,0:T(8,128)(2,1)S(1)}, u32[]{:S(2)}, u32[]{:S(2)}) collective-permute-start(bf16[2,128,256]{2,1,0:T(8,128)(2,1)S(1)} %get-tuple-element.83), channel_id=1, source_target_pairs={{0,24},{4,28},{8,16},{12,20},{16,8},{20,12},{24,0},{28,4},{1,25},{... | collective-permute-start | bytes 393224 | tf_op jit(solution)/shard_map/ppermute | solution.py:91
  75.0 6.5 %collective-permute-start.23 = (bf16[2,128,256]{2,1,0:T(8,128)(2,1)S(1)}, bf16[2,128,256]{2,1,0:T(8,128)(2,1)S(1)}, u32[]{:S(2)}, u32[]{:S(2)}) collective-permute-start(bf16[2,128,256]{2,1,0:T(8,128)(2,1)S(1)} %get-tuple-element.84), channel_id=1, source_target_pairs={{0,28},{4,24},{8,20},{12,16},{16,12},{20,8},{24,4},{28,0},{1,29},{... | collective-permute-start | bytes 393224 | tf_op jit(solution)/shard_map/ppermute | solution.py:91
  81.7 27.0 %collective-permute-start.24 = (bf16[8,128,256]{2,1,0:T(8,128)(2,1)S(1)}, bf16[8,128,256]{2,1,0:T(8,128)(2,1)S(1)}, u32[]{:S(2)}, u32[]{:S(2)}) collective-permute-start(bf16[8,128,256]{2,1,0:T(8,128)(2,1)S(1)} %get-tuple-element.85), channel_id=1, source_target_pairs={{0,1},{1,0},{2,3},{3,2},{4,5},{5,4},{6,7},{7,6},{8,9},{9,8},{10,11... | collective-permute-start | bytes 1572872 | tf_op jit(solution)/shard_map/ppermute | solution.py:86
  83.2 25.5 %collective-permute-start.25 = (bf16[8,128,256]{2,1,0:T(8,128)(2,1)S(1)}, bf16[8,128,256]{2,1,0:T(8,128)(2,1)S(1)}, u32[]{:S(2)}, u32[]{:S(2)}) collective-permute-start(bf16[8,128,256]{2,1,0:T(8,128)(2,1)S(1)} %get-tuple-element.86), channel_id=1, source_target_pairs={{0,3},{1,2},{2,1},{3,0},{4,7},{5,6},{6,5},{7,4},{8,11},{9,10},{10,... | collective-permute-start | bytes 1572872 | tf_op jit(solution)/shard_map/ppermute | solution.py:86
  86.4 6.4 %collective-permute-start.28 = (bf16[2,128,256]{2,1,0:T(8,128)(2,1)S(1)}, bf16[2,128,256]{2,1,0:T(8,128)(2,1)S(1)}, u32[]{:S(2)}, u32[]{:S(2)}) collective-permute-start(bf16[2,128,256]{2,1,0:T(8,128)(2,1)S(1)} %get-tuple-element.90), channel_id=1, source_target_pairs={{0,8},{4,12},{8,0},{12,4},{16,24},{20,28},{24,16},{28,20},{1,9},{5... | collective-permute-start | bytes 393224 | tf_op jit(solution)/shard_map/ppermute | solution.py:91
  88.0 6.7 %collective-permute-start.29 = (bf16[2,128,256]{2,1,0:T(8,128)(2,1)S(1)}, bf16[2,128,256]{2,1,0:T(8,128)(2,1)S(1)}, u32[]{:S(2)}, u32[]{:S(2)}) collective-permute-start(bf16[2,128,256]{2,1,0:T(8,128)(2,1)S(1)} %get-tuple-element.91), channel_id=1, source_target_pairs={{0,12},{4,8},{8,4},{12,0},{16,28},{20,24},{24,20},{28,16},{1,13},{... | collective-permute-start | bytes 393224 | tf_op jit(solution)/shard_map/ppermute | solution.py:91
  88.3 8.9 %collective-permute-start.30 = (bf16[2,128,256]{2,1,0:T(8,128)(2,1)S(1)}, bf16[2,128,256]{2,1,0:T(8,128)(2,1)S(1)}, u32[]{:S(2)}, u32[]{:S(2)}) collective-permute-start(bf16[2,128,256]{2,1,0:T(8,128)(2,1)S(1)} %get-tuple-element.92), channel_id=1, source_target_pairs={{0,16},{4,20},{8,24},{12,28},{16,0},{20,4},{24,8},{28,12},{1,17},{... | collective-permute-start | bytes 393224 | tf_op jit(solution)/shard_map/ppermute | solution.py:91
  92.8 5.7 %collective-permute-start.31 = (bf16[2,128,256]{2,1,0:T(8,128)(2,1)S(1)}, bf16[2,128,256]{2,1,0:T(8,128)(2,1)S(1)}, u32[]{:S(2)}, u32[]{:S(2)}) collective-permute-start(bf16[2,128,256]{2,1,0:T(8,128)(2,1)S(1)} %get-tuple-element.93), channel_id=1, source_target_pairs={{0,20},{4,16},{8,28},{12,24},{16,4},{20,0},{24,12},{28,8},{1,21},{... | collective-permute-start | bytes 393224 | tf_op jit(solution)/shard_map/ppermute | solution.py:91
  94.7 7.2 %collective-permute-start.32 = (bf16[2,128,256]{2,1,0:T(8,128)(2,1)S(1)}, bf16[2,128,256]{2,1,0:T(8,128)(2,1)S(1)}, u32[]{:S(2)}, u32[]{:S(2)}) collective-permute-start(bf16[2,128,256]{2,1,0:T(8,128)(2,1)S(1)} %get-tuple-element.94), channel_id=1, source_target_pairs={{0,24},{4,28},{8,16},{12,20},{16,8},{20,12},{24,0},{28,4},{1,25},{... | collective-permute-start | bytes 393224 | tf_op jit(solution)/shard_map/ppermute | solution.py:91
  97.2 6.9 %collective-permute-start.33 = (bf16[2,128,256]{2,1,0:T(8,128)(2,1)S(1)}, bf16[2,128,256]{2,1,0:T(8,128)(2,1)S(1)}, u32[]{:S(2)}, u32[]{:S(2)}) collective-permute-start(bf16[2,128,256]{2,1,0:T(8,128)(2,1)S(1)} %get-tuple-element.95), channel_id=1, source_target_pairs={{0,28},{4,24},{8,20},{12,16},{16,12},{20,8},{24,4},{28,0},{1,29},{... | collective-permute-start | bytes 393224 | tf_op jit(solution)/shard_map/ppermute | solution.py:91
  (5 other events, 29.7 us)

commit v7 on v6

--- a/solution.py
+++ b/solution.py
@@ -8,6 +8,8 @@
 from jax.sharding import PartitionSpec as P
 
 MIB = 1024 * 1024
+FWD = (3, 2)
+BACK = (2, 3)
 
 
 def whole(space=pltpu.VMEM):
@@ -74,11 +76,11 @@
     return (g + 0.95 * (0.95 * m + g)).astype(jnp.bfloat16)
 
 
-def plans(shards):
-    z2 = [(2, u) for u in range(shards)]
-    p31 = [[(3, u), (1, u)] for u in range(shards)]
-    a0 = [(0, u) for u in range(shards)]
-    return [z2], p31, [a0]
+def plans(shards, early_k, late_k):
+    early = [(early_k, u) for u in range(shards)]
+    late = [[(late_k, u), (1, u)] for u in range(shards)]
+    own = [(0, u) for u in range(shards)]
+    return [early], late, [own]
 
 
 def swap_tensor(piece, k):
@@ -112,17 +114,17 @@
     )(*arrays)
 
 
-def exchange(z2, p31, a0, moved):
+def exchange(z2, p31, a0, moved, early_k, late_k):
     shards = len(p31)
-    z2 = swap_tensor(z2, 2)
+    z2 = swap_tensor(z2, early_k)
     p31 = [p31[0]] + [swap_shard(p31[u], u) for u in range(1, shards)]
     w3, w1 = regroup(p31, [[(u, i, False, not moved) for u in range(shards)] for i in range(2)])
-    z3 = swap_tensor(w3, 3)
+    z3 = swap_tensor(w3, late_k)
     z1 = swap_tensor(w1, 1)
     p20 = regroup((z2, a0), [[(0, u, moved, False), (1, u, False, False)] for u in range(shards)])
     p20 = [p20[0]] + [swap_shard(p20[u], u) for u in range(1, shards)]
-    outs = {k: [(a, i) for a in p20] for i, k in enumerate((2, 0))}
-    for k, a in ((3, z3), (1, z1)):
+    outs = {k: [(a, i) for a in p20] for i, k in enumerate((early_k, 0))}
+    for k, a in ((late_k, z3), (1, z1)):
         outs[k] = [(a, u) for u in range(shards)] if moved else [(a, None)]
     return outs
 
@@ -337,20 +339,26 @@
     count, rows, cols = grads.shape
     shard_count = lax.axis_size("shard")
     t = lax.axis_index("tensor")
-    z2_plan, p31_plan, a0_plan = plans(shard_count)
-    z2 = nesterov_group(grads, momentum, t ^ 2, shard_count)
+    ks = early_k, late_k = FWD
+    _, p31_plan, a0_plan = plans(shard_count, *ks)
+    z2 = nesterov_group(grads, momentum, t ^ early_k, shard_count)
     z2, grads, momentum = lax.optimization_barrier((z2, grads, momentum))
     p31 = nesterov(grads, momentum, p31_plan, shard_count)
     (a0,) = nesterov(grads, momentum, a0_plan, shard_count)
-    chunks = exchange(z2, p31, a0, True)
+    chunks = exchange(z2, p31, a0, True, *ks)
     momentum_next, token = next_momentum(grads, momentum, chunks[0][0][0])
-    before, part, sums = early({k: chunks[k] for k in (0, 2)})
-    x, g, z2 = first((0, 2), before, part, sums, {k: chunks[k][0][0] for k in (1, 3)}, z2_plan, token)
+    before, part, sums = early({k: chunks[k] for k in (0, early_k)})
+    late = {k: chunks[k][0][0] for k in (1, late_k)}
+    fk = early_k
+
+    ks = early_k, late_k = BACK
+    z2_plan, p31_plan, a0_plan = plans(shard_count, *ks)
+    x, g, z2 = first((0, fk), before, part, sums, late, z2_plan, token)
     p31 = list(last(x, g, p31_plan, rows, cols))
     (a0,) = last(x, g, a0_plan, rows, cols)
-    back = exchange(z2, p31, a0, False)
-    update = place({k: back[k] for k in (0, 2)}, shard_count, grads.shape, None)
-    update = place({k: back[k] for k in (1, 3)}, shard_count, grads.shape, update)
+    back = exchange(z2, p31, a0, False, *ks)
+    update = place({k: back[k] for k in (0, early_k)}, shard_count, grads.shape, None)
+    update = place({k: back[k] for k in (1, late_k)}, shard_count, grads.shape, update)
     return (momentum_next, update)
 
 

time: 110 us -> 109 us (level)
  waiting for transfers between devices: 42.8 us -> 41.4 us
  transfers between devices with their start and end apart: 34 -> 34, of which waited for: 19 -> 18; matrix products, arithmetic and copies ran while one was open for 0% -> 0% of each run, Pallas kernels for 11% -> 11%
where the time goes in v7:
time: 109 us
  starting transfers between devices  41.5 us (38%)
  waiting for transfers between devices  41.4 us (38%)
  Pallas kernels  20.9 us (19%)
  local copies, waits for them, and re-layouts  2.2 us (2%)
  other arithmetic  1.7 us (2%)
    ppermute x28, waiting for transfers between devices, swap_shard(): return lax.ppermute(piece, 'shard', [(s, s ^ u) for s in range(count)])  31.7 us
    ppermute x28, starting transfers between devices, swap_shard(): return lax.ppermute(piece, 'shard', [(s, s ^ u) for s in range(count)])  31 us
    ppermute x6, starting transfers between devices, swap_tensor(): return lax.ppermute(piece, 'tensor', [(t, t ^ k) for t in range(count)])  10.5 us
    ppermute x6, waiting for transfers between devices, swap_tensor(): return lax.ppermute(piece, 'tensor', [(t, t ^ k) for t in range(count)])  9.73 us
    pallas_call x1, Pallas kernels, first(): pl.pallas_call(functools.partial(first_kernel, early_ks, late_ks, plan),...  7.97 us
    pallas_call x2, Pallas kernels, last(): pl.pallas_call(functools.partial(last_kernel, plan), in_specs=[whole()] *...  5.57 us
    pallas_call x1, Pallas kernels, next_momentum(): pl.pallas_call(momentum_kernel, grid=(steps,), in_specs=[spec, spec, whol...  3.56 us
    unnamed x6, local copies, waits for them, and re-layouts  2.2 us
  transfers between devices with their start and end apart: 34, of which 18 were waited for; matrix products, arithmetic and copies ran while one was open for 0% of the time, Pallas kernels for 11%

profile of v7, /device:TPU:0, one launch (start us, length us, event | category | flops | bytes accessed | tf_op | source)
XLA Modules:
  0.0 108.7 jit_solution(1476155538297233878)
XLA Ops:
  0.6 1.7 %fusion.1 = bf16[8,128,256]{2,1,0:T(8,128)(2,1)S(1)} fusion(f32[32,128,256]{2,1,0:T(8,128)} %m_ref.2, s32[]{:T(128)S(6)} %select_n.4, bf16[32,128,256]{2,1,0:T(8,128)(2,1)} %g_ref.2), kind=kLoop, calls=%fused_computation.3 | loop fusion | flops 1572864 | bytes 2097156 | tf_op jit(solution)/shard_map/convert_element_type | solution.py:76
  2.3 5.1 %collective-permute-start = (bf16[8,128,256]{2,1,0:T(8,128)(2,1)S(1)}, bf16[8,128,256]{2,1,0:T(8,128)(2,1)S(1)}, u32[]{:S(2)}, u32[]{:S(2)}) collective-permute-start(bf16[8,128,256]{2,1,0:T(8,128)(2,1)S(1)} %fusion.1), channel_id=1, source_target_pairs={{0,3},{1,2},{2,1},{3,0},{4,7},{5,6},{6,5},{7,4},{8,11},{9,10},{10,... | collective-permute-start | bytes 1572872 | tf_op jit(solution)/shard_map/ppermute | solution.py:88
  7.5 2.2 %copy-done = f32[32,128,256]{2,1,0:T(8,128)S(1)} copy-done((f32[32,128,256]{2,1,0:T(8,128)S(1)}, f32[32,128,256]{2,1,0:T(8,128)}, u32[]{:S(2)}) %copy-start) | copy-done | bytes 4194328
  10.1 1.6 %collective-permute-start.9 = (bf16[2,128,256]{2,1,0:T(8,128)(2,1)S(1)}, bf16[2,128,256]{2,1,0:T(8,128)(2,1)S(1)}, u32[]{:S(2)}, u32[]{:S(2)}) collective-permute-start(bf16[2,128,256]{2,1,0:T(8,128)(2,1)S(1)} %get-tuple-element.66), channel_id=1, source_target_pairs={{0,8},{4,12},{8,0},{12,4},{16,24},{20,28},{24,16},{28,20},{1,9},{5... | collective-permute-start | bytes 393224 | tf_op jit(solution)/shard_map/ppermute | solution.py:93
  13.7 2.8 %collective-permute-done.9.refs_2_ = bf16[2,128,256]{2,1,0:T(8,128)(2,1)S(1)} collective-permute-done((bf16[2,128,256]{2,1,0:T(8,128)(2,1)S(1)}, bf16[2,128,256]{2,1,0:T(8,128)(2,1)S(1)}, u32[]{:S(2)}, u32[]{:S(2)}) %collective-permute-start.9) | collective-permute-done | bytes 131104 | tf_op jit(solution)/shard_map/ppermute | solution.py:93
  16.5 2.4 %collective-permute-start.13 = (bf16[2,128,256]{2,1,0:T(8,128)(2,1)S(1)}, bf16[2,128,256]{2,1,0:T(8,128)(2,1)S(1)}, u32[]{:S(2)}, u32[]{:S(2)}) collective-permute-start(bf16[2,128,256]{2,1,0:T(8,128)(2,1)S(1)} %get-tuple-element.70), channel_id=1, source_target_pairs={{0,24},{4,28},{8,16},{12,20},{16,8},{20,12},{24,0},{28,4},{1,25},{... | collective-permute-start | bytes 393224 | tf_op jit(solution)/shard_map/ppermute | solution.py:93
  18.9 2.5 %collective-permute-start.14 = (bf16[2,128,256]{2,1,0:T(8,128)(2,1)S(1)}, bf16[2,128,256]{2,1,0:T(8,128)(2,1)S(1)}, u32[]{:S(2)}, u32[]{:S(2)}) collective-permute-start(bf16[2,128,256]{2,1,0:T(8,128)(2,1)S(1)} %get-tuple-element.71), channel_id=1, source_target_pairs={{0,28},{4,24},{8,20},{12,16},{16,12},{20,8},{24,4},{28,0},{1,29},{... | collective-permute-start | bytes 393224 | tf_op jit(solution)/shard_map/ppermute | solution.py:93
  21.5 3.7 %collective-permute-done.12.refs_5_ = bf16[2,128,256]{2,1,0:T(8,128)(2,1)S(1)} collective-permute-done((bf16[2,128,256]{2,1,0:T(8,128)(2,1)S(1)}, bf16[2,128,256]{2,1,0:T(8,128)(2,1)S(1)}, u32[]{:S(2)}, u32[]{:S(2)}) %collective-permute-start.12) | collective-permute-done | bytes 131104 | tf_op jit(solution)/shard_map/ppermute | solution.py:93
  26.8 1.7 %collective-permute-start.2 = (bf16[2,128,256]{2,1,0:T(8,128)(2,1)S(1)}, bf16[2,128,256]{2,1,0:T(8,128)(2,1)S(1)}, u32[]{:S(2)}, u32[]{:S(2)}) collective-permute-start(bf16[2,128,256]{2,1,0:T(8,128)(2,1)S(1)} %get-tuple-element.55), channel_id=1, source_target_pairs={{0,8},{4,12},{8,0},{12,4},{16,24},{20,28},{24,16},{28,20},{1,9},{5... | collective-permute-start | bytes 393224 | tf_op jit(solution)/shard_map/ppermute | solution.py:93
  28.7 1.7 %collective-permute-start.4 = (bf16[2,128,256]{2,1,0:T(8,128)(2,1)S(1)}, bf16[2,128,256]{2,1,0:T(8,128)(2,1)S(1)}, u32[]{:S(2)}, u32[]{:S(2)}) collective-permute-start(bf16[2,128,256]{2,1,0:T(8,128)(2,1)S(1)} %get-tuple-element.57), channel_id=1, source_target_pairs={{0,16},{4,20},{8,24},{12,28},{16,0},{20,4},{24,8},{28,12},{1,17},{... | collective-permute-start | bytes 393224 | tf_op jit(solution)/shard_map/ppermute | solution.py:93
  30.3 2.8 %collective-permute-done.2.refs_2_ = bf16[2,128,256]{2,1,0:T(8,128)(2,1)S(1)} collective-permute-done((bf16[2,128,256]{2,1,0:T(8,128)(2,1)S(1)}, bf16[2,128,256]{2,1,0:T(8,128)(2,1)S(1)}, u32[]{:S(2)}, u32[]{:S(2)}) %collective-permute-start.2) | collective-permute-done | bytes 131104 | tf_op jit(solution)/shard_map/ppermute | solution.py:93
  35.1 2.6 %collective-permute-start.6 = (bf16[2,128,256]{2,1,0:T(8,128)(2,1)S(1)}, bf16[2,128,256]{2,1,0:T(8,128)(2,1)S(1)}, u32[]{:S(2)}, u32[]{:S(2)}) collective-permute-start(bf16[2,128,256]{2,1,0:T(8,128)(2,1)S(1)} %get-tuple-element.59), channel_id=1, source_target_pairs={{0,24},{4,28},{8,16},{12,20},{16,8},{20,12},{24,0},{28,4},{1,25},{... | collective-permute-start | bytes 393224 | tf_op jit(solution)/shard_map/ppermute | solution.py:93
  37.9 3.6 %shard_map.43 = (f32[32,128,256]{2,1,0:T(8,128)}, f32[8,128]{1,0:T(8,128)S(1)}) custom-call(bf16[32,128,256]{2,1,0:T(8,128)(2,1)S(1)} %copy-done.2, f32[32,128,256]{2,1,0:T(8,128)S(1)} %copy-done.1, bf16[2,128,256]{2,1,0:T(8,128)(2,1)S(1)} %get-tuple-element.52.after_ref.refs_0_), custom_call_target="tpu_custom_call" | custom-call | flops 1000 | bytes 1000 | tf_op jit(solution)/shard_map/pallas_call | solution.py:59
  42.3 2.2 %collective-permute-done.7.refs_7_ = bf16[2,128,256]{2,1,0:T(8,128)(2,1)S(1)} collective-permute-done((bf16[2,128,256]{2,1,0:T(8,128)(2,1)S(1)}, bf16[2,128,256]{2,1,0:T(8,128)(2,1)S(1)}, u32[]{:S(2)}, u32[]{:S(2)}) %collective-permute-start.7) | collective-permute-done | bytes 131104 | tf_op jit(solution)/shard_map/ppermute | solution.py:93
  45.3 4.0 %collective-permute-done.15.refs_3_ = bf16[8,128,256]{2,1,0:T(8,128)(2,1)S(1)} collective-permute-done((bf16[8,128,256]{2,1,0:T(8,128)(2,1)S(1)}, bf16[8,128,256]{2,1,0:T(8,128)(2,1)S(1)}, u32[]{:S(2)}, u32[]{:S(2)}) %collective-permute-start.15) | collective-permute-done | bytes 524320 | tf_op jit(solution)/shard_map/ppermute | solution.py:88
  49.3 2.9 %collective-permute-done.16.refs_4_ = bf16[8,128,256]{2,1,0:T(8,128)(2,1)S(1)} collective-permute-done((bf16[8,128,256]{2,1,0:T(8,128)(2,1)S(1)}, bf16[8,128,256]{2,1,0:T(8,128)(2,1)S(1)}, u32[]{:S(2)}, u32[]{:S(2)}) %collective-permute-start.16) | collective-permute-done | bytes 524320 | tf_op jit(solution)/shard_map/ppermute | solution.py:88
  52.3 8.0 %shard_map.47 = (bf16[1024,1024]{1,0:T(8,128)(2,1)S(1)}, bf16[1024,1024]{1,0:T(8,128)(2,1)S(1)}, bf16[8,128,256]{2,1,0:T(8,128)(2,1)S(1)}) custom-call(bf16[1024,512]{1,0:T(8,128)(2,1)S(1)} %get-tuple-element.61.refs_0_, f32[1024,1024]{1,0:T(8,128)S(1)} %get-tuple-element.62.refs_1_, f32[8,512]{1,0:T(8,128)S(1)} %get-tuple-element.63.refs_2_, ...), custom_call_target="tpu_custom_call" | custom-call | flops 7516192768 | bytes 12582912 | tf_op jit(solution)/shard_map/pallas_call | solution.py:271
  60.5 3.3 %shard_map.48 = (bf16[2,128,256]{2,1,0:T(8,128)(2,1)S(1)}, bf16[2,128,256]{2,1,0:T(8,128)(2,1)S(1)}, bf16[2,128,256]{2,1,0:T(8,128)(2,1)S(1)}, bf16[2,128,256]{2...) custom-call(bf16[1024,1024]{1,0:T(8,128)(2,1)S(1)} %get-tuple-elemen, ...), custom_call_target="tpu_custom_call" | custom-call | flops 2147483648 | bytes 8388608 | tf_op jit(solution)/shard_map/pallas_call | solution.py:295
  63.9 1.6 %collective-permute-start.18 = (bf16[2,128,256]{2,1,0:T(8,128)(2,1)S(1)}, bf16[2,128,256]{2,1,0:T(8,128)(2,1)S(1)}, u32[]{:S(2)}, u32[]{:S(2)}) collective-permute-start(bf16[2,128,256]{2,1,0:T(8,128)(2,1)S(1)} %get-tuple-element.79), channel_id=1, source_target_pairs={{0,8},{4,12},{8,0},{12,4},{16,24},{20,28},{24,16},{28,20},{1,9},{5... | collective-permute-start | bytes 393224 | tf_op jit(solution)/shard_map/ppermute | solution.py:93
  67.5 2.8 %collective-permute-done.18.refs_2_ = bf16[2,128,256]{2,1,0:T(8,128)(2,1)S(1)} collective-permute-done((bf16[2,128,256]{2,1,0:T(8,128)(2,1)S(1)}, bf16[2,128,256]{2,1,0:T(8,128)(2,1)S(1)}, u32[]{:S(2)}, u32[]{:S(2)}) %collective-permute-start.18) | collective-permute-done | bytes 131104 | tf_op jit(solution)/shard_map/ppermute | solution.py:93
  70.3 2.4 %collective-permute-start.22 = (bf16[2,128,256]{2,1,0:T(8,128)(2,1)S(1)}, bf16[2,128,256]{2,1,0:T(8,128)(2,1)S(1)}, u32[]{:S(2)}, u32[]{:S(2)}) collective-permute-start(bf16[2,128,256]{2,1,0:T(8,128)(2,1)S(1)} %get-tuple-element.83), channel_id=1, source_target_pairs={{0,24},{4,28},{8,16},{12,20},{16,8},{20,12},{24,0},{28,4},{1,25},{... | collective-permute-start | bytes 393224 | tf_op jit(solution)/shard_map/ppermute | solution.py:93
  72.7 2.5 %collective-permute-start.23 = (bf16[2,128,256]{2,1,0:T(8,128)(2,1)S(1)}, bf16[2,128,256]{2,1,0:T(8,128)(2,1)S(1)}, u32[]{:S(2)}, u32[]{:S(2)}) collective-permute-start(bf16[2,128,256]{2,1,0:T(8,128)(2,1)S(1)} %get-tuple-element.84), channel_id=1, source_target_pairs={{0,28},{4,24},{8,20},{12,16},{16,12},{20,8},{24,4},{28,0},{1,29},{... | collective-permute-start | bytes 393224 | tf_op jit(solution)/shard_map/ppermute | solution.py:93
  75.3 3.7 %collective-permute-done.21.refs_5_ = bf16[2,128,256]{2,1,0:T(8,128)(2,1)S(1)} collective-permute-done((bf16[2,128,256]{2,1,0:T(8,128)(2,1)S(1)}, bf16[2,128,256]{2,1,0:T(8,128)(2,1)S(1)}, u32[]{:S(2)}, u32[]{:S(2)}) %collective-permute-start.21) | collective-permute-done | bytes 131104 | tf_op jit(solution)/shard_map/ppermute | solution.py:93
  79.4 2.9 %collective-permute-start.24 = (bf16[8,128,256]{2,1,0:T(8,128)(2,1)S(1)}, bf16[8,128,256]{2,1,0:T(8,128)(2,1)S(1)}, u32[]{:S(2)}, u32[]{:S(2)}) collective-permute-start(bf16[8,128,256]{2,1,0:T(8,128)(2,1)S(1)} %get-tuple-element.85), channel_id=1, source_target_pairs={{0,1},{1,0},{2,3},{3,2},{4,5},{5,4},{6,7},{7,6},{8,9},{9,8},{10,11... | collective-permute-start | bytes 1572872 | tf_op jit(solution)/shard_map/ppermute | solution.py:88
  83.6 2.2 %shard_map.50.refs_1_ = bf16[8,128,256]{2,1,0:T(8,128)(2,1)S(1)} custom-call(bf16[1024,1024]{1,0:T(8,128)(2,1)S(1)} %get-tuple-element.75.x_ref, bf16[1024,1024]{1,0:T(8,128)(2,1)S(1)} %get-tuple-element.76.g_ref), custom_call_target="tpu_custom_call" | custom-call | flops 1073741824 | bytes 8388608 | tf_op jit(solution)/shard_map/pallas_call | solution.py:295
  86.1 1.7 %collective-permute-start.28 = (bf16[2,128,256]{2,1,0:T(8,128)(2,1)S(1)}, bf16[2,128,256]{2,1,0:T(8,128)(2,1)S(1)}, u32[]{:S(2)}, u32[]{:S(2)}) collective-permute-start(bf16[2,128,256]{2,1,0:T(8,128)(2,1)S(1)} %get-tuple-element.90), channel_id=1, source_target_pairs={{0,8},{4,12},{8,0},{12,4},{16,24},{20,28},{24,16},{28,20},{1,9},{5... | collective-permute-start | bytes 393224 | tf_op jit(solution)/shard_map/ppermute | solution.py:93
  87.9 1.7 %collective-permute-start.30 = (bf16[2,128,256]{2,1,0:T(8,128)(2,1)S(1)}, bf16[2,128,256]{2,1,0:T(8,128)(2,1)S(1)}, u32[]{:S(2)}, u32[]{:S(2)}) collective-permute-start(bf16[2,128,256]{2,1,0:T(8,128)(2,1)S(1)} %get-tuple-element.92), channel_id=1, source_target_pairs={{0,16},{4,20},{8,24},{12,28},{16,0},{20,4},{24,8},{28,12},{1,17},{... | collective-permute-start | bytes 393224 | tf_op jit(solution)/shard_map/ppermute | solution.py:93
  89.6 2.8 %collective-permute-done.28.refs_2_ = bf16[2,128,256]{2,1,0:T(8,128)(2,1)S(1)} collective-permute-done((bf16[2,128,256]{2,1,0:T(8,128)(2,1)S(1)}, bf16[2,128,256]{2,1,0:T(8,128)(2,1)S(1)}, u32[]{:S(2)}, u32[]{:S(2)}) %collective-permute-start.28) | collective-permute-done | bytes 131104 | tf_op jit(solution)/shard_map/ppermute | solution.py:93
  94.3 2.6 %collective-permute-start.32 = (bf16[2,128,256]{2,1,0:T(8,128)(2,1)S(1)}, bf16[2,128,256]{2,1,0:T(8,128)(2,1)S(1)}, u32[]{:S(2)}, u32[]{:S(2)}) collective-permute-start(bf16[2,128,256]{2,1,0:T(8,128)(2,1)S(1)} %get-tuple-element.94), channel_id=1, source_target_pairs={{0,24},{4,28},{8,16},{12,20},{16,8},{20,12},{24,0},{28,4},{1,25},{... | collective-permute-start | bytes 393224 | tf_op jit(solution)/shard_map/ppermute | solution.py:93
  98.0 3.5 %collective-permute-done.32.refs_6_ = bf16[2,128,256]{2,1,0:T(8,128)(2,1)S(1)} collective-permute-done((bf16[2,128,256]{2,1,0:T(8,128)(2,1)S(1)}, bf16[2,128,256]{2,1,0:T(8,128)(2,1)S(1)}, u32[]{:S(2)}, u32[]{:S(2)}) %collective-permute-start.32) | collective-permute-done | bytes 131104 | tf_op jit(solution)/shard_map/ppermute | solution.py:93
  101.5 2.2 %collective-permute-done.33.refs_7_ = bf16[2,128,256]{2,1,0:T(8,128)(2,1)S(1)} collective-permute-done((bf16[2,128,256]{2,1,0:T(8,128)(2,1)S(1)}, bf16[2,128,256]{2,1,0:T(8,128)(2,1)S(1)}, u32[]{:S(2)}, u32[]{:S(2)}) %collective-permute-start.33) | collective-permute-done | bytes 131104 | tf_op jit(solution)/shard_map/ppermute | solution.py:93
  104.8 2.8 %collective-permute-done.24.refs_0_ = bf16[8,128,256]{2,1,0:T(8,128)(2,1)S(1)} collective-permute-done((bf16[8,128,256]{2,1,0:T(8,128)(2,1)S(1)}, bf16[8,128,256]{2,1,0:T(8,128)(2,1)S(1)}, u32[]{:S(2)}, u32[]{:S(2)}) %collective-permute-start.24) | collective-permute-done | bytes 524320 | tf_op jit(solution)/shard_map/ppermute | solution.py:88
  (56 shorter events, 17.4 us)
Async XLA Ops:
  2.3 24.3 %collective-permute-start = (bf16[8,128,256]{2,1,0:T(8,128)(2,1)S(1)}, bf16[8,128,256]{2,1,0:T(8,128)(2,1)S(1)}, u32[]{:S(2)}, u32[]{:S(2)}) collective-permute-start(bf16[8,128,256]{2,1,0:T(8,128)(2,1)S(1)} %fusion.1), channel_id=1, source_target_pairs={{0,3},{1,2},{2,1},{3,0},{4,7},{5,6},{6,5},{7,4},{8,11},{9,10},{10,... | collective-permute-start | bytes 1572872 | tf_op jit(solution)/shard_map/ppermute | solution.py:88
  10.0 3.5 %collective-permute-start.8 = (bf16[2,128,256]{2,1,0:T(8,128)(2,1)S(1)}, bf16[2,128,256]{2,1,0:T(8,128)(2,1)S(1)}, u32[]{:S(2)}, u32[]{:S(2)}) collective-permute-start(bf16[2,128,256]{2,1,0:T(8,128)(2,1)S(1)} %get-tuple-element.65), channel_id=1, source_target_pairs={{0,4},{4,0},{8,12},{12,8},{16,20},{20,16},{24,28},{28,24},{1,5},{5... | collective-permute-start | bytes 393224 | tf_op jit(solution)/shard_map/ppermute | solution.py:93
  10.1 6.4 %collective-permute-start.9 = (bf16[2,128,256]{2,1,0:T(8,128)(2,1)S(1)}, bf16[2,128,256]{2,1,0:T(8,128)(2,1)S(1)}, u32[]{:S(2)}, u32[]{:S(2)}) collective-permute-start(bf16[2,128,256]{2,1,0:T(8,128)(2,1)S(1)} %get-tuple-element.66), channel_id=1, source_target_pairs={{0,8},{4,12},{8,0},{12,4},{16,24},{20,28},{24,16},{28,20},{1,9},{5... | collective-permute-start | bytes 393224 | tf_op jit(solution)/shard_map/ppermute | solution.py:93
  11.7 7.3 %collective-permute-start.10 = (bf16[2,128,256]{2,1,0:T(8,128)(2,1)S(1)}, bf16[2,128,256]{2,1,0:T(8,128)(2,1)S(1)}, u32[]{:S(2)}, u32[]{:S(2)}) collective-permute-start(bf16[2,128,256]{2,1,0:T(8,128)(2,1)S(1)} %get-tuple-element.67), channel_id=1, source_target_pairs={{0,12},{4,8},{8,4},{12,0},{16,28},{20,24},{24,20},{28,16},{1,13},{... | collective-permute-start | bytes 393224 | tf_op jit(solution)/shard_map/ppermute | solution.py:93
  12.0 9.5 %collective-permute-start.11 = (bf16[2,128,256]{2,1,0:T(8,128)(2,1)S(1)}, bf16[2,128,256]{2,1,0:T(8,128)(2,1)S(1)}, u32[]{:S(2)}, u32[]{:S(2)}) collective-permute-start(bf16[2,128,256]{2,1,0:T(8,128)(2,1)S(1)} %get-tuple-element.68), channel_id=1, source_target_pairs={{0,16},{4,20},{8,24},{12,28},{16,0},{20,4},{24,8},{28,12},{1,17},{... | collective-permute-start | bytes 393224 | tf_op jit(solution)/shard_map/ppermute | solution.py:93
  13.5 11.7 %collective-permute-start.12 = (bf16[2,128,256]{2,1,0:T(8,128)(2,1)S(1)}, bf16[2,128,256]{2,1,0:T(8,128)(2,1)S(1)}, u32[]{:S(2)}, u32[]{:S(2)}) collective-permute-start(bf16[2,128,256]{2,1,0:T(8,128)(2,1)S(1)} %get-tuple-element.69), channel_id=1, source_target_pairs={{0,20},{4,16},{8,28},{12,24},{16,4},{20,0},{24,12},{28,8},{1,21},{... | collective-permute-start | bytes 393224 | tf_op jit(solution)/shard_map/ppermute | solution.py:93
  16.5 8.7 %collective-permute-start.13 = (bf16[2,128,256]{2,1,0:T(8,128)(2,1)S(1)}, bf16[2,128,256]{2,1,0:T(8,128)(2,1)S(1)}, u32[]{:S(2)}, u32[]{:S(2)}) collective-permute-start(bf16[2,128,256]{2,1,0:T(8,128)(2,1)S(1)} %get-tuple-element.70), channel_id=1, source_target_pairs={{0,24},{4,28},{8,16},{12,20},{16,8},{20,12},{24,0},{28,4},{1,25},{... | collective-permute-start | bytes 393224 | tf_op jit(solution)/shard_map/ppermute | solution.py:93
  18.9 6.5 %collective-permute-start.14 = (bf16[2,128,256]{2,1,0:T(8,128)(2,1)S(1)}, bf16[2,128,256]{2,1,0:T(8,128)(2,1)S(1)}, u32[]{:S(2)}, u32[]{:S(2)}) collective-permute-start(bf16[2,128,256]{2,1,0:T(8,128)(2,1)S(1)} %get-tuple-element.71), channel_id=1, source_target_pairs={{0,28},{4,24},{8,20},{12,16},{16,12},{20,8},{24,4},{28,0},{1,29},{... | collective-permute-start | bytes 393224 | tf_op jit(solution)/shard_map/ppermute | solution.py:93
  25.5 23.8 %collective-permute-start.15 = (bf16[8,128,256]{2,1,0:T(8,128)(2,1)S(1)}, bf16[8,128,256]{2,1,0:T(8,128)(2,1)S(1)}, u32[]{:S(2)}, u32[]{:S(2)}) collective-permute-start(bf16[8,128,256]{2,1,0:T(8,128)(2,1)S(1)} %get-tuple-element.72), channel_id=1, source_target_pairs={{0,1},{1,0},{2,3},{3,2},{4,5},{5,4},{6,7},{7,6},{8,9},{9,8},{10,11... | collective-permute-start | bytes 1572872 | tf_op jit(solution)/shard_map/ppermute | solution.py:88
  25.6 26.7 %collective-permute-start.16 = (bf16[8,128,256]{2,1,0:T(8,128)(2,1)S(1)}, bf16[8,128,256]{2,1,0:T(8,128)(2,1)S(1)}, u32[]{:S(2)}, u32[]{:S(2)}) collective-permute-start(bf16[8,128,256]{2,1,0:T(8,128)(2,1)S(1)} %get-tuple-element.73), channel_id=1, source_target_pairs={{0,2},{1,3},{2,0},{3,1},{4,6},{5,7},{6,4},{7,5},{8,10},{9,11},{10,... | collective-permute-start | bytes 1572872 | tf_op jit(solution)/shard_map/ppermute | solution.py:88
  26.8 6.4 %collective-permute-start.2 = (bf16[2,128,256]{2,1,0:T(8,128)(2,1)S(1)}, bf16[2,128,256]{2,1,0:T(8,128)(2,1)S(1)}, u32[]{:S(2)}, u32[]{:S(2)}) collective-permute-start(bf16[2,128,256]{2,1,0:T(8,128)(2,1)S(1)} %get-tuple-element.55), channel_id=1, source_target_pairs={{0,8},{4,12},{8,0},{12,4},{16,24},{20,28},{24,16},{28,20},{1,9},{5... | collective-permute-start | bytes 393224 | tf_op jit(solution)/shard_map/ppermute | solution.py:93
  28.5 6.6 %collective-permute-start.3 = (bf16[2,128,256]{2,1,0:T(8,128)(2,1)S(1)}, bf16[2,128,256]{2,1,0:T(8,128)(2,1)S(1)}, u32[]{:S(2)}, u32[]{:S(2)}) collective-permute-start(bf16[2,128,256]{2,1,0:T(8,128)(2,1)S(1)} %get-tuple-element.56), channel_id=1, source_target_pairs={{0,12},{4,8},{8,4},{12,0},{16,28},{20,24},{24,20},{28,16},{1,13},{... | collective-permute-start | bytes 393224 | tf_op jit(solution)/shard_map/ppermute | solution.py:93
  28.7 9.0 %collective-permute-start.4 = (bf16[2,128,256]{2,1,0:T(8,128)(2,1)S(1)}, bf16[2,128,256]{2,1,0:T(8,128)(2,1)S(1)}, u32[]{:S(2)}, u32[]{:S(2)}) collective-permute-start(bf16[2,128,256]{2,1,0:T(8,128)(2,1)S(1)} %get-tuple-element.57), channel_id=1, source_target_pairs={{0,16},{4,20},{8,24},{12,28},{16,0},{20,4},{24,8},{28,12},{1,17},{... | collective-permute-start | bytes 393224 | tf_op jit(solution)/shard_map/ppermute | solution.py:93
  33.2 8.3 %collective-permute-start.5 = (bf16[2,128,256]{2,1,0:T(8,128)(2,1)S(1)}, bf16[2,128,256]{2,1,0:T(8,128)(2,1)S(1)}, u32[]{:S(2)}, u32[]{:S(2)}) collective-permute-start(bf16[2,128,256]{2,1,0:T(8,128)(2,1)S(1)} %get-tuple-element.58), channel_id=1, source_target_pairs={{0,20},{4,16},{8,28},{12,24},{16,4},{20,0},{24,12},{28,8},{1,21},{... | collective-permute-start | bytes 393224 | tf_op jit(solution)/shard_map/ppermute | solution.py:93
  35.1 7.2 %collective-permute-start.6 = (bf16[2,128,256]{2,1,0:T(8,128)(2,1)S(1)}, bf16[2,128,256]{2,1,0:T(8,128)(2,1)S(1)}, u32[]{:S(2)}, u32[]{:S(2)}) collective-permute-start(bf16[2,128,256]{2,1,0:T(8,128)(2,1)S(1)} %get-tuple-element.59), channel_id=1, source_target_pairs={{0,24},{4,28},{8,16},{12,20},{16,8},{20,12},{24,0},{28,4},{1,25},{... | collective-permute-start | bytes 393224 | tf_op jit(solution)/shard_map/ppermute | solution.py:93
  37.7 6.8 %collective-permute-start.7 = (bf16[2,128,256]{2,1,0:T(8,128)(2,1)S(1)}, bf16[2,128,256]{2,1,0:T(8,128)(2,1)S(1)}, u32[]{:S(2)}, u32[]{:S(2)}) collective-permute-start(bf16[2,128,256]{2,1,0:T(8,128)(2,1)S(1)} %get-tuple-element.60), channel_id=1, source_target_pairs={{0,28},{4,24},{8,20},{12,16},{16,12},{20,8},{24,4},{28,0},{1,29},{... | collective-permute-start | bytes 393224 | tf_op jit(solution)/shard_map/ppermute | solution.py:93
  60.3 25.6 %collective-permute-start.26 = (bf16[8,128,256]{2,1,0:T(8,128)(2,1)S(1)}, bf16[8,128,256]{2,1,0:T(8,128)(2,1)S(1)}, u32[]{:S(2)}, u32[]{:S(2)}) collective-permute-start(bf16[8,128,256]{2,1,0:T(8,128)(2,1)S(1)} %get-tuple-element.87), channel_id=1, source_target_pairs={{0,2},{1,3},{2,0},{3,1},{4,6},{5,7},{6,4},{7,5},{8,10},{9,11},{10,... | collective-permute-start | bytes 1572872 | tf_op jit(solution)/shard_map/ppermute | solution.py:88
  63.9 3.5 %collective-permute-start.17 = (bf16[2,128,256]{2,1,0:T(8,128)(2,1)S(1)}, bf16[2,128,256]{2,1,0:T(8,128)(2,1)S(1)}, u32[]{:S(2)}, u32[]{:S(2)}) collective-permute-start(bf16[2,128,256]{2,1,0:T(8,128)(2,1)S(1)} %get-tuple-element.78), channel_id=1, source_target_pairs={{0,4},{4,0},{8,12},{12,8},{16,20},{20,16},{24,28},{28,24},{1,5},{5... | collective-permute-start | bytes 393224 | tf_op jit(solution)/shard_map/ppermute | solution.py:93
  63.9 6.4 %collective-permute-start.18 = (bf16[2,128,256]{2,1,0:T(8,128)(2,1)S(1)}, bf16[2,128,256]{2,1,0:T(8,128)(2,1)S(1)}, u32[]{:S(2)}, u32[]{:S(2)}) collective-permute-start(bf16[2,128,256]{2,1,0:T(8,128)(2,1)S(1)} %get-tuple-element.79), channel_id=1, source_target_pairs={{0,8},{4,12},{8,0},{12,4},{16,24},{20,28},{24,16},{28,20},{1,9},{5... | collective-permute-start | bytes 393224 | tf_op jit(solution)/shard_map/ppermute | solution.py:93
  65.5 7.3 %collective-permute-start.19 = (bf16[2,128,256]{2,1,0:T(8,128)(2,1)S(1)}, bf16[2,128,256]{2,1,0:T(8,128)(2,1)S(1)}, u32[]{:S(2)}, u32[]{:S(2)}) collective-permute-start(bf16[2,128,256]{2,1,0:T(8,128)(2,1)S(1)} %get-tuple-element.80), channel_id=1, source_target_pairs={{0,12},{4,8},{8,4},{12,0},{16,28},{20,24},{24,20},{28,16},{1,13},{... | collective-permute-start | bytes 393224 | tf_op jit(solution)/shard_map/ppermute | solution.py:93
  65.8 9.5 %collective-permute-start.20 = (bf16[2,128,256]{2,1,0:T(8,128)(2,1)S(1)}, bf16[2,128,256]{2,1,0:T(8,128)(2,1)S(1)}, u32[]{:S(2)}, u32[]{:S(2)}) collective-permute-start(bf16[2,128,256]{2,1,0:T(8,128)(2,1)S(1)} %get-tuple-element.81), channel_id=1, source_target_pairs={{0,16},{4,20},{8,24},{12,28},{16,0},{20,4},{24,8},{28,12},{1,17},{... | collective-permute-start | bytes 393224 | tf_op jit(solution)/shard_map/ppermute | solution.py:93
  67.3 11.7 %collective-permute-start.21 = (bf16[2,128,256]{2,1,0:T(8,128)(2,1)S(1)}, bf16[2,128,256]{2,1,0:T(8,128)(2,1)S(1)}, u32[]{:S(2)}, u32[]{:S(2)}) collective-permute-start(bf16[2,128,256]{2,1,0:T(8,128)(2,1)S(1)} %get-tuple-element.82), channel_id=1, source_target_pairs={{0,20},{4,16},{8,28},{12,24},{16,4},{20,0},{24,12},{28,8},{1,21},{... | collective-permute-start | bytes 393224 | tf_op jit(solution)/shard_map/ppermute | solution.py:93
  70.3 8.7 %collective-permute-start.22 = (bf16[2,128,256]{2,1,0:T(8,128)(2,1)S(1)}, bf16[2,128,256]{2,1,0:T(8,128)(2,1)S(1)}, u32[]{:S(2)}, u32[]{:S(2)}) collective-permute-start(bf16[2,128,256]{2,1,0:T(8,128)(2,1)S(1)} %get-tuple-element.83), channel_id=1, source_target_pairs={{0,24},{4,28},{8,16},{12,20},{16,8},{20,12},{24,0},{28,4},{1,25},{... | collective-permute-start | bytes 393224 | tf_op jit(solution)/shard_map/ppermute | solution.py:93
  72.7 6.5 %collective-permute-start.23 = (bf16[2,128,256]{2,1,0:T(8,128)(2,1)S(1)}, bf16[2,128,256]{2,1,0:T(8,128)(2,1)S(1)}, u32[]{:S(2)}, u32[]{:S(2)}) collective-permute-start(bf16[2,128,256]{2,1,0:T(8,128)(2,1)S(1)} %get-tuple-element.84), channel_id=1, source_target_pairs={{0,28},{4,24},{8,20},{12,16},{16,12},{20,8},{24,4},{28,0},{1,29},{... | collective-permute-start | bytes 393224 | tf_op jit(solution)/shard_map/ppermute | solution.py:93
  79.4 28.2 %collective-permute-start.24 = (bf16[8,128,256]{2,1,0:T(8,128)(2,1)S(1)}, bf16[8,128,256]{2,1,0:T(8,128)(2,1)S(1)}, u32[]{:S(2)}, u32[]{:S(2)}) collective-permute-start(bf16[8,128,256]{2,1,0:T(8,128)(2,1)S(1)} %get-tuple-element.85), channel_id=1, source_target_pairs={{0,1},{1,0},{2,3},{3,2},{4,5},{5,4},{6,7},{7,6},{8,9},{9,8},{10,11... | collective-permute-start | bytes 1572872 | tf_op jit(solution)/shard_map/ppermute | solution.py:88
  82.3 25.3 %collective-permute-start.25 = (bf16[8,128,256]{2,1,0:T(8,128)(2,1)S(1)}, bf16[8,128,256]{2,1,0:T(8,128)(2,1)S(1)}, u32[]{:S(2)}, u32[]{:S(2)}) collective-permute-start(bf16[8,128,256]{2,1,0:T(8,128)(2,1)S(1)} %get-tuple-element.86), channel_id=1, source_target_pairs={{0,3},{1,2},{2,1},{3,0},{4,7},{5,6},{6,5},{7,4},{8,11},{9,10},{10,... | collective-permute-start | bytes 1572872 | tf_op jit(solution)/shard_map/ppermute | solution.py:88
  86.1 6.4 %collective-permute-start.28 = (bf16[2,128,256]{2,1,0:T(8,128)(2,1)S(1)}, bf16[2,128,256]{2,1,0:T(8,128)(2,1)S(1)}, u32[]{:S(2)}, u32[]{:S(2)}) collective-permute-start(bf16[2,128,256]{2,1,0:T(8,128)(2,1)S(1)} %get-tuple-element.90), channel_id=1, source_target_pairs={{0,8},{4,12},{8,0},{12,4},{16,24},{20,28},{24,16},{28,20},{1,9},{5... | collective-permute-start | bytes 393224 | tf_op jit(solution)/shard_map/ppermute | solution.py:93
  87.8 6.6 %collective-permute-start.29 = (bf16[2,128,256]{2,1,0:T(8,128)(2,1)S(1)}, bf16[2,128,256]{2,1,0:T(8,128)(2,1)S(1)}, u32[]{:S(2)}, u32[]{:S(2)}) collective-permute-start(bf16[2,128,256]{2,1,0:T(8,128)(2,1)S(1)} %get-tuple-element.91), channel_id=1, source_target_pairs={{0,12},{4,8},{8,4},{12,0},{16,28},{20,24},{24,20},{28,16},{1,13},{... | collective-permute-start | bytes 393224 | tf_op jit(solution)/shard_map/ppermute | solution.py:93
  87.9 9.0 %collective-permute-start.30 = (bf16[2,128,256]{2,1,0:T(8,128)(2,1)S(1)}, bf16[2,128,256]{2,1,0:T(8,128)(2,1)S(1)}, u32[]{:S(2)}, u32[]{:S(2)}) collective-permute-start(bf16[2,128,256]{2,1,0:T(8,128)(2,1)S(1)} %get-tuple-element.92), channel_id=1, source_target_pairs={{0,16},{4,20},{8,24},{12,28},{16,0},{20,4},{24,8},{28,12},{1,17},{... | collective-permute-start | bytes 393224 | tf_op jit(solution)/shard_map/ppermute | solution.py:93
  92.4 5.6 %collective-permute-start.31 = (bf16[2,128,256]{2,1,0:T(8,128)(2,1)S(1)}, bf16[2,128,256]{2,1,0:T(8,128)(2,1)S(1)}, u32[]{:S(2)}, u32[]{:S(2)}) collective-permute-start(bf16[2,128,256]{2,1,0:T(8,128)(2,1)S(1)} %get-tuple-element.93), channel_id=1, source_target_pairs={{0,20},{4,16},{8,28},{12,24},{16,4},{20,0},{24,12},{28,8},{1,21},{... | collective-permute-start | bytes 393224 | tf_op jit(solution)/shard_map/ppermute | solution.py:93
  94.3 7.2 %collective-permute-start.32 = (bf16[2,128,256]{2,1,0:T(8,128)(2,1)S(1)}, bf16[2,128,256]{2,1,0:T(8,128)(2,1)S(1)}, u32[]{:S(2)}, u32[]{:S(2)}) collective-permute-start(bf16[2,128,256]{2,1,0:T(8,128)(2,1)S(1)} %get-tuple-element.94), channel_id=1, source_target_pairs={{0,24},{4,28},{8,16},{12,20},{16,8},{20,12},{24,0},{28,4},{1,25},{... | collective-permute-start | bytes 393224 | tf_op jit(solution)/shard_map/ppermute | solution.py:93
  96.9 6.8 %collective-permute-start.33 = (bf16[2,128,256]{2,1,0:T(8,128)(2,1)S(1)}, bf16[2,128,256]{2,1,0:T(8,128)(2,1)S(1)}, u32[]{:S(2)}, u32[]{:S(2)}) collective-permute-start(bf16[2,128,256]{2,1,0:T(8,128)(2,1)S(1)} %get-tuple-element.95), channel_id=1, source_target_pairs={{0,28},{4,24},{8,20},{12,16},{16,12},{20,8},{24,4},{28,0},{1,29},{... | collective-permute-start | bytes 393224 | tf_op jit(solution)/shard_map/ppermute | solution.py:93
  (5 other events, 29.7 us)

commit v8 on v7

--- a/solution.py
+++ b/solution.py
@@ -71,8 +71,8 @@
 
 
 def nesterov_group(grads, momentum, group, shards):
-    g = lax.dynamic_slice_in_dim(grads, group * shards, shards, 0).astype(jnp.float32)
-    m = lax.dynamic_slice_in_dim(momentum, group * shards, shards, 0)
+    g = lax.dynamic_slice_in_dim(grads, group * shards, shards, 0, allow_negative_indices=False).astype(jnp.float32)
+    m = lax.dynamic_slice_in_dim(momentum, group * shards, shards, 0, allow_negative_indices=False)
     return (g + 0.95 * (0.95 * m + g)).astype(jnp.bfloat16)
 
 
@@ -253,10 +253,11 @@
 
     symmetric(x_ref, g_ref, finish=normalised)
     symmetric(g_ref, w_ref, finish=weights, diagonal=shift)
-    for k in range(order // cols):
-        c = slice(k * cols, (k + 1) * cols)
-        x = (scale * chunk(k).astype(jnp.float32)).astype(jnp.bfloat16)
-        y_ref[:, c] = ((3.4445 - shift) * x.astype(jnp.float32) + mm(w_ref[...], x)).astype(jnp.bfloat16)
+    for ref, ks in ((before_ref, early_ks), (x_ref, late_ks)):
+        x = (scale * ref[...].astype(jnp.float32)).astype(jnp.bfloat16)
+        new = ((3.4445 - shift) * x.astype(jnp.float32) + mm(w_ref[...], x)).astype(jnp.bfloat16)
+        for i, k in enumerate(ks):
+            y_ref[:, k * cols : (k + 1) * cols] = new[:, i * cols : (i + 1) * cols]
     symmetric(y_ref, h_ref)
     for k in sorted({k for pieces in plan for k, _ in pieces}):
         new = step_columns(h_ref, y_ref[:, k * cols : (k + 1) * cols], power_ref)

time: 109 us -> 109 us (level)
  no operation moved by 1% of the time
where the time goes in v8:
time: 109 us
  starting transfers between devices  41.5 us (38%)
  waiting for transfers between devices  41.4 us (38%)
  Pallas kernels  20.9 us (19%)
  local copies, waits for them, and re-layouts  2.2 us (2%)
  other arithmetic  1.7 us (2%)
    ppermute x28, waiting for transfers between devices, swap_shard(): return lax.ppermute(piece, 'shard', [(s, s ^ u) for s in range(count)])  31.7 us
    ppermute x28, starting transfers between devices, swap_shard(): return lax.ppermute(piece, 'shard', [(s, s ^ u) for s in range(count)])  31 us
    ppermute x6, starting transfers between devices, swap_tensor(): return lax.ppermute(piece, 'tensor', [(t, t ^ k) for t in range(count)])  10.5 us
    ppermute x6, waiting for transfers between devices, swap_tensor(): return lax.ppermute(piece, 'tensor', [(t, t ^ k) for t in range(count)])  9.72 us
    pallas_call x1, Pallas kernels, first(): pl.pallas_call(functools.partial(first_kernel, early_ks, late_ks, plan),...  7.97 us
    pallas_call x2, Pallas kernels, last(): pl.pallas_call(functools.partial(last_kernel, plan), in_specs=[whole()] *...  5.57 us
    pallas_call x1, Pallas kernels, next_momentum(): pl.pallas_call(momentum_kernel, grid=(steps,), in_specs=[spec, spec, whol...  3.56 us
    unnamed x6, local copies, waits for them, and re-layouts  2.2 us
  transfers between devices with their start and end apart: 34, of which 18 were waited for; matrix products, arithmetic and copies ran while one was open for 0% of the time, Pallas kernels for 11%

profile of v8, /device:TPU:0, one launch (start us, length us, event | category | flops | bytes accessed | tf_op | source)
XLA Modules:
  0.0 108.7 jit_solution(17250361179542818137)
XLA Ops:
  0.6 1.7 %fusion.1 = bf16[8,128,256]{2,1,0:T(8,128)(2,1)S(1)} fusion(f32[32,128,256]{2,1,0:T(8,128)} %m_ref.2, s32[]{:T(128)S(6)} %mul.10, bf16[32,128,256]{2,1,0:T(8,128)(2,1)} %g_ref.2), kind=kLoop, calls=%fused_computation.3 | loop fusion | flops 1572864 | bytes 2097156 | tf_op jit(solution)/shard_map/convert_element_type | solution.py:76
  2.3 5.1 %collective-permute-start = (bf16[8,128,256]{2,1,0:T(8,128)(2,1)S(1)}, bf16[8,128,256]{2,1,0:T(8,128)(2,1)S(1)}, u32[]{:S(2)}, u32[]{:S(2)}) collective-permute-start(bf16[8,128,256]{2,1,0:T(8,128)(2,1)S(1)} %fusion.1), channel_id=1, source_target_pairs={{0,3},{1,2},{2,1},{3,0},{4,7},{5,6},{6,5},{7,4},{8,11},{9,10},{10,... | collective-permute-start | bytes 1572872 | tf_op jit(solution)/shard_map/ppermute | solution.py:88
  7.5 2.2 %copy-done = f32[32,128,256]{2,1,0:T(8,128)S(1)} copy-done((f32[32,128,256]{2,1,0:T(8,128)S(1)}, f32[32,128,256]{2,1,0:T(8,128)}, u32[]{:S(2)}) %copy-start) | copy-done | bytes 4194328
  10.1 1.6 %collective-permute-start.9 = (bf16[2,128,256]{2,1,0:T(8,128)(2,1)S(1)}, bf16[2,128,256]{2,1,0:T(8,128)(2,1)S(1)}, u32[]{:S(2)}, u32[]{:S(2)}) collective-permute-start(bf16[2,128,256]{2,1,0:T(8,128)(2,1)S(1)} %get-tuple-element.66), channel_id=1, source_target_pairs={{0,8},{4,12},{8,0},{12,4},{16,24},{20,28},{24,16},{28,20},{1,9},{5... | collective-permute-start | bytes 393224 | tf_op jit(solution)/shard_map/ppermute | solution.py:93
  13.7 2.8 %collective-permute-done.9.refs_2_ = bf16[2,128,256]{2,1,0:T(8,128)(2,1)S(1)} collective-permute-done((bf16[2,128,256]{2,1,0:T(8,128)(2,1)S(1)}, bf16[2,128,256]{2,1,0:T(8,128)(2,1)S(1)}, u32[]{:S(2)}, u32[]{:S(2)}) %collective-permute-start.9) | collective-permute-done | bytes 131104 | tf_op jit(solution)/shard_map/ppermute | solution.py:93
  16.5 2.4 %collective-permute-start.13 = (bf16[2,128,256]{2,1,0:T(8,128)(2,1)S(1)}, bf16[2,128,256]{2,1,0:T(8,128)(2,1)S(1)}, u32[]{:S(2)}, u32[]{:S(2)}) collective-permute-start(bf16[2,128,256]{2,1,0:T(8,128)(2,1)S(1)} %get-tuple-element.70), channel_id=1, source_target_pairs={{0,24},{4,28},{8,16},{12,20},{16,8},{20,12},{24,0},{28,4},{1,25},{... | collective-permute-start | bytes 393224 | tf_op jit(solution)/shard_map/ppermute | solution.py:93
  18.9 2.5 %collective-permute-start.14 = (bf16[2,128,256]{2,1,0:T(8,128)(2,1)S(1)}, bf16[2,128,256]{2,1,0:T(8,128)(2,1)S(1)}, u32[]{:S(2)}, u32[]{:S(2)}) collective-permute-start(bf16[2,128,256]{2,1,0:T(8,128)(2,1)S(1)} %get-tuple-element.71), channel_id=1, source_target_pairs={{0,28},{4,24},{8,20},{12,16},{16,12},{20,8},{24,4},{28,0},{1,29},{... | collective-permute-start | bytes 393224 | tf_op jit(solution)/shard_map/ppermute | solution.py:93
  21.5 3.7 %collective-permute-done.12.refs_5_ = bf16[2,128,256]{2,1,0:T(8,128)(2,1)S(1)} collective-permute-done((bf16[2,128,256]{2,1,0:T(8,128)(2,1)S(1)}, bf16[2,128,256]{2,1,0:T(8,128)(2,1)S(1)}, u32[]{:S(2)}, u32[]{:S(2)}) %collective-permute-start.12) | collective-permute-done | bytes 131104 | tf_op jit(solution)/shard_map/ppermute | solution.py:93
  26.8 1.7 %collective-permute-start.2 = (bf16[2,128,256]{2,1,0:T(8,128)(2,1)S(1)}, bf16[2,128,256]{2,1,0:T(8,128)(2,1)S(1)}, u32[]{:S(2)}, u32[]{:S(2)}) collective-permute-start(bf16[2,128,256]{2,1,0:T(8,128)(2,1)S(1)} %get-tuple-element.55), channel_id=1, source_target_pairs={{0,8},{4,12},{8,0},{12,4},{16,24},{20,28},{24,16},{28,20},{1,9},{5... | collective-permute-start | bytes 393224 | tf_op jit(solution)/shard_map/ppermute | solution.py:93
  28.7 1.7 %collective-permute-start.4 = (bf16[2,128,256]{2,1,0:T(8,128)(2,1)S(1)}, bf16[2,128,256]{2,1,0:T(8,128)(2,1)S(1)}, u32[]{:S(2)}, u32[]{:S(2)}) collective-permute-start(bf16[2,128,256]{2,1,0:T(8,128)(2,1)S(1)} %get-tuple-element.57), channel_id=1, source_target_pairs={{0,16},{4,20},{8,24},{12,28},{16,0},{20,4},{24,8},{28,12},{1,17},{... | collective-permute-start | bytes 393224 | tf_op jit(solution)/shard_map/ppermute | solution.py:93
  30.3 2.8 %collective-permute-done.2.refs_2_ = bf16[2,128,256]{2,1,0:T(8,128)(2,1)S(1)} collective-permute-done((bf16[2,128,256]{2,1,0:T(8,128)(2,1)S(1)}, bf16[2,128,256]{2,1,0:T(8,128)(2,1)S(1)}, u32[]{:S(2)}, u32[]{:S(2)}) %collective-permute-start.2) | collective-permute-done | bytes 131104 | tf_op jit(solution)/shard_map/ppermute | solution.py:93
  35.1 2.6 %collective-permute-start.6 = (bf16[2,128,256]{2,1,0:T(8,128)(2,1)S(1)}, bf16[2,128,256]{2,1,0:T(8,128)(2,1)S(1)}, u32[]{:S(2)}, u32[]{:S(2)}) collective-permute-start(bf16[2,128,256]{2,1,0:T(8,128)(2,1)S(1)} %get-tuple-element.59), channel_id=1, source_target_pairs={{0,24},{4,28},{8,16},{12,20},{16,8},{20,12},{24,0},{28,4},{1,25},{... | collective-permute-start | bytes 393224 | tf_op jit(solution)/shard_map/ppermute | solution.py:93
  37.9 3.6 %shard_map.43 = (f32[32,128,256]{2,1,0:T(8,128)}, f32[8,128]{1,0:T(8,128)S(1)}) custom-call(bf16[32,128,256]{2,1,0:T(8,128)(2,1)S(1)} %copy-done.2, f32[32,128,256]{2,1,0:T(8,128)S(1)} %copy-done.1, bf16[2,128,256]{2,1,0:T(8,128)(2,1)S(1)} %get-tuple-element.52.after_ref.refs_0_), custom_call_target="tpu_custom_call" | custom-call | flops 1000 | bytes 1000 | tf_op jit(solution)/shard_map/pallas_call | solution.py:59
  42.3 2.2 %collective-permute-done.7.refs_7_ = bf16[2,128,256]{2,1,0:T(8,128)(2,1)S(1)} collective-permute-done((bf16[2,128,256]{2,1,0:T(8,128)(2,1)S(1)}, bf16[2,128,256]{2,1,0:T(8,128)(2,1)S(1)}, u32[]{:S(2)}, u32[]{:S(2)}) %collective-permute-start.7) | collective-permute-done | bytes 131104 | tf_op jit(solution)/shard_map/ppermute | solution.py:93
  45.3 4.0 %collective-permute-done.15.refs_3_ = bf16[8,128,256]{2,1,0:T(8,128)(2,1)S(1)} collective-permute-done((bf16[8,128,256]{2,1,0:T(8,128)(2,1)S(1)}, bf16[8,128,256]{2,1,0:T(8,128)(2,1)S(1)}, u32[]{:S(2)}, u32[]{:S(2)}) %collective-permute-start.15) | collective-permute-done | bytes 524320 | tf_op jit(solution)/shard_map/ppermute | solution.py:88
  49.3 2.9 %collective-permute-done.16.refs_4_ = bf16[8,128,256]{2,1,0:T(8,128)(2,1)S(1)} collective-permute-done((bf16[8,128,256]{2,1,0:T(8,128)(2,1)S(1)}, bf16[8,128,256]{2,1,0:T(8,128)(2,1)S(1)}, u32[]{:S(2)}, u32[]{:S(2)}) %collective-permute-start.16) | collective-permute-done | bytes 524320 | tf_op jit(solution)/shard_map/ppermute | solution.py:88
  52.3 8.0 %shard_map.47 = (bf16[1024,1024]{1,0:T(8,128)(2,1)S(1)}, bf16[1024,1024]{1,0:T(8,128)(2,1)S(1)}, bf16[8,128,256]{2,1,0:T(8,128)(2,1)S(1)}) custom-call(bf16[1024,512]{1,0:T(8,128)(2,1)S(1)} %get-tuple-element.61.refs_0_, f32[1024,1024]{1,0:T(8,128)S(1)} %get-tuple-element.62.refs_1_, f32[8,512]{1,0:T(8,128)S(1)} %get-tuple-element.63.refs_2_, ...), custom_call_target="tpu_custom_call" | custom-call | flops 7516192768 | bytes 12582912 | tf_op jit(solution)/shard_map/pallas_call | solution.py:272
  60.5 3.3 %shard_map.48 = (bf16[2,128,256]{2,1,0:T(8,128)(2,1)S(1)}, bf16[2,128,256]{2,1,0:T(8,128)(2,1)S(1)}, bf16[2,128,256]{2,1,0:T(8,128)(2,1)S(1)}, bf16[2,128,256]{2...) custom-call(bf16[1024,1024]{1,0:T(8,128)(2,1)S(1)} %get-tuple-elemen, ...), custom_call_target="tpu_custom_call" | custom-call | flops 2147483648 | bytes 8388608 | tf_op jit(solution)/shard_map/pallas_call | solution.py:296
  63.9 1.6 %collective-permute-start.18 = (bf16[2,128,256]{2,1,0:T(8,128)(2,1)S(1)}, bf16[2,128,256]{2,1,0:T(8,128)(2,1)S(1)}, u32[]{:S(2)}, u32[]{:S(2)}) collective-permute-start(bf16[2,128,256]{2,1,0:T(8,128)(2,1)S(1)} %get-tuple-element.79), channel_id=1, source_target_pairs={{0,8},{4,12},{8,0},{12,4},{16,24},{20,28},{24,16},{28,20},{1,9},{5... | collective-permute-start | bytes 393224 | tf_op jit(solution)/shard_map/ppermute | solution.py:93
  67.5 2.8 %collective-permute-done.18.refs_2_ = bf16[2,128,256]{2,1,0:T(8,128)(2,1)S(1)} collective-permute-done((bf16[2,128,256]{2,1,0:T(8,128)(2,1)S(1)}, bf16[2,128,256]{2,1,0:T(8,128)(2,1)S(1)}, u32[]{:S(2)}, u32[]{:S(2)}) %collective-permute-start.18) | collective-permute-done | bytes 131104 | tf_op jit(solution)/shard_map/ppermute | solution.py:93
  70.3 2.5 %collective-permute-start.22 = (bf16[2,128,256]{2,1,0:T(8,128)(2,1)S(1)}, bf16[2,128,256]{2,1,0:T(8,128)(2,1)S(1)}, u32[]{:S(2)}, u32[]{:S(2)}) collective-permute-start(bf16[2,128,256]{2,1,0:T(8,128)(2,1)S(1)} %get-tuple-element.83), channel_id=1, source_target_pairs={{0,24},{4,28},{8,16},{12,20},{16,8},{20,12},{24,0},{28,4},{1,25},{... | collective-permute-start | bytes 393224 | tf_op jit(solution)/shard_map/ppermute | solution.py:93
  72.7 2.5 %collective-permute-start.23 = (bf16[2,128,256]{2,1,0:T(8,128)(2,1)S(1)}, bf16[2,128,256]{2,1,0:T(8,128)(2,1)S(1)}, u32[]{:S(2)}, u32[]{:S(2)}) collective-permute-start(bf16[2,128,256]{2,1,0:T(8,128)(2,1)S(1)} %get-tuple-element.84), channel_id=1, source_target_pairs={{0,28},{4,24},{8,20},{12,16},{16,12},{20,8},{24,4},{28,0},{1,29},{... | collective-permute-start | bytes 393224 | tf_op jit(solution)/shard_map/ppermute | solution.py:93
  75.3 3.7 %collective-permute-done.21.refs_5_ = bf16[2,128,256]{2,1,0:T(8,128)(2,1)S(1)} collective-permute-done((bf16[2,128,256]{2,1,0:T(8,128)(2,1)S(1)}, bf16[2,128,256]{2,1,0:T(8,128)(2,1)S(1)}, u32[]{:S(2)}, u32[]{:S(2)}) %collective-permute-start.21) | collective-permute-done | bytes 131104 | tf_op jit(solution)/shard_map/ppermute | solution.py:93
  79.4 2.9 %collective-permute-start.24 = (bf16[8,128,256]{2,1,0:T(8,128)(2,1)S(1)}, bf16[8,128,256]{2,1,0:T(8,128)(2,1)S(1)}, u32[]{:S(2)}, u32[]{:S(2)}) collective-permute-start(bf16[8,128,256]{2,1,0:T(8,128)(2,1)S(1)} %get-tuple-element.85), channel_id=1, source_target_pairs={{0,1},{1,0},{2,3},{3,2},{4,5},{5,4},{6,7},{7,6},{8,9},{9,8},{10,11... | collective-permute-start | bytes 1572872 | tf_op jit(solution)/shard_map/ppermute | solution.py:88
  83.7 2.2 %shard_map.50.refs_1_ = bf16[8,128,256]{2,1,0:T(8,128)(2,1)S(1)} custom-call(bf16[1024,1024]{1,0:T(8,128)(2,1)S(1)} %get-tuple-element.75.x_ref, bf16[1024,1024]{1,0:T(8,128)(2,1)S(1)} %get-tuple-element.76.g_ref), custom_call_target="tpu_custom_call" | custom-call | flops 1073741824 | bytes 8388608 | tf_op jit(solution)/shard_map/pallas_call | solution.py:296
  86.1 1.7 %collective-permute-start.28 = (bf16[2,128,256]{2,1,0:T(8,128)(2,1)S(1)}, bf16[2,128,256]{2,1,0:T(8,128)(2,1)S(1)}, u32[]{:S(2)}, u32[]{:S(2)}) collective-permute-start(bf16[2,128,256]{2,1,0:T(8,128)(2,1)S(1)} %get-tuple-element.90), channel_id=1, source_target_pairs={{0,8},{4,12},{8,0},{12,4},{16,24},{20,28},{24,16},{28,20},{1,9},{5... | collective-permute-start | bytes 393224 | tf_op jit(solution)/shard_map/ppermute | solution.py:93
  87.9 1.7 %collective-permute-start.30 = (bf16[2,128,256]{2,1,0:T(8,128)(2,1)S(1)}, bf16[2,128,256]{2,1,0:T(8,128)(2,1)S(1)}, u32[]{:S(2)}, u32[]{:S(2)}) collective-permute-start(bf16[2,128,256]{2,1,0:T(8,128)(2,1)S(1)} %get-tuple-element.92), channel_id=1, source_target_pairs={{0,16},{4,20},{8,24},{12,28},{16,0},{20,4},{24,8},{28,12},{1,17},{... | collective-permute-start | bytes 393224 | tf_op jit(solution)/shard_map/ppermute | solution.py:93
  89.6 2.8 %collective-permute-done.28.refs_2_ = bf16[2,128,256]{2,1,0:T(8,128)(2,1)S(1)} collective-permute-done((bf16[2,128,256]{2,1,0:T(8,128)(2,1)S(1)}, bf16[2,128,256]{2,1,0:T(8,128)(2,1)S(1)}, u32[]{:S(2)}, u32[]{:S(2)}) %collective-permute-start.28) | collective-permute-done | bytes 131104 | tf_op jit(solution)/shard_map/ppermute | solution.py:93
  94.3 2.6 %collective-permute-start.32 = (bf16[2,128,256]{2,1,0:T(8,128)(2,1)S(1)}, bf16[2,128,256]{2,1,0:T(8,128)(2,1)S(1)}, u32[]{:S(2)}, u32[]{:S(2)}) collective-permute-start(bf16[2,128,256]{2,1,0:T(8,128)(2,1)S(1)} %get-tuple-element.94), channel_id=1, source_target_pairs={{0,24},{4,28},{8,16},{12,20},{16,8},{20,12},{24,0},{28,4},{1,25},{... | collective-permute-start | bytes 393224 | tf_op jit(solution)/shard_map/ppermute | solution.py:93
  98.0 3.5 %collective-permute-done.32.refs_6_ = bf16[2,128,256]{2,1,0:T(8,128)(2,1)S(1)} collective-permute-done((bf16[2,128,256]{2,1,0:T(8,128)(2,1)S(1)}, bf16[2,128,256]{2,1,0:T(8,128)(2,1)S(1)}, u32[]{:S(2)}, u32[]{:S(2)}) %collective-permute-start.32) | collective-permute-done | bytes 131104 | tf_op jit(solution)/shard_map/ppermute | solution.py:93
  101.5 2.2 %collective-permute-done.33.refs_7_ = bf16[2,128,256]{2,1,0:T(8,128)(2,1)S(1)} collective-permute-done((bf16[2,128,256]{2,1,0:T(8,128)(2,1)S(1)}, bf16[2,128,256]{2,1,0:T(8,128)(2,1)S(1)}, u32[]{:S(2)}, u32[]{:S(2)}) %collective-permute-start.33) | collective-permute-done | bytes 131104 | tf_op jit(solution)/shard_map/ppermute | solution.py:93
  104.8 2.8 %collective-permute-done.24.refs_0_ = bf16[8,128,256]{2,1,0:T(8,128)(2,1)S(1)} collective-permute-done((bf16[8,128,256]{2,1,0:T(8,128)(2,1)S(1)}, bf16[8,128,256]{2,1,0:T(8,128)(2,1)S(1)}, u32[]{:S(2)}, u32[]{:S(2)}) %collective-permute-start.24) | collective-permute-done | bytes 524320 | tf_op jit(solution)/shard_map/ppermute | solution.py:88
  (56 shorter events, 17.5 us)
Async XLA Ops:
  2.3 24.3 %collective-permute-start = (bf16[8,128,256]{2,1,0:T(8,128)(2,1)S(1)}, bf16[8,128,256]{2,1,0:T(8,128)(2,1)S(1)}, u32[]{:S(2)}, u32[]{:S(2)}) collective-permute-start(bf16[8,128,256]{2,1,0:T(8,128)(2,1)S(1)} %fusion.1), channel_id=1, source_target_pairs={{0,3},{1,2},{2,1},{3,0},{4,7},{5,6},{6,5},{7,4},{8,11},{9,10},{10,... | collective-permute-start | bytes 1572872 | tf_op jit(solution)/shard_map/ppermute | solution.py:88
  10.0 3.5 %collective-permute-start.8 = (bf16[2,128,256]{2,1,0:T(8,128)(2,1)S(1)}, bf16[2,128,256]{2,1,0:T(8,128)(2,1)S(1)}, u32[]{:S(2)}, u32[]{:S(2)}) collective-permute-start(bf16[2,128,256]{2,1,0:T(8,128)(2,1)S(1)} %get-tuple-element.65), channel_id=1, source_target_pairs={{0,4},{4,0},{8,12},{12,8},{16,20},{20,16},{24,28},{28,24},{1,5},{5... | collective-permute-start | bytes 393224 | tf_op jit(solution)/shard_map/ppermute | solution.py:93
  10.1 6.4 %collective-permute-start.9 = (bf16[2,128,256]{2,1,0:T(8,128)(2,1)S(1)}, bf16[2,128,256]{2,1,0:T(8,128)(2,1)S(1)}, u32[]{:S(2)}, u32[]{:S(2)}) collective-permute-start(bf16[2,128,256]{2,1,0:T(8,128)(2,1)S(1)} %get-tuple-element.66), channel_id=1, source_target_pairs={{0,8},{4,12},{8,0},{12,4},{16,24},{20,28},{24,16},{28,20},{1,9},{5... | collective-permute-start | bytes 393224 | tf_op jit(solution)/shard_map/ppermute | solution.py:93
  11.7 7.3 %collective-permute-start.10 = (bf16[2,128,256]{2,1,0:T(8,128)(2,1)S(1)}, bf16[2,128,256]{2,1,0:T(8,128)(2,1)S(1)}, u32[]{:S(2)}, u32[]{:S(2)}) collective-permute-start(bf16[2,128,256]{2,1,0:T(8,128)(2,1)S(1)} %get-tuple-element.67), channel_id=1, source_target_pairs={{0,12},{4,8},{8,4},{12,0},{16,28},{20,24},{24,20},{28,16},{1,13},{... | collective-permute-start | bytes 393224 | tf_op jit(solution)/shard_map/ppermute | solution.py:93
  12.0 9.5 %collective-permute-start.11 = (bf16[2,128,256]{2,1,0:T(8,128)(2,1)S(1)}, bf16[2,128,256]{2,1,0:T(8,128)(2,1)S(1)}, u32[]{:S(2)}, u32[]{:S(2)}) collective-permute-start(bf16[2,128,256]{2,1,0:T(8,128)(2,1)S(1)} %get-tuple-element.68), channel_id=1, source_target_pairs={{0,16},{4,20},{8,24},{12,28},{16,0},{20,4},{24,8},{28,12},{1,17},{... | collective-permute-start | bytes 393224 | tf_op jit(solution)/shard_map/ppermute | solution.py:93
  13.5 11.7 %collective-permute-start.12 = (bf16[2,128,256]{2,1,0:T(8,128)(2,1)S(1)}, bf16[2,128,256]{2,1,0:T(8,128)(2,1)S(1)}, u32[]{:S(2)}, u32[]{:S(2)}) collective-permute-start(bf16[2,128,256]{2,1,0:T(8,128)(2,1)S(1)} %get-tuple-element.69), channel_id=1, source_target_pairs={{0,20},{4,16},{8,28},{12,24},{16,4},{20,0},{24,12},{28,8},{1,21},{... | collective-permute-start | bytes 393224 | tf_op jit(solution)/shard_map/ppermute | solution.py:93
  16.5 8.7 %collective-permute-start.13 = (bf16[2,128,256]{2,1,0:T(8,128)(2,1)S(1)}, bf16[2,128,256]{2,1,0:T(8,128)(2,1)S(1)}, u32[]{:S(2)}, u32[]{:S(2)}) collective-permute-start(bf16[2,128,256]{2,1,0:T(8,128)(2,1)S(1)} %get-tuple-element.70), channel_id=1, source_target_pairs={{0,24},{4,28},{8,16},{12,20},{16,8},{20,12},{24,0},{28,4},{1,25},{... | collective-permute-start | bytes 393224 | tf_op jit(solution)/shard_map/ppermute | solution.py:93
  18.9 6.5 %collective-permute-start.14 = (bf16[2,128,256]{2,1,0:T(8,128)(2,1)S(1)}, bf16[2,128,256]{2,1,0:T(8,128)(2,1)S(1)}, u32[]{:S(2)}, u32[]{:S(2)}) collective-permute-start(bf16[2,128,256]{2,1,0:T(8,128)(2,1)S(1)} %get-tuple-element.71), channel_id=1, source_target_pairs={{0,28},{4,24},{8,20},{12,16},{16,12},{20,8},{24,4},{28,0},{1,29},{... | collective-permute-start | bytes 393224 | tf_op jit(solution)/shard_map/ppermute | solution.py:93
  25.5 23.8 %collective-permute-start.15 = (bf16[8,128,256]{2,1,0:T(8,128)(2,1)S(1)}, bf16[8,128,256]{2,1,0:T(8,128)(2,1)S(1)}, u32[]{:S(2)}, u32[]{:S(2)}) collective-permute-start(bf16[8,128,256]{2,1,0:T(8,128)(2,1)S(1)} %get-tuple-element.72), channel_id=1, source_target_pairs={{0,1},{1,0},{2,3},{3,2},{4,5},{5,4},{6,7},{7,6},{8,9},{9,8},{10,11... | collective-permute-start | bytes 1572872 | tf_op jit(solution)/shard_map/ppermute | solution.py:88
  25.6 26.7 %collective-permute-start.16 = (bf16[8,128,256]{2,1,0:T(8,128)(2,1)S(1)}, bf16[8,128,256]{2,1,0:T(8,128)(2,1)S(1)}, u32[]{:S(2)}, u32[]{:S(2)}) collective-permute-start(bf16[8,128,256]{2,1,0:T(8,128)(2,1)S(1)} %get-tuple-element.73), channel_id=1, source_target_pairs={{0,2},{1,3},{2,0},{3,1},{4,6},{5,7},{6,4},{7,5},{8,10},{9,11},{10,... | collective-permute-start | bytes 1572872 | tf_op jit(solution)/shard_map/ppermute | solution.py:88
  26.8 6.4 %collective-permute-start.2 = (bf16[2,128,256]{2,1,0:T(8,128)(2,1)S(1)}, bf16[2,128,256]{2,1,0:T(8,128)(2,1)S(1)}, u32[]{:S(2)}, u32[]{:S(2)}) collective-permute-start(bf16[2,128,256]{2,1,0:T(8,128)(2,1)S(1)} %get-tuple-element.55), channel_id=1, source_target_pairs={{0,8},{4,12},{8,0},{12,4},{16,24},{20,28},{24,16},{28,20},{1,9},{5... | collective-permute-start | bytes 393224 | tf_op jit(solution)/shard_map/ppermute | solution.py:93
  28.5 6.6 %collective-permute-start.3 = (bf16[2,128,256]{2,1,0:T(8,128)(2,1)S(1)}, bf16[2,128,256]{2,1,0:T(8,128)(2,1)S(1)}, u32[]{:S(2)}, u32[]{:S(2)}) collective-permute-start(bf16[2,128,256]{2,1,0:T(8,128)(2,1)S(1)} %get-tuple-element.56), channel_id=1, source_target_pairs={{0,12},{4,8},{8,4},{12,0},{16,28},{20,24},{24,20},{28,16},{1,13},{... | collective-permute-start | bytes 393224 | tf_op jit(solution)/shard_map/ppermute | solution.py:93
  28.7 9.0 %collective-permute-start.4 = (bf16[2,128,256]{2,1,0:T(8,128)(2,1)S(1)}, bf16[2,128,256]{2,1,0:T(8,128)(2,1)S(1)}, u32[]{:S(2)}, u32[]{:S(2)}) collective-permute-start(bf16[2,128,256]{2,1,0:T(8,128)(2,1)S(1)} %get-tuple-element.57), channel_id=1, source_target_pairs={{0,16},{4,20},{8,24},{12,28},{16,0},{20,4},{24,8},{28,12},{1,17},{... | collective-permute-start | bytes 393224 | tf_op jit(solution)/shard_map/ppermute | solution.py:93
  33.2 8.3 %collective-permute-start.5 = (bf16[2,128,256]{2,1,0:T(8,128)(2,1)S(1)}, bf16[2,128,256]{2,1,0:T(8,128)(2,1)S(1)}, u32[]{:S(2)}, u32[]{:S(2)}) collective-permute-start(bf16[2,128,256]{2,1,0:T(8,128)(2,1)S(1)} %get-tuple-element.58), channel_id=1, source_target_pairs={{0,20},{4,16},{8,28},{12,24},{16,4},{20,0},{24,12},{28,8},{1,21},{... | collective-permute-start | bytes 393224 | tf_op jit(solution)/shard_map/ppermute | solution.py:93
  35.1 7.2 %collective-permute-start.6 = (bf16[2,128,256]{2,1,0:T(8,128)(2,1)S(1)}, bf16[2,128,256]{2,1,0:T(8,128)(2,1)S(1)}, u32[]{:S(2)}, u32[]{:S(2)}) collective-permute-start(bf16[2,128,256]{2,1,0:T(8,128)(2,1)S(1)} %get-tuple-element.59), channel_id=1, source_target_pairs={{0,24},{4,28},{8,16},{12,20},{16,8},{20,12},{24,0},{28,4},{1,25},{... | collective-permute-start | bytes 393224 | tf_op jit(solution)/shard_map/ppermute | solution.py:93
  37.7 6.8 %collective-permute-start.7 = (bf16[2,128,256]{2,1,0:T(8,128)(2,1)S(1)}, bf16[2,128,256]{2,1,0:T(8,128)(2,1)S(1)}, u32[]{:S(2)}, u32[]{:S(2)}) collective-permute-start(bf16[2,128,256]{2,1,0:T(8,128)(2,1)S(1)} %get-tuple-element.60), channel_id=1, source_target_pairs={{0,28},{4,24},{8,20},{12,16},{16,12},{20,8},{24,4},{28,0},{1,29},{... | collective-permute-start | bytes 393224 | tf_op jit(solution)/shard_map/ppermute | solution.py:93
  60.3 25.6 %collective-permute-start.26 = (bf16[8,128,256]{2,1,0:T(8,128)(2,1)S(1)}, bf16[8,128,256]{2,1,0:T(8,128)(2,1)S(1)}, u32[]{:S(2)}, u32[]{:S(2)}) collective-permute-start(bf16[8,128,256]{2,1,0:T(8,128)(2,1)S(1)} %get-tuple-element.87), channel_id=1, source_target_pairs={{0,2},{1,3},{2,0},{3,1},{4,6},{5,7},{6,4},{7,5},{8,10},{9,11},{10,... | collective-permute-start | bytes 1572872 | tf_op jit(solution)/shard_map/ppermute | solution.py:88
  63.8 3.5 %collective-permute-start.17 = (bf16[2,128,256]{2,1,0:T(8,128)(2,1)S(1)}, bf16[2,128,256]{2,1,0:T(8,128)(2,1)S(1)}, u32[]{:S(2)}, u32[]{:S(2)}) collective-permute-start(bf16[2,128,256]{2,1,0:T(8,128)(2,1)S(1)} %get-tuple-element.78), channel_id=1, source_target_pairs={{0,4},{4,0},{8,12},{12,8},{16,20},{20,16},{24,28},{28,24},{1,5},{5... | collective-permute-start | bytes 393224 | tf_op jit(solution)/shard_map/ppermute | solution.py:93
  63.9 6.4 %collective-permute-start.18 = (bf16[2,128,256]{2,1,0:T(8,128)(2,1)S(1)}, bf16[2,128,256]{2,1,0:T(8,128)(2,1)S(1)}, u32[]{:S(2)}, u32[]{:S(2)}) collective-permute-start(bf16[2,128,256]{2,1,0:T(8,128)(2,1)S(1)} %get-tuple-element.79), channel_id=1, source_target_pairs={{0,8},{4,12},{8,0},{12,4},{16,24},{20,28},{24,16},{28,20},{1,9},{5... | collective-permute-start | bytes 393224 | tf_op jit(solution)/shard_map/ppermute | solution.py:93
  65.5 7.3 %collective-permute-start.19 = (bf16[2,128,256]{2,1,0:T(8,128)(2,1)S(1)}, bf16[2,128,256]{2,1,0:T(8,128)(2,1)S(1)}, u32[]{:S(2)}, u32[]{:S(2)}) collective-permute-start(bf16[2,128,256]{2,1,0:T(8,128)(2,1)S(1)} %get-tuple-element.80), channel_id=1, source_target_pairs={{0,12},{4,8},{8,4},{12,0},{16,28},{20,24},{24,20},{28,16},{1,13},{... | collective-permute-start | bytes 393224 | tf_op jit(solution)/shard_map/ppermute | solution.py:93
  65.8 9.5 %collective-permute-start.20 = (bf16[2,128,256]{2,1,0:T(8,128)(2,1)S(1)}, bf16[2,128,256]{2,1,0:T(8,128)(2,1)S(1)}, u32[]{:S(2)}, u32[]{:S(2)}) collective-permute-start(bf16[2,128,256]{2,1,0:T(8,128)(2,1)S(1)} %get-tuple-element.81), channel_id=1, source_target_pairs={{0,16},{4,20},{8,24},{12,28},{16,0},{20,4},{24,8},{28,12},{1,17},{... | collective-permute-start | bytes 393224 | tf_op jit(solution)/shard_map/ppermute | solution.py:93
  67.3 11.7 %collective-permute-start.21 = (bf16[2,128,256]{2,1,0:T(8,128)(2,1)S(1)}, bf16[2,128,256]{2,1,0:T(8,128)(2,1)S(1)}, u32[]{:S(2)}, u32[]{:S(2)}) collective-permute-start(bf16[2,128,256]{2,1,0:T(8,128)(2,1)S(1)} %get-tuple-element.82), channel_id=1, source_target_pairs={{0,20},{4,16},{8,28},{12,24},{16,4},{20,0},{24,12},{28,8},{1,21},{... | collective-permute-start | bytes 393224 | tf_op jit(solution)/shard_map/ppermute | solution.py:93
  70.3 8.7 %collective-permute-start.22 = (bf16[2,128,256]{2,1,0:T(8,128)(2,1)S(1)}, bf16[2,128,256]{2,1,0:T(8,128)(2,1)S(1)}, u32[]{:S(2)}, u32[]{:S(2)}) collective-permute-start(bf16[2,128,256]{2,1,0:T(8,128)(2,1)S(1)} %get-tuple-element.83), channel_id=1, source_target_pairs={{0,24},{4,28},{8,16},{12,20},{16,8},{20,12},{24,0},{28,4},{1,25},{... | collective-permute-start | bytes 393224 | tf_op jit(solution)/shard_map/ppermute | solution.py:93
  72.7 6.5 %collective-permute-start.23 = (bf16[2,128,256]{2,1,0:T(8,128)(2,1)S(1)}, bf16[2,128,256]{2,1,0:T(8,128)(2,1)S(1)}, u32[]{:S(2)}, u32[]{:S(2)}) collective-permute-start(bf16[2,128,256]{2,1,0:T(8,128)(2,1)S(1)} %get-tuple-element.84), channel_id=1, source_target_pairs={{0,28},{4,24},{8,20},{12,16},{16,12},{20,8},{24,4},{28,0},{1,29},{... | collective-permute-start | bytes 393224 | tf_op jit(solution)/shard_map/ppermute | solution.py:93
  79.4 28.2 %collective-permute-start.24 = (bf16[8,128,256]{2,1,0:T(8,128)(2,1)S(1)}, bf16[8,128,256]{2,1,0:T(8,128)(2,1)S(1)}, u32[]{:S(2)}, u32[]{:S(2)}) collective-permute-start(bf16[8,128,256]{2,1,0:T(8,128)(2,1)S(1)} %get-tuple-element.85), channel_id=1, source_target_pairs={{0,1},{1,0},{2,3},{3,2},{4,5},{5,4},{6,7},{7,6},{8,9},{9,8},{10,11... | collective-permute-start | bytes 1572872 | tf_op jit(solution)/shard_map/ppermute | solution.py:88
  82.3 25.3 %collective-permute-start.25 = (bf16[8,128,256]{2,1,0:T(8,128)(2,1)S(1)}, bf16[8,128,256]{2,1,0:T(8,128)(2,1)S(1)}, u32[]{:S(2)}, u32[]{:S(2)}) collective-permute-start(bf16[8,128,256]{2,1,0:T(8,128)(2,1)S(1)} %get-tuple-element.86), channel_id=1, source_target_pairs={{0,3},{1,2},{2,1},{3,0},{4,7},{5,6},{6,5},{7,4},{8,11},{9,10},{10,... | collective-permute-start | bytes 1572872 | tf_op jit(solution)/shard_map/ppermute | solution.py:88
  86.1 6.4 %collective-permute-start.28 = (bf16[2,128,256]{2,1,0:T(8,128)(2,1)S(1)}, bf16[2,128,256]{2,1,0:T(8,128)(2,1)S(1)}, u32[]{:S(2)}, u32[]{:S(2)}) collective-permute-start(bf16[2,128,256]{2,1,0:T(8,128)(2,1)S(1)} %get-tuple-element.90), channel_id=1, source_target_pairs={{0,8},{4,12},{8,0},{12,4},{16,24},{20,28},{24,16},{28,20},{1,9},{5... | collective-permute-start | bytes 393224 | tf_op jit(solution)/shard_map/ppermute | solution.py:93
  87.8 6.6 %collective-permute-start.29 = (bf16[2,128,256]{2,1,0:T(8,128)(2,1)S(1)}, bf16[2,128,256]{2,1,0:T(8,128)(2,1)S(1)}, u32[]{:S(2)}, u32[]{:S(2)}) collective-permute-start(bf16[2,128,256]{2,1,0:T(8,128)(2,1)S(1)} %get-tuple-element.91), channel_id=1, source_target_pairs={{0,12},{4,8},{8,4},{12,0},{16,28},{20,24},{24,20},{28,16},{1,13},{... | collective-permute-start | bytes 393224 | tf_op jit(solution)/shard_map/ppermute | solution.py:93
  87.9 9.0 %collective-permute-start.30 = (bf16[2,128,256]{2,1,0:T(8,128)(2,1)S(1)}, bf16[2,128,256]{2,1,0:T(8,128)(2,1)S(1)}, u32[]{:S(2)}, u32[]{:S(2)}) collective-permute-start(bf16[2,128,256]{2,1,0:T(8,128)(2,1)S(1)} %get-tuple-element.92), channel_id=1, source_target_pairs={{0,16},{4,20},{8,24},{12,28},{16,0},{20,4},{24,8},{28,12},{1,17},{... | collective-permute-start | bytes 393224 | tf_op jit(solution)/shard_map/ppermute | solution.py:93
  92.4 5.6 %collective-permute-start.31 = (bf16[2,128,256]{2,1,0:T(8,128)(2,1)S(1)}, bf16[2,128,256]{2,1,0:T(8,128)(2,1)S(1)}, u32[]{:S(2)}, u32[]{:S(2)}) collective-permute-start(bf16[2,128,256]{2,1,0:T(8,128)(2,1)S(1)} %get-tuple-element.93), channel_id=1, source_target_pairs={{0,20},{4,16},{8,28},{12,24},{16,4},{20,0},{24,12},{28,8},{1,21},{... | collective-permute-start | bytes 393224 | tf_op jit(solution)/shard_map/ppermute | solution.py:93
  94.3 7.2 %collective-permute-start.32 = (bf16[2,128,256]{2,1,0:T(8,128)(2,1)S(1)}, bf16[2,128,256]{2,1,0:T(8,128)(2,1)S(1)}, u32[]{:S(2)}, u32[]{:S(2)}) collective-permute-start(bf16[2,128,256]{2,1,0:T(8,128)(2,1)S(1)} %get-tuple-element.94), channel_id=1, source_target_pairs={{0,24},{4,28},{8,16},{12,20},{16,8},{20,12},{24,0},{28,4},{1,25},{... | collective-permute-start | bytes 393224 | tf_op jit(solution)/shard_map/ppermute | solution.py:93
  96.9 6.8 %collective-permute-start.33 = (bf16[2,128,256]{2,1,0:T(8,128)(2,1)S(1)}, bf16[2,128,256]{2,1,0:T(8,128)(2,1)S(1)}, u32[]{:S(2)}, u32[]{:S(2)}) collective-permute-start(bf16[2,128,256]{2,1,0:T(8,128)(2,1)S(1)} %get-tuple-element.95), channel_id=1, source_target_pairs={{0,28},{4,24},{8,20},{12,16},{16,12},{20,8},{24,4},{28,0},{1,29},{... | collective-permute-start | bytes 393224 | tf_op jit(solution)/shard_map/ppermute | solution.py:93
  (5 other events, 29.7 us)

commit v9 on v8

--- a/solution.py
+++ b/solution.py
@@ -285,10 +285,13 @@
 
 def last_kernel(plan, x_ref, g_ref, *refs):
     outs, power_ref = refs[:-1], refs[-1]
-    order, cols = power_ref.shape
-    for k in sorted({k for pieces in plan for k, _ in pieces}, reverse=True):
-        new = step_columns(g_ref, x_ref[:, k * cols : (k + 1) * cols], power_ref)
-        finish(new.astype(jnp.bfloat16), k, plan, outs)
+    order = x_ref.shape[0]
+    ks = sorted({k for pieces in plan for k, _ in pieces}, reverse=True)
+    cols = power_ref.shape[1] // len(ks)
+    x = jnp.concatenate([x_ref[:, k * cols : (k + 1) * cols] for k in ks], axis=1)
+    new = step_columns(g_ref, x, power_ref).astype(jnp.bfloat16)
+    for i, k in enumerate(ks):
+        finish(new[:, i * cols : (i + 1) * cols], k, plan, outs)
 
 
 def last(x, g, plan, rows, cols):
@@ -298,7 +301,7 @@
         in_specs=[whole()] * 2,
         out_specs=[whole()] * len(plan),
         out_shape=[jax.ShapeDtypeStruct((len(pieces), rows, cols), jnp.bfloat16) for pieces in plan],
-        scratch_shapes=[pltpu.VMEM((order, cols), jnp.float32)],
+        scratch_shapes=[pltpu.VMEM((order, len({k for p in plan for k, _ in p}) * cols), jnp.float32)],
         compiler_params=params(16),
         cost_estimate=cost(len(plan) // 8 * order**3 + order**3, 8 * order**2),
     )(x, g)

time: 109 us -> 109 us (level)
  waiting for transfers between devices: 41.4 us -> 42.6 us
  transfers between devices with their start and end apart: 34 -> 34, of which waited for: 18 -> 19; matrix products, arithmetic and copies ran while one was open for 0% -> 0% of each run, Pallas kernels for 11% -> 10%
where the time goes in v9:
time: 109 us
  waiting for transfers between devices  42.6 us (39%)
  starting transfers between devices  41.2 us (38%)
  Pallas kernels  20.1 us (18%)
  local copies, waits for them, and re-layouts  2.2 us (2%)
  other arithmetic  1.7 us (2%)
    ppermute x28, waiting for transfers between devices, swap_shard(): return lax.ppermute(piece, 'shard', [(s, s ^ u) for s in range(count)])  32 us
    ppermute x28, starting transfers between devices, swap_shard(): return lax.ppermute(piece, 'shard', [(s, s ^ u) for s in range(count)])  30.7 us
    ppermute x6, waiting for transfers between devices, swap_tensor(): return lax.ppermute(piece, 'tensor', [(t, t ^ k) for t in range(count)])  10.6 us
    ppermute x6, starting transfers between devices, swap_tensor(): return lax.ppermute(piece, 'tensor', [(t, t ^ k) for t in range(count)])  10.5 us
    pallas_call x1, Pallas kernels, first(): pl.pallas_call(functools.partial(first_kernel, early_ks, late_ks, plan),...  7.97 us
    pallas_call x2, Pallas kernels, last(): pl.pallas_call(functools.partial(last_kernel, plan), in_specs=[whole()] *...  4.75 us
    pallas_call x1, Pallas kernels, next_momentum(): pl.pallas_call(momentum_kernel, grid=(steps,), in_specs=[spec, spec, whol...  3.56 us
    unnamed x6, local copies, waits for them, and re-layouts  2.2 us
  transfers between devices with their start and end apart: 34, of which 19 were waited for; matrix products, arithmetic and copies ran while one was open for 0% of the time, Pallas kernels for 10%

profile of v9, /device:TPU:0, one launch (start us, length us, event | category | flops | bytes accessed | tf_op | source)
XLA Modules:
  0.0 108.7 jit_solution(5639400663408875157)
XLA Ops:
  0.6 1.7 %fusion.1 = bf16[8,128,256]{2,1,0:T(8,128)(2,1)S(1)} fusion(f32[32,128,256]{2,1,0:T(8,128)} %m_ref.2, s32[]{:T(128)S(6)} %mul.10, bf16[32,128,256]{2,1,0:T(8,128)(2,1)} %g_ref.2), kind=kLoop, calls=%fused_computation.3 | loop fusion | flops 1572864 | bytes 2097156 | tf_op jit(solution)/shard_map/convert_element_type | solution.py:76
  2.3 5.1 %collective-permute-start = (bf16[8,128,256]{2,1,0:T(8,128)(2,1)S(1)}, bf16[8,128,256]{2,1,0:T(8,128)(2,1)S(1)}, u32[]{:S(2)}, u32[]{:S(2)}) collective-permute-start(bf16[8,128,256]{2,1,0:T(8,128)(2,1)S(1)} %fusion.1), channel_id=1, source_target_pairs={{0,3},{1,2},{2,1},{3,0},{4,7},{5,6},{6,5},{7,4},{8,11},{9,10},{10,... | collective-permute-start | bytes 1572872 | tf_op jit(solution)/shard_map/ppermute | solution.py:88
  7.5 2.2 %copy-done = f32[32,128,256]{2,1,0:T(8,128)S(1)} copy-done((f32[32,128,256]{2,1,0:T(8,128)S(1)}, f32[32,128,256]{2,1,0:T(8,128)}, u32[]{:S(2)}) %copy-start) | copy-done | bytes 4194328
  10.1 1.6 %collective-permute-start.9 = (bf16[2,128,256]{2,1,0:T(8,128)(2,1)S(1)}, bf16[2,128,256]{2,1,0:T(8,128)(2,1)S(1)}, u32[]{:S(2)}, u32[]{:S(2)}) collective-permute-start(bf16[2,128,256]{2,1,0:T(8,128)(2,1)S(1)} %get-tuple-element.66), channel_id=1, source_target_pairs={{0,8},{4,12},{8,0},{12,4},{16,24},{20,28},{24,16},{28,20},{1,9},{5... | collective-permute-start | bytes 393224 | tf_op jit(solution)/shard_map/ppermute | solution.py:93
  13.7 2.8 %collective-permute-done.9.refs_2_ = bf16[2,128,256]{2,1,0:T(8,128)(2,1)S(1)} collective-permute-done((bf16[2,128,256]{2,1,0:T(8,128)(2,1)S(1)}, bf16[2,128,256]{2,1,0:T(8,128)(2,1)S(1)}, u32[]{:S(2)}, u32[]{:S(2)}) %collective-permute-start.9) | collective-permute-done | bytes 131104 | tf_op jit(solution)/shard_map/ppermute | solution.py:93
  16.5 2.4 %collective-permute-start.13 = (bf16[2,128,256]{2,1,0:T(8,128)(2,1)S(1)}, bf16[2,128,256]{2,1,0:T(8,128)(2,1)S(1)}, u32[]{:S(2)}, u32[]{:S(2)}) collective-permute-start(bf16[2,128,256]{2,1,0:T(8,128)(2,1)S(1)} %get-tuple-element.70), channel_id=1, source_target_pairs={{0,24},{4,28},{8,16},{12,20},{16,8},{20,12},{24,0},{28,4},{1,25},{... | collective-permute-start | bytes 393224 | tf_op jit(solution)/shard_map/ppermute | solution.py:93
  18.9 2.5 %collective-permute-start.14 = (bf16[2,128,256]{2,1,0:T(8,128)(2,1)S(1)}, bf16[2,128,256]{2,1,0:T(8,128)(2,1)S(1)}, u32[]{:S(2)}, u32[]{:S(2)}) collective-permute-start(bf16[2,128,256]{2,1,0:T(8,128)(2,1)S(1)} %get-tuple-element.71), channel_id=1, source_target_pairs={{0,28},{4,24},{8,20},{12,16},{16,12},{20,8},{24,4},{28,0},{1,29},{... | collective-permute-start | bytes 393224 | tf_op jit(solution)/shard_map/ppermute | solution.py:93
  21.5 3.7 %collective-permute-done.12.refs_5_ = bf16[2,128,256]{2,1,0:T(8,128)(2,1)S(1)} collective-permute-done((bf16[2,128,256]{2,1,0:T(8,128)(2,1)S(1)}, bf16[2,128,256]{2,1,0:T(8,128)(2,1)S(1)}, u32[]{:S(2)}, u32[]{:S(2)}) %collective-permute-start.12) | collective-permute-done | bytes 131104 | tf_op jit(solution)/shard_map/ppermute | solution.py:93
  26.8 1.7 %collective-permute-start.2 = (bf16[2,128,256]{2,1,0:T(8,128)(2,1)S(1)}, bf16[2,128,256]{2,1,0:T(8,128)(2,1)S(1)}, u32[]{:S(2)}, u32[]{:S(2)}) collective-permute-start(bf16[2,128,256]{2,1,0:T(8,128)(2,1)S(1)} %get-tuple-element.55), channel_id=1, source_target_pairs={{0,8},{4,12},{8,0},{12,4},{16,24},{20,28},{24,16},{28,20},{1,9},{5... | collective-permute-start | bytes 393224 | tf_op jit(solution)/shard_map/ppermute | solution.py:93
  28.7 1.7 %collective-permute-start.4 = (bf16[2,128,256]{2,1,0:T(8,128)(2,1)S(1)}, bf16[2,128,256]{2,1,0:T(8,128)(2,1)S(1)}, u32[]{:S(2)}, u32[]{:S(2)}) collective-permute-start(bf16[2,128,256]{2,1,0:T(8,128)(2,1)S(1)} %get-tuple-element.57), channel_id=1, source_target_pairs={{0,16},{4,20},{8,24},{12,28},{16,0},{20,4},{24,8},{28,12},{1,17},{... | collective-permute-start | bytes 393224 | tf_op jit(solution)/shard_map/ppermute | solution.py:93
  30.3 2.8 %collective-permute-done.2.refs_2_ = bf16[2,128,256]{2,1,0:T(8,128)(2,1)S(1)} collective-permute-done((bf16[2,128,256]{2,1,0:T(8,128)(2,1)S(1)}, bf16[2,128,256]{2,1,0:T(8,128)(2,1)S(1)}, u32[]{:S(2)}, u32[]{:S(2)}) %collective-permute-start.2) | collective-permute-done | bytes 131104 | tf_op jit(solution)/shard_map/ppermute | solution.py:93
  35.1 2.6 %collective-permute-start.6 = (bf16[2,128,256]{2,1,0:T(8,128)(2,1)S(1)}, bf16[2,128,256]{2,1,0:T(8,128)(2,1)S(1)}, u32[]{:S(2)}, u32[]{:S(2)}) collective-permute-start(bf16[2,128,256]{2,1,0:T(8,128)(2,1)S(1)} %get-tuple-element.59), channel_id=1, source_target_pairs={{0,24},{4,28},{8,16},{12,20},{16,8},{20,12},{24,0},{28,4},{1,25},{... | collective-permute-start | bytes 393224 | tf_op jit(solution)/shard_map/ppermute | solution.py:93
  37.9 3.6 %shard_map.43 = (f32[32,128,256]{2,1,0:T(8,128)}, f32[8,128]{1,0:T(8,128)S(1)}) custom-call(bf16[32,128,256]{2,1,0:T(8,128)(2,1)S(1)} %copy-done.2, f32[32,128,256]{2,1,0:T(8,128)S(1)} %copy-done.1, bf16[2,128,256]{2,1,0:T(8,128)(2,1)S(1)} %get-tuple-element.52.after_ref.refs_0_), custom_call_target="tpu_custom_call" | custom-call | flops 1000 | bytes 1000 | tf_op jit(solution)/shard_map/pallas_call | solution.py:59
  42.3 2.2 %collective-permute-done.7.refs_7_ = bf16[2,128,256]{2,1,0:T(8,128)(2,1)S(1)} collective-permute-done((bf16[2,128,256]{2,1,0:T(8,128)(2,1)S(1)}, bf16[2,128,256]{2,1,0:T(8,128)(2,1)S(1)}, u32[]{:S(2)}, u32[]{:S(2)}) %collective-permute-start.7) | collective-permute-done | bytes 131104 | tf_op jit(solution)/shard_map/ppermute | solution.py:93
  45.3 4.0 %collective-permute-done.15.refs_3_ = bf16[8,128,256]{2,1,0:T(8,128)(2,1)S(1)} collective-permute-done((bf16[8,128,256]{2,1,0:T(8,128)(2,1)S(1)}, bf16[8,128,256]{2,1,0:T(8,128)(2,1)S(1)}, u32[]{:S(2)}, u32[]{:S(2)}) %collective-permute-start.15) | collective-permute-done | bytes 524320 | tf_op jit(solution)/shard_map/ppermute | solution.py:88
  49.3 2.9 %collective-permute-done.16.refs_4_ = bf16[8,128,256]{2,1,0:T(8,128)(2,1)S(1)} collective-permute-done((bf16[8,128,256]{2,1,0:T(8,128)(2,1)S(1)}, bf16[8,128,256]{2,1,0:T(8,128)(2,1)S(1)}, u32[]{:S(2)}, u32[]{:S(2)}) %collective-permute-start.16) | collective-permute-done | bytes 524320 | tf_op jit(solution)/shard_map/ppermute | solution.py:88
  52.3 8.0 %shard_map.47 = (bf16[1024,1024]{1,0:T(8,128)(2,1)S(1)}, bf16[1024,1024]{1,0:T(8,128)(2,1)S(1)}, bf16[8,128,256]{2,1,0:T(8,128)(2,1)S(1)}) custom-call(bf16[1024,512]{1,0:T(8,128)(2,1)S(1)} %get-tuple-element.61.refs_0_, f32[1024,1024]{1,0:T(8,128)S(1)} %get-tuple-element.62.refs_1_, f32[8,512]{1,0:T(8,128)S(1)} %get-tuple-element.63.refs_2_, ...), custom_call_target="tpu_custom_call" | custom-call | flops 7516192768 | bytes 12582912 | tf_op jit(solution)/shard_map/pallas_call | solution.py:272
  60.5 2.5 %shard_map.48 = (bf16[2,128,256]{2,1,0:T(8,128)(2,1)S(1)}, bf16[2,128,256]{2,1,0:T(8,128)(2,1)S(1)}, bf16[2,128,256]{2,1,0:T(8,128)(2,1)S(1)}, bf16[2,128,256]{2...) custom-call(bf16[1024,1024]{1,0:T(8,128)(2,1)S(1)} %get-tuple-elemen, ...), custom_call_target="tpu_custom_call" | custom-call | flops 2147483648 | bytes 8388608 | tf_op jit(solution)/shard_map/pallas_call | solution.py:299
  63.1 1.6 %collective-permute-start.18 = (bf16[2,128,256]{2,1,0:T(8,128)(2,1)S(1)}, bf16[2,128,256]{2,1,0:T(8,128)(2,1)S(1)}, u32[]{:S(2)}, u32[]{:S(2)}) collective-permute-start(bf16[2,128,256]{2,1,0:T(8,128)(2,1)S(1)} %get-tuple-element.79), channel_id=1, source_target_pairs={{0,8},{4,12},{8,0},{12,4},{16,24},{20,28},{24,16},{28,20},{1,9},{5... | collective-permute-start | bytes 393224 | tf_op jit(solution)/shard_map/ppermute | solution.py:93
  66.7 2.8 %collective-permute-done.18.refs_2_ = bf16[2,128,256]{2,1,0:T(8,128)(2,1)S(1)} collective-permute-done((bf16[2,128,256]{2,1,0:T(8,128)(2,1)S(1)}, bf16[2,128,256]{2,1,0:T(8,128)(2,1)S(1)}, u32[]{:S(2)}, u32[]{:S(2)}) %collective-permute-start.18) | collective-permute-done | bytes 131104 | tf_op jit(solution)/shard_map/ppermute | solution.py:93
  69.5 2.5 %collective-permute-start.22 = (bf16[2,128,256]{2,1,0:T(8,128)(2,1)S(1)}, bf16[2,128,256]{2,1,0:T(8,128)(2,1)S(1)}, u32[]{:S(2)}, u32[]{:S(2)}) collective-permute-start(bf16[2,128,256]{2,1,0:T(8,128)(2,1)S(1)} %get-tuple-element.83), channel_id=1, source_target_pairs={{0,24},{4,28},{8,16},{12,20},{16,8},{20,12},{24,0},{28,4},{1,25},{... | collective-permute-start | bytes 393224 | tf_op jit(solution)/shard_map/ppermute | solution.py:93
  71.9 2.5 %collective-permute-start.23 = (bf16[2,128,256]{2,1,0:T(8,128)(2,1)S(1)}, bf16[2,128,256]{2,1,0:T(8,128)(2,1)S(1)}, u32[]{:S(2)}, u32[]{:S(2)}) collective-permute-start(bf16[2,128,256]{2,1,0:T(8,128)(2,1)S(1)} %get-tuple-element.84), channel_id=1, source_target_pairs={{0,28},{4,24},{8,20},{12,16},{16,12},{20,8},{24,4},{28,0},{1,29},{... | collective-permute-start | bytes 393224 | tf_op jit(solution)/shard_map/ppermute | solution.py:93
  74.5 3.7 %collective-permute-done.21.refs_5_ = bf16[2,128,256]{2,1,0:T(8,128)(2,1)S(1)} collective-permute-done((bf16[2,128,256]{2,1,0:T(8,128)(2,1)S(1)}, bf16[2,128,256]{2,1,0:T(8,128)(2,1)S(1)}, u32[]{:S(2)}, u32[]{:S(2)}) %collective-permute-start.21) | collective-permute-done | bytes 131104 | tf_op jit(solution)/shard_map/ppermute | solution.py:93
  78.6 2.9 %collective-permute-start.24 = (bf16[8,128,256]{2,1,0:T(8,128)(2,1)S(1)}, bf16[8,128,256]{2,1,0:T(8,128)(2,1)S(1)}, u32[]{:S(2)}, u32[]{:S(2)}) collective-permute-start(bf16[8,128,256]{2,1,0:T(8,128)(2,1)S(1)} %get-tuple-element.85), channel_id=1, source_target_pairs={{0,1},{1,0},{2,3},{3,2},{4,5},{5,4},{6,7},{7,6},{8,9},{9,8},{10,11... | collective-permute-start | bytes 1572872 | tf_op jit(solution)/shard_map/ppermute | solution.py:88
  82.8 2.2 %shard_map.50.refs_1_ = bf16[8,128,256]{2,1,0:T(8,128)(2,1)S(1)} custom-call(bf16[1024,1024]{1,0:T(8,128)(2,1)S(1)} %get-tuple-element.75.x_ref, bf16[1024,1024]{1,0:T(8,128)(2,1)S(1)} %get-tuple-element.76.g_ref), custom_call_target="tpu_custom_call" | custom-call | flops 1073741824 | bytes 8388608 | tf_op jit(solution)/shard_map/pallas_call | solution.py:299
  85.4 1.6 %collective-permute-start.28 = (bf16[2,128,256]{2,1,0:T(8,128)(2,1)S(1)}, bf16[2,128,256]{2,1,0:T(8,128)(2,1)S(1)}, u32[]{:S(2)}, u32[]{:S(2)}) collective-permute-start(bf16[2,128,256]{2,1,0:T(8,128)(2,1)S(1)} %get-tuple-element.90), channel_id=1, source_target_pairs={{0,8},{4,12},{8,0},{12,4},{16,24},{20,28},{24,16},{28,20},{1,9},{5... | collective-permute-start | bytes 393224 | tf_op jit(solution)/shard_map/ppermute | solution.py:93
  88.8 3.0 %collective-permute-done.28.refs_2_ = bf16[2,128,256]{2,1,0:T(8,128)(2,1)S(1)} collective-permute-done((bf16[2,128,256]{2,1,0:T(8,128)(2,1)S(1)}, bf16[2,128,256]{2,1,0:T(8,128)(2,1)S(1)}, u32[]{:S(2)}, u32[]{:S(2)}) %collective-permute-start.28) | collective-permute-done | bytes 131104 | tf_op jit(solution)/shard_map/ppermute | solution.py:93
  92.1 1.6 %collective-permute-done.29.refs_3_ = bf16[2,128,256]{2,1,0:T(8,128)(2,1)S(1)} collective-permute-done((bf16[2,128,256]{2,1,0:T(8,128)(2,1)S(1)}, bf16[2,128,256]{2,1,0:T(8,128)(2,1)S(1)}, u32[]{:S(2)}, u32[]{:S(2)}) %collective-permute-start.29) | collective-permute-done | bytes 131104 | tf_op jit(solution)/shard_map/ppermute | solution.py:93
  93.6 2.4 %collective-permute-start.32 = (bf16[2,128,256]{2,1,0:T(8,128)(2,1)S(1)}, bf16[2,128,256]{2,1,0:T(8,128)(2,1)S(1)}, u32[]{:S(2)}, u32[]{:S(2)}) collective-permute-start(bf16[2,128,256]{2,1,0:T(8,128)(2,1)S(1)} %get-tuple-element.94), channel_id=1, source_target_pairs={{0,24},{4,28},{8,16},{12,20},{16,8},{20,12},{24,0},{28,4},{1,25},{... | collective-permute-start | bytes 393224 | tf_op jit(solution)/shard_map/ppermute | solution.py:93
  97.5 3.4 %collective-permute-done.32.refs_6_ = bf16[2,128,256]{2,1,0:T(8,128)(2,1)S(1)} collective-permute-done((bf16[2,128,256]{2,1,0:T(8,128)(2,1)S(1)}, bf16[2,128,256]{2,1,0:T(8,128)(2,1)S(1)}, u32[]{:S(2)}, u32[]{:S(2)}) %collective-permute-start.32) | collective-permute-done | bytes 131104 | tf_op jit(solution)/shard_map/ppermute | solution.py:93
  100.8 2.2 %collective-permute-done.33.refs_7_ = bf16[2,128,256]{2,1,0:T(8,128)(2,1)S(1)} collective-permute-done((bf16[2,128,256]{2,1,0:T(8,128)(2,1)S(1)}, bf16[2,128,256]{2,1,0:T(8,128)(2,1)S(1)}, u32[]{:S(2)}, u32[]{:S(2)}) %collective-permute-start.33) | collective-permute-done | bytes 131104 | tf_op jit(solution)/shard_map/ppermute | solution.py:93
  104.1 3.5 %collective-permute-done.24.refs_0_ = bf16[8,128,256]{2,1,0:T(8,128)(2,1)S(1)} collective-permute-done((bf16[8,128,256]{2,1,0:T(8,128)(2,1)S(1)}, bf16[8,128,256]{2,1,0:T(8,128)(2,1)S(1)}, u32[]{:S(2)}, u32[]{:S(2)}) %collective-permute-start.24) | collective-permute-done | bytes 524320 | tf_op jit(solution)/shard_map/ppermute | solution.py:88
  (56 shorter events, 18.0 us)
Async XLA Ops:
  2.3 24.3 %collective-permute-start = (bf16[8,128,256]{2,1,0:T(8,128)(2,1)S(1)}, bf16[8,128,256]{2,1,0:T(8,128)(2,1)S(1)}, u32[]{:S(2)}, u32[]{:S(2)}) collective-permute-start(bf16[8,128,256]{2,1,0:T(8,128)(2,1)S(1)} %fusion.1), channel_id=1, source_target_pairs={{0,3},{1,2},{2,1},{3,0},{4,7},{5,6},{6,5},{7,4},{8,11},{9,10},{10,... | collective-permute-start | bytes 1572872 | tf_op jit(solution)/shard_map/ppermute | solution.py:88
  10.0 3.5 %collective-permute-start.8 = (bf16[2,128,256]{2,1,0:T(8,128)(2,1)S(1)}, bf16[2,128,256]{2,1,0:T(8,128)(2,1)S(1)}, u32[]{:S(2)}, u32[]{:S(2)}) collective-permute-start(bf16[2,128,256]{2,1,0:T(8,128)(2,1)S(1)} %get-tuple-element.65), channel_id=1, source_target_pairs={{0,4},{4,0},{8,12},{12,8},{16,20},{20,16},{24,28},{28,24},{1,5},{5... | collective-permute-start | bytes 393224 | tf_op jit(solution)/shard_map/ppermute | solution.py:93
  10.1 6.4 %collective-permute-start.9 = (bf16[2,128,256]{2,1,0:T(8,128)(2,1)S(1)}, bf16[2,128,256]{2,1,0:T(8,128)(2,1)S(1)}, u32[]{:S(2)}, u32[]{:S(2)}) collective-permute-start(bf16[2,128,256]{2,1,0:T(8,128)(2,1)S(1)} %get-tuple-element.66), channel_id=1, source_target_pairs={{0,8},{4,12},{8,0},{12,4},{16,24},{20,28},{24,16},{28,20},{1,9},{5... | collective-permute-start | bytes 393224 | tf_op jit(solution)/shard_map/ppermute | solution.py:93
  11.7 7.3 %collective-permute-start.10 = (bf16[2,128,256]{2,1,0:T(8,128)(2,1)S(1)}, bf16[2,128,256]{2,1,0:T(8,128)(2,1)S(1)}, u32[]{:S(2)}, u32[]{:S(2)}) collective-permute-start(bf16[2,128,256]{2,1,0:T(8,128)(2,1)S(1)} %get-tuple-element.67), channel_id=1, source_target_pairs={{0,12},{4,8},{8,4},{12,0},{16,28},{20,24},{24,20},{28,16},{1,13},{... | collective-permute-start | bytes 393224 | tf_op jit(solution)/shard_map/ppermute | solution.py:93
  12.0 9.5 %collective-permute-start.11 = (bf16[2,128,256]{2,1,0:T(8,128)(2,1)S(1)}, bf16[2,128,256]{2,1,0:T(8,128)(2,1)S(1)}, u32[]{:S(2)}, u32[]{:S(2)}) collective-permute-start(bf16[2,128,256]{2,1,0:T(8,128)(2,1)S(1)} %get-tuple-element.68), channel_id=1, source_target_pairs={{0,16},{4,20},{8,24},{12,28},{16,0},{20,4},{24,8},{28,12},{1,17},{... | collective-permute-start | bytes 393224 | tf_op jit(solution)/shard_map/ppermute | solution.py:93
  13.5 11.7 %collective-permute-start.12 = (bf16[2,128,256]{2,1,0:T(8,128)(2,1)S(1)}, bf16[2,128,256]{2,1,0:T(8,128)(2,1)S(1)}, u32[]{:S(2)}, u32[]{:S(2)}) collective-permute-start(bf16[2,128,256]{2,1,0:T(8,128)(2,1)S(1)} %get-tuple-element.69), channel_id=1, source_target_pairs={{0,20},{4,16},{8,28},{12,24},{16,4},{20,0},{24,12},{28,8},{1,21},{... | collective-permute-start | bytes 393224 | tf_op jit(solution)/shard_map/ppermute | solution.py:93
  16.5 8.7 %collective-permute-start.13 = (bf16[2,128,256]{2,1,0:T(8,128)(2,1)S(1)}, bf16[2,128,256]{2,1,0:T(8,128)(2,1)S(1)}, u32[]{:S(2)}, u32[]{:S(2)}) collective-permute-start(bf16[2,128,256]{2,1,0:T(8,128)(2,1)S(1)} %get-tuple-element.70), channel_id=1, source_target_pairs={{0,24},{4,28},{8,16},{12,20},{16,8},{20,12},{24,0},{28,4},{1,25},{... | collective-permute-start | bytes 393224 | tf_op jit(solution)/shard_map/ppermute | solution.py:93
  18.9 6.5 %collective-permute-start.14 = (bf16[2,128,256]{2,1,0:T(8,128)(2,1)S(1)}, bf16[2,128,256]{2,1,0:T(8,128)(2,1)S(1)}, u32[]{:S(2)}, u32[]{:S(2)}) collective-permute-start(bf16[2,128,256]{2,1,0:T(8,128)(2,1)S(1)} %get-tuple-element.71), channel_id=1, source_target_pairs={{0,28},{4,24},{8,20},{12,16},{16,12},{20,8},{24,4},{28,0},{1,29},{... | collective-permute-start | bytes 393224 | tf_op jit(solution)/shard_map/ppermute | solution.py:93
  25.5 23.8 %collective-permute-start.15 = (bf16[8,128,256]{2,1,0:T(8,128)(2,1)S(1)}, bf16[8,128,256]{2,1,0:T(8,128)(2,1)S(1)}, u32[]{:S(2)}, u32[]{:S(2)}) collective-permute-start(bf16[8,128,256]{2,1,0:T(8,128)(2,1)S(1)} %get-tuple-element.72), channel_id=1, source_target_pairs={{0,1},{1,0},{2,3},{3,2},{4,5},{5,4},{6,7},{7,6},{8,9},{9,8},{10,11... | collective-permute-start | bytes 1572872 | tf_op jit(solution)/shard_map/ppermute | solution.py:88
  25.6 26.7 %collective-permute-start.16 = (bf16[8,128,256]{2,1,0:T(8,128)(2,1)S(1)}, bf16[8,128,256]{2,1,0:T(8,128)(2,1)S(1)}, u32[]{:S(2)}, u32[]{:S(2)}) collective-permute-start(bf16[8,128,256]{2,1,0:T(8,128)(2,1)S(1)} %get-tuple-element.73), channel_id=1, source_target_pairs={{0,2},{1,3},{2,0},{3,1},{4,6},{5,7},{6,4},{7,5},{8,10},{9,11},{10,... | collective-permute-start | bytes 1572872 | tf_op jit(solution)/shard_map/ppermute | solution.py:88
  26.8 6.4 %collective-permute-start.2 = (bf16[2,128,256]{2,1,0:T(8,128)(2,1)S(1)}, bf16[2,128,256]{2,1,0:T(8,128)(2,1)S(1)}, u32[]{:S(2)}, u32[]{:S(2)}) collective-permute-start(bf16[2,128,256]{2,1,0:T(8,128)(2,1)S(1)} %get-tuple-element.55), channel_id=1, source_target_pairs={{0,8},{4,12},{8,0},{12,4},{16,24},{20,28},{24,16},{28,20},{1,9},{5... | collective-permute-start | bytes 393224 | tf_op jit(solution)/shard_map/ppermute | solution.py:93
  28.5 6.6 %collective-permute-start.3 = (bf16[2,128,256]{2,1,0:T(8,128)(2,1)S(1)}, bf16[2,128,256]{2,1,0:T(8,128)(2,1)S(1)}, u32[]{:S(2)}, u32[]{:S(2)}) collective-permute-start(bf16[2,128,256]{2,1,0:T(8,128)(2,1)S(1)} %get-tuple-element.56), channel_id=1, source_target_pairs={{0,12},{4,8},{8,4},{12,0},{16,28},{20,24},{24,20},{28,16},{1,13},{... | collective-permute-start | bytes 393224 | tf_op jit(solution)/shard_map/ppermute | solution.py:93
  28.7 9.0 %collective-permute-start.4 = (bf16[2,128,256]{2,1,0:T(8,128)(2,1)S(1)}, bf16[2,128,256]{2,1,0:T(8,128)(2,1)S(1)}, u32[]{:S(2)}, u32[]{:S(2)}) collective-permute-start(bf16[2,128,256]{2,1,0:T(8,128)(2,1)S(1)} %get-tuple-element.57), channel_id=1, source_target_pairs={{0,16},{4,20},{8,24},{12,28},{16,0},{20,4},{24,8},{28,12},{1,17},{... | collective-permute-start | bytes 393224 | tf_op jit(solution)/shard_map/ppermute | solution.py:93
  33.2 8.3 %collective-permute-start.5 = (bf16[2,128,256]{2,1,0:T(8,128)(2,1)S(1)}, bf16[2,128,256]{2,1,0:T(8,128)(2,1)S(1)}, u32[]{:S(2)}, u32[]{:S(2)}) collective-permute-start(bf16[2,128,256]{2,1,0:T(8,128)(2,1)S(1)} %get-tuple-element.58), channel_id=1, source_target_pairs={{0,20},{4,16},{8,28},{12,24},{16,4},{20,0},{24,12},{28,8},{1,21},{... | collective-permute-start | bytes 393224 | tf_op jit(solution)/shard_map/ppermute | solution.py:93
  35.1 7.2 %collective-permute-start.6 = (bf16[2,128,256]{2,1,0:T(8,128)(2,1)S(1)}, bf16[2,128,256]{2,1,0:T(8,128)(2,1)S(1)}, u32[]{:S(2)}, u32[]{:S(2)}) collective-permute-start(bf16[2,128,256]{2,1,0:T(8,128)(2,1)S(1)} %get-tuple-element.59), channel_id=1, source_target_pairs={{0,24},{4,28},{8,16},{12,20},{16,8},{20,12},{24,0},{28,4},{1,25},{... | collective-permute-start | bytes 393224 | tf_op jit(solution)/shard_map/ppermute | solution.py:93
  37.7 6.8 %collective-permute-start.7 = (bf16[2,128,256]{2,1,0:T(8,128)(2,1)S(1)}, bf16[2,128,256]{2,1,0:T(8,128)(2,1)S(1)}, u32[]{:S(2)}, u32[]{:S(2)}) collective-permute-start(bf16[2,128,256]{2,1,0:T(8,128)(2,1)S(1)} %get-tuple-element.60), channel_id=1, source_target_pairs={{0,28},{4,24},{8,20},{12,16},{16,12},{20,8},{24,4},{28,0},{1,29},{... | collective-permute-start | bytes 393224 | tf_op jit(solution)/shard_map/ppermute | solution.py:93
  60.3 25.0 %collective-permute-start.26 = (bf16[8,128,256]{2,1,0:T(8,128)(2,1)S(1)}, bf16[8,128,256]{2,1,0:T(8,128)(2,1)S(1)}, u32[]{:S(2)}, u32[]{:S(2)}) collective-permute-start(bf16[8,128,256]{2,1,0:T(8,128)(2,1)S(1)} %get-tuple-element.87), channel_id=1, source_target_pairs={{0,2},{1,3},{2,0},{3,1},{4,6},{5,7},{6,4},{7,5},{8,10},{9,11},{10,... | collective-permute-start | bytes 1572872 | tf_op jit(solution)/shard_map/ppermute | solution.py:88
  63.0 3.5 %collective-permute-start.17 = (bf16[2,128,256]{2,1,0:T(8,128)(2,1)S(1)}, bf16[2,128,256]{2,1,0:T(8,128)(2,1)S(1)}, u32[]{:S(2)}, u32[]{:S(2)}) collective-permute-start(bf16[2,128,256]{2,1,0:T(8,128)(2,1)S(1)} %get-tuple-element.78), channel_id=1, source_target_pairs={{0,4},{4,0},{8,12},{12,8},{16,20},{20,16},{24,28},{28,24},{1,5},{5... | collective-permute-start | bytes 393224 | tf_op jit(solution)/shard_map/ppermute | solution.py:93
  63.1 6.4 %collective-permute-start.18 = (bf16[2,128,256]{2,1,0:T(8,128)(2,1)S(1)}, bf16[2,128,256]{2,1,0:T(8,128)(2,1)S(1)}, u32[]{:S(2)}, u32[]{:S(2)}) collective-permute-start(bf16[2,128,256]{2,1,0:T(8,128)(2,1)S(1)} %get-tuple-element.79), channel_id=1, source_target_pairs={{0,8},{4,12},{8,0},{12,4},{16,24},{20,28},{24,16},{28,20},{1,9},{5... | collective-permute-start | bytes 393224 | tf_op jit(solution)/shard_map/ppermute | solution.py:93
  64.7 7.3 %collective-permute-start.19 = (bf16[2,128,256]{2,1,0:T(8,128)(2,1)S(1)}, bf16[2,128,256]{2,1,0:T(8,128)(2,1)S(1)}, u32[]{:S(2)}, u32[]{:S(2)}) collective-permute-start(bf16[2,128,256]{2,1,0:T(8,128)(2,1)S(1)} %get-tuple-element.80), channel_id=1, source_target_pairs={{0,12},{4,8},{8,4},{12,0},{16,28},{20,24},{24,20},{28,16},{1,13},{... | collective-permute-start | bytes 393224 | tf_op jit(solution)/shard_map/ppermute | solution.py:93
  65.0 9.5 %collective-permute-start.20 = (bf16[2,128,256]{2,1,0:T(8,128)(2,1)S(1)}, bf16[2,128,256]{2,1,0:T(8,128)(2,1)S(1)}, u32[]{:S(2)}, u32[]{:S(2)}) collective-permute-start(bf16[2,128,256]{2,1,0:T(8,128)(2,1)S(1)} %get-tuple-element.81), channel_id=1, source_target_pairs={{0,16},{4,20},{8,24},{12,28},{16,0},{20,4},{24,8},{28,12},{1,17},{... | collective-permute-start | bytes 393224 | tf_op jit(solution)/shard_map/ppermute | solution.py:93
  66.5 11.7 %collective-permute-start.21 = (bf16[2,128,256]{2,1,0:T(8,128)(2,1)S(1)}, bf16[2,128,256]{2,1,0:T(8,128)(2,1)S(1)}, u32[]{:S(2)}, u32[]{:S(2)}) collective-permute-start(bf16[2,128,256]{2,1,0:T(8,128)(2,1)S(1)} %get-tuple-element.82), channel_id=1, source_target_pairs={{0,20},{4,16},{8,28},{12,24},{16,4},{20,0},{24,12},{28,8},{1,21},{... | collective-permute-start | bytes 393224 | tf_op jit(solution)/shard_map/ppermute | solution.py:93
  69.5 8.7 %collective-permute-start.22 = (bf16[2,128,256]{2,1,0:T(8,128)(2,1)S(1)}, bf16[2,128,256]{2,1,0:T(8,128)(2,1)S(1)}, u32[]{:S(2)}, u32[]{:S(2)}) collective-permute-start(bf16[2,128,256]{2,1,0:T(8,128)(2,1)S(1)} %get-tuple-element.83), channel_id=1, source_target_pairs={{0,24},{4,28},{8,16},{12,20},{16,8},{20,12},{24,0},{28,4},{1,25},{... | collective-permute-start | bytes 393224 | tf_op jit(solution)/shard_map/ppermute | solution.py:93
  71.9 6.6 %collective-permute-start.23 = (bf16[2,128,256]{2,1,0:T(8,128)(2,1)S(1)}, bf16[2,128,256]{2,1,0:T(8,128)(2,1)S(1)}, u32[]{:S(2)}, u32[]{:S(2)}) collective-permute-start(bf16[2,128,256]{2,1,0:T(8,128)(2,1)S(1)} %get-tuple-element.84), channel_id=1, source_target_pairs={{0,28},{4,24},{8,20},{12,16},{16,12},{20,8},{24,4},{28,0},{1,29},{... | collective-permute-start | bytes 393224 | tf_op jit(solution)/shard_map/ppermute | solution.py:93
  78.6 29.0 %collective-permute-start.24 = (bf16[8,128,256]{2,1,0:T(8,128)(2,1)S(1)}, bf16[8,128,256]{2,1,0:T(8,128)(2,1)S(1)}, u32[]{:S(2)}, u32[]{:S(2)}) collective-permute-start(bf16[8,128,256]{2,1,0:T(8,128)(2,1)S(1)} %get-tuple-element.85), channel_id=1, source_target_pairs={{0,1},{1,0},{2,3},{3,2},{4,5},{5,4},{6,7},{7,6},{8,9},{9,8},{10,11... | collective-permute-start | bytes 1572872 | tf_op jit(solution)/shard_map/ppermute | solution.py:88
  81.5 26.1 %collective-permute-start.25 = (bf16[8,128,256]{2,1,0:T(8,128)(2,1)S(1)}, bf16[8,128,256]{2,1,0:T(8,128)(2,1)S(1)}, u32[]{:S(2)}, u32[]{:S(2)}) collective-permute-start(bf16[8,128,256]{2,1,0:T(8,128)(2,1)S(1)} %get-tuple-element.86), channel_id=1, source_target_pairs={{0,3},{1,2},{2,1},{3,0},{4,7},{5,6},{6,5},{7,4},{8,11},{9,10},{10,... | collective-permute-start | bytes 1572872 | tf_op jit(solution)/shard_map/ppermute | solution.py:88
  85.4 6.4 %collective-permute-start.28 = (bf16[2,128,256]{2,1,0:T(8,128)(2,1)S(1)}, bf16[2,128,256]{2,1,0:T(8,128)(2,1)S(1)}, u32[]{:S(2)}, u32[]{:S(2)}) collective-permute-start(bf16[2,128,256]{2,1,0:T(8,128)(2,1)S(1)} %get-tuple-element.90), channel_id=1, source_target_pairs={{0,8},{4,12},{8,0},{12,4},{16,24},{20,28},{24,16},{28,20},{1,9},{5... | collective-permute-start | bytes 393224 | tf_op jit(solution)/shard_map/ppermute | solution.py:93
  86.9 6.7 %collective-permute-start.29 = (bf16[2,128,256]{2,1,0:T(8,128)(2,1)S(1)}, bf16[2,128,256]{2,1,0:T(8,128)(2,1)S(1)}, u32[]{:S(2)}, u32[]{:S(2)}) collective-permute-start(bf16[2,128,256]{2,1,0:T(8,128)(2,1)S(1)} %get-tuple-element.91), channel_id=1, source_target_pairs={{0,12},{4,8},{8,4},{12,0},{16,28},{20,24},{24,20},{28,16},{1,13},{... | collective-permute-start | bytes 393224 | tf_op jit(solution)/shard_map/ppermute | solution.py:93
  87.2 8.9 %collective-permute-start.30 = (bf16[2,128,256]{2,1,0:T(8,128)(2,1)S(1)}, bf16[2,128,256]{2,1,0:T(8,128)(2,1)S(1)}, u32[]{:S(2)}, u32[]{:S(2)}) collective-permute-start(bf16[2,128,256]{2,1,0:T(8,128)(2,1)S(1)} %get-tuple-element.92), channel_id=1, source_target_pairs={{0,16},{4,20},{8,24},{12,28},{16,0},{20,4},{24,8},{28,12},{1,17},{... | collective-permute-start | bytes 393224 | tf_op jit(solution)/shard_map/ppermute | solution.py:93
  91.7 5.7 %collective-permute-start.31 = (bf16[2,128,256]{2,1,0:T(8,128)(2,1)S(1)}, bf16[2,128,256]{2,1,0:T(8,128)(2,1)S(1)}, u32[]{:S(2)}, u32[]{:S(2)}) collective-permute-start(bf16[2,128,256]{2,1,0:T(8,128)(2,1)S(1)} %get-tuple-element.93), channel_id=1, source_target_pairs={{0,20},{4,16},{8,28},{12,24},{16,4},{20,0},{24,12},{28,8},{1,21},{... | collective-permute-start | bytes 393224 | tf_op jit(solution)/shard_map/ppermute | solution.py:93
  93.6 7.2 %collective-permute-start.32 = (bf16[2,128,256]{2,1,0:T(8,128)(2,1)S(1)}, bf16[2,128,256]{2,1,0:T(8,128)(2,1)S(1)}, u32[]{:S(2)}, u32[]{:S(2)}) collective-permute-start(bf16[2,128,256]{2,1,0:T(8,128)(2,1)S(1)} %get-tuple-element.94), channel_id=1, source_target_pairs={{0,24},{4,28},{8,16},{12,20},{16,8},{20,12},{24,0},{28,4},{1,25},{... | collective-permute-start | bytes 393224 | tf_op jit(solution)/shard_map/ppermute | solution.py:93
  96.1 6.9 %collective-permute-start.33 = (bf16[2,128,256]{2,1,0:T(8,128)(2,1)S(1)}, bf16[2,128,256]{2,1,0:T(8,128)(2,1)S(1)}, u32[]{:S(2)}, u32[]{:S(2)}) collective-permute-start(bf16[2,128,256]{2,1,0:T(8,128)(2,1)S(1)} %get-tuple-element.95), channel_id=1, source_target_pairs={{0,28},{4,24},{8,20},{12,16},{16,12},{20,8},{24,4},{28,0},{1,29},{... | collective-permute-start | bytes 393224 | tf_op jit(solution)/shard_map/ppermute | solution.py:93
  (5 other events, 29.7 us)
